TPU v7x, 32 devices: a whole 2x2x4 slice. The times are simulated.
32 devices in a mesh: list: 4 (over z), fsdp: 8 (over y, x, core).
Axes of the slice: x: 2, y: 2, z: 4, core: 2. Of those that a mesh axis runs over, the one named last changes fastest.
Arguments:
- hidden: bfloat16 [512, 64, 2048], P(('list', 'fsdp')), may hold values from -6 to 6
- norm_gain: float32 [2048], replicated, may hold values from 0.5 to 1.5
- w_qkv: bfloat16 [2048, 1536], P('fsdp'), may hold values from -0.125 to 0.125
- w_out: bfloat16 [1024, 2048], P('fsdp'), may hold values from -0.1875 to 0.1875
- final_gain: float32 [2048], replicated, may hold values from 0.5 to 1.5
- w_score: float32 [2048], replicated, may hold values from -0.125 to 0.125
- prior: float32 [512], P(('list', 'fsdp')), may hold values from -8 to 400
- labels: int32 [512], P(('list', 'fsdp')), may hold values from 0 to 3
- lengths: int32 [16], replicated, may hold values from 1 to 48, 512 in all
Outputs:
- loss: float32 [], replicated
- grad_qkv: float32 [2048, 1536], P('fsdp', 'list')
- grad_out: float32 [1024, 2048], P('fsdp', 'list')
Inputs may be any that keep to these rules, and one draw needn't show every extreme that they name: `lengths`: the longest list holds exactly 48 passages.
All inputs are finite; a program needn't handle non-finite values.
Results may differ from a plain program's by a relative error of at most 0.025.
Values may be sent and summed in bfloat16 or wider, within the bound.
No kernel may reach another device: no remote copies, remote signals or barrier semaphores. Data moves between devices by JAX's collectives and lax.ppermute only.
A program may use at most 128 MiB of HBM per device.

v0:
```python
import jax
import jax.numpy as jnp
from jax import lax
from jax.sharding import PartitionSpec as P

HEADS = 16
KV_HEADS = 4
HEAD_DIM = 64
PASSAGE_LEN = 64


epsilon = 1e-05
loss_scale = 64.0


def combined_all(value, axis, join):
    pieces = jax.tree.map(lambda part: lax.all_gather(part, axis), value)
    head = jax.tree.map(lambda part: part[0], pieces)
    tail = jax.tree.map(lambda part: part[1:], pieces)
    so_far, _ = lax.scan(lambda so_far, slab: (join(so_far, slab), None), head, tail)
    return so_far


def normed(hidden, norm_gain):
    values = hidden.astype(jnp.float32)
    mean_square = jnp.mean(values * values, -1, keepdims=True)
    return (values * lax.rsqrt(mean_square + epsilon) * norm_gain).astype(jnp.bfloat16)


def attend(projected, passages):
    width_q = HEADS * HEAD_DIM
    width_k = KV_HEADS * HEAD_DIM
    ratio = HEADS // KV_HEADS
    query_part = projected[:, :width_q].reshape(passages, PASSAGE_LEN, KV_HEADS, ratio, HEAD_DIM)
    key_part = projected[:, width_q : width_q + width_k].reshape(
        passages, PASSAGE_LEN, KV_HEADS, HEAD_DIM
    )
    value_part = projected[:, width_q + width_k :].reshape(
        passages, PASSAGE_LEN, KV_HEADS, HEAD_DIM
    )
    scores = jnp.einsum(
        "bqgre,bkge->bgrqk", query_part, key_part, preferred_element_type=jnp.float32
    ) * HEAD_DIM ** (-0.5)
    peak = jnp.max(scores, -1, keepdims=True)
    expo = jnp.exp(scores - peak)
    probs = (expo / jnp.sum(expo, -1, keepdims=True)).astype(jnp.bfloat16)
    attended = jnp.einsum(
        "bgrqk,bkge->bqgre", probs, value_part, preferred_element_type=jnp.float32
    ).astype(jnp.bfloat16)
    return (
        query_part,
        key_part,
        value_part,
        probs,
        attended.reshape(passages, PASSAGE_LEN, width_q),
    )


def attend_back(query_part, key_part, value_part, probs, d_attended, passages):
    d_heads = d_attended.reshape(passages, KV_HEADS, HEADS // KV_HEADS, HEAD_DIM)
    d_probs = jnp.einsum("bgre,bkge->bgrk", d_heads, value_part, preferred_element_type=jnp.float32)
    probs_f = probs.astype(jnp.float32)
    inner = jnp.sum(probs_f * d_probs[:, :, :, None, :], -1, keepdims=True)
    d_scores = (probs_f * (d_probs[:, :, :, None, :] - inner) * HEAD_DIM ** (-0.5)).astype(
        jnp.bfloat16
    )
    d_query = jnp.einsum(
        "bgrqk,bkge->bqgre", d_scores, key_part, preferred_element_type=jnp.float32
    ).astype(jnp.bfloat16)
    d_key = jnp.einsum(
        "bgrqk,bqgre->bkge", d_scores, query_part, preferred_element_type=jnp.float32
    ).astype(jnp.bfloat16)
    d_value = jnp.einsum(
        "bgrqk,bgre->bkge", probs, d_heads, preferred_element_type=jnp.float32
    ).astype(jnp.bfloat16)
    rows = passages * PASSAGE_LEN
    return jnp.concatenate(
        [d_query.reshape(rows, -1), d_key.reshape(rows, -1), d_value.reshape(rows, -1)], 1
    )


def combine_stats(first, second):
    peak = jnp.maximum(first[0], second[0])
    total = first[1] * jnp.exp(first[0] - peak) + second[1] * jnp.exp(second[0] - peak)
    return (peak, total, first[2] + second[2])


def local(hidden, norm_gain, w_qkv, w_out, final_gain, w_score, prior, labels, lengths):
    passages = hidden.shape[0]
    width = hidden.shape[2]
    normal_rows = normed(hidden, norm_gain).reshape(passages * PASSAGE_LEN, width)
    full_qkv, full_out = (
        lax.all_gather(w_qkv, "fsdp", axis=0, tiled=True),
        lax.all_gather(w_out, "fsdp", axis=0, tiled=True),
    )
    projected = jnp.dot(normal_rows, full_qkv, preferred_element_type=jnp.float32).astype(
        jnp.bfloat16
    )
    query_part, key_part, value_part, probs, attended = attend(projected, passages)
    mixed = jnp.dot(
        attended.reshape(passages * PASSAGE_LEN, -1), full_out, preferred_element_type=jnp.float32
    )
    residual = hidden.astype(jnp.float32) + mixed.reshape(passages, PASSAGE_LEN, width)
    pooled = jnp.mean(residual, 1)
    inverse = lax.rsqrt(jnp.mean(pooled * pooled, -1, keepdims=True) + epsilon)
    unit = pooled * inverse
    score = jnp.sum(unit * final_gain * w_score, -1) + prior
    queries = lengths.shape[0]
    position = lax.axis_index(("list", "fsdp")) * passages + jnp.arange(passages, dtype=jnp.int32)
    ends = jnp.cumsum(lengths)
    owner = jnp.sum((position[:, None] >= ends[None, :]).astype(jnp.int32), 1)
    member = (owner[:, None] == jnp.arange(queries, dtype=jnp.int32)[None, :]).astype(jnp.float32)
    label_weight = jnp.exp(labels.astype(jnp.float32))
    label_local = jnp.sum(member * label_weight[:, None], 0)
    local_peak = jnp.max(jnp.where(member > 0, score[:, None], -1e30), 0)
    own_peak = jnp.sum(member * local_peak[None, :], 1)
    expo_local = jnp.sum(member * jnp.exp(score - own_peak)[:, None], 0)
    peak, total, label_total = combined_all(
        (local_peak, expo_local, label_local), ("list", "fsdp"), combine_stats
    )
    log_norm = peak + jnp.log(total)
    log_prob = score - jnp.sum(member * log_norm[None, :], 1)
    target = label_weight / jnp.sum(member * label_total[None, :], 1)
    loss = lax.psum(-loss_scale * jnp.sum(target * log_prob), ("list", "fsdp"))
    d_score = loss_scale * (jnp.exp(log_prob) - target)
    d_unit = d_score[:, None] * w_score[None, :] * final_gain[None, :]
    d_pooled = inverse * (d_unit - unit * jnp.mean(d_unit * unit, -1, keepdims=True))
    d_rows = (d_pooled / PASSAGE_LEN).astype(jnp.bfloat16)
    attn_sum = jnp.sum(attended, 1, dtype=jnp.float32).astype(jnp.bfloat16)
    d_attended = lax.dot_general(
        d_rows, full_out, (((1,), (1,)), ((), ())), preferred_element_type=jnp.float32
    ).astype(jnp.bfloat16)
    d_projected = attend_back(query_part, key_part, value_part, probs, d_attended, passages)
    columns = normal_rows
    qkv_part = lax.psum_scatter(
        lax.dot_general(
            columns, d_projected, (((0,), (0,)), ((), ())), preferred_element_type=jnp.float32
        ).astype(jnp.bfloat16),
        "fsdp",
        scatter_dimension=0,
        tiled=True,
    )
    columns = attn_sum
    out_part = lax.psum_scatter(
        lax.dot_general(
            columns, d_rows, (((0,), (0,)), ((), ())), preferred_element_type=jnp.float32
        ).astype(jnp.bfloat16),
        "fsdp",
        scatter_dimension=0,
        tiled=True,
    )
    grad_qkv, grad_out = (
        lax.psum_scatter(qkv_part, "list", scatter_dimension=1, tiled=True).astype(jnp.float32),
        lax.psum_scatter(out_part, "list", scatter_dimension=1, tiled=True).astype(jnp.float32),
    )
    return (loss, grad_qkv, grad_out)


def solution(mesh):
    placed = (
        P(("list", "fsdp"), None, None),
        P(),
        P("fsdp", None),
        P("fsdp", None),
        P(),
        P(),
        P(("list", "fsdp")),
        P(("list", "fsdp")),
        P(),
    )
    return jax.shard_map(
        local,
        mesh=mesh,
        in_specs=placed,
        out_specs=(P(), P("fsdp", "list"), P("fsdp", "list")),
        check_vma=False,
    )
```

profile of v0, /device:TPU:0, one launch (start us, length us, event | category | flops | bytes accessed | tf_op | source)
XLA Modules:
  0.0 344.6 jit_solution(1498260265201764673)
XLA Ops:
  9.8 3.2 fusion.10
  13.1 3.0 fusion.12
  16.1 42.1 %all-gather.6.cloned.1.call-done = bf16[2048,1536]{1,0:T(8,128)(2,1)} async-done(((bf16[256,1536]{1,0:T(8,128)(2,1)}), bf16[2048,1536]{1,0:T(8,128)(2,1)}) %all-gather.6.cloned.1.call-update) | async-done | bytes 6291472 | tf_op jit(solution)/shard_map/all_gather | solution.py:93
  58.1 10.0 %convolution_convert_fusion.1 = bf16[1024,1536]{1,0:T(8,128)(2,1)S(1)} fusion(bf16[1024,2048]{1,0:T(8,128)(2,1)} %bitcast.84, bf16[2048,1536]{1,0:T(8,128)(2,1)} %all-gather.6.cloned.1.call-done), kind=kOutput, calls=%fused_computation.38 | convolution fusion | flops 6444023808 | bytes 13631488 | tf_op jit(solution)/shard_map/dot_general | solution.py:96
  68.5 1.0 fusion.50
  69.5 2.0 reshape.102
  71.6 1.3 copy.67
  72.9 4.0 %reshape.103 = bf16[16,64,4,4,64]{4,3,2,1,0:T(4,128)(2,1)} reshape(bf16[1024,1024]{1,0:T(8,128)(2,1)S(1)} %slice.44) | data formatting | bytes 4194304 | tf_op jit(solution)/shard_map/reshape | solution.py:34
  76.9 8.4 %copy.60 = bf16[16,64,4,4,64]{1,4,3,2,0:T(8,128)(2,1)} copy(bf16[16,64,4,4,64]{4,3,2,1,0:T(4,128)(2,1)} %reshape.103) | data formatting | bytes 4194304 | tf_op jit(solution)/shard_map/reshape | solution.py:34
  85.7 8.6 %fusion.51 = (f32[16,4,4,64]{3,2,1,0:T(4,128)S(1)}, f32[16,4,4,64,64]{3,4,2,1,0:T(8,128)}) fusion(bf16[16,64,4,64,1]{1,3,4,2,0:T(8,128)(2,1)S(1)} %copy-done.2, bf16[16,64,4,4,64]{1,4,3,2,0:T(8,128)(2,1)} %copy.60), kind=kOutput, calls=%fused_computation.88 | convolution fusion | flops 137363520 | bytes 6881280 | tf_op jit(solution)/shard_map/sub | solution.py:45
  94.4 5.7 %convert_reduce_fusion = (bf16[16,4,4,64]{3,2,1,0:T(4,128)(2,1)S(1)}, bf16[16,4,4,64,64]{3,4,2,1,0:T(8,128)(2,1)S(1)}) fusion(f32[16,4,4,64,64]{3,4,2,1,0:T(8,128)} %get-tuple-element.78, f32[16,4,4,64]{3,2,1,0:T(4,128)S(1)} %get-tuple-element.77), kind=kLoop, calls=%fused_computation.12 | loop fusion | flops 4177920 | bytes 6389760 | tf_op jit(solution)/shard_map/bgrqk,bgre->bkge/reduce_sum | solution.py:73
  100.1 2.1 fusion.52
  102.3 5.4 %copy.55 = bf16[16,64,4,4,64]{4,3,2,1,0:T(4,128)(2,1)} copy(bf16[16,64,4,4,64]{4,1,3,2,0:T(8,128)(2,1)S(1)} %get-tuple-element.80) | data formatting | bytes 4194304 | tf_op jit(solution)/shard_map/convert_element_type | solution.py:49
  107.7 7.9 %dot_general.38 = bf16[16,64,1024]{2,1,0:T(8,128)(2,1)} reshape(bf16[16,64,4,4,64]{4,3,2,1,0:T(4,128)(2,1)} %copy.55) | data formatting | bytes 4194304 | tf_op jit(solution)/shard_map/dot_general | solution.py:100
  115.6 8.6 %fusion.13 = f32[16,2048]{1,0:T(8,128)S(1)} fusion(bf16[16,64,2048]{2,1,0:T(8,128)(2,1)} %param.11, bf16[16,64,1024]{2,1,0:T(8,128)(2,1)} %dot_general.38, bf16[1024,2048]{1,0:T(8,128)(2,1)} %all-gather.8.cloned.1.call-done), kind=kOutput, calls=%fused_computation.22 | convolution fusion | flops 4301225984 | bytes 10616832 | tf_op jit(solution)/shard_map/dot_general | solution.py:100
  125.7 39.4 %all-reduce.3 = (f32[512]{0:T(512)S(1)}, f32[512]{0:T(512)S(1)}, f32[512]{0:T(512)S(1)}) all-reduce(f32[512]{0:T(512)S(1)} %dynamic-update-slice, f32[512]{0:T(512)S(1)} %dynamic-update-slice.1, f32[512]{0:T(512)S(1)} %dynamic-update-slice.2), channel_id=2, replica_groups=mesh['list'=4,'fsdp'=8] {'list','fsdp'}, use_global_device_ids=true, to_apply=%add | all-reduce | flops 1536 | bytes 12288
  165.6 1.3 while.14
  167.4 3.2 convolution_convert_fusion.2
  170.7 3.4 convolution_convert_fusion.4
  175.4 1.5 reshape.107
  177.6 9.4 %fusion.34 = bf16[16,64,4,64]{1,3,2,0:T(8,128)(2,1)S(1)} fusion(bf16[16,64,4,4,64]{1,4,3,2,0:T(8,128)(2,1)} %copy.60, bf16[16,4,4,64,64]{3,4,2,1,0:T(8,128)(2,1)} %copy-done, f32[16,4,4,64]{3,2,1,0:T(4,128)S(1)} %fusion.37), kind=kOutput, calls=%fused_computation.49 | convolution fusion | flops 141836352 | bytes 4784128 | tf_op jit(solution)/shard_map/bgrqk,bqgre->bkge/dot_general | solution.py:70
  187.7 1.6 reshape.106
  189.3 9.0 %convert_bitcast_fusion = bf16[16,64,4,4,64]{1,4,3,2,0:T(8,128)(2,1)} fusion(bf16[16,64,4,64,1]{1,3,4,2,0:T(8,128)(2,1)S(1)} %copy-done.2, bf16[16,4,4,64,64]{3,4,2,1,0:T(8,128)(2,1)} %copy-done, f32[16,4,4,64]{3,2,1,0:T(4,128)S(1)} %fusion.37), kind=kOutput, calls=%fused_computation.34 | convolution fusion | flops 142622784 | bytes 4784128 | tf_op jit(solution)/shard_map/bgrqk,bkge->bqgre/dot_general | solution.py:67
  198.2 7.7 %copy.59 = bf16[16,64,4,4,64]{1,0,4,3,2:T(8,128)(2,1)} copy(bf16[16,64,4,4,64]{1,4,3,2,0:T(8,128)(2,1)} %convert_bitcast_fusion) | data formatting | bytes 4194304 | tf_op jit(solution)/shard_map/convert_element_type | solution.py:69
  205.9 5.6 %reshape.105 = bf16[1024,1024]{0,1:T(8,128)(2,1)S(1)} reshape(bf16[16,64,4,4,64]{1,0,4,3,2:T(8,128)(2,1)} %copy.59) | data formatting | bytes 4194304 | tf_op jit(solution)/shard_map/reshape | solution.py:78
  211.5 12.1 %convolution_convert_fusion = bf16[2048,1536]{1,0:T(8,128)(2,1)} fusion(bf16[1024,2048]{1,0:T(8,128)(2,1)} %bitcast.85, bf16[1024,256]{0,1:T(8,128)(2,1)S(1)} %copy-done.4, bf16[1024,256]{0,1:T(8,128)(2,1)S(1)} %copy-done.5, bf16[1024,1024]{0,1:T(8,128)(2,1)S(1)} %reshape.105), kind=kOutput, calls=%fused_computation.30 | convolution fusion | flops 6455033856 | bytes 13631488 | tf_op jit(solution)/shard_map/dot_general | solution.py:136
  224.3 63.7 %reduce-scatter.7.cloned.1.call-done = bf16[256,1536]{1,0:T(8,128)(2,1)} async-done(((bf16[2048,1536]{1,0:T(8,128)(2,1)}), bf16[256,1536]{1,0:T(8,128)(2,1)}) %reduce-scatter.7.cloned.1.call-update) | async-done | bytes 786448 | tf_op jit(solution)/shard_map/reduce_scatter | solution.py:135
  288.0 2.3 copy.77
  291.6 39.3 %psum.7 = f32[]{:T(128)} all-reduce(f32[]{:T(128)S(6)} %mul_shard_map.3), channel_id=1, replica_groups=mesh['list'=4,'fsdp'=8] {'list','fsdp'}, use_global_device_ids=true, to_apply=%region_17.18 | all-reduce | flops 1 | bytes 8 | tf_op jit(solution)/shard_map/psum | solution.py:124
  330.9 1.6 convert_element_type.95
  332.6 3.1 reduce-scatter.13.cloned.1.call-done
  335.7 1.1 copy.78
  (112 shorter events, 11.3 us)
Async XLA Ops:
  7.2 5.9 %copy-start.8 = (f32[2048]{0:T(1024)S(1)}, f32[2048]{0:T(1024)}, u32[]{:S(2)}) copy-start(f32[2048]{0:T(1024)} %param.12) | copy-start | bytes 24580
  7.2 51.0 %all-gather.6.cloned.1.call-start = ((), (), s32[]{:S(2)}) async-start(), calls=%async_computation.4 | async-start | bytes 7077888 | tf_op jit(solution)/shard_map/all_gather | solution.py:93
  7.9 107.7 %all-gather.8.cloned.1.call-start = ((), (), s32[]{:S(2)}) async-start(), calls=%async_computation.5 | async-start | bytes 4718592 | tf_op jit(solution)/shard_map/all_gather | solution.py:94
  8.7 215.1 %reduce-scatter.9.cloned.1.call-start = ((), (), s32[]{:S(2)}) async-start(), calls=%async_computation.7 | async-start | bytes 4718592 | tf_op jit(solution)/shard_map/reduce_scatter | solution.py:144
  9.6 3.5 %copy-start.1 = (bf16[16,64,2048]{2,1,0:T(8,128)(2,1)S(1)}, bf16[16,64,2048]{2,1,0:T(8,128)(2,1)}, u32[]{:S(2)}) copy-start(bf16[16,64,2048]{2,1,0:T(8,128)(2,1)} %param.11) | copy-start | bytes 12582916
  76.9 8.4 %copy-start.3 = (bf16[1024,256]{1,0:T(8,128)(2,1)S(1)}, bf16[1024,256]{1,0:T(8,128)(2,1)}, u32[]{:S(2)}) copy-start(bf16[1024,256]{1,0:T(8,128)(2,1)} %get-tuple-element.73) | copy-start | bytes 1572868
  76.9 8.8 %copy-start.2 = (bf16[16,64,4,64,1]{1,3,4,2,0:T(8,128)(2,1)S(1)}, bf16[16,64,4,64,1]{1,3,4,2,0:T(8,128)(2,1)}, u32[]{:S(2)}) copy-start(bf16[16,64,4,64,1]{1,3,4,2,0:T(8,128)(2,1)} %copy.67) | copy-start | bytes 1572868
  100.1 2.2 copy-start
  115.6 8.8 %copy-start.6 = (f32[2048]{0:T(1024)S(1)}, f32[2048]{0:T(1024)}, u32[]{:S(2)}) copy-start(f32[2048]{0:T(1024)} %param.16) | copy-start | bytes 24580
  115.6 8.8 %copy-start.7 = (f32[2048]{0:T(1024)S(1)}, f32[2048]{0:T(1024)}, u32[]{:S(2)}) copy-start(f32[2048]{0:T(1024)} %param.15) | copy-start | bytes 24580
  115.6 9.0 %copy-start.10 = (f32[16]{0:T(128)S(1)}, f32[16]{0:T(128)}, u32[]{:S(2)}) copy-start(f32[16]{0:T(128)} %param.17) | copy-start | bytes 196
  115.6 9.5 %copy-start.9 = (s32[16]{0:T(128)S(1)}, s32[16]{0:T(128)}, u32[]{:S(2)}) copy-start(s32[16]{0:T(128)} %param.18) | copy-start | bytes 196
  170.7 117.3 %reduce-scatter.7.cloned.1.call-start = ((), (), s32[]{:S(2)}) async-start(), calls=%async_computation.6 | async-start | bytes 7077888 | tf_op jit(solution)/shard_map/reduce_scatter | solution.py:135
  205.9 5.6 %copy-start.4 = (bf16[1024,256]{0,1:T(8,128)(2,1)S(1)}, bf16[1024,256]{0,1:T(8,128)(2,1)}, u32[]{:S(2)}) copy-start(bf16[1024,256]{0,1:T(8,128)(2,1)} %reshape.107) | copy-start | bytes 1572868
  205.9 5.6 %copy-start.5 = (bf16[1024,256]{0,1:T(8,128)(2,1)S(1)}, bf16[1024,256]{0,1:T(8,128)(2,1)}, u32[]{:S(2)}) copy-start(bf16[1024,256]{0,1:T(8,128)(2,1)} %reshape.106) | copy-start | bytes 1572868
  223.7 107.2 %reduce-scatter.11.cloned.1.call-start = ((), (), s32[]{:S(2)}) async-start(), calls=%async_computation.8 | async-start | bytes 655360 | tf_op jit(solution)/shard_map/reduce_scatter | solution.py:154
  224.3 111.4 %reduce-scatter.13.cloned.1.call-start = ((), (), s32[]{:S(2)}) async-start(), calls=%async_computation.9 | async-start | bytes 983040
Sparse Core Ops, SparseCore 0:
  9.9 48.2 all-gather.5
  60.0 36.7 all-gather.7
  170.8 51.7 reduce-scatter.8
  226.2 61.7 reduce-scatter.6
  290.1 21.6 reduce-scatter.10
  314.0 21.6 reduce-scatter.12
where the time goes:
time: 351 us; the launch traced here: 345 us
  waiting for transfers between devices  111 us (32%)
  blocking collectives  78.8 us (22%)
  matrix products  67.6 us (19%)
  local copies, waits for them, and re-layouts  54.1 us (15%)
  other arithmetic  17.3 us (5%)
  between operations  15.2 us (4%)
    reduce_scatter x1, waiting for transfers between devices, local(): lax.psum_scatter(lax.dot_general(columns, d_projected, (((0,), (0,)), (()...  63.7 us
    all_gather x1, waiting for transfers between devices, local(): lax.all_gather(w_qkv, 'fsdp', axis=0, tiled=True)  42.1 us
    unnamed x1, blocking collectives  39.4 us
    psum x1, blocking collectives, local(): loss = lax.psum(-loss_scale * jnp.sum(target * log_prob), ('list', 'fsdp'))  39.3 us
    reshape x2, local copies, waits for them, and re-layouts, attend(): projected[:, :width_q]  12.4 us
    dot_general x1, matrix products, local(): lax.dot_general(columns, d_projected, (((0,), (0,)), ((), ())), preferred...  12.1 us
    dot_general x1, matrix products, local(): jnp.dot(normal_rows, full_qkv, preferred_element_type=jnp.float32)  10 us
    dot_general x1, matrix products, attend_back(): jnp.einsum('bgrqk,bqgre->bkge', d_scores, query_part, preferred_element_t...  9.38 us
  transfers between devices with their start and end apart: 6, of which 3 were waited for; matrix products, arithmetic and copies ran while one was open for 35% of the time, Pallas kernels for 0%

commit v1 on v0

v1 whole, which is shorter than its diff:
```python
import functools

import jax
import jax.numpy as jnp
from jax import lax
from jax.experimental import pallas as pl
from jax.experimental.pallas import tpu as pltpu
from jax.sharding import PartitionSpec as P

HEADS = 16
KV_HEADS = 4
HEAD_DIM = 64
PASSAGE_LEN = 64
LONGEST = 48
RATIO = HEADS // KV_HEADS
GROUP = RATIO * HEAD_DIM

epsilon = 1e-05
loss_scale = 64.0
scale = HEAD_DIM ** (-0.5)
VMEM = 48 * 1024 * 1024
BF16 = jnp.bfloat16
F32 = jnp.float32


def params(grid=1):
    return pltpu.CompilerParams(
        vmem_limit_bytes=VMEM, dimension_semantics=("arbitrary",) * grid
    )


def mm(a, b, dims=((1,), (0,))):
    return lax.dot_general(a, b, (dims, ((), ())), preferred_element_type=F32)


def norm_kernel(hidden_ref, gain_ref, normal_ref, sum_ref):
    values = hidden_ref[...].astype(F32)
    mean_square = jnp.mean(values * values, -1, keepdims=True)
    out = values * lax.rsqrt(mean_square + epsilon) * gain_ref[...][None]
    normal_ref[...] = out.astype(BF16)
    sum_ref[0] = jnp.sum(values, 1)


def norm(hidden, gain):
    passages, length, width = hidden.shape
    step = 4 if passages % 4 == 0 else 1
    steps = passages // step
    normal, sums = pl.pallas_call(
        norm_kernel,
        grid=(steps,),
        in_specs=[
            pl.BlockSpec((step, length, width), lambda i: (i, 0, 0)),
            pl.BlockSpec((1, width), lambda i: (0, 0)),
        ],
        out_specs=[
            pl.BlockSpec((step, length, width), lambda i: (i, 0, 0)),
            pl.BlockSpec((1, step, width), lambda i: (i, 0, 0)),
        ],
        out_shape=[
            jax.ShapeDtypeStruct((passages, length, width), BF16),
            jax.ShapeDtypeStruct((steps, step, width), F32),
        ],
        compiler_params=params(),
        cost_estimate=pl.CostEstimate(
            flops=6 * hidden.size, bytes_accessed=4 * hidden.size, transcendentals=0
        ),
        name="norm_rows",
    )(hidden, gain[None])
    return normal.reshape(passages * length, width), sums.reshape(passages, width)


def block_mask(rows, cols):
    row = lax.broadcasted_iota(jnp.int32, (rows, cols), 0) // HEAD_DIM
    col = lax.broadcasted_iota(jnp.int32, (rows, cols), 1) // HEAD_DIM
    return row == col


def doubled(pair, low):
    wide = pair.astype(F32)
    turned = pltpu.roll(wide, HEAD_DIM, 1)
    return jnp.where(low, wide, turned).astype(BF16), jnp.where(low, turned, wide).astype(BF16)


def spread(double, mask):
    row = jnp.concatenate([double] * (RATIO // 2), 1)
    return jnp.where(mask, jnp.concatenate([row] * RATIO, 0), jnp.zeros((), BF16))


def low_lanes():
    return lax.broadcasted_iota(jnp.int32, (HEAD_DIM, 2 * HEAD_DIM), 1) < HEAD_DIM


def segment_max(scores, low):
    tiles = []
    for start in range(0, scores.shape[1], 2 * HEAD_DIM):
        tile = scores[:, start : start + 2 * HEAD_DIM]
        first = jnp.max(jnp.where(low, tile, -jnp.inf), 1, keepdims=True)
        second = jnp.max(jnp.where(low, -jnp.inf, tile), 1, keepdims=True)
        tiles.append(jnp.where(low, first, second))
    return jnp.concatenate(tiles, 1)


def forward_kernel(pieces, groups, where_ref, rows_ref, *refs):
    weights = refs[: 2 * pieces]
    projected_ref, probs_ref, sum_ref = refs[2 * pieces :]
    chip = where_ref[0]
    depth = weights[0].shape[0]
    first, second = None, None
    for s in range(pieces):
        start = pl.multiple_of((chip ^ s) * depth, depth)
        block = rows_ref[:, pl.ds(start, depth)]
        a, b = mm(block, weights[2 * s][...]), mm(block, weights[2 * s + 1][...])
        first = a if first is None else first + a
        second = b if second is None else second + b
    projected = jnp.concatenate([first, second], 1).astype(BF16)
    projected_ref[...] = projected
    low = low_lanes()
    mask = block_mask(GROUP, GROUP)
    ones = jnp.where(mask, 1.0, 0.0).astype(BF16)
    width_q = groups * GROUP
    width_k = groups * HEAD_DIM
    for i in range(rows_ref.shape[0] // PASSAGE_LEN):
        rows = slice(i * PASSAGE_LEN, (i + 1) * PASSAGE_LEN)
        keys = doubled(projected[rows, width_q : width_q + width_k], low)
        values = doubled(projected[rows, width_q + width_k :], low)
        for g in range(groups):
            cols = slice(g * GROUP, (g + 1) * GROUP)
            scores = mm(projected[rows, cols], spread(keys[g], mask), ((1,), (1,))) * scale
            expo = jnp.exp(scores - segment_max(scores, low))
            total = mm(expo.astype(BF16), ones)
            probs = (expo / total).astype(BF16)
            probs_ref[rows, cols] = probs
            attended = mm(probs, spread(values[g], mask)).astype(BF16).astype(F32)
            sum_ref[0, i : i + 1, cols] = jnp.sum(attended, 0, keepdims=True)


def forward(where, rows, weights, groups):
    total, width = rows.shape
    pieces = len(weights)
    flat = [part for s in range(pieces) for part in weights[s]]
    out_width = flat[0].shape[1] + flat[1].shape[1]
    step = 4 * PASSAGE_LEN if total % (4 * PASSAGE_LEN) == 0 else PASSAGE_LEN
    steps, per = total // step, step // PASSAGE_LEN
    heads = groups * GROUP
    projected, probs, sums = pl.pallas_call(
        functools.partial(forward_kernel, pieces, groups),
        grid_spec=pltpu.PrefetchScalarGridSpec(
            num_scalar_prefetch=1,
            grid=(steps,),
            in_specs=[pl.BlockSpec((step, width), lambda i, w: (i, 0))]
            + [pl.BlockSpec(part.shape, lambda i, w: (0, 0)) for part in flat],
            out_specs=[
                pl.BlockSpec((step, out_width), lambda i, w: (i, 0)),
                pl.BlockSpec((step, heads), lambda i, w: (i, 0)),
                pl.BlockSpec((1, per, heads), lambda i, w: (i, 0, 0)),
            ],
        ),
        out_shape=[
            jax.ShapeDtypeStruct((total, out_width), BF16),
            jax.ShapeDtypeStruct((total, heads), BF16),
            jax.ShapeDtypeStruct((steps, per, heads), F32),
        ],
        compiler_params=params(),
        cost_estimate=pl.CostEstimate(
            flops=2 * total * width * out_width,
            bytes_accessed=2 * (rows.size + width * out_width + total * (out_width + heads)),
            transcendentals=total * heads,
        ),
        name="project_attend",
    )(where, rows, *flat)
    return projected, probs, sums.reshape(steps * per, heads)


def folded(first, second, low):
    half = HEAD_DIM
    kept = jnp.where(low, first[:half], first[half:]) + jnp.where(low, second[:half], second[half:])
    return kept + pltpu.roll(kept, half, 1)


def backward_kernel(groups, probs_ref, projected_ref, d_ref, out_ref):
    low = low_lanes()
    mask = block_mask(GROUP, GROUP)
    ones = jnp.where(mask, 1.0, 0.0).astype(BF16)
    width_q = groups * GROUP
    width_k = groups * HEAD_DIM
    half = GROUP // 2
    for i in range(probs_ref.shape[0] // PASSAGE_LEN):
        rows = slice(i * PASSAGE_LEN, (i + 1) * PASSAGE_LEN)
        keys = doubled(projected_ref[rows, width_q : width_q + width_k], low)
        values = doubled(projected_ref[rows, width_q + width_k :], low)
        d_keys, d_values = [], []
        for g in range(groups):
            cols = slice(g * GROUP, (g + 1) * GROUP)
            probs = probs_ref[rows, cols]
            queries = projected_ref[rows, cols]
            d_rows = jnp.broadcast_to(d_ref[0, i : i + 1, cols], (PASSAGE_LEN, GROUP)).astype(BF16)
            d_probs = mm(d_rows[:16], spread(values[g], mask), ((1,), (1,)))[:1]
            probs_f = probs.astype(F32)
            product = probs_f * d_probs
            upper = product.astype(BF16)
            lower = (product - upper.astype(F32)).astype(BF16)
            inner = mm(upper, ones) + mm(lower, ones)
            d_scores = (probs_f * (d_probs - inner) * scale).astype(BF16)
            out_ref[rows, cols] = mm(d_scores, spread(keys[g], mask)).astype(BF16)
            down = ((0,), (0,))
            d_keys.append(
                folded(
                    mm(d_scores[:, :half], queries[:, :half], down),
                    mm(d_scores[:, half:], queries[:, half:], down),
                    low,
                )
            )
            d_values.append(
                folded(
                    mm(probs[:, :half], d_rows[:, :half], down),
                    mm(probs[:, half:], d_rows[:, half:], down),
                    low,
                )
            )
        out_ref[rows, width_q : width_q + width_k] = jnp.where(low, *d_keys).astype(BF16)
        out_ref[rows, width_q + width_k :] = jnp.where(low, *d_values).astype(BF16)


def backward(probs, projected, d_attended, groups):
    total, heads = probs.shape
    out_width = projected.shape[1]
    step = 4 * PASSAGE_LEN if total % (4 * PASSAGE_LEN) == 0 else PASSAGE_LEN
    steps, per = total // step, step // PASSAGE_LEN
    return pl.pallas_call(
        functools.partial(backward_kernel, groups),
        grid=(steps,),
        in_specs=[
            pl.BlockSpec((step, heads), lambda i: (i, 0)),
            pl.BlockSpec((step, out_width), lambda i: (i, 0)),
            pl.BlockSpec((1, per, heads), lambda i: (i, 0, 0)),
        ],
        out_specs=pl.BlockSpec((step, out_width), lambda i: (i, 0)),
        out_shape=jax.ShapeDtypeStruct((total, out_width), BF16),
        compiler_params=params(),
        cost_estimate=pl.CostEstimate(
            flops=16 * total * heads * GROUP,
            bytes_accessed=2 * total * (heads + 2 * out_width),
            transcendentals=0,
        ),
        name="attend_back",
    )(probs, projected, d_attended.astype(F32).reshape(steps, per, heads))


def score_kernel(where_ref, mine_ref, other_ref, sum_ref, w_ref, final_ref, ws_ref, prior_ref,
                 unit_ref, inverse_ref, score_ref, attn_ref):
    core = where_ref[1]
    mine, other = mine_ref[...], other_ref[...]
    attn = jnp.concatenate(
        [jnp.where(core == 0, mine, other), jnp.where(core == 0, other, mine)], 1
    )
    count = attn.shape[0]
    upper = attn.astype(BF16)
    lower = (attn - upper.astype(F32)).astype(BF16)
    product = mm(jnp.concatenate([upper, lower], 0), w_ref[...])
    pooled = (sum_ref[...] + product[:count] + product[count:]) * (1.0 / PASSAGE_LEN)
    inverse = lax.rsqrt(jnp.mean(pooled * pooled, -1, keepdims=True) + epsilon)
    unit = pooled * inverse
    score = jnp.sum(unit * (final_ref[...] * ws_ref[...]), -1, keepdims=True)
    unit_ref[...] = unit
    inverse_ref[...] = jnp.broadcast_to(inverse, inverse_ref.shape)
    score_ref[...] = score + prior_ref[...]
    attn_ref[...] = upper


def score_pass(where, mine, other, sums, w_out, final_gain, w_score, prior):
    count, width = sums.shape
    lanes = prior.shape[1]
    inner = w_out.shape[0]
    vmem = pl.BlockSpec(memory_space=pltpu.VMEM)
    return pl.pallas_call(
        score_kernel,
        in_specs=[pl.BlockSpec(memory_space=pltpu.SMEM)] + [vmem] * 7,
        out_specs=[vmem] * 4,
        out_shape=[
            jax.ShapeDtypeStruct((count, width), F32),
            jax.ShapeDtypeStruct((count, lanes), F32),
            jax.ShapeDtypeStruct((count, lanes), F32),
            jax.ShapeDtypeStruct((count, inner), BF16),
        ],
        compiler_params=pltpu.CompilerParams(vmem_limit_bytes=VMEM),
        cost_estimate=pl.CostEstimate(
            flops=4 * count * width * inner, bytes_accessed=2 * w_out.size, transcendentals=0
        ),
        name="pool_score",
    )(where, mine, other, sums, w_out, final_gain[None], w_score[None], prior)


def list_kernel(blocks, passages, where_ref, place_ref, bounds_ref, unit_ref, inverse_ref, w_ref,
                final_ref, ws_ref, *refs):
    scores = [ref[...] for ref in refs[:blocks]]
    weights = [ref[...] for ref in refs[blocks : 2 * blocks]]
    d_rows_ref, d_att_ref, loss_ref = refs[2 * blocks :]
    core = where_ref[1]
    starts, ends = bounds_ref[0:1], bounds_ref[1:2]
    pair = 2 * passages
    lanes = starts.shape[1]
    row = lax.broadcasted_iota(jnp.int32, (pair, lanes), 0)
    offset = jnp.where(
        row < passages, core * passages + row, (1 - core) * passages + row - passages
    )
    members = []
    for j in range(blocks):
        place = place_ref[j] * pair + offset
        members.append((place >= starts) & (place < ends))
    column = [jnp.broadcast_to(score[:, :1], (pair, lanes)) for score in scores]
    heavy = [jnp.broadcast_to(weight[:, :1], (pair, lanes)) for weight in weights]
    peak = functools.reduce(
        jnp.maximum,
        [jnp.max(jnp.where(m, s, -1e30), 0, keepdims=True) for m, s in zip(members, column)],
    )
    total = sum(
        jnp.sum(jnp.where(m, jnp.exp(jnp.where(m, s - peak, 0.0)), 0.0), 0, keepdims=True)
        for m, s in zip(members, column)
    )
    label_total = sum(
        jnp.sum(jnp.where(m, w, 0.0), 0, keepdims=True) for m, w in zip(members, heavy)
    )
    log_norm = peak + jnp.log(total)
    own = members[0]
    log_prob = column[0][:, :1] - jnp.sum(jnp.where(own, log_norm, 0.0), 1, keepdims=True)
    target = heavy[0][:, :1] / jnp.sum(jnp.where(own, label_total, 0.0), 1, keepdims=True)
    loss = -loss_scale * jnp.sum((target * log_prob)[:passages], 0, keepdims=True)
    loss_ref[...] = jnp.broadcast_to(loss, loss_ref.shape)
    d_score = loss_scale * (jnp.exp(log_prob) - target)
    unit = unit_ref[...]
    d_unit = d_score * (ws_ref[...] * final_ref[...])
    mean = jnp.mean(d_unit * unit, -1, keepdims=True)
    d_pooled = inverse_ref[:, :1] * (d_unit - unit * mean)
    d_rows = (d_pooled * (1.0 / PASSAGE_LEN)).astype(BF16)
    d_rows_ref[...] = d_rows
    d_att = mm(d_rows, w_ref[...], ((1,), (1,))).astype(BF16).astype(F32)
    half = d_att.shape[1] // 2
    d_att_ref[...] = jnp.where(core == 0, d_att[:, :half], d_att[:, half:])


def list_pass(where, places, bounds, unit, inverse, w_out, final_gain, w_score, scores, weights,
              passages):
    count, width = unit.shape
    inner = w_out.shape[0]
    vmem = pl.BlockSpec(memory_space=pltpu.VMEM)
    smem = pl.BlockSpec(memory_space=pltpu.SMEM)
    return pl.pallas_call(
        functools.partial(list_kernel, len(scores), passages),
        in_specs=[smem] * 2 + [vmem] * (6 + 2 * len(scores)),
        out_specs=[vmem] * 3,
        out_shape=[
            jax.ShapeDtypeStruct((count, width), BF16),
            jax.ShapeDtypeStruct((count, inner // 2), F32),
            jax.ShapeDtypeStruct((8, 128), F32),
        ],
        compiler_params=pltpu.CompilerParams(vmem_limit_bytes=VMEM),
        cost_estimate=pl.CostEstimate(
            flops=2 * count * width * inner, bytes_accessed=2 * w_out.size, transcendentals=count
        ),
        name="list_grad",
    )(where, places, bounds, unit, inverse, w_out, final_gain[None], w_score[None], *scores,
      *weights)


def grad_kernel(where_ref, own_ref, sib_ref, d_own_ref, d_sib_ref, a_ref, b_ref):
    down = ((0,), (0,))
    out = mm(own_ref[...], d_own_ref[...], down) + mm(sib_ref[...], d_sib_ref[...], down)
    out = out.astype(BF16)
    a_ref[...] = out[:, : a_ref.shape[1]]
    b_ref[...] = out[:, a_ref.shape[1] :]


def grad_block(where, s, own, sib, d_own, d_sib, depth):
    rows = own.shape[0]
    width = d_own.shape[1]
    tile = min(depth, 256)
    tiles = depth // tile
    part = width // 2

    def lhs(i, w):
        return (0, (w[0] ^ s) * tiles + i)

    whole = lambda i, w: (0, 0)
    return pl.pallas_call(
        grad_kernel,
        grid_spec=pltpu.PrefetchScalarGridSpec(
            num_scalar_prefetch=1,
            grid=(tiles,),
            in_specs=[
                pl.BlockSpec((rows, tile), lhs),
                pl.BlockSpec((rows, tile), lhs),
                pl.BlockSpec((rows, width), whole),
                pl.BlockSpec((rows, width), whole),
            ],
            out_specs=[pl.BlockSpec((tile, part), lambda i, w: (i, 0))] * 2,
        ),
        out_shape=[jax.ShapeDtypeStruct((depth, part), BF16)] * 2,
        compiler_params=params(),
        cost_estimate=pl.CostEstimate(
            flops=4 * rows * depth * width,
            bytes_accessed=4 * rows * (depth + width) + 2 * depth * width,
            transcendentals=0,
        ),
        name="grad_rows",
    )(where, own, sib, d_own, d_sib)


def solution(mesh):
    n_list, n_fsdp = mesh.shape["list"], mesh.shape["fsdp"]
    bits = [1 << k for k in range(1, n_fsdp.bit_length() - 1)]
    pairs = n_list * n_fsdp // 2

    def across(value, distance):
        return lax.ppermute(value, "fsdp", [(i, i ^ distance) for i in range(n_fsdp)])

    def along(value, distance):
        return lax.ppermute(value, "list", [(i, i ^ distance) for i in range(n_list)])

    def partner(kind, pair):
        return (
            pair ^ 1,
            ((pair + 1) ^ 1) - 1,
            pair ^ 2,
            ((pair + 2) ^ 2) - 2,
        )[kind]

    def neighbour(value, kind):
        moves = []
        for pair in range(pairs):
            other = partner(kind, pair)
            if 0 <= other < pairs:
                moves += [(2 * pair + core, 2 * other + core) for core in (0, 1)]
        return lax.ppermute(value, ("list", "fsdp"), moves)

    def gathered(value, order):
        have = {0: value}
        for bit in order:
            have.update({s ^ (bit >> 1): across(part, bit) for s, part in list(have.items())})
        return have

    def scattered(parts, order):
        current = dict(parts)
        for bit in order:
            flag = bit >> 1
            come = {s ^ flag: across(current[s], bit) for s in sorted(current)[::-1] if s & flag}
            current = {
                s: (current[s].astype(F32) + come[s].astype(F32)).astype(BF16)
                for s in current
                if not s & flag
            }
        return current[0]

    def local(hidden, norm_gain, w_qkv, w_out, final_gain, w_score, prior, labels, lengths):
        passages, _, width = hidden.shape
        assert 4 * passages >= LONGEST - 1
        groups = KV_HEADS // 2
        width_q, width_k = groups * GROUP, groups * HEAD_DIM
        index = lax.axis_index("fsdp")
        core = index % 2
        chip = index // 2
        where = jnp.stack([chip, core]).astype(jnp.int32)
        first_core = core == 0

        def ordered(mine, other, axis):
            return jnp.where(
                first_core,
                jnp.concatenate([mine, other], axis),
                jnp.concatenate([other, mine], axis),
            )

        starts = (0, 2 * width_q, 2 * (width_q + width_k))
        sizes = (width_q, width_k, width_k)

        def half(h):
            return jnp.concatenate(
                [w_qkv[:, a + h * n : a + (h + 1) * n] for a, n in zip(starts, sizes)], 1
            )

        halves = half(0), half(1)
        keep = jnp.where(first_core, *halves)
        give = jnp.where(first_core, halves[1], halves[0])
        pair_rows = ordered(keep, across(give, 1), 0)
        middle = pair_rows.shape[1] // 2
        part_a = gathered(pair_rows[:, :middle], bits)
        part_b = gathered(pair_rows[:, middle:], bits[::-1])
        weights = [(part_a[s], part_b[s]) for s in range(n_fsdp // 2)]
        full_out = lax.all_gather(w_out, "fsdp", axis=0, tiled=True)

        normal, sums = norm(hidden, norm_gain)
        normal_sib, sums_sib = across(normal, 1), across(sums, 1)
        sums = jnp.concatenate([sums, sums_sib], 0)
        lanes = -(-lengths.shape[0] // 128) * 128
        label_weight = jnp.exp(labels.astype(F32))
        small = jnp.broadcast_to(
            jnp.concatenate([prior, label_weight])[:, None], (2 * passages, 128)
        )
        small_sib = across(small, 1)
        prior_pair = jnp.concatenate([small[:passages], small_sib[:passages]], 0)
        heavy = jnp.concatenate([small[passages:], small_sib[passages:]], 0)
        heavies = [heavy] + [neighbour(heavy, kind) for kind in range(4)]
        pair = lax.axis_index("list") * (n_fsdp // 2) + chip
        places = jnp.stack([pair] + [partner(kind, pair) for kind in range(4)]).astype(jnp.int32)
        ends = jnp.cumsum(lengths)
        bounds = jnp.pad(jnp.stack([ends - lengths, ends]), ((0, 0), (0, lanes - lengths.shape[0])))

        proj_sib, probs_sib, attn_sib = forward(where, normal_sib, weights, groups)
        attn_sib_other = across(attn_sib, 1)
        proj_own, probs_own, attn_own = forward(where, normal, weights, groups)
        attn_own_other = across(attn_own, 1)
        mine = jnp.concatenate([attn_own, attn_sib], 0)
        other = jnp.concatenate([attn_sib_other, attn_own_other], 0)
        unit, inverse, score, attn = score_pass(
            where, mine, other, sums, full_out, final_gain, w_score, prior_pair
        )
        scores = [score] + [neighbour(score, kind) for kind in range(4)]
        d_rows, d_attended, loss_part = list_pass(
            where, places, bounds, unit, inverse, full_out, final_gain, w_score, scores, heavies,
            passages,
        )

        d_own = backward(probs_own, proj_own, d_attended[:passages], groups)
        d_sib = backward(probs_sib, proj_sib, d_attended[passages:], groups)
        depth = pair_rows.shape[0]
        blocks = {
            s: grad_block(where, s, normal, normal_sib, d_own, d_sib, depth)
            for s in sorted(range(n_fsdp // 2), key=lambda s: -bin(s).count("1"))
        }
        sum_a = scattered({s: blocks[s][0] for s in blocks}, bits)
        sum_b = scattered({s: blocks[s][1] for s in blocks}, bits[::-1])
        chip_sum = jnp.concatenate([sum_a, sum_b], 1)
        upper, lower = chip_sum[: depth // 2], chip_sum[depth // 2 :]
        keep = jnp.where(first_core, upper, lower)
        come = across(jnp.where(first_core, lower, upper), 1)
        columns = []
        at = 0
        for n in sizes:
            columns.append(ordered(keep[:, at : at + n], come[:, at : at + n], 1))
            at += n
        rows_sum = jnp.concatenate(columns, 1)
        place = lax.axis_index("list")

        def list_scatter(value):
            n = value.shape[1] // n_list
            block = lambda which: lax.dynamic_slice_in_dim(value, which * n, n, 1)
            total = block(place).astype(F32)
            for distance in range(1, n_list):
                total = total + along(block(place ^ distance).astype(BF16), distance).astype(F32)
            return total

        grad_qkv = list_scatter(rows_sum)

        payload = jnp.concatenate([attn[:passages], d_rows[:passages]], 1)
        plane = lax.all_gather(payload, "fsdp", axis=0, tiled=True)
        inner = attn.shape[1]
        own_rows = inner // n_fsdp
        left = lax.dynamic_slice_in_dim(plane, index * own_rows, own_rows, 1)
        grad_out = list_scatter(
            lax.dot_general(
                left, plane[:, inner:], (((0,), (0,)), ((), ())), preferred_element_type=F32
            )
        )

        loss = loss_part
        for distance in [1] + bits:
            loss = loss + across(loss, distance)
        distance = 1
        while distance < n_list:
            loss = loss + along(loss, distance)
            distance *= 2
        return (loss[0, 0], grad_qkv, grad_out)

    placed = (
        P(("list", "fsdp"), None, None),
        P(),
        P("fsdp", None),
        P("fsdp", None),
        P(),
        P(),
        P(("list", "fsdp")),
        P(("list", "fsdp")),
        P(),
    )
    return jax.shard_map(
        local,
        mesh=mesh,
        in_specs=placed,
        out_specs=(P(), P("fsdp", "list"), P("fsdp", "list")),
        check_vma=False,
    )
```

time: 351 us -> 248 us (0.71); the launches traced: 345 us -> 246 us
  Pallas kernels: 0 us -> 79.7 us
  matrix products: 67.6 us -> 0.33 us
  blocking collectives: 78.8 us -> 16.9 us
  starting transfers between devices: 0.24 us -> 44.6 us
  local copies, waits for them, and re-layouts: 54.1 us -> 12.7 us
  waiting for transfers between devices: 111 us -> 71.4 us
  other arithmetic: 17.3 us -> 6.02 us
    pallas_call x0 -> x11, Pallas kernels: none -> 79.7 us  [the longest x2 28.2 us: forward(): pl.pallas_call(functools.partial(forward_kernel, pieces, groups), grid_sp...]
    ppermute x0 -> x38, waiting for transfers between devices: none -> 70.7 us  [the longest x22 51.6 us: across(): lax.ppermute(value, 'fsdp', [(i, i ^ distance) for i in range(n_fsdp)])]
    reduce_scatter x3 -> x0, waiting for transfers between devices: 63.7 us -> none  [the longest x1 63.7 us: local(): lax.psum_scatter(lax.dot_general(columns, d_projected, (((0,), (0,)), (()...]
    dot_general x10 -> x1, matrix products: 59 us -> 0.33 us  [local(): lax.dot_general(left, plane[:, inner:], (((0,), (0,)), ((), ())), preferr...]
    ppermute x0 -> x38, starting transfers between devices: none -> 44.5 us  [the longest x22 20.6 us: across(): lax.ppermute(value, 'fsdp', [(i, i ^ distance) for i in range(n_fsdp)])]
    all_gather x2 -> x1, waiting for transfers between devices: 42.1 us -> 0.01 us  [local(): full_out = lax.all_gather(w_out, 'fsdp', axis=0, tiled=True)]
    unnamed x1 -> x0, blocking collectives: 39.4 us -> none
    psum x1 -> x0, blocking collectives: 39.3 us -> none  [local(): loss = lax.psum(-loss_scale * jnp.sum(target * log_prob), ('list', 'fsdp'))]
  transfers between devices with their start and end apart: 6 -> 39, of which waited for: 3 -> 12; matrix products, arithmetic and copies ran while one was open for 35% -> 3% of each run, Pallas kernels for 0% -> 19%
where the time goes in v1:
time: 248 us; the launch traced here: 246 us
  Pallas kernels  79.7 us (32%)
  waiting for transfers between devices  71.4 us (29%)
  starting transfers between devices  44.6 us (18%)
  blocking collectives  16.9 us (7%)
  between operations  14.6 us (6%)
  local copies, waits for them, and re-layouts  12.7 us (5%)
  other arithmetic  6.02 us (2%)
    ppermute x22, waiting for transfers between devices, across(): lax.ppermute(value, 'fsdp', [(i, i ^ distance) for i in range(n_fsdp)])  51.6 us
    pallas_call x2, Pallas kernels, forward(): pl.pallas_call(functools.partial(forward_kernel, pieces, groups), grid_sp...  28.2 us
    pallas_call x2, Pallas kernels, backward(): pl.pallas_call(functools.partial(backward_kernel, groups), grid=(steps,),...  26.6 us
    ppermute x22, starting transfers between devices, across(): lax.ppermute(value, 'fsdp', [(i, i ^ distance) for i in range(n_fsdp)])  20.6 us
    ppermute x8, waiting for transfers between devices, along(): lax.ppermute(value, 'list', [(i, i ^ distance) for i in range(n_list)])  18.4 us
    all_gather x1, blocking collectives, local(): plane = lax.all_gather(payload, 'fsdp', axis=0, tiled=True)  16.9 us
    pallas_call x4, Pallas kernels, grad_block(): pl.pallas_call(grad_kernel, grid_spec=pltpu.PrefetchScalarGridSpec(num_sc...  15.3 us
    ppermute x8, starting transfers between devices, along(): lax.ppermute(value, 'list', [(i, i ^ distance) for i in range(n_list)])  12.7 us
  transfers between devices with their start and end apart: 39, of which 12 were waited for; matrix products, arithmetic and copies ran while one was open for 3% of the time, Pallas kernels for 19%

profile of v1, /device:TPU:0, one launch (start us, length us, event | category | flops | bytes accessed | tf_op | source)
XLA Modules:
  0.0 246.2 jit_solution(14670769006561765533)
XLA Ops:
  8.6 5.8 %norm_rows.1 = (bf16[16,64,2048]{2,1,0:T(8,128)(2,1)}, f32[4,4,2048]{2,1,0:T(4,128)S(1)}) custom-call(bf16[16,64,2048]{2,1,0:T(8,128)(2,1)} %hidden_ref.1, f32[1,2048]{1,0:T(1,128)S(1)} %bitcast.20), custom_call_target="tpu_custom_call" | custom-call | flops 12582912 | bytes 8388608 | tf_op jit(solution)/shard_map/norm_rows/pallas_call | solution.py:48
  16.6 5.7 %collective-permute-done = bf16[256,768]{1,0:T(8,128)(2,1)S(1)} collective-permute-done((bf16[256,768]{1,0:T(8,128)(2,1)S(1)}, bf16[256,768]{1,0:T(8,128)(2,1)S(1)}, u32[]{:S(2)}, u32[]{:S(2)}) %collective-permute-start) | collective-permute-done | bytes 393248 | tf_op jit(solution)/shard_map/ppermute | solution.py:414
  22.7 2.6 %collective-permute-start.1 = (bf16[512,384]{1,0:T(8,128)(2,1)S(1)}, bf16[512,384]{1,0:T(8,128)(2,1)S(1)}, u32[]{:S(2)}, u32[]{:S(2)}) collective-permute-start(bf16[512,384]{1,0:T(8,128)(2,1)S(1)} %get-tuple-element.58.refs_0_), channel_id=1, source_target_pairs={{0,2},{1,3},{2,0},{3,1},{4,6},{5,7},{6,4},{7,5},{8,10},{9,11},{10,... | collective-permute-start | bytes 1179656 | tf_op jit(solution)/shard_map/ppermute | solution.py:414
  27.6 9.4 %collective-permute-done.1.refs_2_ = bf16[512,384]{1,0:T(8,128)(2,1)S(1)} collective-permute-done((bf16[512,384]{1,0:T(8,128)(2,1)S(1)}, bf16[512,384]{1,0:T(8,128)(2,1)S(1)}, u32[]{:S(2)}, u32[]{:S(2)}) %collective-permute-start.1) | collective-permute-done | bytes 393248 | tf_op jit(solution)/shard_map/ppermute | solution.py:414
  40.2 12.8 %collective-permute-done.2.refs_3_ = bf16[512,384]{1,0:T(8,128)(2,1)S(1)} collective-permute-done((bf16[512,384]{1,0:T(8,128)(2,1)S(1)}, bf16[512,384]{1,0:T(8,128)(2,1)S(1)}, u32[]{:S(2)}, u32[]{:S(2)}) %collective-permute-start.2) | collective-permute-done | bytes 393248 | tf_op jit(solution)/shard_map/ppermute | solution.py:414
  54.7 10.6 %collective-permute-done.5.refs_6_ = bf16[512,384]{1,0:T(8,128)(2,1)S(1)} collective-permute-done((bf16[512,384]{1,0:T(8,128)(2,1)S(1)}, bf16[512,384]{1,0:T(8,128)(2,1)S(1)}, u32[]{:S(2)}, u32[]{:S(2)}) %collective-permute-start.5) | collective-permute-done | bytes 393248 | tf_op jit(solution)/shard_map/ppermute | solution.py:414
  66.1 14.1 %project_attend.2 = (bf16[1024,768]{1,0:T(8,128)(2,1)S(1)}, bf16[1024,512]{1,0:T(8,128)(2,1)S(1)}, f32[4,4,512]{2,1,0:T(4,128)S(1)}) custom-call(s32[2]{0:T(128)S(1)} %pad_add_fusion.1.where_ref, bf16[1024,2048]{1,0:T(8,128)(2,1)} %bitcast.10.rows_ref.own_ref, bf16[512,384]{1,0:T(8,128)(2,1)S(1)} %get-tuple-element.58.refs_0_, ...), custom_call_target="tpu_custom_call" | custom-call | flops 3221225472 | bytes 9961472 | tf_op jit(solution)/shard_map/project_attend/pallas_call | solution.py:145
  82.9 14.1 %project_attend.3 = (bf16[1024,768]{1,0:T(8,128)(2,1)S(1)}, bf16[1024,512]{1,0:T(8,128)(2,1)S(1)}, f32[4,4,512]{2,1,0:T(4,128)S(1)}) custom-call(s32[2]{0:T(128)S(1)} %pad_add_fusion.1.where_ref, bf16[1024,2048]{1,0:T(8,128)(2,1)} %collective-permute-done.7.rows_ref.sib_ref, bf16[512,384]{1,0:T(8,128)(2,1)S(1)} %get-tuple-element.58.refs_0_, ...), custom_call_target="tpu_custom_call" | custom-call | flops 3221225472 | bytes 9961472 | tf_op jit(solution)/shard_map/project_attend/pallas_call | solution.py:145
  102.0 2.2 copy-done
  108.0 5.5 %collective-permute-start.14 = (f32[32,128]{1,0:T(8,128)S(1)}, f32[32,128]{1,0:T(8,128)S(1)}, u32[]{:S(2)}, u32[]{:S(2)}) collective-permute-start(f32[32,128]{1,0:T(8,128)S(1)} %get-tuple-element.32.refs_0_), channel_id=1, source_target_pairs={{0,4},{1,5},{2,6},{3,7},{4,0},{5,1},{6,2},{7,3},{8,12},{9,13},{10,... | collective-permute-start | bytes 49160 | tf_op jit(solution)/shard_map/ppermute | solution.py:433
  115.2 2.2 copy-done.1
  117.4 2.3 list_grad.1
  121.0 13.3 %attend_back.3.d_sib_ref = bf16[1024,768]{1,0:T(8,128)(2,1)S(1)} custom-call(bf16[1024,512]{1,0:T(8,128)(2,1)S(1)} %copy-done.12, bf16[1024,768]{1,0:T(8,128)(2,1)S(1)} %copy-done.8, f32[4,4,512]{2,1,0:T(4,128)S(1)} %reshape.40.d_ref), custom_call_target="tpu_custom_call" | custom-call | flops 2147483648 | bytes 4194304 | tf_op jit(solution)/shard_map/attend_back/pallas_call | solution.py:229
  134.3 13.3 %attend_back.2.d_own_ref = bf16[1024,768]{1,0:T(8,128)(2,1)S(1)} custom-call(bf16[1024,512]{1,0:T(8,128)(2,1)S(1)} %copy-done.10, bf16[1024,768]{1,0:T(8,128)(2,1)S(1)} %copy-done.6, f32[4,4,512]{2,1,0:T(4,128)S(1)} %reshape.39.d_ref), custom_call_target="tpu_custom_call" | custom-call | flops 2147483648 | bytes 4194304 | tf_op jit(solution)/shard_map/attend_back/pallas_call | solution.py:229
  147.6 3.8 %grad_rows.7 = (bf16[512,384]{1,0:T(8,128)(2,1)S(1)}, bf16[512,384]{1,0:T(8,128)(2,1)S(1)}) custom-call(s32[2]{0:T(128)S(1)} %pad_add_fusion.1.where_ref, bf16[1024,2048]{1,0:T(8,128)(2,1)} %bitcast.10.rows_ref.own_ref, bf16[1024,2048]{1,0:T(8,128)(2,1)} %collective-permute-done.7.rows_ref.sib_ref, bf16[1024,768]{1,0:T(8,128)(2,1)S(1)} %attend_back.2.d_own_ref, ...), custom_call_target="tpu_custom_call" | custom-call | flops 1610612736 | bytes 6029312 | tf_op jit(solution)/shard_map/grad_rows/pallas_call | solution.py:384
  151.4 3.5 %collective-permute-start.26 = (bf16[512,384]{1,0:T(8,128)(2,1)S(1)}, bf16[512,384]{1,0:T(8,128)(2,1)S(1)}, u32[]{:S(2)}, u32[]{:S(2)}) collective-permute-start(bf16[512,384]{1,0:T(8,128)(2,1)S(1)} %get-tuple-element.42), channel_id=1, source_target_pairs={{0,2},{1,3},{2,0},{3,1},{4,6},{5,7},{6,4},{7,5},{8,10},{9,11},{10,... | collective-permute-start | bytes 1179656 | tf_op jit(solution)/shard_map/ppermute | solution.py:414
  155.0 16.9 %all_gather.7 = bf16[128,3072]{1,0:T(8,128)(2,1)S(1)} all-gather(bf16[16,3072]{1,0:T(8,128)(2,1)S(1)} %pad_maximum_fusion.5), channel_id=1, replica_groups=mesh['list'=4,'fsdp'=8] {'fsdp'}, dimensions={0}, use_global_device_ids=true | all-gather | bytes 884736 | tf_op jit(solution)/shard_map/all_gather | solution.py:553
  171.9 3.8 %grad_rows.5 = (bf16[512,384]{1,0:T(8,128)(2,1)S(1)}, bf16[512,384]{1,0:T(8,128)(2,1)S(1)}) custom-call(s32[2]{0:T(128)S(1)} %pad_add_fusion.1.where_ref, bf16[1024,2048]{1,0:T(8,128)(2,1)} %bitcast.10.rows_ref.own_ref, bf16[1024,2048]{1,0:T(8,128)(2,1)} %collective-permute-done.7.rows_ref.sib_ref, bf16[1024,768]{1,0:T(8,128)(2,1)S(1)} %attend_back.2.d_own_ref, ...), custom_call_target="tpu_custom_call" | custom-call | flops 1610612736 | bytes 6029312 | tf_op jit(solution)/shard_map/grad_rows/pallas_call | solution.py:384
  175.7 2.3 collective-permute-start.25
  178.1 1.9 collective-permute-start.21
  180.0 3.8 %grad_rows.6 = (bf16[512,384]{1,0:T(8,128)(2,1)S(1)}, bf16[512,384]{1,0:T(8,128)(2,1)S(1)}) custom-call(s32[2]{0:T(128)S(1)} %pad_add_fusion.1.where_ref, bf16[1024,2048]{1,0:T(8,128)(2,1)} %bitcast.10.rows_ref.own_ref, bf16[1024,2048]{1,0:T(8,128)(2,1)} %collective-permute-done.7.rows_ref.sib_ref, bf16[1024,768]{1,0:T(8,128)(2,1)S(1)} %attend_back.2.d_own_ref, ...), custom_call_target="tpu_custom_call" | custom-call | flops 1610612736 | bytes 6029312 | tf_op jit(solution)/shard_map/grad_rows/pallas_call | solution.py:384
  184.0 3.7 %collective-permute-done.21 = f32[8,128]{1,0:T(8,128)S(1)} collective-permute-done((f32[8,128]{1,0:T(8,128)S(1)}, f32[8,128]{1,0:T(8,128)S(1)}, u32[]{:S(2)}, u32[]{:S(2)}) %collective-permute-start.21) | collective-permute-done | bytes 4128 | tf_op jit(solution)/shard_map/ppermute | solution.py:414
  190.1 1.8 collective-permute-start.30
  191.8 3.8 %grad_rows.4 = (bf16[512,384]{1,0:T(8,128)(2,1)S(1)}, bf16[512,384]{1,0:T(8,128)(2,1)S(1)}) custom-call(s32[2]{0:T(128)S(1)} %pad_add_fusion.1.where_ref, bf16[1024,2048]{1,0:T(8,128)(2,1)} %bitcast.10.rows_ref.own_ref, bf16[1024,2048]{1,0:T(8,128)(2,1)} %collective-permute-done.7.rows_ref.sib_ref, bf16[1024,768]{1,0:T(8,128)(2,1)S(1)} %attend_back.2.d_own_ref, ...), custom_call_target="tpu_custom_call" | custom-call | flops 1610612736 | bytes 6029312 | tf_op jit(solution)/shard_map/grad_rows/pallas_call | solution.py:384
  195.7 2.8 %collective-permute-done.22 = f32[8,128]{1,0:T(8,128)S(1)} collective-permute-done((f32[8,128]{1,0:T(8,128)S(1)}, f32[8,128]{1,0:T(8,128)S(1)}, u32[]{:S(2)}, u32[]{:S(2)}) %collective-permute-start.22) | collective-permute-done | bytes 4128 | tf_op jit(solution)/shard_map/ppermute | solution.py:414
  200.0 6.1 %collective-permute-done.27 = bf16[512,384]{1,0:T(8,128)(2,1)S(1)} collective-permute-done((bf16[512,384]{1,0:T(8,128)(2,1)S(1)}, bf16[512,384]{1,0:T(8,128)(2,1)S(1)}, u32[]{:S(2)}, u32[]{:S(2)}) %collective-permute-start.27) | collective-permute-done | bytes 393248 | tf_op jit(solution)/shard_map/ppermute | solution.py:414
  207.0 2.1 collective-permute-start.24
  211.6 2.0 collective-permute-start.37
  214.7 2.3 collective-permute-start.33
  217.0 2.3 collective-permute-start.34
  219.3 3.8 %collective-permute-done.36 = bf16[128,512]{1,0:T(8,128)(2,1)S(1)} collective-permute-done((bf16[128,512]{1,0:T(8,128)(2,1)S(1)}, bf16[128,512]{1,0:T(8,128)(2,1)S(1)}, u32[]{:S(2)}, u32[]{:S(2)}) %collective-permute-start.36) | collective-permute-done | bytes 131104 | tf_op jit(solution)/shard_map/ppermute | solution.py:417
  225.3 13.2 %collective-permute-done.33 = bf16[256,384]{1,0:T(8,128)(2,1)S(1)} collective-permute-done((bf16[256,384]{1,0:T(8,128)(2,1)S(1)}, bf16[256,384]{1,0:T(8,128)(2,1)S(1)}, u32[]{:S(2)}, u32[]{:S(2)}) %collective-permute-start.33) | collective-permute-done | bytes 196640 | tf_op jit(solution)/shard_map/ppermute | solution.py:417
  (149 shorter events, 37.8 us)
Async XLA Ops:
  7.2 94.8 %all-gather.2.cloned.1.call-start = ((), (), s32[]{:S(2)}) async-start(), calls=%async_computation | async-start | bytes 4718592 | tf_op jit(solution)/shard_map/all_gather | solution.py:487
  14.4 68.5 %collective-permute-start.7 = (bf16[1024,2048]{1,0:T(8,128)(2,1)}, bf16[1024,2048]{1,0:T(8,128)(2,1)}, u32[]{:S(2)}, u32[]{:S(2)}) collective-permute-start(bf16[1024,2048]{1,0:T(8,128)(2,1)} %bitcast.10.rows_ref.own_ref), channel_id=1, source_target_pairs={{0,1},{1,0},{2,3},{3,2},{4,5},{5,4},{6,7},{7,6},{8,9},{9,8},{10,11... | collective-permute-start | bytes 12582920 | tf_op jit(solution)/shard_map/ppermute | solution.py:414
  15.7 11.2 %collective-permute-start.11 = (f32[32,128]{1,0:T(8,128)S(1)}, f32[32,128]{1,0:T(8,128)S(1)}, u32[]{:S(2)}, u32[]{:S(2)}) collective-permute-start(f32[32,128]{1,0:T(8,128)S(1)} %broadcast_in_dim.25), channel_id=1, source_target_pairs={{0,1},{1,0},{2,3},{3,2},{4,5},{5,4},{6,7},{7,6},{8,9},{9,8},{10,11... | collective-permute-start | bytes 49160 | tf_op jit(solution)/shard_map/ppermute | solution.py:414
  15.9 11.6 %collective-permute-start.10 = (f32[16,2048]{1,0:T(8,128)S(1)}, f32[16,2048]{1,0:T(8,128)}, u32[]{:S(2)}, u32[]{:S(2)}) collective-permute-start(f32[16,2048]{1,0:T(8,128)S(1)} %reshape.38), channel_id=1, source_target_pairs={{0,1},{1,0},{2,3},{3,2},{4,5},{5,4},{6,7},{7,6},{8,9},{9,8},{10,11... | collective-permute-start | bytes 393224 | tf_op jit(solution)/shard_map/ppermute | solution.py:414
  22.7 14.3 %collective-permute-start.1 = (bf16[512,384]{1,0:T(8,128)(2,1)S(1)}, bf16[512,384]{1,0:T(8,128)(2,1)S(1)}, u32[]{:S(2)}, u32[]{:S(2)}) collective-permute-start(bf16[512,384]{1,0:T(8,128)(2,1)S(1)} %get-tuple-element.58.refs_0_), channel_id=1, source_target_pairs={{0,2},{1,3},{2,0},{3,1},{4,6},{5,7},{6,4},{7,5},{8,10},{9,11},{10,... | collective-permute-start | bytes 1179656 | tf_op jit(solution)/shard_map/ppermute | solution.py:414
  25.4 13.2 %collective-permute-start.4 = (bf16[512,384]{1,0:T(8,128)(2,1)S(1)}, bf16[512,384]{1,0:T(8,128)(2,1)S(1)}, u32[]{:S(2)}, u32[]{:S(2)}) collective-permute-start(bf16[512,384]{1,0:T(8,128)(2,1)S(1)} %get-tuple-element.57.refs_1_), channel_id=1, source_target_pairs={{0,4},{1,5},{2,6},{3,7},{4,0},{5,1},{6,2},{7,3},{8,12},{9,13},{10,... | collective-permute-start | bytes 1179656 | tf_op jit(solution)/shard_map/ppermute | solution.py:414
  27.0 26.0 %collective-permute-start.2 = (bf16[512,384]{1,0:T(8,128)(2,1)S(1)}, bf16[512,384]{1,0:T(8,128)(2,1)S(1)}, u32[]{:S(2)}, u32[]{:S(2)}) collective-permute-start(bf16[512,384]{1,0:T(8,128)(2,1)S(1)} %get-tuple-element.57.refs_1_), channel_id=1, source_target_pairs={{0,2},{1,3},{2,0},{3,1},{4,6},{5,7},{6,4},{7,5},{8,10},{9,11},{10,... | collective-permute-start | bytes 1179656 | tf_op jit(solution)/shard_map/ppermute | solution.py:414
  27.5 26.5 %collective-permute-start.3 = (bf16[512,384]{1,0:T(8,128)(2,1)S(1)}, bf16[512,384]{1,0:T(8,128)(2,1)S(1)}, u32[]{:S(2)}, u32[]{:S(2)}) collective-permute-start(bf16[512,384]{1,0:T(8,128)(2,1)S(1)} %get-tuple-element.58.refs_0_), channel_id=1, source_target_pairs={{0,4},{1,5},{2,6},{3,7},{4,0},{5,1},{6,2},{7,3},{8,12},{9,13},{10,... | collective-permute-start | bytes 1179656 | tf_op jit(solution)/shard_map/ppermute | solution.py:414
  37.0 28.3 %collective-permute-start.5 = (bf16[512,384]{1,0:T(8,128)(2,1)S(1)}, bf16[512,384]{1,0:T(8,128)(2,1)S(1)}, u32[]{:S(2)}, u32[]{:S(2)}) collective-permute-start(bf16[512,384]{1,0:T(8,128)(2,1)S(1)} %collective-permute-done.1.refs_2_), channel_id=1, source_target_pairs={{0,4},{1,5},{2,6},{3,7},{4,0},{5,1},{6,2},{7,3},{8,12},{9,13},{10,... | collective-permute-start | bytes 1179656 | tf_op jit(solution)/shard_map/ppermute | solution.py:414
  38.5 27.5 %collective-permute-start.6 = (bf16[512,384]{1,0:T(8,128)(2,1)S(1)}, bf16[512,384]{1,0:T(8,128)(2,1)S(1)}, u32[]{:S(2)}, u32[]{:S(2)}) collective-permute-start(bf16[512,384]{1,0:T(8,128)(2,1)S(1)} %collective-permute-done.4.refs_5_), channel_id=1, source_target_pairs={{0,2},{1,3},{2,0},{3,1},{4,6},{5,7},{6,4},{7,5},{8,10},{9,11},{10,... | collective-permute-start | bytes 1179656 | tf_op jit(solution)/shard_map/ppermute | solution.py:414
  53.0 54.3 %collective-permute-start.16 = (f32[32,128]{1,0:T(8,128)S(1)}, f32[32,128]{1,0:T(8,128)S(1)}, u32[]{:S(2)}, u32[]{:S(2)}) collective-permute-start(f32[32,128]{1,0:T(8,128)S(1)} %pad_maximum_fusion.9.refs_5_), channel_id=1, source_target_pairs={{0,2},{1,3},{2,0},{3,1},{4,6},{5,7},{6,4},{7,5},{8,10},{9,11},{10,... | collective-permute-start | bytes 49160 | tf_op jit(solution)/shard_map/ppermute | solution.py:433
  54.0 53.9 %collective-permute-start.17 = (f32[32,128]{1,0:T(8,128)S(1)}, f32[32,128]{1,0:T(8,128)S(1)}, u32[]{:S(2)}, u32[]{:S(2)}) collective-permute-start(f32[32,128]{1,0:T(8,128)S(1)} %pad_maximum_fusion.9.refs_5_), channel_id=1, source_target_pairs={{2,4},{3,5},{4,2},{5,3},{6,8},{7,9},{8,6},{9,7},{10,12},{11,13},{1... | collective-permute-start | bytes 49160 | tf_op jit(solution)/shard_map/ppermute | solution.py:433
  65.2 48.2 %collective-permute-start.18 = (f32[32,128]{1,0:T(8,128)S(1)}, f32[32,128]{1,0:T(8,128)S(1)}, u32[]{:S(2)}, u32[]{:S(2)}) collective-permute-start(f32[32,128]{1,0:T(8,128)S(1)} %pad_maximum_fusion.9.refs_5_), channel_id=1, source_target_pairs={{0,4},{1,5},{2,6},{3,7},{4,0},{5,1},{6,2},{7,3},{8,12},{9,13},{10,... | collective-permute-start | bytes 49160 | tf_op jit(solution)/shard_map/ppermute | solution.py:433
  82.9 17.6 %collective-permute-start.9 = (f32[16,512]{1,0:T(8,128)}, f32[16,512]{1,0:T(8,128)}, u32[]{:S(2)}, u32[]{:S(2)}) collective-permute-start(f32[16,512]{1,0:T(8,128)} %reshape.36), channel_id=1, source_target_pairs={{0,1},{1,0},{2,3},{3,2},{4,5},{5,4},{6,7},{7,6},{8,9},{9,8},{10,11... | collective-permute-start | bytes 98312 | tf_op jit(solution)/shard_map/ppermute | solution.py:414
  100.5 14.0 %collective-permute-start.19 = (f32[32,128]{1,0:T(8,128)S(1)}, f32[32,128]{1,0:T(8,128)S(1)}, u32[]{:S(2)}, u32[]{:S(2)}) collective-permute-start(f32[32,128]{1,0:T(8,128)S(1)} %pad_maximum_fusion.9.refs_5_), channel_id=1, source_target_pairs={{4,8},{5,9},{6,10},{7,11},{8,4},{9,5},{10,6},{11,7},{12,16},{13,17... | collective-permute-start | bytes 49160 | tf_op jit(solution)/shard_map/ppermute | solution.py:433
  105.7 8.8 %collective-permute-start.12 = (f32[32,128]{1,0:T(8,128)S(1)}, f32[32,128]{1,0:T(8,128)S(1)}, u32[]{:S(2)}, u32[]{:S(2)}) collective-permute-start(f32[32,128]{1,0:T(8,128)S(1)} %get-tuple-element.32.refs_0_), channel_id=1, source_target_pairs={{0,2},{1,3},{2,0},{3,1},{4,6},{5,7},{6,4},{7,5},{8,10},{9,11},{10,... | collective-permute-start | bytes 49160 | tf_op jit(solution)/shard_map/ppermute | solution.py:433
  151.4 38.1 %collective-permute-start.26 = (bf16[512,384]{1,0:T(8,128)(2,1)S(1)}, bf16[512,384]{1,0:T(8,128)(2,1)S(1)}, u32[]{:S(2)}, u32[]{:S(2)}) collective-permute-start(bf16[512,384]{1,0:T(8,128)(2,1)S(1)} %get-tuple-element.42), channel_id=1, source_target_pairs={{0,2},{1,3},{2,0},{3,1},{4,6},{5,7},{6,4},{7,5},{8,10},{9,11},{10,... | collective-permute-start | bytes 1179656 | tf_op jit(solution)/shard_map/ppermute | solution.py:414
  155.0 23.1 %collective-permute-start.20 = (f32[8,128]{1,0:T(8,128)S(1)}, f32[8,128]{1,0:T(8,128)S(1)}, u32[]{:S(2)}, u32[]{:S(2)}) collective-permute-start(f32[8,128]{1,0:T(8,128)S(1)} %get-tuple-element.33), channel_id=1, source_target_pairs={{0,1},{1,0},{2,3},{3,2},{4,5},{5,4},{6,7},{7,6},{8,9},{9,8},{10,11... | collective-permute-start | bytes 12296 | tf_op jit(solution)/shard_map/ppermute | solution.py:414
  175.7 24.3 %collective-permute-start.25 = (bf16[512,384]{1,0:T(8,128)(2,1)S(1)}, bf16[512,384]{1,0:T(8,128)(2,1)S(1)}, u32[]{:S(2)}, u32[]{:S(2)}) collective-permute-start(bf16[512,384]{1,0:T(8,128)(2,1)S(1)} %get-tuple-element.40), channel_id=1, source_target_pairs={{0,2},{1,3},{2,0},{3,1},{4,6},{5,7},{6,4},{7,5},{8,10},{9,11},{10,... | collective-permute-start | bytes 1179656 | tf_op jit(solution)/shard_map/ppermute | solution.py:414
  178.0 12.0 %collective-permute-start.29 = (bf16[512,384]{1,0:T(8,128)(2,1)S(1)}, bf16[512,384]{1,0:T(8,128)(2,1)S(1)}, u32[]{:S(2)}, u32[]{:S(2)}) collective-permute-start(bf16[512,384]{1,0:T(8,128)(2,1)S(1)} %get-tuple-element.46), channel_id=1, source_target_pairs={{0,4},{1,5},{2,6},{3,7},{4,0},{5,1},{6,2},{7,3},{8,12},{9,13},{10,... | collective-permute-start | bytes 1179656 | tf_op jit(solution)/shard_map/ppermute | solution.py:414
  178.1 9.6 %collective-permute-start.21 = (f32[8,128]{1,0:T(8,128)S(1)}, f32[8,128]{1,0:T(8,128)S(1)}, u32[]{:S(2)}, u32[]{:S(2)}) collective-permute-start(f32[8,128]{1,0:T(8,128)S(1)} %add.100), channel_id=1, source_target_pairs={{0,2},{1,3},{2,0},{3,1},{4,6},{5,7},{6,4},{7,5},{8,10},{9,11},{10,... | collective-permute-start | bytes 12296 | tf_op jit(solution)/shard_map/ppermute | solution.py:414
  183.9 22.3 %collective-permute-start.28 = (bf16[512,384]{1,0:T(8,128)(2,1)S(1)}, bf16[512,384]{1,0:T(8,128)(2,1)S(1)}, u32[]{:S(2)}, u32[]{:S(2)}) collective-permute-start(bf16[512,384]{1,0:T(8,128)(2,1)S(1)} %get-tuple-element.44), channel_id=1, source_target_pairs={{0,4},{1,5},{2,6},{3,7},{4,0},{5,1},{6,2},{7,3},{8,12},{9,13},{10,... | collective-permute-start | bytes 1179656 | tf_op jit(solution)/shard_map/ppermute | solution.py:414
  187.7 10.8 %collective-permute-start.22 = (f32[8,128]{1,0:T(8,128)S(1)}, f32[8,128]{1,0:T(8,128)S(1)}, u32[]{:S(2)}, u32[]{:S(2)}) collective-permute-start(f32[8,128]{1,0:T(8,128)S(1)} %add.101), channel_id=1, source_target_pairs={{0,4},{1,5},{2,6},{3,7},{4,0},{5,1},{6,2},{7,3},{8,12},{9,13},{10,... | collective-permute-start | bytes 12296 | tf_op jit(solution)/shard_map/ppermute | solution.py:414
  189.6 16.5 %collective-permute-start.27 = (bf16[512,384]{1,0:T(8,128)(2,1)S(1)}, bf16[512,384]{1,0:T(8,128)(2,1)S(1)}, u32[]{:S(2)}, u32[]{:S(2)}) collective-permute-start(bf16[512,384]{1,0:T(8,128)(2,1)S(1)} %add_convert_fusion.4), channel_id=1, source_target_pairs={{0,4},{1,5},{2,6},{3,7},{4,0},{5,1},{6,2},{7,3},{8,12},{9,13},{10,... | collective-permute-start | bytes 1179656 | tf_op jit(solution)/shard_map/ppermute | solution.py:414
  190.1 16.1 %collective-permute-start.30 = (bf16[512,384]{1,0:T(8,128)(2,1)S(1)}, bf16[512,384]{1,0:T(8,128)(2,1)S(1)}, u32[]{:S(2)}, u32[]{:S(2)}) collective-permute-start(bf16[512,384]{1,0:T(8,128)(2,1)S(1)} %add_convert_fusion.1), channel_id=1, source_target_pairs={{0,2},{1,3},{2,0},{3,1},{4,6},{5,7},{6,4},{7,5},{8,10},{9,11},{10,... | collective-permute-start | bytes 1179656 | tf_op jit(solution)/shard_map/ppermute | solution.py:414
  198.5 8.5 %collective-permute-start.23 = (f32[8,128]{1,0:T(8,128)S(1)}, f32[8,128]{1,0:T(8,128)S(1)}, u32[]{:S(2)}, u32[]{:S(2)}) collective-permute-start(f32[8,128]{1,0:T(8,128)S(1)} %add.102), channel_id=1, source_target_pairs={{0,8},{8,0},{16,24},{24,16},{1,9},{9,1},{17,25},{25,17},{2,10},{10... | collective-permute-start | bytes 12296 | tf_op jit(solution)/shard_map/ppermute | solution.py:417
  209.1 7.9 %collective-permute-start.35 = (bf16[128,512]{1,0:T(8,128)(2,1)S(1)}, bf16[128,512]{1,0:T(8,128)(2,1)S(1)}, u32[]{:S(2)}, u32[]{:S(2)}) collective-permute-start(bf16[128,512]{1,0:T(8,128)(2,1)S(1)} %get-tuple-element.49), channel_id=1, source_target_pairs={{0,8},{8,0},{16,24},{24,16},{1,9},{9,1},{17,25},{25,17},{2,10},{10... | collective-permute-start | bytes 393224 | tf_op jit(solution)/shard_map/ppermute | solution.py:417
  210.1 12.9 %collective-permute-start.36 = (bf16[128,512]{1,0:T(8,128)(2,1)S(1)}, bf16[128,512]{1,0:T(8,128)(2,1)S(1)}, u32[]{:S(2)}, u32[]{:S(2)}) collective-permute-start(bf16[128,512]{1,0:T(8,128)(2,1)S(1)} %get-tuple-element.51), channel_id=1, source_target_pairs={{0,16},{8,24},{16,0},{24,8},{1,17},{9,25},{17,1},{25,9},{2,18},{10... | collective-permute-start | bytes 393224 | tf_op jit(solution)/shard_map/ppermute | solution.py:417
  211.6 11.5 %collective-permute-start.37 = (bf16[128,512]{1,0:T(8,128)(2,1)S(1)}, bf16[128,512]{1,0:T(8,128)(2,1)S(1)}, u32[]{:S(2)}, u32[]{:S(2)}) collective-permute-start(bf16[128,512]{1,0:T(8,128)(2,1)S(1)} %get-tuple-element.50), channel_id=1, source_target_pairs={{0,24},{8,16},{16,8},{24,0},{1,25},{9,17},{17,9},{25,1},{2,26},{10... | collective-permute-start | bytes 393224 | tf_op jit(solution)/shard_map/ppermute | solution.py:417
  214.6 10.7 %collective-permute-start.32 = (bf16[256,384]{1,0:T(8,128)(2,1)S(1)}, bf16[256,384]{1,0:T(8,128)(2,1)S(1)}, u32[]{:S(2)}, u32[]{:S(2)}) collective-permute-start(bf16[256,384]{1,0:T(8,128)(2,1)S(1)} %get-tuple-element.52), channel_id=1, source_target_pairs={{0,8},{8,0},{16,24},{24,16},{1,9},{9,1},{17,25},{25,17},{2,10},{10... | collective-permute-start | bytes 589832 | tf_op jit(solution)/shard_map/ppermute | solution.py:417
  214.7 23.8 %collective-permute-start.33 = (bf16[256,384]{1,0:T(8,128)(2,1)S(1)}, bf16[256,384]{1,0:T(8,128)(2,1)S(1)}, u32[]{:S(2)}, u32[]{:S(2)}) collective-permute-start(bf16[256,384]{1,0:T(8,128)(2,1)S(1)} %get-tuple-element.54), channel_id=1, source_target_pairs={{0,16},{8,24},{16,0},{24,8},{1,17},{9,25},{17,1},{25,9},{2,18},{10... | collective-permute-start | bytes 589832 | tf_op jit(solution)/shard_map/ppermute | solution.py:417
  217.0 21.5 %collective-permute-start.34 = (bf16[256,384]{1,0:T(8,128)(2,1)S(1)}, bf16[256,384]{1,0:T(8,128)(2,1)S(1)}, u32[]{:S(2)}, u32[]{:S(2)}) collective-permute-start(bf16[256,384]{1,0:T(8,128)(2,1)S(1)} %get-tuple-element.53), channel_id=1, source_target_pairs={{0,24},{8,16},{16,8},{24,0},{1,25},{9,17},{17,9},{25,1},{2,26},{10... | collective-permute-start | bytes 589832 | tf_op jit(solution)/shard_map/ppermute | solution.py:417
  (25 other events, 137.8 us)
Sparse Core Ops, SparseCore 0:
  9.9 52.0 all-gather.1

commit v2 on v1

v2 whole, which is shorter than its diff:
```python
import functools

import jax
import jax.numpy as jnp
from jax import lax
from jax.experimental import pallas as pl
from jax.experimental.pallas import tpu as pltpu
from jax.sharding import PartitionSpec as P

HEADS = 16
KV_HEADS = 4
HEAD_DIM = 64
PASSAGE_LEN = 64
LONGEST = 48
RATIO = HEADS // KV_HEADS
GROUP = RATIO * HEAD_DIM

epsilon = 1e-05
loss_scale = 64.0
scale = HEAD_DIM ** (-0.5)
VMEM = 48 * 1024 * 1024
BF16 = jnp.bfloat16
F32 = jnp.float32


def params(grid=1):
    return pltpu.CompilerParams(
        vmem_limit_bytes=VMEM, dimension_semantics=("arbitrary",) * grid
    )


def mm(a, b, dims=((1,), (0,))):
    return lax.dot_general(a, b, (dims, ((), ())), preferred_element_type=F32)


def norm_kernel(hidden_ref, gain_ref, normal_ref, sum_ref):
    values = hidden_ref[...].astype(F32)
    mean_square = jnp.mean(values * values, -1, keepdims=True)
    out = values * lax.rsqrt(mean_square + epsilon) * gain_ref[...][None]
    normal_ref[...] = out.astype(BF16)
    sum_ref[0] = jnp.sum(values, 1)


def norm(hidden, gain):
    passages, length, width = hidden.shape
    step = 4 if passages % 4 == 0 else 1
    steps = passages // step
    normal, sums = pl.pallas_call(
        norm_kernel,
        grid=(steps,),
        in_specs=[
            pl.BlockSpec((step, length, width), lambda i: (i, 0, 0)),
            pl.BlockSpec((1, width), lambda i: (0, 0)),
        ],
        out_specs=[
            pl.BlockSpec((step, length, width), lambda i: (i, 0, 0)),
            pl.BlockSpec((1, step, width), lambda i: (i, 0, 0)),
        ],
        out_shape=[
            jax.ShapeDtypeStruct((passages, length, width), BF16),
            jax.ShapeDtypeStruct((steps, step, width), F32),
        ],
        compiler_params=params(),
        cost_estimate=pl.CostEstimate(
            flops=6 * hidden.size, bytes_accessed=4 * hidden.size, transcendentals=0
        ),
        name="norm_rows",
    )(hidden, gain[None])
    return normal.reshape(passages * length, width), sums.reshape(passages, width)


WIDE = 2 * HEAD_DIM
BATCH = 8


def low_lanes(rows):
    return lax.broadcasted_iota(jnp.int32, (rows, WIDE), 1) < HEAD_DIM


def ones_block(repeat):
    row = lax.broadcasted_iota(jnp.int32, (repeat * WIDE, WIDE), 0) // HEAD_DIM % 2
    col = lax.broadcasted_iota(jnp.int32, (repeat * WIDE, WIDE), 1) // HEAD_DIM
    return jnp.where(row == col, 1.0, 0.0).astype(BF16)


def diagonals(pair, factor):
    low = low_lanes(HEAD_DIM)
    wide = pair.astype(F32) * factor
    turned = pltpu.roll(wide, HEAD_DIM, 1)
    out = []
    for first, second in ((wide, turned), (turned, wide)):
        block = [jnp.where(low, first, 0.0), jnp.where(low, 0.0, second)]
        out.append(jnp.concatenate(block, 0).astype(BF16))
    return out


def segment_max(scores):
    low = low_lanes(scores.shape[0])
    first = jnp.max(jnp.where(low, scores, -jnp.inf), 1, keepdims=True)
    second = jnp.max(jnp.where(low, -jnp.inf, scores), 1, keepdims=True)
    return jnp.where(low, first, second)


def stacked(ref, rows, g):
    at = g * GROUP
    return jnp.concatenate([ref[rows, at : at + WIDE], ref[rows, at + WIDE : at + GROUP]], 0)


def project(refs, pieces, whole):
    blocks, refs = refs[:pieces], refs[pieces:]
    weights, refs = refs[: 2 * pieces], refs[2 * pieces :]
    join(weights, whole)
    rows = blocks[0][...]
    if pieces > 1:
        rows = jnp.concatenate([rows] + [block[...] for block in blocks[1:]], 1)
    return mm(rows, whole[...]), refs


def partial_kernel(pieces, before, where_ref, *refs):
    refs, whole = refs[:-1], refs[-1]
    product, refs = project(refs, pieces, whole)
    refs[-1][...] = product + refs[0][...] if before else product


def first_kernel(where_ref, rows_ref, a_ref, b_ref, out_ref, turned_ref):
    depth, part = a_ref.shape
    start = pl.multiple_of(where_ref[0] * depth, depth)
    block = rows_ref[:, pl.ds(start, depth)]
    out_ref[:, :part] = mm(block, a_ref[...])
    out_ref[:, part:] = mm(block, b_ref[...])
    turned_ref[...] = rows_ref[...].T


def forward_kernel(pieces, groups, where_ref, *refs):
    refs, whole = refs[:-1], refs[-1]
    projected, refs = project(refs, pieces, whole)
    before_ref, projected_ref, probs_ref, sum_ref = refs
    projected = projected + before_ref[...]
    projected_ref[...] = projected.astype(BF16)
    ones = ones_block(1)
    width_q = groups * GROUP
    width_k = groups * HEAD_DIM
    count = projected_ref.shape[0] // PASSAGE_LEN
    spans = [slice(i * PASSAGE_LEN, (i + 1) * PASSAGE_LEN) for i in range(count)]
    keys = [diagonals(projected_ref[r, width_q : width_q + width_k], scale) for r in spans]
    values = [diagonals(projected_ref[r, width_q + width_k :], 1.0) for r in spans]
    for g in range(groups):
        scores = jnp.concatenate(
            [mm(stacked(projected_ref, r, g), keys[i][g], ((1,), (1,))) for i, r in enumerate(spans)],
            0,
        )
        expo = jnp.exp(scores - segment_max(scores))
        total = mm(expo.astype(BF16), ones)
        probs = (expo / total).astype(BF16)
        probs_ref[0, g] = probs
        for i in range(count):
            attended = mm(probs[i * WIDE : (i + 1) * WIDE], values[i][g])
            attended = attended.astype(BF16).astype(F32)
            for j in range(2):
                at = g * GROUP + j * WIDE
                sum_ref[0, i : i + 1, at : at + WIDE] = jnp.sum(
                    attended[j * HEAD_DIM : (j + 1) * HEAD_DIM], 0, keepdims=True
                )


def join(weights, whole):
    @pl.when(pl.program_id(0) == 0)
    def _():
        depth, part = weights[0].shape
        for k in range(len(weights) // 2):
            rows = slice(k * depth, (k + 1) * depth)
            whole[rows, :part] = weights[2 * k][...]
            whole[rows, part:] = weights[2 * k + 1][...]


def row_step(total, batch):
    batch = batch if total % (batch * PASSAGE_LEN) == 0 else 1
    return batch, batch * PASSAGE_LEN


def block_of(step, depth, s):
    return pl.BlockSpec((step, depth), lambda i, w: (i, w[0] ^ s))


def first_project(where, rows, weights):
    total, width = rows.shape
    depth, part = weights[0].shape
    _, step = row_step(total, 4)
    whole = lambda i, w: (0, 0)
    return pl.pallas_call(
        first_kernel,
        grid_spec=pltpu.PrefetchScalarGridSpec(
            num_scalar_prefetch=1,
            grid=(total // step,),
            in_specs=[
                pl.BlockSpec((step, width), lambda i, w: (i, 0)),
                pl.BlockSpec((depth, part), whole),
                pl.BlockSpec((depth, part), whole),
            ],
            out_specs=[
                pl.BlockSpec((step, 2 * part), lambda i, w: (i, 0)),
                pl.BlockSpec((width, step), lambda i, w: (0, i)),
            ],
        ),
        out_shape=[
            jax.ShapeDtypeStruct((total, 2 * part), F32),
            jax.ShapeDtypeStruct((width, total), BF16),
        ],
        compiler_params=params(),
        cost_estimate=pl.CostEstimate(
            flops=4 * total * depth * part, bytes_accessed=4 * rows.size + 8 * total * part,
            transcendentals=0,
        ),
        name="project_first",
    )(where, rows, *weights)


def partial_project(where, rows, weights, before):
    total, width = rows.shape
    depth, part = next(iter(weights.values()))[0].shape
    _, step = row_step(total, BATCH)
    pieces = len(weights)
    flat = [x for s in weights for x in weights[s]]
    out = pl.BlockSpec((step, 2 * part), lambda i, w: (i, 0))
    return pl.pallas_call(
        functools.partial(partial_kernel, pieces, True),
        grid_spec=pltpu.PrefetchScalarGridSpec(
            num_scalar_prefetch=1,
            grid=(total // step,),
            in_specs=[block_of(step, depth, s) for s in weights]
            + [pl.BlockSpec(x.shape, lambda i, w: (0, 0)) for x in flat]
            + [out],
            out_specs=out,
            scratch_shapes=[pltpu.VMEM((pieces * depth, 2 * part), BF16)],
        ),
        out_shape=jax.ShapeDtypeStruct((total, 2 * part), F32),
        compiler_params=params(),
        cost_estimate=pl.CostEstimate(
            flops=4 * total * depth * part * pieces,
            bytes_accessed=2 * total * depth * pieces + 16 * total * part,
            transcendentals=0,
        ),
        name="project_more",
    )(where, *([rows] * pieces), *flat, before)


def forward(where, rows, weights, groups, before):
    total, width = rows.shape
    pieces = len(weights)
    flat = [x for s in weights for x in weights[s]]
    depth, part = flat[0].shape
    out_width = 2 * part
    batch, step = row_step(total, BATCH)
    steps = total // step
    heads = groups * GROUP
    return pl.pallas_call(
        functools.partial(forward_kernel, pieces, groups),
        grid_spec=pltpu.PrefetchScalarGridSpec(
            num_scalar_prefetch=1,
            grid=(steps,),
            in_specs=[block_of(step, depth, s) for s in weights]
            + [pl.BlockSpec(x.shape, lambda i, w: (0, 0)) for x in flat]
            + [pl.BlockSpec((step, out_width), lambda i, w: (i, 0))],
            out_specs=[
                pl.BlockSpec((step, out_width), lambda i, w: (i, 0)),
                pl.BlockSpec((1, groups, batch * WIDE, WIDE), lambda i, w: (i, 0, 0, 0)),
                pl.BlockSpec((1, batch, heads), lambda i, w: (i, 0, 0)),
            ],
            scratch_shapes=[pltpu.VMEM((pieces * depth, out_width), BF16)],
        ),
        out_shape=[
            jax.ShapeDtypeStruct((total, out_width), BF16),
            jax.ShapeDtypeStruct((steps, groups, batch * WIDE, WIDE), BF16),
            jax.ShapeDtypeStruct((steps, batch, heads), F32),
        ],
        compiler_params=params(),
        cost_estimate=pl.CostEstimate(
            flops=2 * total * depth * pieces * out_width + 8 * total * heads * GROUP,
            bytes_accessed=2 * total * (depth * pieces + 3 * out_width + heads),
            transcendentals=total * heads,
        ),
        name="project_attend",
    )(where, *([rows] * pieces), *flat, before)


def backward_kernel(groups, probs_ref, projected_ref, d_ref, out_ref):
    low = low_lanes(HEAD_DIM)
    ones = ones_block(2)
    width_q = groups * GROUP
    width_k = groups * HEAD_DIM
    count = projected_ref.shape[0] // PASSAGE_LEN
    spans = [slice(i * PASSAGE_LEN, (i + 1) * PASSAGE_LEN) for i in range(count)]
    keys = [diagonals(projected_ref[r, width_q : width_q + width_k], scale) for r in spans]
    values = [diagonals(projected_ref[r, width_q + width_k :], 1.0) for r in spans]
    down = ((0,), (0,))
    d_keys = [[] for _ in spans]
    d_values = [[] for _ in spans]

    def fold(product):
        kept = jnp.where(low, product[:HEAD_DIM], product[HEAD_DIM:])
        return kept + pltpu.roll(kept, HEAD_DIM, 1)

    for g in range(groups):
        probs = probs_ref[0, g]
        d_rows = []
        for i in range(count):
            row = [
                d_ref[0, i : i + 1, g * GROUP + j * WIDE : g * GROUP + (j + 1) * WIDE]
                for j in range(2)
            ]
            d_rows.append(
                jnp.concatenate(
                    [jnp.broadcast_to(x, (HEAD_DIM, WIDE)) for x in row], 0
                ).astype(BF16)
            )
        d_probs = jnp.concatenate(
            [mm(d_rows[i], values[i][g], ((1,), (1,))) for i in range(count)], 0
        )
        probs_f = probs.astype(F32)
        product = probs_f * d_probs
        upper = product.astype(BF16)
        lower = (product - upper.astype(F32)).astype(BF16)
        inner = mm(jnp.concatenate([upper, lower], 1), ones)
        d_scores = (probs_f * (d_probs - inner)).astype(BF16)
        for i, r in enumerate(spans):
            block = slice(i * WIDE, (i + 1) * WIDE)
            d_query = mm(d_scores[block], keys[i][g]).astype(BF16)
            at = g * GROUP
            out_ref[r, at : at + WIDE] = d_query[:HEAD_DIM]
            out_ref[r, at + WIDE : at + GROUP] = d_query[HEAD_DIM:]
            d_keys[i].append(fold(mm(d_scores[block], stacked(projected_ref, r, g), down)) * scale)
            d_values[i].append(fold(mm(probs[block], d_rows[i], down)))
    for i, r in enumerate(spans):
        out_ref[r, width_q : width_q + width_k] = jnp.where(low, *d_keys[i]).astype(BF16)
        out_ref[r, width_q + width_k :] = jnp.where(low, *d_values[i]).astype(BF16)


def backward(probs, projected, d_attended, groups):
    total, out_width = projected.shape
    steps = probs.shape[0]
    step = total // steps
    batch = step // PASSAGE_LEN
    heads = groups * GROUP
    return pl.pallas_call(
        functools.partial(backward_kernel, groups),
        grid=(steps,),
        in_specs=[
            pl.BlockSpec((1,) + probs.shape[1:], lambda i: (i, 0, 0, 0)),
            pl.BlockSpec((step, out_width), lambda i: (i, 0)),
            pl.BlockSpec((1, batch, heads), lambda i: (i, 0, 0)),
        ],
        out_specs=pl.BlockSpec((step, out_width), lambda i: (i, 0)),
        out_shape=jax.ShapeDtypeStruct((total, out_width), BF16),
        compiler_params=params(),
        cost_estimate=pl.CostEstimate(
            flops=16 * total * heads * GROUP,
            bytes_accessed=2 * total * (heads + 2 * out_width),
            transcendentals=0,
        ),
        name="attend_back",
    )(probs, projected, d_attended.reshape(steps, batch, heads))


def score_kernel(chips, where_ref, mine_ref, other_ref, sum_ref, final_ref, ws_ref, prior_ref,
                 *refs):
    pieces, refs = refs[: 4 * chips], refs[4 * chips :]
    unit_ref, inverse_ref, score_ref, attn_ref, product_ref = refs
    chip, core = where_ref[0], where_ref[1]
    mine, other = mine_ref[...], other_ref[...]
    attn = jnp.concatenate(
        [jnp.where(core == 0, mine, other), jnp.where(core == 0, other, mine)], 1
    )
    count = attn.shape[0]
    upper = attn.astype(BF16)
    attn_ref[...] = upper
    both = jnp.concatenate([upper.astype(F32), attn - upper.astype(F32)], 0)
    product_ref[...] = both
    depth, part = pieces[0].shape
    out = [None] * 4
    for s in range(chips):
        start = pl.multiple_of((chip ^ s) * depth, depth)
        block = product_ref[:, pl.ds(start, depth)].astype(BF16)
        for k in range(4):
            x = mm(block, pieces[4 * s + k][...])
            out[k] = x if out[k] is None else out[k] + x
    out = [x[:count] + x[count:] for x in out]
    own, far = jnp.concatenate(out[:2], 1), jnp.concatenate(out[2:], 1)
    product = jnp.concatenate(
        [jnp.where(core == 0, own, far), jnp.where(core == 0, far, own)], 1
    )
    pooled = (sum_ref[...] + product) * (1.0 / PASSAGE_LEN)
    inverse = lax.rsqrt(jnp.mean(pooled * pooled, -1, keepdims=True) + epsilon)
    unit = pooled * inverse
    score = jnp.sum(unit * (final_ref[...] * ws_ref[...]), -1, keepdims=True)
    unit_ref[...] = unit
    inverse_ref[...] = jnp.broadcast_to(inverse, inverse_ref.shape)
    score_ref[...] = score + prior_ref[...]


def score_pass(where, mine, other, sums, final_gain, w_score, prior, pieces):
    count, width = sums.shape
    lanes = prior.shape[1]
    inner = 2 * mine.shape[1]
    vmem = pl.BlockSpec(memory_space=pltpu.VMEM)
    return pl.pallas_call(
        functools.partial(score_kernel, len(pieces) // 4),
        in_specs=[pl.BlockSpec(memory_space=pltpu.SMEM)] + [vmem] * (6 + len(pieces)),
        out_specs=[vmem] * 4,
        out_shape=[
            jax.ShapeDtypeStruct((count, width), F32),
            jax.ShapeDtypeStruct((count, lanes), F32),
            jax.ShapeDtypeStruct((count, lanes), F32),
            jax.ShapeDtypeStruct((count, inner), BF16),
        ],
        scratch_shapes=[pltpu.VMEM((2 * count, inner), F32)],
        compiler_params=pltpu.CompilerParams(vmem_limit_bytes=VMEM),
        cost_estimate=pl.CostEstimate(
            flops=4 * count * width * inner, bytes_accessed=2 * width * inner, transcendentals=0
        ),
        name="pool_score",
    )(where, mine, other, sums, final_gain[None], w_score[None], prior, *pieces)


def list_kernel(blocks, chips, passages, where_ref, place_ref, bounds_ref, unit_ref, inverse_ref,
                final_ref, ws_ref, *refs):
    scores = [ref[...] for ref in refs[:blocks]]
    weights = [ref[...] for ref in refs[blocks : 2 * blocks]]
    pieces, refs = refs[2 * blocks : 2 * blocks + 4 * chips], refs[2 * blocks + 4 * chips :]
    d_rows_ref, d_att_ref, loss_ref, back_ref = refs
    chip, core = where_ref[0], where_ref[1]
    starts, ends = bounds_ref[0:1], bounds_ref[1:2]
    pair = 2 * passages
    lanes = starts.shape[1]
    row = lax.broadcasted_iota(jnp.int32, (pair, lanes), 0)
    offset = jnp.where(
        row < passages, core * passages + row, (1 - core) * passages + row - passages
    )
    members = []
    for j in range(blocks):
        place = place_ref[j] * pair + offset
        members.append((place >= starts) & (place < ends))
    column = [jnp.broadcast_to(score[:, :1], (pair, lanes)) for score in scores]
    heavy = [jnp.broadcast_to(weight[:, :1], (pair, lanes)) for weight in weights]
    peak = functools.reduce(
        jnp.maximum,
        [jnp.max(jnp.where(m, s, -1e30), 0, keepdims=True) for m, s in zip(members, column)],
    )
    total = sum(
        jnp.sum(jnp.where(m, jnp.exp(jnp.where(m, s - peak, 0.0)), 0.0), 0, keepdims=True)
        for m, s in zip(members, column)
    )
    label_total = sum(
        jnp.sum(jnp.where(m, w, 0.0), 0, keepdims=True) for m, w in zip(members, heavy)
    )
    log_norm = peak + jnp.log(total)
    own = members[0]
    log_prob = column[0][:, :1] - jnp.sum(jnp.where(own, log_norm, 0.0), 1, keepdims=True)
    target = heavy[0][:, :1] / jnp.sum(jnp.where(own, label_total, 0.0), 1, keepdims=True)
    loss = -loss_scale * jnp.sum((target * log_prob)[:passages], 0, keepdims=True)
    loss_ref[...] = jnp.broadcast_to(loss, loss_ref.shape)
    d_score = loss_scale * (jnp.exp(log_prob) - target)
    unit = unit_ref[...]
    d_unit = d_score * (ws_ref[...] * final_ref[...])
    mean = jnp.mean(d_unit * unit, -1, keepdims=True)
    d_pooled = inverse_ref[:, :1] * (d_unit - unit * mean)
    d_rows = (d_pooled * (1.0 / PASSAGE_LEN)).astype(BF16)
    d_rows_ref[...] = d_rows
    depth, part = pieces[0].shape
    half = d_rows.shape[1] // 2
    own = jnp.where(core == 0, d_pooled[:, :half], d_pooled[:, half:])
    far = jnp.where(core == 0, d_pooled[:, half:], d_pooled[:, :half])
    cut = [own[:, :part], own[:, part:], far[:, :part], far[:, part:]]
    cut = [(x * (1.0 / PASSAGE_LEN)).astype(BF16) for x in cut]
    for s in range(chips):
        back = sum(mm(cut[k], pieces[4 * s + k][...], ((1,), (1,))) for k in range(4))
        start = pl.multiple_of((chip ^ s) * depth, depth)
        back_ref[:, pl.ds(start, depth)] = back.astype(BF16).astype(F32)
    back = back_ref[...]
    half = back.shape[1] // 2
    d_att_ref[...] = jnp.where(core == 0, back[:, :half], back[:, half:])


def list_pass(where, places, bounds, unit, inverse, final_gain, w_score, scores, weights, pieces,
              passages):
    count, width = unit.shape
    chips = len(pieces) // 4
    inner = chips * pieces[0].shape[0]
    vmem = pl.BlockSpec(memory_space=pltpu.VMEM)
    smem = pl.BlockSpec(memory_space=pltpu.SMEM)
    return pl.pallas_call(
        functools.partial(list_kernel, len(scores), chips, passages),
        in_specs=[smem] * 2 + [vmem] * (5 + 2 * len(scores) + len(pieces)),
        out_specs=[vmem] * 3,
        out_shape=[
            jax.ShapeDtypeStruct((count, width), BF16),
            jax.ShapeDtypeStruct((count, inner // 2), F32),
            jax.ShapeDtypeStruct((8, 128), F32),
        ],
        scratch_shapes=[pltpu.VMEM((count, inner), F32)],
        compiler_params=pltpu.CompilerParams(vmem_limit_bytes=VMEM),
        cost_estimate=pl.CostEstimate(
            flops=2 * count * width * inner, bytes_accessed=2 * width * inner, transcendentals=count
        ),
        name="list_grad",
    )(where, places, bounds, unit, inverse, final_gain[None], w_score[None], *scores, *weights,
      *pieces)


def grad_kernel(where_ref, own_ref, sib_ref, d_own_ref, d_sib_ref, a_ref, b_ref):
    out = mm(own_ref[...], d_own_ref[...]) + mm(sib_ref[...], d_sib_ref[...])
    out = out.astype(BF16)
    a_ref[...] = out[:, : a_ref.shape[1]]
    b_ref[...] = out[:, a_ref.shape[1] :]


def grad_block(where, s, own, sib, d_own, d_sib, depth):
    rows = own.shape[1]
    width = d_own.shape[1]
    tile = min(depth, 256)
    tiles = depth // tile
    part = width // 2

    def lhs(i, w):
        return ((w[0] ^ s) * tiles + i, 0)

    whole = lambda i, w: (0, 0)
    return pl.pallas_call(
        grad_kernel,
        grid_spec=pltpu.PrefetchScalarGridSpec(
            num_scalar_prefetch=1,
            grid=(tiles,),
            in_specs=[
                pl.BlockSpec((tile, rows), lhs),
                pl.BlockSpec((tile, rows), lhs),
                pl.BlockSpec((rows, width), whole),
                pl.BlockSpec((rows, width), whole),
            ],
            out_specs=[pl.BlockSpec((tile, part), lambda i, w: (i, 0))] * 2,
        ),
        out_shape=[jax.ShapeDtypeStruct((depth, part), BF16)] * 2,
        compiler_params=params(),
        cost_estimate=pl.CostEstimate(
            flops=4 * rows * depth * width,
            bytes_accessed=4 * rows * (depth + width) + 2 * depth * width,
            transcendentals=0,
        ),
        name="grad_rows",
    )(where, own, sib, d_own, d_sib)


def solution(mesh):
    n_list, n_fsdp = mesh.shape["list"], mesh.shape["fsdp"]
    bits = [1 << k for k in range(1, n_fsdp.bit_length() - 1)]
    pairs = n_list * n_fsdp // 2

    def across(value, distance):
        return lax.ppermute(value, "fsdp", [(i, i ^ distance) for i in range(n_fsdp)])

    def along(value, distance):
        return lax.ppermute(value, "list", [(i, i ^ distance) for i in range(n_list)])

    def partner(kind, pair):
        return (
            pair ^ 1,
            ((pair + 1) ^ 1) - 1,
            pair ^ 2,
            ((pair + 2) ^ 2) - 2,
        )[kind]

    def neighbour(value, kind):
        moves = []
        for pair in range(pairs):
            other = partner(kind, pair)
            if 0 <= other < pairs:
                moves += [(2 * pair + core, 2 * other + core) for core in (0, 1)]
        return lax.ppermute(value, ("list", "fsdp"), moves)

    def gathered(value, order):
        have = {0: value}
        for bit in order:
            have.update({s ^ (bit >> 1): across(part, bit) for s, part in list(have.items())})
        return have

    def scattered(parts, order):
        current = dict(parts)
        for bit in order:
            flag = bit >> 1
            come = {s ^ flag: across(current[s], bit) for s in sorted(current)[::-1] if s & flag}
            current = {
                s: (current[s].astype(F32) + come[s].astype(F32)).astype(BF16)
                for s in current
                if not s & flag
            }
        return current[0]

    def local(hidden, norm_gain, w_qkv, w_out, final_gain, w_score, prior, labels, lengths):
        passages, _, width = hidden.shape
        assert 4 * passages >= LONGEST - 1
        groups = KV_HEADS // 2
        width_q, width_k = groups * GROUP, groups * HEAD_DIM
        index = lax.axis_index("fsdp")
        core = index % 2
        chip = index // 2
        where = jnp.stack([chip, core]).astype(jnp.int32)
        first_core = core == 0

        def ordered(mine, other, axis):
            return jnp.where(
                first_core,
                jnp.concatenate([mine, other], axis),
                jnp.concatenate([other, mine], axis),
            )

        starts = (0, 2 * width_q, 2 * (width_q + width_k))
        sizes = (width_q, width_k, width_k)

        def half(h):
            return jnp.concatenate(
                [w_qkv[:, a + h * n : a + (h + 1) * n] for a, n in zip(starts, sizes)], 1
            )

        halves = half(0), half(1)
        keep = jnp.where(first_core, *halves)
        give = jnp.where(first_core, halves[1], halves[0])
        come = across(give, 1)
        pair_rows = ordered(keep, come, 0)
        middle = pair_rows.shape[1] // 2
        part_a = gathered(pair_rows[:, :middle], bits)
        part_b = gathered(pair_rows[:, middle:], bits[::-1])
        chips = n_fsdp // 2
        last = max(bin(s).count("1") for s in range(chips))
        weights = [{}, {}, {}]
        for s in range(chips):
            ones = bin(s).count("1")
            weights[2 if ones == last else 1 if ones else 0][s] = (part_a[s], part_b[s])

        hidden, w_out, part_a[0] = lax.optimization_barrier((hidden, w_out, part_a[0]))
        cols = w_out.shape[1] // 2
        out_halves = w_out[:, :cols], w_out[:, cols:]
        out_keep = jnp.where(first_core, *out_halves)
        out_pair = ordered(out_keep, across(jnp.where(first_core, *out_halves[::-1]), 1), 0)
        out_a = gathered(out_pair[:, : cols // 2], bits)
        out_b = gathered(out_pair[:, cols // 2 :], bits[::-1])
        pieces = []
        for s in range(chips):
            pieces += [out_a[s], out_b[s], across(out_a[s], 1), across(out_b[s], 1)]

        normal, sums = norm(hidden, norm_gain)
        normal_sib, sums_sib = across(normal, 1), across(sums, 1)
        sums = jnp.concatenate([sums, sums_sib], 0)
        lanes = -(-lengths.shape[0] // 128) * 128
        label_weight = jnp.exp(labels.astype(F32))
        small = jnp.broadcast_to(
            jnp.concatenate([prior, label_weight])[:, None], (2 * passages, 128)
        )
        small_sib = across(small, 1)
        prior_pair = jnp.concatenate([small[:passages], small_sib[:passages]], 0)
        heavy = jnp.concatenate([small[passages:], small_sib[passages:]], 0)
        heavies = [heavy] + [neighbour(heavy, kind) for kind in range(4)]
        pair = lax.axis_index("list") * (n_fsdp // 2) + chip
        places = jnp.stack([pair] + [partner(kind, pair) for kind in range(4)]).astype(jnp.int32)
        ends = jnp.cumsum(lengths)
        bounds = jnp.pad(jnp.stack([ends - lengths, ends]), ((0, 0), (0, lanes - lengths.shape[0])))

        def begin(rows):
            before, turned = first_project(where, rows, weights[0][0])
            if weights[1]:
                before = partial_project(where, rows, weights[1], before)
            return before, turned

        before_own, turned_own = begin(normal)
        before_sib, turned_sib = begin(normal_sib)
        proj_sib, probs_sib, attn_sib = forward(where, normal_sib, weights[2], groups, before_sib)
        attn_sib = attn_sib.reshape(passages, -1)
        attn_sib_other = across(attn_sib, 1)
        proj_own, probs_own, attn_own = forward(where, normal, weights[2], groups, before_own)
        attn_own = attn_own.reshape(passages, -1)
        attn_own_other = across(attn_own, 1)
        mine = jnp.concatenate([attn_own, attn_sib], 0)
        other = jnp.concatenate([attn_sib_other, attn_own_other], 0)
        unit, inverse, score, attn = score_pass(
            where, mine, other, sums, final_gain, w_score, prior_pair, pieces
        )
        scores = [score] + [neighbour(score, kind) for kind in range(4)]
        d_rows, d_attended, loss_part = list_pass(
            where, places, bounds, unit, inverse, final_gain, w_score, scores, heavies, pieces,
            passages,
        )

        d_own = backward(probs_own, proj_own, d_attended[:passages], groups)
        d_sib = backward(probs_sib, proj_sib, d_attended[passages:], groups)
        depth = pair_rows.shape[0]
        blocks = {
            s: grad_block(where, s, turned_own, turned_sib, d_own, d_sib, depth)
            for s in sorted(range(n_fsdp // 2), key=lambda s: -bin(s).count("1"))
        }
        sum_a = scattered({s: blocks[s][0] for s in blocks}, bits)
        sum_b = scattered({s: blocks[s][1] for s in blocks}, bits[::-1])
        chip_sum = jnp.concatenate([sum_a, sum_b], 1)
        upper, lower = chip_sum[: depth // 2], chip_sum[depth // 2 :]
        keep = jnp.where(first_core, upper, lower)
        come = across(jnp.where(first_core, lower, upper), 1)
        columns = []
        at = 0
        for n in sizes:
            columns.append(ordered(keep[:, at : at + n], come[:, at : at + n], 1))
            at += n
        rows_sum = jnp.concatenate(columns, 1)
        place = lax.axis_index("list")

        def list_scatter(value):
            n = value.shape[1] // n_list
            block = lambda which: lax.dynamic_slice_in_dim(value, which * n, n, 1)
            total = block(place).astype(F32)
            for distance in range(1, n_list):
                total = total + along(block(place ^ distance).astype(BF16), distance).astype(F32)
            return total

        grad_qkv = list_scatter(rows_sum)

        inner = attn.shape[1]
        attn_halves = attn[:, : inner // 2], attn[:, inner // 2 :]
        row_halves = d_rows[:, :cols], d_rows[:, cols:]
        payload = jnp.concatenate(
            [jnp.where(first_core, *attn_halves), jnp.where(first_core, *row_halves)], 1
        )
        plane = gathered(payload, bits)
        plane = jnp.concatenate([plane[s] for s in range(chips)], 0)
        far = across(plane, 1)
        own_rows = inner // n_fsdp
        far = far.reshape(chips, 2, passages, -1)[:, ::-1].reshape(plane.shape)
        left = ordered(plane[:, : inner // 2], far[:, : inner // 2], 1)
        right = ordered(plane[:, inner // 2 :], far[:, inner // 2 :], 1)
        left = lax.dynamic_slice_in_dim(left, index * own_rows, own_rows, 1)
        grad_out = list_scatter(
            lax.dot_general(left, right, (((0,), (0,)), ((), ())), preferred_element_type=F32)
        )

        loss = loss_part
        for distance in [1] + bits:
            loss = loss + across(loss, distance)
        distance = 1
        while distance < n_list:
            loss = loss + along(loss, distance)
            distance *= 2
        return (loss[0, 0], grad_qkv, grad_out)

    placed = (
        P(("list", "fsdp"), None, None),
        P(),
        P("fsdp", None),
        P("fsdp", None),
        P(),
        P(),
        P(("list", "fsdp")),
        P(("list", "fsdp")),
        P(),
    )
    return jax.shard_map(
        local,
        mesh=mesh,
        in_specs=placed,
        out_specs=(P(), P("fsdp", "list"), P("fsdp", "list")),
        check_vma=False,
    )
```

time: 248 us -> 202 us (0.81)
  starting transfers between devices: 44.6 us -> 66.4 us
  waiting for transfers between devices: 71.4 us -> 50.4 us
  blocking collectives: 16.9 us -> 0 us
  Pallas kernels: 79.7 us -> 65 us
  between operations: 14.6 us -> 1.31 us
  local copies, waits for them, and re-layouts: 12.7 us -> 10.1 us
    ppermute x22 -> x41, waiting for transfers between devices: 51.6 us -> 30.4 us  [across(): lax.ppermute(value, 'fsdp', [(i, i ^ distance) for i in range(n_fsdp)])]
    pallas_call x2 -> x6, Pallas kernels: 3.84 us -> 24.7 us  [the longest x2 11.9 us: first_project(): pl.pallas_call(first_kernel, grid_spec=pltpu.PrefetchScalarGridSpec(num_s...]
    pallas_call x2, Pallas kernels: 26.6 us -> 6.88 us  [backward(): pl.pallas_call(functools.partial(backward_kernel, groups), grid=(steps,),...]
    all_gather x1 -> x0, blocking collectives: 16.9 us -> none  [local(): plane = lax.all_gather(payload, 'fsdp', axis=0, tiled=True)]
    pallas_call x2, Pallas kernels: 28.2 us -> 12.5 us  [forward(): pl.pallas_call(functools.partial(forward_kernel, pieces, groups), grid_sp...]
    ppermute x22 -> x41, starting transfers between devices: 20.6 us -> 36.1 us  [across(): lax.ppermute(value, 'fsdp', [(i, i ^ distance) for i in range(n_fsdp)])]
    ppermute x8, starting transfers between devices: 11.2 us -> 15.7 us  [neighbour(): return lax.ppermute(value, ('list', 'fsdp'), moves)]
    unnamed x36 -> x22, local copies, waits for them, and re-layouts: 10.8 us -> 6.83 us
  transfers between devices with their start and end apart: 39 -> 57, of which waited for: 12 -> 14; matrix products, arithmetic and copies ran while one was open for 3% -> 3% of each run, Pallas kernels for 19% -> 28%
where the time goes in v2:
time: 202 us; the launch traced here: 201 us
  starting transfers between devices  66.4 us (33%)
  Pallas kernels  65 us (32%)
  waiting for transfers between devices  50.4 us (25%)
  local copies, waits for them, and re-layouts  10.1 us (5%)
  other arithmetic  7.36 us (4%)
    ppermute x41, starting transfers between devices, across(): lax.ppermute(value, 'fsdp', [(i, i ^ distance) for i in range(n_fsdp)])  36.1 us
    ppermute x41, waiting for transfers between devices, across(): lax.ppermute(value, 'fsdp', [(i, i ^ distance) for i in range(n_fsdp)])  30.4 us
    ppermute x8, waiting for transfers between devices, along(): lax.ppermute(value, 'list', [(i, i ^ distance) for i in range(n_list)])  19.2 us
    ppermute x8, starting transfers between devices, neighbour(): return lax.ppermute(value, ('list', 'fsdp'), moves)  15.7 us
    pallas_call x4, Pallas kernels, grad_block(): pl.pallas_call(grad_kernel, grid_spec=pltpu.PrefetchScalarGridSpec(num_sc...  15 us
    ppermute x8, starting transfers between devices, along(): lax.ppermute(value, 'list', [(i, i ^ distance) for i in range(n_list)])  14.6 us
    pallas_call x2, Pallas kernels, forward(): pl.pallas_call(functools.partial(forward_kernel, pieces, groups), grid_sp...  12.5 us
    pallas_call x2, Pallas kernels, first_project(): pl.pallas_call(first_kernel, grid_spec=pltpu.PrefetchScalarGridSpec(num_s...  11.9 us
  transfers between devices with their start and end apart: 57, of which 14 were waited for; matrix products, arithmetic and copies ran while one was open for 3% of the time, Pallas kernels for 28%

profile of v2, /device:TPU:0, one launch (start us, length us, event | category | flops | bytes accessed | tf_op | source)
XLA Modules:
  0.0 200.9 jit_solution(2094697960781600433)
XLA Ops:
  5.4 5.9 %norm_rows.1 = (bf16[16,64,2048]{2,1,0:T(8,128)(2,1)}, f32[4,4,2048]{2,1,0:T(4,128)S(1)}) custom-call(bf16[16,64,2048]{2,1,0:T(8,128)(2,1)} %hidden_ref, f32[1,2048]{1,0:T(1,128)S(1)} %bitcast.32), custom_call_target="tpu_custom_call" | custom-call | flops 12582912 | bytes 8388608 | tf_op jit(solution)/shard_map/norm_rows/pallas_call | solution.py:48
  13.0 5.0 %collective-permute-done.11 = f32[32,128]{1,0:T(8,128)S(1)} collective-permute-done((f32[32,128]{1,0:T(8,128)S(1)}, f32[32,128]{1,0:T(8,128)S(1)}, u32[]{:S(2)}, u32[]{:S(2)}) %collective-permute-start.11) | collective-permute-done | bytes 16416 | tf_op jit(solution)/shard_map/ppermute | solution.py:557
  17.9 2.6 %collective-permute-start.1 = (bf16[512,384]{1,0:T(8,128)(2,1)S(1)}, bf16[512,384]{1,0:T(8,128)(2,1)S(1)}, u32[]{:S(2)}, u32[]{:S(2)}) collective-permute-start(bf16[512,384]{1,0:T(8,128)(2,1)S(1)} %get-tuple-element.70.a_ref), channel_id=1, source_target_pairs={{0,2},{1,3},{2,0},{3,1},{4,6},{5,7},{6,4},{7,5},{8,10},{9,11},{10,... | collective-permute-start | bytes 1179656 | tf_op jit(solution)/shard_map/ppermute | solution.py:557
  22.7 6.0 %project_first.2 = (f32[1024,768]{1,0:T(8,128)S(1)}, bf16[2048,1024]{1,0:T(8,128)(2,1)}) custom-call(s32[2]{0:T(128)S(1)} %pad_add_fusion.1.where_ref, bf16[1024,2048]{1,0:T(8,128)(2,1)} %bitcast.10.rows_ref.refs_0_.refs_1_, bf16[512,384]{1,0:T(8,128)(2,1)S(1)} %get-tuple-element.70.a_ref, bf16[512,384]{1,0:T(8,128)(2,1)S(1)} %get-tuple-element.69.b_ref), custom_call_target="tpu_custom_call" | custom-call | flops 805306368 | bytes 11534336 | tf_op jit(solution)/shard_map/project_first/pallas_call | solution.py:190
  34.1 4.8 %collective-permute-done.5.refs_3_ = bf16[512,384]{1,0:T(8,128)(2,1)S(1)} collective-permute-done((bf16[512,384]{1,0:T(8,128)(2,1)S(1)}, bf16[512,384]{1,0:T(8,128)(2,1)S(1)}, u32[]{:S(2)}, u32[]{:S(2)}) %collective-permute-start.5) | collective-permute-done | bytes 393248 | tf_op jit(solution)/shard_map/ppermute | solution.py:557
  41.0 4.5 %project_more.2.refs_3_ = f32[1024,768]{1,0:T(8,128)S(1)} custom-call(s32[2]{0:T(128)S(1)} %pad_add_fusion.1.where_ref, bf16[1024,2048]{1,0:T(8,128)(2,1)} %bitcast.10.rows_ref.refs_0_.refs_1_, bf16[1024,2048]{1,0:T(8,128)(2,1)} %bitcast.10.rows_ref.refs_0_.refs_1_, bf16[512,384]{1,0:T(8,128)(2,1)S(1)} %collective-permute-done.1.refs_2_, ...), custom_call_target="tpu_custom_call" | custom-call | flops 1610612736 | bytes 8388608 | tf_op jit(solution)/shard_map/project_more/pallas_call | solution.py:225
  50.7 6.3 %project_attend.2 = (bf16[1024,768]{1,0:T(8,128)(2,1)S(1)}, bf16[2,2,1024,128]{3,2,1,0:T(8,128)(2,1)S(1)}, f32[2,8,512]{2,1,0:T(8,128)S(1)}) custom-call(s32[2]{0:T(128)S(1)} %pad_add_fusion.1.where_ref, bf16[1024,2048]{1,0:T(8,128)(2,1)} %bitcast.10.rows_ref.refs_0_.refs_1_, bf16[512,384]{1,0:T(8,128)(2,1)S(1)} %collective-permute-done.2.refs_1_, ...), custom_call_target="tpu_custom_call" | custom-call | flops 1879048192 | bytes 6815744 | tf_op jit(solution)/shard_map/project_attend/pallas_call | solution.py:256
  56.9 5.9 %project_first.3 = (f32[1024,768]{1,0:T(8,128)S(1)}, bf16[2048,1024]{1,0:T(8,128)(2,1)}) custom-call(s32[2]{0:T(128)S(1)} %pad_add_fusion.1.where_ref, bf16[1024,2048]{1,0:T(8,128)(2,1)} %collective-permute-done.7.rows_ref.refs_0_.refs_1_, bf16[512,384]{1,0:T(8,128)(2,1)S(1)} %get-tuple-element.70.a_ref, bf16[512,384]{1,0:T(8,128)(2,1)S(1)} %get-tuple-element.69.b_ref), custom_call_target="tpu_custom_call" | custom-call | flops 805306368 | bytes 11534336 | tf_op jit(solution)/shard_map/project_first/pallas_call | solution.py:190
  66.5 4.5 %project_more.3.refs_3_ = f32[1024,768]{1,0:T(8,128)S(1)} custom-call(s32[2]{0:T(128)S(1)} %pad_add_fusion.1.where_ref, bf16[1024,2048]{1,0:T(8,128)(2,1)} %collective-permute-done.7.rows_ref.refs_0_.refs_1_, bf16[1024,2048]{1,0:T(8,128)(2,1)} %collective-permute-done.7.rows_ref.refs_0_.refs_1_, bf16[512,384]{1,0:T(8,128)(2,1)S(1)} %collective-permute-done.1.refs_2_, ...), custom_call_target="tpu_custom_call" | custom-call | flops 1610612736 | bytes 8388608 | tf_op jit(solution)/shard_map/project_more/pallas_call | solution.py:225
  74.7 6.2 %project_attend.3 = (bf16[1024,768]{1,0:T(8,128)(2,1)S(1)}, bf16[2,2,1024,128]{3,2,1,0:T(8,128)(2,1)S(1)}, f32[2,8,512]{2,1,0:T(8,128)S(1)}) custom-call(s32[2]{0:T(128)S(1)} %pad_add_fusion.1.where_ref, bf16[1024,2048]{1,0:T(8,128)(2,1)} %collective-permute-done.7.rows_ref.refs_0_.refs_1_, bf16[512,384]{1,0:T(8,128)(2,1)S(1)} %collective-permute-done.2.refs_1_, ...), custom_call_target="tpu_custom_call" | custom-call | flops 1879048192 | bytes 6815744 | tf_op jit(solution)/shard_map/project_attend/pallas_call | solution.py:256
  85.7 3.3 %collective-permute-start.33 = (f32[32,128]{1,0:T(8,128)S(1)}, f32[32,128]{1,0:T(8,128)S(1)}, u32[]{:S(2)}, u32[]{:S(2)}) collective-permute-start(f32[32,128]{1,0:T(8,128)S(1)} %pad_maximum_fusion.10.refs_5_), channel_id=1, source_target_pairs={{0,4},{1,5},{2,6},{3,7},{4,0},{5,1},{6,2},{7,3},{8,12},{9,13},{10,... | collective-permute-start | bytes 49160 | tf_op jit(solution)/shard_map/ppermute | solution.py:576
  91.4 2.5 %collective-permute-start.27 = (f32[32,128]{1,0:T(8,128)S(1)}, f32[32,128]{1,0:T(8,128)S(1)}, u32[]{:S(2)}, u32[]{:S(2)}) collective-permute-start(f32[32,128]{1,0:T(8,128)S(1)} %get-tuple-element.42.refs_0_), channel_id=1, source_target_pairs={{0,2},{1,3},{2,0},{3,1},{4,6},{5,7},{6,4},{7,5},{8,10},{9,11},{10,... | collective-permute-start | bytes 49160 | tf_op jit(solution)/shard_map/ppermute | solution.py:576
  94.5 5.6 %collective-permute-start.29 = (f32[32,128]{1,0:T(8,128)S(1)}, f32[32,128]{1,0:T(8,128)S(1)}, u32[]{:S(2)}, u32[]{:S(2)}) collective-permute-start(f32[32,128]{1,0:T(8,128)S(1)} %get-tuple-element.42.refs_0_), channel_id=1, source_target_pairs={{0,4},{1,5},{2,6},{3,7},{4,0},{5,1},{6,2},{7,3},{8,12},{9,13},{10,... | collective-permute-start | bytes 49160 | tf_op jit(solution)/shard_map/ppermute | solution.py:576
  101.9 2.3 %list_grad.1 = (bf16[32,2048]{1,0:T(8,128)(2,1)S(1)}, f32[32,512]{1,0:T(8,128)S(1)}, f32[8,128]{1,0:T(8,128)S(1)}) custom-call(s32[2]{0:T(128)S(1)} %pad_add_fusion.1.where_ref, s32[5]{0:T(128)S(1)} %stack.44.place_ref, s32[2,128]{1,0:T(2,128)S(1)} %pad.4.bounds_ref, f32[32,2048]{1,0:T(8,128)S(1)} %get-tuple-element.40.unit_ref, ...), custom_call_target="tpu_custom_call" | custom-call | flops 134217728 | bytes 4194304 | tf_op jit(solution)/shard_map/list_grad/pallas_call | solution.py:490
  104.2 3.4 %attend_back.2.d_own_ref = bf16[1024,768]{1,0:T(8,128)(2,1)S(1)} custom-call(bf16[2,2,1024,128]{3,2,1,0:T(8,128)(2,1)S(1)} %get-tuple-element.46.probs_ref, bf16[1024,768]{1,0:T(8,128)(2,1)S(1)} %get-tuple-element.47.projected_ref, f32[2,8,512]{2,1,0:T(8,128)S(1)} %get-tuple-element.88.d_ref), custom_call_target="tpu_custom_call" | custom-call | flops 2147483648 | bytes 4194304 | tf_op jit(solution)/shard_map/attend_back/pallas_call | solution.py:344
  107.7 3.4 %attend_back.3.d_sib_ref = bf16[1024,768]{1,0:T(8,128)(2,1)S(1)} custom-call(bf16[2,2,1024,128]{3,2,1,0:T(8,128)(2,1)S(1)} %get-tuple-element.49.probs_ref, bf16[1024,768]{1,0:T(8,128)(2,1)S(1)} %get-tuple-element.50.projected_ref, f32[2,8,512]{2,1,0:T(8,128)S(1)} %get-tuple-element.87.d_ref), custom_call_target="tpu_custom_call" | custom-call | flops 2147483648 | bytes 4194304 | tf_op jit(solution)/shard_map/attend_back/pallas_call | solution.py:344
  111.1 3.8 %grad_rows.7 = (bf16[512,384]{1,0:T(8,128)(2,1)S(1)}, bf16[512,384]{1,0:T(8,128)(2,1)S(1)}) custom-call(s32[2]{0:T(128)S(1)} %pad_add_fusion.1.where_ref, bf16[2048,1024]{1,0:T(8,128)(2,1)} %get-tuple-element.44.own_ref, bf16[2048,1024]{1,0:T(8,128)(2,1)} %get-tuple-element.45.sib_ref, bf16[1024,768]{1,0:T(8,128)(2,1)S(1)} %attend_back.2.d_own_ref, ...), custom_call_target="tpu_custom_call" | custom-call | flops 1610612736 | bytes 6029312 | tf_op jit(solution)/shard_map/grad_rows/pallas_call | solution.py:527
  114.9 5.0 %collective-permute-start.44 = (bf16[512,384]{1,0:T(8,128)(2,1)S(1)}, bf16[512,384]{1,0:T(8,128)(2,1)S(1)}, u32[]{:S(2)}, u32[]{:S(2)}) collective-permute-start(bf16[512,384]{1,0:T(8,128)(2,1)S(1)} %get-tuple-element.58), channel_id=1, source_target_pairs={{0,4},{1,5},{2,6},{3,7},{4,0},{5,1},{6,2},{7,3},{8,12},{9,13},{10,... | collective-permute-start | bytes 1179656 | tf_op jit(solution)/shard_map/ppermute | solution.py:557
  119.9 3.4 %collective-permute-start.36 = (f32[8,128]{1,0:T(8,128)S(1)}, f32[8,128]{1,0:T(8,128)S(1)}, u32[]{:S(2)}, u32[]{:S(2)}) collective-permute-start(f32[8,128]{1,0:T(8,128)S(1)} %add.100), channel_id=1, source_target_pairs={{0,2},{1,3},{2,0},{3,1},{4,6},{5,7},{6,4},{7,5},{8,10},{9,11},{10,... | collective-permute-start | bytes 12296 | tf_op jit(solution)/shard_map/ppermute | solution.py:557
  125.0 3.8 %grad_rows.5 = (bf16[512,384]{1,0:T(8,128)(2,1)S(1)}, bf16[512,384]{1,0:T(8,128)(2,1)S(1)}) custom-call(s32[2]{0:T(128)S(1)} %pad_add_fusion.1.where_ref, bf16[2048,1024]{1,0:T(8,128)(2,1)} %get-tuple-element.44.own_ref, bf16[2048,1024]{1,0:T(8,128)(2,1)} %get-tuple-element.45.sib_ref, bf16[1024,768]{1,0:T(8,128)(2,1)S(1)} %attend_back.2.d_own_ref, ...), custom_call_target="tpu_custom_call" | custom-call | flops 1610612736 | bytes 6029312 | tf_op jit(solution)/shard_map/grad_rows/pallas_call | solution.py:527
  128.7 2.1 %collective-permute-start.51 = (bf16[32,1536]{1,0:T(8,128)(2,1)S(1)}, bf16[32,1536]{1,0:T(8,128)(2,1)S(1)}, u32[]{:S(2)}, u32[]{:S(2)}) collective-permute-start(bf16[32,1536]{1,0:T(8,128)(2,1)S(1)} %pad_maximum_fusion.6), channel_id=1, source_target_pairs={{0,4},{1,5},{2,6},{3,7},{4,0},{5,1},{6,2},{7,3},{8,12},{9,13},{10,... | collective-permute-start | bytes 294920 | tf_op jit(solution)/shard_map/ppermute | solution.py:557
  130.8 2.4 %collective-permute-start.38 = (f32[8,128]{1,0:T(8,128)S(1)}, f32[8,128]{1,0:T(8,128)S(1)}, u32[]{:S(2)}, u32[]{:S(2)}) collective-permute-start(f32[8,128]{1,0:T(8,128)S(1)} %add.102), channel_id=1, source_target_pairs={{0,8},{8,0},{16,24},{24,16},{1,9},{9,1},{17,25},{25,17},{2,10},{10... | collective-permute-start | bytes 12296 | tf_op jit(solution)/shard_map/ppermute | solution.py:560
  134.3 3.8 %grad_rows.6 = (bf16[512,384]{1,0:T(8,128)(2,1)S(1)}, bf16[512,384]{1,0:T(8,128)(2,1)S(1)}) custom-call(s32[2]{0:T(128)S(1)} %pad_add_fusion.1.where_ref, bf16[2048,1024]{1,0:T(8,128)(2,1)} %get-tuple-element.44.own_ref, bf16[2048,1024]{1,0:T(8,128)(2,1)} %get-tuple-element.45.sib_ref, bf16[1024,768]{1,0:T(8,128)(2,1)S(1)} %attend_back.2.d_own_ref, ...), custom_call_target="tpu_custom_call" | custom-call | flops 1610612736 | bytes 6029312 | tf_op jit(solution)/shard_map/grad_rows/pallas_call | solution.py:527
  143.6 7.6 %collective-permute-done.41 = bf16[512,384]{1,0:T(8,128)(2,1)S(1)} collective-permute-done((bf16[512,384]{1,0:T(8,128)(2,1)S(1)}, bf16[512,384]{1,0:T(8,128)(2,1)S(1)}, u32[]{:S(2)}, u32[]{:S(2)}) %collective-permute-start.41) | collective-permute-done | bytes 393248 | tf_op jit(solution)/shard_map/ppermute | solution.py:557
  155.5 3.8 %grad_rows.4 = (bf16[512,384]{1,0:T(8,128)(2,1)S(1)}, bf16[512,384]{1,0:T(8,128)(2,1)S(1)}) custom-call(s32[2]{0:T(128)S(1)} %pad_add_fusion.1.where_ref, bf16[2048,1024]{1,0:T(8,128)(2,1)} %get-tuple-element.44.own_ref, bf16[2048,1024]{1,0:T(8,128)(2,1)} %get-tuple-element.45.sib_ref, bf16[1024,768]{1,0:T(8,128)(2,1)S(1)} %attend_back.2.d_own_ref, ...), custom_call_target="tpu_custom_call" | custom-call | flops 1610612736 | bytes 6029312 | tf_op jit(solution)/shard_map/grad_rows/pallas_call | solution.py:527
  159.9 5.9 %collective-permute-done.45 = bf16[512,384]{1,0:T(8,128)(2,1)} collective-permute-done((bf16[512,384]{1,0:T(8,128)(2,1)}, bf16[512,384]{1,0:T(8,128)(2,1)}, u32[]{:S(2)}, u32[]{:S(2)}) %collective-permute-start.45) | collective-permute-done | bytes 393248 | tf_op jit(solution)/shard_map/ppermute | solution.py:557
  168.9 2.2 %collective-permute-start.56 = (bf16[128,512]{1,0:T(8,128)(2,1)S(1)}, bf16[128,512]{1,0:T(8,128)(2,1)S(1)}, u32[]{:S(2)}, u32[]{:S(2)}) collective-permute-start(bf16[128,512]{1,0:T(8,128)(2,1)S(1)} %get-tuple-element.62), channel_id=1, source_target_pairs={{0,24},{8,16},{16,8},{24,0},{1,25},{9,17},{17,9},{25,1},{2,26},{10... | collective-permute-start | bytes 393224 | tf_op jit(solution)/shard_map/ppermute | solution.py:560
  171.1 2.3 %collective-permute-start.54 = (bf16[128,512]{1,0:T(8,128)(2,1)S(1)}, bf16[128,512]{1,0:T(8,128)(2,1)S(1)}, u32[]{:S(2)}, u32[]{:S(2)}) collective-permute-start(bf16[128,512]{1,0:T(8,128)(2,1)S(1)} %get-tuple-element.61), channel_id=1, source_target_pairs={{0,8},{8,0},{16,24},{24,16},{1,9},{9,1},{17,25},{25,17},{2,10},{10... | collective-permute-start | bytes 393224 | tf_op jit(solution)/shard_map/ppermute | solution.py:560
  173.8 2.2 %collective-permute-start.49 = (bf16[256,384]{1,0:T(8,128)(2,1)S(1)}, bf16[256,384]{1,0:T(8,128)(2,1)S(1)}, u32[]{:S(2)}, u32[]{:S(2)}) collective-permute-start(bf16[256,384]{1,0:T(8,128)(2,1)S(1)} %get-tuple-element.65), channel_id=1, source_target_pairs={{0,24},{8,16},{16,8},{24,0},{1,25},{9,17},{17,9},{25,1},{2,26},{10... | collective-permute-start | bytes 589832 | tf_op jit(solution)/shard_map/ppermute | solution.py:560
  177.2 4.2 %collective-permute-start.47 = (bf16[256,384]{1,0:T(8,128)(2,1)S(1)}, bf16[256,384]{1,0:T(8,128)(2,1)S(1)}, u32[]{:S(2)}, u32[]{:S(2)}) collective-permute-start(bf16[256,384]{1,0:T(8,128)(2,1)S(1)} %get-tuple-element.64), channel_id=1, source_target_pairs={{0,8},{8,0},{16,24},{24,16},{1,9},{9,1},{17,25},{25,17},{2,10},{10... | collective-permute-start | bytes 589832 | tf_op jit(solution)/shard_map/ppermute | solution.py:560
  181.4 10.7 %collective-permute-done.55 = bf16[128,512]{1,0:T(8,128)(2,1)S(1)} collective-permute-done((bf16[128,512]{1,0:T(8,128)(2,1)S(1)}, bf16[128,512]{1,0:T(8,128)(2,1)S(1)}, u32[]{:S(2)}, u32[]{:S(2)}) %collective-permute-start.55) | collective-permute-done | bytes 131104 | tf_op jit(solution)/shard_map/ppermute | solution.py:560
  192.8 7.3 %collective-permute-done.48 = bf16[256,384]{1,0:T(8,128)(2,1)S(1)} collective-permute-done((bf16[256,384]{1,0:T(8,128)(2,1)S(1)}, bf16[256,384]{1,0:T(8,128)(2,1)S(1)}, u32[]{:S(2)}, u32[]{:S(2)}) %collective-permute-start.48) | collective-permute-done | bytes 196640 | tf_op jit(solution)/shard_map/ppermute | solution.py:560
  (178 shorter events, 57.3 us)
Async XLA Ops:
  11.3 37.5 %collective-permute-start.7 = (bf16[1024,2048]{1,0:T(8,128)(2,1)}, bf16[1024,2048]{1,0:T(8,128)(2,1)}, u32[]{:S(2)}, u32[]{:S(2)}) collective-permute-start(bf16[1024,2048]{1,0:T(8,128)(2,1)} %bitcast.10.rows_ref.refs_0_.refs_1_), channel_id=1, source_target_pairs={{0,1},{1,0},{2,3},{3,2},{4,5},{5,4},{6,7},{7,6},{8,9},{9,8},{10,11... | collective-permute-start | bytes 12582920 | tf_op jit(solution)/shard_map/ppermute | solution.py:557
  17.9 12.6 %collective-permute-start.1 = (bf16[512,384]{1,0:T(8,128)(2,1)S(1)}, bf16[512,384]{1,0:T(8,128)(2,1)S(1)}, u32[]{:S(2)}, u32[]{:S(2)}) collective-permute-start(bf16[512,384]{1,0:T(8,128)(2,1)S(1)} %get-tuple-element.70.a_ref), channel_id=1, source_target_pairs={{0,2},{1,3},{2,0},{3,1},{4,6},{5,7},{6,4},{7,5},{8,10},{9,11},{10,... | collective-permute-start | bytes 1179656 | tf_op jit(solution)/shard_map/ppermute | solution.py:557
  20.6 12.0 %collective-permute-start.3 = (bf16[512,384]{1,0:T(8,128)(2,1)S(1)}, bf16[512,384]{1,0:T(8,128)(2,1)S(1)}, u32[]{:S(2)}, u32[]{:S(2)}) collective-permute-start(bf16[512,384]{1,0:T(8,128)(2,1)S(1)} %get-tuple-element.69.b_ref), channel_id=1, source_target_pairs={{0,4},{1,5},{2,6},{3,7},{4,0},{5,1},{6,2},{7,3},{8,12},{9,13},{10,... | collective-permute-start | bytes 1179656 | tf_op jit(solution)/shard_map/ppermute | solution.py:557
  22.2 16.8 %collective-permute-start.5 = (bf16[512,384]{1,0:T(8,128)(2,1)S(1)}, bf16[512,384]{1,0:T(8,128)(2,1)S(1)}, u32[]{:S(2)}, u32[]{:S(2)}) collective-permute-start(bf16[512,384]{1,0:T(8,128)(2,1)S(1)} %get-tuple-element.69.b_ref), channel_id=1, source_target_pairs={{0,2},{1,3},{2,0},{3,1},{4,6},{5,7},{6,4},{7,5},{8,10},{9,11},{10,... | collective-permute-start | bytes 1179656 | tf_op jit(solution)/shard_map/ppermute | solution.py:557
  22.7 18.3 %collective-permute-start.6 = (bf16[512,384]{1,0:T(8,128)(2,1)S(1)}, bf16[512,384]{1,0:T(8,128)(2,1)S(1)}, u32[]{:S(2)}, u32[]{:S(2)}) collective-permute-start(bf16[512,384]{1,0:T(8,128)(2,1)S(1)} %get-tuple-element.70.a_ref), channel_id=1, source_target_pairs={{0,4},{1,5},{2,6},{3,7},{4,0},{5,1},{6,2},{7,3},{8,12},{9,13},{10,... | collective-permute-start | bytes 1179656 | tf_op jit(solution)/shard_map/ppermute | solution.py:557
  30.5 18.0 %collective-permute-start.2 = (bf16[512,384]{1,0:T(8,128)(2,1)S(1)}, bf16[512,384]{1,0:T(8,128)(2,1)S(1)}, u32[]{:S(2)}, u32[]{:S(2)}) collective-permute-start(bf16[512,384]{1,0:T(8,128)(2,1)S(1)} %collective-permute-done.1.refs_2_), channel_id=1, source_target_pairs={{0,4},{1,5},{2,6},{3,7},{4,0},{5,1},{6,2},{7,3},{8,12},{9,13},{10,... | collective-permute-start | bytes 1179656 | tf_op jit(solution)/shard_map/ppermute | solution.py:557
  32.6 16.2 %collective-permute-start.4 = (bf16[512,384]{1,0:T(8,128)(2,1)S(1)}, bf16[512,384]{1,0:T(8,128)(2,1)S(1)}, u32[]{:S(2)}, u32[]{:S(2)}) collective-permute-start(bf16[512,384]{1,0:T(8,128)(2,1)S(1)} %collective-permute-done.3.refs_5_), channel_id=1, source_target_pairs={{0,2},{1,3},{2,0},{3,1},{4,6},{5,7},{6,4},{7,5},{8,10},{9,11},{10,... | collective-permute-start | bytes 1179656 | tf_op jit(solution)/shard_map/ppermute | solution.py:557
  38.9 25.5 %collective-permute-start.10 = (f32[16,2048]{1,0:T(8,128)S(1)}, f32[16,2048]{1,0:T(8,128)S(1)}, u32[]{:S(2)}, u32[]{:S(2)}) collective-permute-start(f32[16,2048]{1,0:T(8,128)S(1)} %reshape.44), channel_id=1, source_target_pairs={{0,1},{1,0},{2,3},{3,2},{4,5},{5,4},{6,7},{7,6},{8,9},{9,8},{10,11... | collective-permute-start | bytes 393224 | tf_op jit(solution)/shard_map/ppermute | solution.py:557
  41.0 25.0 %collective-permute-start.13 = (bf16[256,512]{1,0:T(8,128)(2,1)S(1)}, bf16[256,512]{1,0:T(8,128)(2,1)S(1)}, u32[]{:S(2)}, u32[]{:S(2)}) collective-permute-start(bf16[256,512]{1,0:T(8,128)(2,1)S(1)} %get-tuple-element.80.refs_0_.refs_10_), channel_id=1, source_target_pairs={{0,1},{1,0},{2,3},{3,2},{4,5},{5,4},{6,7},{7,6},{8,9},{9,8},{10,11... | collective-permute-start | bytes 786440 | tf_op jit(solution)/shard_map/ppermute | solution.py:557
  48.5 24.1 %collective-permute-start.15 = (bf16[256,512]{1,0:T(8,128)(2,1)S(1)}, bf16[256,512]{1,0:T(8,128)(2,1)S(1)}, u32[]{:S(2)}, u32[]{:S(2)}) collective-permute-start(bf16[256,512]{1,0:T(8,128)(2,1)S(1)} %get-tuple-element.80.refs_0_.refs_10_), channel_id=1, source_target_pairs={{0,2},{1,3},{2,0},{3,1},{4,6},{5,7},{6,4},{7,5},{8,10},{9,11},{10,... | collective-permute-start | bytes 786440 | tf_op jit(solution)/shard_map/ppermute | solution.py:557
  48.8 23.8 %collective-permute-start.14 = (bf16[256,512]{1,0:T(8,128)(2,1)S(1)}, bf16[256,512]{1,0:T(8,128)(2,1)S(1)}, u32[]{:S(2)}, u32[]{:S(2)}) collective-permute-start(bf16[256,512]{1,0:T(8,128)(2,1)S(1)} %get-tuple-element.79.refs_1_.refs_11_), channel_id=1, source_target_pairs={{0,1},{1,0},{2,3},{3,2},{4,5},{5,4},{6,7},{7,6},{8,9},{9,8},{10,11... | collective-permute-start | bytes 786440 | tf_op jit(solution)/shard_map/ppermute | solution.py:557
  48.8 25.3 %collective-permute-start.20 = (bf16[256,512]{1,0:T(8,128)(2,1)S(1)}, bf16[256,512]{1,0:T(8,128)(2,1)S(1)}, u32[]{:S(2)}, u32[]{:S(2)}) collective-permute-start(bf16[256,512]{1,0:T(8,128)(2,1)S(1)} %get-tuple-element.79.refs_1_.refs_11_), channel_id=1, source_target_pairs={{0,4},{1,5},{2,6},{3,7},{4,0},{5,1},{6,2},{7,3},{8,12},{9,13},{10,... | collective-permute-start | bytes 786440 | tf_op jit(solution)/shard_map/ppermute | solution.py:557
  64.4 16.5 %collective-permute-start.16 = (bf16[256,512]{1,0:T(8,128)(2,1)S(1)}, bf16[256,512]{1,0:T(8,128)(2,1)S(1)}, u32[]{:S(2)}, u32[]{:S(2)}) collective-permute-start(bf16[256,512]{1,0:T(8,128)(2,1)S(1)} %get-tuple-element.79.refs_1_.refs_11_), channel_id=1, source_target_pairs={{0,2},{1,3},{2,0},{3,1},{4,6},{5,7},{6,4},{7,5},{8,10},{9,11},{10,... | collective-permute-start | bytes 786440 | tf_op jit(solution)/shard_map/ppermute | solution.py:557
  65.9 15.1 %collective-permute-start.19 = (bf16[256,512]{1,0:T(8,128)(2,1)S(1)}, bf16[256,512]{1,0:T(8,128)(2,1)S(1)}, u32[]{:S(2)}, u32[]{:S(2)}) collective-permute-start(bf16[256,512]{1,0:T(8,128)(2,1)S(1)} %get-tuple-element.80.refs_0_.refs_10_), channel_id=1, source_target_pairs={{0,4},{1,5},{2,6},{3,7},{4,0},{5,1},{6,2},{7,3},{8,12},{9,13},{10,... | collective-permute-start | bytes 786440 | tf_op jit(solution)/shard_map/ppermute | solution.py:557
  83.6 10.3 %collective-permute-start.31 = (f32[32,128]{1,0:T(8,128)S(1)}, f32[32,128]{1,0:T(8,128)S(1)}, u32[]{:S(2)}, u32[]{:S(2)}) collective-permute-start(f32[32,128]{1,0:T(8,128)S(1)} %pad_maximum_fusion.10.refs_5_), channel_id=1, source_target_pairs={{0,2},{1,3},{2,0},{3,1},{4,6},{5,7},{6,4},{7,5},{8,10},{9,11},{10,... | collective-permute-start | bytes 49160 | tf_op jit(solution)/shard_map/ppermute | solution.py:576
  85.7 14.4 %collective-permute-start.33 = (f32[32,128]{1,0:T(8,128)S(1)}, f32[32,128]{1,0:T(8,128)S(1)}, u32[]{:S(2)}, u32[]{:S(2)}) collective-permute-start(f32[32,128]{1,0:T(8,128)S(1)} %pad_maximum_fusion.10.refs_5_), channel_id=1, source_target_pairs={{0,4},{1,5},{2,6},{3,7},{4,0},{5,1},{6,2},{7,3},{8,12},{9,13},{10,... | collective-permute-start | bytes 49160 | tf_op jit(solution)/shard_map/ppermute | solution.py:576
  89.0 12.0 %collective-permute-start.34 = (f32[32,128]{1,0:T(8,128)S(1)}, f32[32,128]{1,0:T(8,128)S(1)}, u32[]{:S(2)}, u32[]{:S(2)}) collective-permute-start(f32[32,128]{1,0:T(8,128)S(1)} %pad_maximum_fusion.10.refs_5_), channel_id=1, source_target_pairs={{4,8},{5,9},{6,10},{7,11},{8,4},{9,5},{10,6},{11,7},{12,16},{13,17... | collective-permute-start | bytes 49160 | tf_op jit(solution)/shard_map/ppermute | solution.py:576
  104.1 15.8 %collective-permute-start.35 = (f32[8,128]{1,0:T(8,128)S(1)}, f32[8,128]{1,0:T(8,128)S(1)}, u32[]{:S(2)}, u32[]{:S(2)}) collective-permute-start(f32[8,128]{1,0:T(8,128)S(1)} %get-tuple-element.43), channel_id=1, source_target_pairs={{0,1},{1,0},{2,3},{3,2},{4,5},{5,4},{6,7},{7,6},{8,9},{9,8},{10,11... | collective-permute-start | bytes 12296 | tf_op jit(solution)/shard_map/ppermute | solution.py:557
  114.9 27.7 %collective-permute-start.44 = (bf16[512,384]{1,0:T(8,128)(2,1)S(1)}, bf16[512,384]{1,0:T(8,128)(2,1)S(1)}, u32[]{:S(2)}, u32[]{:S(2)}) collective-permute-start(bf16[512,384]{1,0:T(8,128)(2,1)S(1)} %get-tuple-element.58), channel_id=1, source_target_pairs={{0,4},{1,5},{2,6},{3,7},{4,0},{5,1},{6,2},{7,3},{8,12},{9,13},{10,... | collective-permute-start | bytes 1179656 | tf_op jit(solution)/shard_map/ppermute | solution.py:557
  128.7 12.1 %collective-permute-start.51 = (bf16[32,1536]{1,0:T(8,128)(2,1)S(1)}, bf16[32,1536]{1,0:T(8,128)(2,1)S(1)}, u32[]{:S(2)}, u32[]{:S(2)}) collective-permute-start(bf16[32,1536]{1,0:T(8,128)(2,1)S(1)} %pad_maximum_fusion.6), channel_id=1, source_target_pairs={{0,4},{1,5},{2,6},{3,7},{4,0},{5,1},{6,2},{7,3},{8,12},{9,13},{10,... | collective-permute-start | bytes 294920 | tf_op jit(solution)/shard_map/ppermute | solution.py:557
  138.1 21.9 %collective-permute-start.43 = (bf16[512,384]{1,0:T(8,128)(2,1)S(1)}, bf16[512,384]{1,0:T(8,128)(2,1)S(1)}, u32[]{:S(2)}, u32[]{:S(2)}) collective-permute-start(bf16[512,384]{1,0:T(8,128)(2,1)S(1)} %get-tuple-element.56), channel_id=1, source_target_pairs={{0,4},{1,5},{2,6},{3,7},{4,0},{5,1},{6,2},{7,3},{8,12},{9,13},{10,... | collective-permute-start | bytes 1179656 | tf_op jit(solution)/shard_map/ppermute | solution.py:557
  139.1 12.1 %collective-permute-start.41 = (bf16[512,384]{1,0:T(8,128)(2,1)S(1)}, bf16[512,384]{1,0:T(8,128)(2,1)S(1)}, u32[]{:S(2)}, u32[]{:S(2)}) collective-permute-start(bf16[512,384]{1,0:T(8,128)(2,1)S(1)} %get-tuple-element.54), channel_id=1, source_target_pairs={{0,2},{1,3},{2,0},{3,1},{4,6},{5,7},{6,4},{7,5},{8,10},{9,11},{10,... | collective-permute-start | bytes 1179656 | tf_op jit(solution)/shard_map/ppermute | solution.py:557
  140.8 26.2 %collective-permute-start.40 = (bf16[512,384]{1,0:T(8,128)(2,1)S(1)}, bf16[512,384]{1,0:T(8,128)(2,1)}, u32[]{:S(2)}, u32[]{:S(2)}) collective-permute-start(bf16[512,384]{1,0:T(8,128)(2,1)S(1)} %get-tuple-element.52), channel_id=1, source_target_pairs={{0,2},{1,3},{2,0},{3,1},{4,6},{5,7},{6,4},{7,5},{8,10},{9,11},{10,... | collective-permute-start | bytes 1179656 | tf_op jit(solution)/shard_map/ppermute | solution.py:557
  141.1 12.6 %collective-permute-start.39 = (f32[8,128]{1,0:T(8,128)S(1)}, f32[8,128]{1,0:T(8,128)S(1)}, u32[]{:S(2)}, u32[]{:S(2)}) collective-permute-start(f32[8,128]{1,0:T(8,128)S(1)} %add.103), channel_id=1, source_target_pairs={{0,16},{8,24},{16,0},{24,8},{1,17},{9,25},{17,1},{25,9},{2,18},{10... | collective-permute-start | bytes 12296 | tf_op jit(solution)/shard_map/ppermute | solution.py:560
  142.6 17.2 %collective-permute-start.53 = (bf16[128,1536]{1,0:T(8,128)(2,1)S(1)}, bf16[128,1536]{1,0:T(8,128)(2,1)S(1)}, u32[]{:S(2)}, u32[]{:S(2)}) collective-permute-start(bf16[128,1536]{1,0:T(8,128)(2,1)S(1)} %pad_maximum_fusion.4), channel_id=1, source_target_pairs={{0,1},{1,0},{2,3},{3,2},{4,5},{5,4},{6,7},{7,6},{8,9},{9,8},{10,11... | collective-permute-start | bytes 1179656 | tf_op jit(solution)/shard_map/ppermute | solution.py:557
  151.1 14.7 %collective-permute-start.45 = (bf16[512,384]{1,0:T(8,128)(2,1)}, bf16[512,384]{1,0:T(8,128)(2,1)}, u32[]{:S(2)}, u32[]{:S(2)}) collective-permute-start(bf16[512,384]{1,0:T(8,128)(2,1)} %add_convert_fusion.1), channel_id=1, source_target_pairs={{0,2},{1,3},{2,0},{3,1},{4,6},{5,7},{6,4},{7,5},{8,10},{9,11},{10,... | collective-permute-start | bytes 1179656 | tf_op jit(solution)/shard_map/ppermute | solution.py:557
  153.7 13.3 %collective-permute-start.42 = (bf16[512,384]{1,0:T(8,128)(2,1)}, bf16[512,384]{1,0:T(8,128)(2,1)}, u32[]{:S(2)}, u32[]{:S(2)}) collective-permute-start(bf16[512,384]{1,0:T(8,128)(2,1)} %add_convert_fusion.4), channel_id=1, source_target_pairs={{0,4},{1,5},{2,6},{3,7},{4,0},{5,1},{6,2},{7,3},{8,12},{9,13},{10,... | collective-permute-start | bytes 1179656 | tf_op jit(solution)/shard_map/ppermute | solution.py:557
  171.1 21.0 %collective-permute-start.55 = (bf16[128,512]{1,0:T(8,128)(2,1)S(1)}, bf16[128,512]{1,0:T(8,128)(2,1)S(1)}, u32[]{:S(2)}, u32[]{:S(2)}) collective-permute-start(bf16[128,512]{1,0:T(8,128)(2,1)S(1)} %get-tuple-element.63), channel_id=1, source_target_pairs={{0,16},{8,24},{16,0},{24,8},{1,17},{9,25},{17,1},{25,9},{2,18},{10... | collective-permute-start | bytes 393224 | tf_op jit(solution)/shard_map/ppermute | solution.py:560
  171.1 21.0 %collective-permute-start.54 = (bf16[128,512]{1,0:T(8,128)(2,1)S(1)}, bf16[128,512]{1,0:T(8,128)(2,1)S(1)}, u32[]{:S(2)}, u32[]{:S(2)}) collective-permute-start(bf16[128,512]{1,0:T(8,128)(2,1)S(1)} %get-tuple-element.61), channel_id=1, source_target_pairs={{0,8},{8,0},{16,24},{24,16},{1,9},{9,1},{17,25},{25,17},{2,10},{10... | collective-permute-start | bytes 393224 | tf_op jit(solution)/shard_map/ppermute | solution.py:560
  173.8 19.0 %collective-permute-start.49 = (bf16[256,384]{1,0:T(8,128)(2,1)S(1)}, bf16[256,384]{1,0:T(8,128)(2,1)S(1)}, u32[]{:S(2)}, u32[]{:S(2)}) collective-permute-start(bf16[256,384]{1,0:T(8,128)(2,1)S(1)} %get-tuple-element.65), channel_id=1, source_target_pairs={{0,24},{8,16},{16,8},{24,0},{1,25},{9,17},{17,9},{25,1},{2,26},{10... | collective-permute-start | bytes 589832 | tf_op jit(solution)/shard_map/ppermute | solution.py:560
  176.0 24.1 %collective-permute-start.48 = (bf16[256,384]{1,0:T(8,128)(2,1)S(1)}, bf16[256,384]{1,0:T(8,128)(2,1)S(1)}, u32[]{:S(2)}, u32[]{:S(2)}) collective-permute-start(bf16[256,384]{1,0:T(8,128)(2,1)S(1)} %get-tuple-element.66), channel_id=1, source_target_pairs={{0,16},{8,24},{16,0},{24,8},{1,17},{9,25},{17,1},{25,9},{2,18},{10... | collective-permute-start | bytes 589832 | tf_op jit(solution)/shard_map/ppermute | solution.py:560
  177.2 22.9 %collective-permute-start.47 = (bf16[256,384]{1,0:T(8,128)(2,1)S(1)}, bf16[256,384]{1,0:T(8,128)(2,1)S(1)}, u32[]{:S(2)}, u32[]{:S(2)}) collective-permute-start(bf16[256,384]{1,0:T(8,128)(2,1)S(1)} %get-tuple-element.64), channel_id=1, source_target_pairs={{0,8},{8,0},{16,24},{24,16},{1,9},{9,1},{17,25},{25,17},{2,10},{10... | collective-permute-start | bytes 589832 | tf_op jit(solution)/shard_map/ppermute | solution.py:560
  (36 other events, 222.9 us)

commit v3 on v2

--- a/solution.py
+++ b/solution.py
@@ -19,6 +19,7 @@
 loss_scale = 64.0
 scale = HEAD_DIM ** (-0.5)
 VMEM = 48 * 1024 * 1024
+COST = pl.CostEstimate(flops=1024, bytes_accessed=1024, transcendentals=0)
 BF16 = jnp.bfloat16
 F32 = jnp.float32
 
@@ -33,40 +34,52 @@
     return lax.dot_general(a, b, (dims, ((), ())), preferred_element_type=F32)
 
 
-def norm_kernel(hidden_ref, gain_ref, normal_ref, sum_ref):
+def norm_kernel(where_ref, hidden_ref, gain_ref, a_ref, b_ref, normal_ref, sum_ref, out_ref):
     values = hidden_ref[...].astype(F32)
     mean_square = jnp.mean(values * values, -1, keepdims=True)
     out = values * lax.rsqrt(mean_square + epsilon) * gain_ref[...][None]
-    normal_ref[...] = out.astype(BF16)
+    normal_ref[...] = out.reshape(normal_ref.shape).astype(BF16)
     sum_ref[0] = jnp.sum(values, 1)
-
-
-def norm(hidden, gain):
+    depth, part = a_ref.shape
+    start = pl.multiple_of(where_ref[0] * depth, depth)
+    block = normal_ref[:, pl.ds(start, depth)]
+    out_ref[:, :part] = mm(block, a_ref[...])
+    out_ref[:, part:] = mm(block, b_ref[...])
+
+
+def norm(where, hidden, gain, weights):
     passages, length, width = hidden.shape
+    depth, part = weights[0].shape
     step = 4 if passages % 4 == 0 else 1
     steps = passages // step
-    normal, sums = pl.pallas_call(
+    whole = lambda i, w: (0, 0)
+    normal, sums, product = pl.pallas_call(
         norm_kernel,
-        grid=(steps,),
-        in_specs=[
-            pl.BlockSpec((step, length, width), lambda i: (i, 0, 0)),
-            pl.BlockSpec((1, width), lambda i: (0, 0)),
-        ],
-        out_specs=[
-            pl.BlockSpec((step, length, width), lambda i: (i, 0, 0)),
-            pl.BlockSpec((1, step, width), lambda i: (i, 0, 0)),
-        ],
+        grid_spec=pltpu.PrefetchScalarGridSpec(
+            num_scalar_prefetch=1,
+            grid=(steps,),
+            in_specs=[
+                pl.BlockSpec((step, length, width), lambda i, w: (i, 0, 0)),
+                pl.BlockSpec((1, width), whole),
+                pl.BlockSpec((depth, part), whole),
+                pl.BlockSpec((depth, part), whole),
+            ],
+            out_specs=[
+                pl.BlockSpec((step * length, width), lambda i, w: (i, 0)),
+                pl.BlockSpec((1, step, width), lambda i, w: (i, 0, 0)),
+                pl.BlockSpec((step * length, 2 * part), lambda i, w: (i, 0)),
+            ],
+        ),
         out_shape=[
-            jax.ShapeDtypeStruct((passages, length, width), BF16),
+            jax.ShapeDtypeStruct((passages * length, width), BF16),
             jax.ShapeDtypeStruct((steps, step, width), F32),
+            jax.ShapeDtypeStruct((passages * length, 2 * part), F32),
         ],
         compiler_params=params(),
-        cost_estimate=pl.CostEstimate(
-            flops=6 * hidden.size, bytes_accessed=4 * hidden.size, transcendentals=0
-        ),
-        name="norm_rows",
-    )(hidden, gain[None])
-    return normal.reshape(passages * length, width), sums.reshape(passages, width)
+        cost_estimate=COST,
+        name="norm_project",
+    )(where, hidden, gain[None], *weights)
+    return normal, sums.reshape(passages, width), product
 
 
 WIDE = 2 * HEAD_DIM
@@ -120,15 +133,6 @@
     refs, whole = refs[:-1], refs[-1]
     product, refs = project(refs, pieces, whole)
     refs[-1][...] = product + refs[0][...] if before else product
-
-
-def first_kernel(where_ref, rows_ref, a_ref, b_ref, out_ref, turned_ref):
-    depth, part = a_ref.shape
-    start = pl.multiple_of(where_ref[0] * depth, depth)
-    block = rows_ref[:, pl.ds(start, depth)]
-    out_ref[:, :part] = mm(block, a_ref[...])
-    out_ref[:, part:] = mm(block, b_ref[...])
-    turned_ref[...] = rows_ref[...].T
 
 
 def forward_kernel(pieces, groups, where_ref, *refs):
@@ -182,39 +186,6 @@
     return pl.BlockSpec((step, depth), lambda i, w: (i, w[0] ^ s))
 
 
-def first_project(where, rows, weights):
-    total, width = rows.shape
-    depth, part = weights[0].shape
-    _, step = row_step(total, 4)
-    whole = lambda i, w: (0, 0)
-    return pl.pallas_call(
-        first_kernel,
-        grid_spec=pltpu.PrefetchScalarGridSpec(
-            num_scalar_prefetch=1,
-            grid=(total // step,),
-            in_specs=[
-                pl.BlockSpec((step, width), lambda i, w: (i, 0)),
-                pl.BlockSpec((depth, part), whole),
-                pl.BlockSpec((depth, part), whole),
-            ],
-            out_specs=[
-                pl.BlockSpec((step, 2 * part), lambda i, w: (i, 0)),
-                pl.BlockSpec((width, step), lambda i, w: (0, i)),
-            ],
-        ),
-        out_shape=[
-            jax.ShapeDtypeStruct((total, 2 * part), F32),
-            jax.ShapeDtypeStruct((width, total), BF16),
-        ],
-        compiler_params=params(),
-        cost_estimate=pl.CostEstimate(
-            flops=4 * total * depth * part, bytes_accessed=4 * rows.size + 8 * total * part,
-            transcendentals=0,
-        ),
-        name="project_first",
-    )(where, rows, *weights)
-
-
 def partial_project(where, rows, weights, before):
     total, width = rows.shape
     depth, part = next(iter(weights.values()))[0].shape
@@ -235,11 +206,7 @@
         ),
         out_shape=jax.ShapeDtypeStruct((total, 2 * part), F32),
         compiler_params=params(),
-        cost_estimate=pl.CostEstimate(
-            flops=4 * total * depth * part * pieces,
-            bytes_accessed=2 * total * depth * pieces + 16 * total * part,
-            transcendentals=0,
-        ),
+        cost_estimate=COST,
         name="project_more",
     )(where, *([rows] * pieces), *flat, before)
 
@@ -274,11 +241,7 @@
             jax.ShapeDtypeStruct((steps, batch, heads), F32),
         ],
         compiler_params=params(),
-        cost_estimate=pl.CostEstimate(
-            flops=2 * total * depth * pieces * out_width + 8 * total * heads * GROUP,
-            bytes_accessed=2 * total * (depth * pieces + 3 * out_width + heads),
-            transcendentals=total * heads,
-        ),
+        cost_estimate=COST,
         name="project_attend",
     )(where, *([rows] * pieces), *flat, before)
 
@@ -352,11 +315,7 @@
         out_specs=pl.BlockSpec((step, out_width), lambda i: (i, 0)),
         out_shape=jax.ShapeDtypeStruct((total, out_width), BF16),
         compiler_params=params(),
-        cost_estimate=pl.CostEstimate(
-            flops=16 * total * heads * GROUP,
-            bytes_accessed=2 * total * (heads + 2 * out_width),
-            transcendentals=0,
-        ),
+        cost_estimate=COST,
         name="attend_back",
     )(probs, projected, d_attended.reshape(steps, batch, heads))
 
@@ -414,9 +373,7 @@
         ],
         scratch_shapes=[pltpu.VMEM((2 * count, inner), F32)],
         compiler_params=pltpu.CompilerParams(vmem_limit_bytes=VMEM),
-        cost_estimate=pl.CostEstimate(
-            flops=4 * count * width * inner, bytes_accessed=2 * width * inner, transcendentals=0
-        ),
+        cost_estimate=COST,
         name="pool_score",
     )(where, mine, other, sums, final_gain[None], w_score[None], prior, *pieces)
 
@@ -498,30 +455,29 @@
         ],
         scratch_shapes=[pltpu.VMEM((count, inner), F32)],
         compiler_params=pltpu.CompilerParams(vmem_limit_bytes=VMEM),
-        cost_estimate=pl.CostEstimate(
-            flops=2 * count * width * inner, bytes_accessed=2 * width * inner, transcendentals=count
-        ),
+        cost_estimate=COST,
         name="list_grad",
     )(where, places, bounds, unit, inverse, final_gain[None], w_score[None], *scores, *weights,
       *pieces)
 
 
 def grad_kernel(where_ref, own_ref, sib_ref, d_own_ref, d_sib_ref, a_ref, b_ref):
-    out = mm(own_ref[...], d_own_ref[...]) + mm(sib_ref[...], d_sib_ref[...])
+    down = ((0,), (0,))
+    out = mm(own_ref[...], d_own_ref[...], down) + mm(sib_ref[...], d_sib_ref[...], down)
     out = out.astype(BF16)
     a_ref[...] = out[:, : a_ref.shape[1]]
     b_ref[...] = out[:, a_ref.shape[1] :]
 
 
 def grad_block(where, s, own, sib, d_own, d_sib, depth):
-    rows = own.shape[1]
+    rows = own.shape[0]
     width = d_own.shape[1]
     tile = min(depth, 256)
     tiles = depth // tile
     part = width // 2
 
     def lhs(i, w):
-        return ((w[0] ^ s) * tiles + i, 0)
+        return (0, (w[0] ^ s) * tiles + i)
 
     whole = lambda i, w: (0, 0)
     return pl.pallas_call(
@@ -530,8 +486,8 @@
             num_scalar_prefetch=1,
             grid=(tiles,),
             in_specs=[
-                pl.BlockSpec((tile, rows), lhs),
-                pl.BlockSpec((tile, rows), lhs),
+                pl.BlockSpec((rows, tile), lhs),
+                pl.BlockSpec((rows, tile), lhs),
                 pl.BlockSpec((rows, width), whole),
                 pl.BlockSpec((rows, width), whole),
             ],
@@ -539,11 +495,7 @@
         ),
         out_shape=[jax.ShapeDtypeStruct((depth, part), BF16)] * 2,
         compiler_params=params(),
-        cost_estimate=pl.CostEstimate(
-            flops=4 * rows * depth * width,
-            bytes_accessed=4 * rows * (depth + width) + 2 * depth * width,
-            transcendentals=0,
-        ),
+        cost_estimate=COST,
         name="grad_rows",
     )(where, own, sib, d_own, d_sib)
 
@@ -614,16 +566,14 @@
         starts = (0, 2 * width_q, 2 * (width_q + width_k))
         sizes = (width_q, width_k, width_k)
 
-        def half(h):
+        def half(value, h):
             return jnp.concatenate(
-                [w_qkv[:, a + h * n : a + (h + 1) * n] for a, n in zip(starts, sizes)], 1
+                [value[:, a + h * n : a + (h + 1) * n] for a, n in zip(starts, sizes)], 1
             )
 
-        halves = half(0), half(1)
-        keep = jnp.where(first_core, *halves)
-        give = jnp.where(first_core, halves[1], halves[0])
-        come = across(give, 1)
-        pair_rows = ordered(keep, come, 0)
+        come = across(w_qkv, 1)
+        both = ordered(w_qkv, come, 0)
+        pair_rows = jnp.where(first_core, half(both, 0), half(both, 1))
         middle = pair_rows.shape[1] // 2
         part_a = gathered(pair_rows[:, :middle], bits)
         part_b = gathered(pair_rows[:, middle:], bits[::-1])
@@ -634,19 +584,20 @@
             ones = bin(s).count("1")
             weights[2 if ones == last else 1 if ones else 0][s] = (part_a[s], part_b[s])
 
-        hidden, w_out, part_a[0] = lax.optimization_barrier((hidden, w_out, part_a[0]))
+        hidden, w_out, come = lax.optimization_barrier((hidden, w_out, come))
+        hidden_sib = across(hidden, 1)
         cols = w_out.shape[1] // 2
-        out_halves = w_out[:, :cols], w_out[:, cols:]
-        out_keep = jnp.where(first_core, *out_halves)
-        out_pair = ordered(out_keep, across(jnp.where(first_core, *out_halves[::-1]), 1), 0)
+        both = ordered(w_out, across(w_out, 1), 0)
+        out_pair = jnp.where(first_core, both[:, :cols], both[:, cols:])
+        out_pair, weights[1] = lax.optimization_barrier((out_pair, weights[1]))
         out_a = gathered(out_pair[:, : cols // 2], bits)
         out_b = gathered(out_pair[:, cols // 2 :], bits[::-1])
         pieces = []
         for s in range(chips):
             pieces += [out_a[s], out_b[s], across(out_a[s], 1), across(out_b[s], 1)]
 
-        normal, sums = norm(hidden, norm_gain)
-        normal_sib, sums_sib = across(normal, 1), across(sums, 1)
+        normal, sums, before_own = norm(where, hidden, norm_gain, weights[0][0])
+        normal_sib, sums_sib, before_sib = norm(where, hidden_sib, norm_gain, weights[0][0])
         sums = jnp.concatenate([sums, sums_sib], 0)
         lanes = -(-lengths.shape[0] // 128) * 128
         label_weight = jnp.exp(labels.astype(F32))
@@ -662,14 +613,12 @@
         ends = jnp.cumsum(lengths)
         bounds = jnp.pad(jnp.stack([ends - lengths, ends]), ((0, 0), (0, lanes - lengths.shape[0])))
 
-        def begin(rows):
-            before, turned = first_project(where, rows, weights[0][0])
-            if weights[1]:
-                before = partial_project(where, rows, weights[1], before)
-            return before, turned
-
-        before_own, turned_own = begin(normal)
-        before_sib, turned_sib = begin(normal_sib)
+        if weights[1]:
+            before_own = partial_project(where, normal, weights[1], before_own)
+            before_sib = partial_project(where, normal_sib, weights[1], before_sib)
+        weights[2], before_own, before_sib, heavies, prior_pair, bounds = lax.optimization_barrier(
+            (weights[2], before_own, before_sib, heavies, prior_pair, bounds)
+        )
         proj_sib, probs_sib, attn_sib = forward(where, normal_sib, weights[2], groups, before_sib)
         attn_sib = attn_sib.reshape(passages, -1)
         attn_sib_other = across(attn_sib, 1)
@@ -691,7 +640,7 @@
         d_sib = backward(probs_sib, proj_sib, d_attended[passages:], groups)
         depth = pair_rows.shape[0]
         blocks = {
-            s: grad_block(where, s, turned_own, turned_sib, d_own, d_sib, depth)
+            s: grad_block(where, s, normal, normal_sib, d_own, d_sib, depth)
             for s in sorted(range(n_fsdp // 2), key=lambda s: -bin(s).count("1"))
         }
         sum_a = scattered({s: blocks[s][0] for s in blocks}, bits)
@@ -721,8 +670,20 @@
         inner = attn.shape[1]
         attn_halves = attn[:, : inner // 2], attn[:, inner // 2 :]
         row_halves = d_rows[:, :cols], d_rows[:, cols:]
+        loss = loss_part[:1]
+        parts = []
+        for _ in range(3):
+            upper = lax.reduce_precision(loss, 8, 7)
+            parts.append(upper.astype(BF16))
+            loss = loss - upper
+        extra = jnp.broadcast_to(jnp.concatenate(parts, 1), (2 * passages, 3 * 128))
         payload = jnp.concatenate(
-            [jnp.where(first_core, *attn_halves), jnp.where(first_core, *row_halves)], 1
+            [
+                jnp.where(first_core, *attn_halves),
+                jnp.where(first_core, *row_halves),
+                extra,
+            ],
+            1,
         )
         plane = gathered(payload, bits)
         plane = jnp.concatenate([plane[s] for s in range(chips)], 0)
@@ -730,15 +691,21 @@
         own_rows = inner // n_fsdp
         far = far.reshape(chips, 2, passages, -1)[:, ::-1].reshape(plane.shape)
         left = ordered(plane[:, : inner // 2], far[:, : inner // 2], 1)
-        right = ordered(plane[:, inner // 2 :], far[:, inner // 2 :], 1)
+        span = slice(inner // 2, inner // 2 + cols)
+        right = ordered(plane[:, span], far[:, span], 1)
         left = lax.dynamic_slice_in_dim(left, index * own_rows, own_rows, 1)
         grad_out = list_scatter(
             lax.dot_general(left, right, (((0,), (0,)), ((), ())), preferred_element_type=F32)
         )
 
-        loss = loss_part
-        for distance in [1] + bits:
-            loss = loss + across(loss, distance)
+        def loss_of(value):
+            rows = value[:, inner // 2 + cols :].reshape(chips, 2 * passages, 3, 128)
+            return sum(rows[:, 0, k, 0].astype(F32) for k in range(3))
+
+        losses = loss_of(plane) + loss_of(far)
+        while losses.shape[0] > 1:
+            losses = losses[0::2] + losses[1::2]
+        loss = jnp.broadcast_to(losses[:, None], (8, 128))
         distance = 1
         while distance < n_list:
             loss = loss + along(loss, distance)

time: 202 us -> 234 us (1.16)
  waiting for transfers between devices: 50.4 us -> 65.4 us
  local copies, waits for them, and re-layouts: 10.1 us -> 20.4 us
  other arithmetic: 7.36 us -> 17.1 us
  starting transfers between devices: 66.4 us -> 58.5 us
    ppermute x41 -> x37, waiting for transfers between devices: 30.4 us -> 45.2 us  [across(): lax.ppermute(value, 'fsdp', [(i, i ^ distance) for i in range(n_fsdp)])]
    unnamed x22 -> x86, local copies, waits for them, and re-layouts: 6.83 us -> 13.4 us
    ppermute x8, starting transfers between devices: 15.7 us -> 9.46 us  [neighbour(): return lax.ppermute(value, ('list', 'fsdp'), moves)]
    ppermute x8, waiting for transfers between devices: 0.85 us -> 5.48 us  [neighbour(): return lax.ppermute(value, ('list', 'fsdp'), moves)]
    ppermute x8, waiting for transfers between devices: 19.2 us -> 14.8 us  [along(): lax.ppermute(value, 'list', [(i, i ^ distance) for i in range(n_list)])]
    pallas_call x3 -> x2, Pallas kernels: 17.7 us -> 14.1 us  [norm(): pl.pallas_call(norm_kernel, grid_spec=pltpu.PrefetchScalarGridSpec(num_sc...]
    ppermute x41 -> x37, starting transfers between devices: 36.1 us -> 34.9 us  [across(): lax.ppermute(value, 'fsdp', [(i, i ^ distance) for i in range(n_fsdp)])]
  transfers between devices with their start and end apart: 57 -> 53, of which waited for: 14 -> 11; matrix products, arithmetic and copies ran while one was open for 3% -> 10% of each run, Pallas kernels for 28% -> 26%
where the time goes in v3:
time: 234 us; the launch traced here: 232 us
  Pallas kernels  66.1 us (28%)
  waiting for transfers between devices  65.4 us (28%)
  starting transfers between devices  58.5 us (25%)
  local copies, waits for them, and re-layouts  20.4 us (9%)
  other arithmetic  17.1 us (7%)
  between operations  2.65 us (1%)
    ppermute x37, waiting for transfers between devices, across(): lax.ppermute(value, 'fsdp', [(i, i ^ distance) for i in range(n_fsdp)])  45.2 us
    ppermute x37, starting transfers between devices, across(): lax.ppermute(value, 'fsdp', [(i, i ^ distance) for i in range(n_fsdp)])  34.9 us
    pallas_call x4, Pallas kernels, grad_block(): pl.pallas_call(grad_kernel, grid_spec=pltpu.PrefetchScalarGridSpec(num_sc...  17.3 us
    ppermute x8, waiting for transfers between devices, along(): lax.ppermute(value, 'list', [(i, i ^ distance) for i in range(n_list)])  14.8 us
    pallas_call x2, Pallas kernels, norm(): pl.pallas_call(norm_kernel, grid_spec=pltpu.PrefetchScalarGridSpec(num_sc...  14.1 us
    ppermute x8, starting transfers between devices, along(): lax.ppermute(value, 'list', [(i, i ^ distance) for i in range(n_list)])  14.1 us
    pallas_call x2, Pallas kernels, forward(): pl.pallas_call(functools.partial(forward_kernel, pieces, groups), grid_sp...  13.7 us
    unnamed x86, local copies, waits for them, and re-layouts  13.4 us
  transfers between devices with their start and end apart: 53, of which 11 were waited for; matrix products, arithmetic and copies ran while one was open for 10% of the time, Pallas kernels for 26%

profile of v3, /device:TPU:0, one launch (start us, length us, event | category | flops | bytes accessed | tf_op | source)
XLA Modules:
  0.0 231.7 jit_solution(13407237223751902781)
XLA Ops:
  1.1 2.1 collective-permute-done
  6.1 4.3 %collective-permute-done.9 = f32[32,128]{1,0:T(8,128)S(1)} collective-permute-done((f32[32,128]{1,0:T(8,128)S(1)}, f32[32,128]{1,0:T(8,128)S(1)}, u32[]{:S(2)}, u32[]{:S(2)}) %collective-permute-start.9) | collective-permute-done | bytes 16416 | tf_op jit(solution)/shard_map/ppermute | solution.py:509
  13.2 2.7 %collective-permute-start.3 = (bf16[512,384]{1,0:T(8,128)(2,1)S(1)}, bf16[512,384]{1,0:T(8,128)(2,1)S(1)}, u32[]{:S(2)}, u32[]{:S(2)}) collective-permute-start(bf16[512,384]{1,0:T(8,128)(2,1)S(1)} %get-tuple-element.107.b_ref), channel_id=1, source_target_pairs={{0,4},{1,5},{2,6},{3,7},{4,0},{5,1},{6,2},{7,3},{8,12},{9,13},{10,... | collective-permute-start | bytes 1179656 | tf_op jit(solution)/shard_map/ppermute | solution.py:509
  18.4 17.1 %collective-permute-done.1.refs_2_ = bf16[512,384]{1,0:T(8,128)(2,1)S(1)} collective-permute-done((bf16[512,384]{1,0:T(8,128)(2,1)S(1)}, bf16[512,384]{1,0:T(8,128)(2,1)S(1)}, u32[]{:S(2)}, u32[]{:S(2)}) %collective-permute-start.1) | collective-permute-done | bytes 393248 | tf_op jit(solution)/shard_map/ppermute | solution.py:509
  37.6 3.3 %collective-permute-start.2 = (bf16[512,384]{1,0:T(8,128)(2,1)S(1)}, bf16[512,384]{1,0:T(8,128)(2,1)S(1)}, u32[]{:S(2)}, u32[]{:S(2)}) collective-permute-start(bf16[512,384]{1,0:T(8,128)(2,1)S(1)} %collective-permute-done.1.refs_2_), channel_id=1, source_target_pairs={{0,4},{1,5},{2,6},{3,7},{4,0},{5,1},{6,2},{7,3},{8,12},{9,13},{10,... | collective-permute-start | bytes 1179656 | tf_op jit(solution)/shard_map/ppermute | solution.py:509
  40.9 2.5 %collective-permute-start.4 = (bf16[512,384]{1,0:T(8,128)(2,1)S(1)}, bf16[512,384]{1,0:T(8,128)(2,1)S(1)}, u32[]{:S(2)}, u32[]{:S(2)}) collective-permute-start(bf16[512,384]{1,0:T(8,128)(2,1)S(1)} %collective-permute-done.3.refs_5_), channel_id=1, source_target_pairs={{0,2},{1,3},{2,0},{3,1},{4,6},{5,7},{6,4},{7,5},{8,10},{9,11},{10,... | collective-permute-start | bytes 1179656 | tf_op jit(solution)/shard_map/ppermute | solution.py:509
  44.5 4.7 %collective-permute-done.12.refs_8_ = f32[32,128]{1,0:T(8,128)S(1)} collective-permute-done((f32[32,128]{1,0:T(8,128)S(1)}, f32[32,128]{1,0:T(8,128)S(1)}, u32[]{:S(2)}, u32[]{:S(2)}) %collective-permute-start.12) | collective-permute-done | bytes 16416 | tf_op jit(solution)/shard_map/ppermute | solution.py:528
  49.2 2.1 collective-permute-start.23
  51.3 2.7 %collective-permute-start.19 = (bf16[256,512]{1,0:T(8,128)(2,1)S(1)}, bf16[256,512]{1,0:T(8,128)(2,1)S(1)}, u32[]{:S(2)}, u32[]{:S(2)}) collective-permute-start(bf16[256,512]{1,0:T(8,128)(2,1)S(1)} %get-tuple-element.109.refs_1_.refs_11_), channel_id=1, source_target_pairs={{0,2},{1,3},{2,0},{3,1},{4,6},{5,7},{6,4},{7,5},{8,10},{9,11},{10,... | collective-permute-start | bytes 786440 | tf_op jit(solution)/shard_map/ppermute | solution.py:509
  54.3 9.3 %collective-permute-done.18.refs_4_.refs_14_ = bf16[256,512]{1,0:T(8,128)(2,1)S(1)} collective-permute-done((bf16[256,512]{1,0:T(8,128)(2,1)S(1)}, bf16[256,512]{1,0:T(8,128)(2,1)S(1)}, u32[]{:S(2)}, u32[]{:S(2)}) %collective-permute-start.18) | collective-permute-done | bytes 262176 | tf_op jit(solution)/shard_map/ppermute | solution.py:509
  67.0 7.1 %norm_project.2 = (bf16[1024,2048]{1,0:T(8,128)(2,1)}, f32[4,4,2048]{2,1,0:T(4,128)S(1)}, f32[1024,768]{1,0:T(8,128)S(1)}) custom-call(s32[2]{0:T(128)S(1)} %pad_add_fusion.1.where_ref, bf16[16,64,2048]{2,1,0:T(8,128)(2,1)} %hidden_ref, f32[1,2048]{1,0:T(1,128)S(1)} %bitcast.24, bf16[512,384]{1,0:T(8,128)(2,1)S(1)} %get-tuple-element.108.a_ref, ...), custom_call_target="tpu_custom_call" | custom-call | flops 1024 | bytes 1024 | tf_op jit(solution)/shard_map/norm_project/pallas_call | solution.py:56
  75.8 4.5 %project_more.2.refs_3_ = f32[1024,768]{1,0:T(8,128)S(1)} custom-call(s32[2]{0:T(128)S(1)} %pad_add_fusion.1.where_ref, bf16[1024,2048]{1,0:T(8,128)(2,1)} %get-tuple-element.49.refs_0_.refs_1_.own_ref, bf16[1024,2048]{1,0:T(8,128)(2,1)} %get-tuple-element.49.refs_0_.refs_1_.own_ref, bf16[512,384]{1,0:T(8,128)(2,1)S(1)} %collective-permute-done.1.refs_2_, ...), custom_call_target="tpu_custom_call" | custom-call | flops 1024 | bytes 1024 | tf_op jit(solution)/shard_map/project_more/pallas_call | solution.py:196
  81.9 7.0 %norm_project.3 = (bf16[1024,2048]{1,0:T(8,128)(2,1)}, f32[4,4,2048]{2,1,0:T(4,128)S(1)}, f32[1024,768]{1,0:T(8,128)S(1)}) custom-call(s32[2]{0:T(128)S(1)} %pad_add_fusion.1.where_ref, bf16[16,64,2048]{2,1,0:T(8,128)(2,1)} %collective-permute-done.8.hidden_ref, f32[1,2048]{1,0:T(1,128)S(1)} %bitcast.25, bf16[512,384]{1,0:T(8,128)(2,1)S(1)} %get-tuple-element.108.a_ref, ...), custom_call_target="tpu_custom_call" | custom-call | flops 1024 | bytes 1024 | tf_op jit(solution)/shard_map/norm_project/pallas_call | solution.py:56
  90.7 4.5 %project_more.3.refs_3_ = f32[1024,768]{1,0:T(8,128)S(1)} custom-call(s32[2]{0:T(128)S(1)} %pad_add_fusion.1.where_ref, bf16[1024,2048]{1,0:T(8,128)(2,1)} %get-tuple-element.56.refs_0_.refs_1_.sib_ref, bf16[1024,2048]{1,0:T(8,128)(2,1)} %get-tuple-element.56.refs_0_.refs_1_.sib_ref, bf16[512,384]{1,0:T(8,128)(2,1)S(1)} %collective-permute-done.1.refs_2_, ...), custom_call_target="tpu_custom_call" | custom-call | flops 1024 | bytes 1024 | tf_op jit(solution)/shard_map/project_more/pallas_call | solution.py:196
  96.9 6.8 %project_attend.2 = (bf16[1024,768]{1,0:T(8,128)(2,1)S(1)}, bf16[2,2,1024,128]{3,2,1,0:T(8,128)(2,1)S(1)}, f32[2,8,512]{2,1,0:T(8,128)}) custom-call(s32[2]{0:T(128)S(1)} %pad_add_fusion.1.where_ref, bf16[1024,2048]{1,0:T(8,128)(2,1)} %get-tuple-element.49.refs_0_.refs_1_.own_ref, bf16[512,384]{1,0:T(8,128)(2,1)S(1)} %collective-permute-done.2.refs_1_, ...), custom_call_target="tpu_custom_call" | custom-call | flops 1024 | bytes 1024 | tf_op jit(solution)/shard_map/project_attend/pallas_call | solution.py:223
  104.7 6.8 %project_attend.3 = (bf16[1024,768]{1,0:T(8,128)(2,1)S(1)}, bf16[2,2,1024,128]{3,2,1,0:T(8,128)(2,1)S(1)}, f32[2,8,512]{2,1,0:T(8,128)}) custom-call(s32[2]{0:T(128)S(1)} %pad_add_fusion.1.where_ref, bf16[1024,2048]{1,0:T(8,128)(2,1)} %get-tuple-element.56.refs_0_.refs_1_.sib_ref, bf16[512,384]{1,0:T(8,128)(2,1)S(1)} %collective-permute-done.2.refs_1_, ...), custom_call_target="tpu_custom_call" | custom-call | flops 1024 | bytes 1024 | tf_op jit(solution)/shard_map/project_attend/pallas_call | solution.py:223
  122.2 2.2 pool_score.1
  125.5 4.5 %collective-permute-start.32 = (f32[32,128]{1,0:T(8,128)S(1)}, f32[32,128]{1,0:T(8,128)S(1)}, u32[]{:S(2)}, u32[]{:S(2)}) collective-permute-start(f32[32,128]{1,0:T(8,128)S(1)} %get-tuple-element.72.refs_0_), channel_id=1, source_target_pairs={{0,4},{1,5},{2,6},{3,7},{4,0},{5,1},{6,2},{7,3},{8,12},{9,13},{10,... | collective-permute-start | bytes 49160 | tf_op jit(solution)/shard_map/ppermute | solution.py:528
  131.8 3.0 %list_grad.1 = (bf16[32,2048]{1,0:T(8,128)(2,1)S(1)}, f32[32,512]{1,0:T(8,128)S(1)}, f32[8,128]{1,0:T(8,128)S(1)}) custom-call(s32[2]{0:T(128)S(1)} %pad_add_fusion.1.where_ref, s32[5]{0:T(128)S(1)} %copy-done.34, s32[2,128]{1,0:T(2,128)S(1)} %pad.4.bounds_ref, f32[32,2048]{1,0:T(8,128)S(1)} %get-tuple-element.70.unit_ref, ...), custom_call_target="tpu_custom_call" | custom-call | flops 1024 | bytes 1024 | tf_op jit(solution)/shard_map/list_grad/pallas_call | solution.py:447
  137.5 3.4 %attend_back.3.d_sib_ref = bf16[1024,768]{1,0:T(8,128)(2,1)S(1)} custom-call(bf16[2,2,1024,128]{3,2,1,0:T(8,128)(2,1)S(1)} %copy-done.12, bf16[1024,768]{1,0:T(8,128)(2,1)S(1)} %get-tuple-element.84.projected_ref, f32[2,8,512]{2,1,0:T(8,128)S(1)} %get-tuple-element.115.d_ref), custom_call_target="tpu_custom_call" | custom-call | flops 1024 | bytes 1024 | tf_op jit(solution)/shard_map/attend_back/pallas_call | solution.py:307
  140.9 3.4 %attend_back.2.d_own_ref = bf16[1024,768]{1,0:T(8,128)(2,1)S(1)} custom-call(bf16[2,2,1024,128]{3,2,1,0:T(8,128)(2,1)S(1)} %copy-done.10, bf16[1024,768]{1,0:T(8,128)(2,1)S(1)} %copy-done.5, f32[2,8,512]{2,1,0:T(8,128)S(1)} %get-tuple-element.116.d_ref), custom_call_target="tpu_custom_call" | custom-call | flops 1024 | bytes 1024 | tf_op jit(solution)/shard_map/attend_back/pallas_call | solution.py:307
  144.4 4.6 %grad_rows.7 = (bf16[512,384]{1,0:T(8,128)(2,1)}, bf16[512,384]{1,0:T(8,128)(2,1)}) custom-call(s32[2]{0:T(128)S(1)} %pad_add_fusion.1.where_ref, bf16[1024,2048]{1,0:T(8,128)(2,1)} %get-tuple-element.49.refs_0_.refs_1_.own_ref, bf16[1024,2048]{1,0:T(8,128)(2,1)} %get-tuple-element.56.refs_0_.refs_1_.sib_ref, bf16[1024,768]{1,0:T(8,128)(2,1)S(1)} %attend_back.2.d_own_ref, ...), custom_call_target="tpu_custom_call" | custom-call | flops 1024 | bytes 1024 | tf_op jit(solution)/shard_map/grad_rows/pallas_call | solution.py:483
  149.0 5.1 %collective-permute-start.35 = (bf16[32,1920]{1,0:T(8,128)(2,1)}, bf16[32,1920]{1,0:T(8,128)(2,1)}, u32[]{:S(2)}, u32[]{:S(2)}) collective-permute-start(bf16[32,1920]{1,0:T(8,128)(2,1)} %pad_maximum_fusion.4), channel_id=1, source_target_pairs={{0,4},{1,5},{2,6},{3,7},{4,0},{5,1},{6,2},{7,3},{8,12},{9,13},{10,... | collective-permute-start | bytes 368648 | tf_op jit(solution)/shard_map/ppermute | solution.py:509
  154.1 4.5 %grad_rows.6 = (bf16[512,384]{1,0:T(8,128)(2,1)S(1)}, bf16[512,384]{1,0:T(8,128)(2,1)}) custom-call(s32[2]{0:T(128)S(1)} %pad_add_fusion.1.where_ref, bf16[1024,2048]{1,0:T(8,128)(2,1)} %get-tuple-element.49.refs_0_.refs_1_.own_ref, bf16[1024,2048]{1,0:T(8,128)(2,1)} %get-tuple-element.56.refs_0_.refs_1_.sib_ref, ...), custom_call_target="tpu_custom_call" | custom-call | flops 1024 | bytes 1024 | tf_op jit(solution)/shard_map/grad_rows/pallas_call | solution.py:483
  159.3 3.8 %grad_rows.4 = (bf16[512,384]{1,0:T(8,128)(2,1)S(1)}, bf16[512,384]{1,0:T(8,128)(2,1)S(1)}) custom-call(s32[2]{0:T(128)S(1)} %pad_add_fusion.1.where_ref, bf16[1024,2048]{1,0:T(8,128)(2,1)} %get-tuple-element.49.refs_0_.refs_1_.own_ref, bf16[1024,2048]{1,0:T(8,128)(2,1)} %get-tuple-element.56.refs_0_.refs_1_.sib_ref, ...), custom_call_target="tpu_custom_call" | custom-call | flops 1024 | bytes 1024 | tf_op jit(solution)/shard_map/grad_rows/pallas_call | solution.py:483
  163.2 4.5 %grad_rows.5 = (bf16[512,384]{1,0:T(8,128)(2,1)}, bf16[512,384]{1,0:T(8,128)(2,1)S(1)}) custom-call(s32[2]{0:T(128)S(1)} %pad_add_fusion.1.where_ref, bf16[1024,2048]{1,0:T(8,128)(2,1)} %get-tuple-element.49.refs_0_.refs_1_.own_ref, bf16[1024,2048]{1,0:T(8,128)(2,1)} %get-tuple-element.56.refs_0_.refs_1_.sib_ref, ...), custom_call_target="tpu_custom_call" | custom-call | flops 1024 | bytes 1024 | tf_op jit(solution)/shard_map/grad_rows/pallas_call | solution.py:483
  178.6 12.3 %collective-permute-done.44 = bf16[512,384]{1,0:T(8,128)(2,1)} collective-permute-done((bf16[512,384]{1,0:T(8,128)(2,1)}, bf16[512,384]{1,0:T(8,128)(2,1)}, u32[]{:S(2)}, u32[]{:S(2)}) %collective-permute-start.44) | collective-permute-done | bytes 393248 | tf_op jit(solution)/shard_map/ppermute | solution.py:509
  196.1 3.5 %collective-permute-start.38 = (f32[8,128]{1,0:T(8,128)S(1)}, f32[8,128]{1,0:T(8,128)S(1)}, u32[]{:S(2)}, u32[]{:S(2)}) collective-permute-start(f32[8,128]{1,0:T(8,128)S(1)} %broadcast_in_dim.46), channel_id=1, source_target_pairs={{0,8},{8,0},{16,24},{24,16},{1,9},{9,1},{17,25},{25,17},{2,10},{10... | collective-permute-start | bytes 12296 | tf_op jit(solution)/shard_map/ppermute | solution.py:512
  210.3 3.1 %collective-permute-done.39 = f32[8,128]{1,0:T(8,128)S(1)} collective-permute-done((f32[8,128]{1,0:T(8,128)S(1)}, f32[8,128]{1,0:T(8,128)S(1)}, u32[]{:S(2)}, u32[]{:S(2)}) %collective-permute-start.39) | collective-permute-done | bytes 4128 | tf_op jit(solution)/shard_map/ppermute | solution.py:512
  214.4 3.0 %collective-permute-start.48 = (bf16[256,384]{1,0:T(8,128)(2,1)S(1)}, bf16[256,384]{1,0:T(8,128)(2,1)S(1)}, u32[]{:S(2)}, u32[]{:S(2)}) collective-permute-start(bf16[256,384]{1,0:T(8,128)(2,1)S(1)} %get-tuple-element.104), channel_id=1, source_target_pairs={{0,16},{8,24},{16,0},{24,8},{1,17},{9,25},{17,1},{25,9},{2,18},{10... | collective-permute-start | bytes 589832 | tf_op jit(solution)/shard_map/ppermute | solution.py:512
  219.6 2.1 collective-permute-done.47
  221.7 9.2 %collective-permute-done.48 = bf16[256,384]{1,0:T(8,128)(2,1)S(1)} collective-permute-done((bf16[256,384]{1,0:T(8,128)(2,1)S(1)}, bf16[256,384]{1,0:T(8,128)(2,1)S(1)}, u32[]{:S(2)}, u32[]{:S(2)}) %collective-permute-start.48) | collective-permute-done | bytes 196640 | tf_op jit(solution)/shard_map/ppermute | solution.py:512
  (244 shorter events, 69.4 us)
Async XLA Ops:
  3.3 61.2 %collective-permute-start.8 = (bf16[16,64,2048]{2,1,0:T(8,128)(2,1)}, bf16[16,64,2048]{2,1,0:T(8,128)(2,1)}, u32[]{:S(2)}, u32[]{:S(2)}) collective-permute-start(bf16[16,64,2048]{2,1,0:T(8,128)(2,1)} %hidden_ref), channel_id=1, source_target_pairs={{0,1},{1,0},{2,3},{3,2},{4,5},{5,4},{6,7},{7,6},{8,9},{9,8},{10,11... | collective-permute-start | bytes 12582920 | tf_op jit(solution)/shard_map/ppermute | solution.py:509
  13.2 23.8 %collective-permute-start.3 = (bf16[512,384]{1,0:T(8,128)(2,1)S(1)}, bf16[512,384]{1,0:T(8,128)(2,1)S(1)}, u32[]{:S(2)}, u32[]{:S(2)}) collective-permute-start(bf16[512,384]{1,0:T(8,128)(2,1)S(1)} %get-tuple-element.107.b_ref), channel_id=1, source_target_pairs={{0,4},{1,5},{2,6},{3,7},{4,0},{5,1},{6,2},{7,3},{8,12},{9,13},{10,... | collective-permute-start | bytes 1179656 | tf_op jit(solution)/shard_map/ppermute | solution.py:509
  15.9 21.7 %collective-permute-start.6 = (bf16[512,384]{1,0:T(8,128)(2,1)S(1)}, bf16[512,384]{1,0:T(8,128)(2,1)S(1)}, u32[]{:S(2)}, u32[]{:S(2)}) collective-permute-start(bf16[512,384]{1,0:T(8,128)(2,1)S(1)} %get-tuple-element.107.b_ref), channel_id=1, source_target_pairs={{0,2},{1,3},{2,0},{3,1},{4,6},{5,7},{6,4},{7,5},{8,10},{9,11},{10,... | collective-permute-start | bytes 1179656 | tf_op jit(solution)/shard_map/ppermute | solution.py:509
  17.4 18.0 %collective-permute-start.1 = (bf16[512,384]{1,0:T(8,128)(2,1)S(1)}, bf16[512,384]{1,0:T(8,128)(2,1)S(1)}, u32[]{:S(2)}, u32[]{:S(2)}) collective-permute-start(bf16[512,384]{1,0:T(8,128)(2,1)S(1)} %get-tuple-element.108.a_ref), channel_id=1, source_target_pairs={{0,2},{1,3},{2,0},{3,1},{4,6},{5,7},{6,4},{7,5},{8,10},{9,11},{10,... | collective-permute-start | bytes 1179656 | tf_op jit(solution)/shard_map/ppermute | solution.py:509
  17.9 23.0 %collective-permute-start.7 = (bf16[512,384]{1,0:T(8,128)(2,1)S(1)}, bf16[512,384]{1,0:T(8,128)(2,1)S(1)}, u32[]{:S(2)}, u32[]{:S(2)}) collective-permute-start(bf16[512,384]{1,0:T(8,128)(2,1)S(1)} %get-tuple-element.108.a_ref), channel_id=1, source_target_pairs={{0,4},{1,5},{2,6},{3,7},{4,0},{5,1},{6,2},{7,3},{8,12},{9,13},{10,... | collective-permute-start | bytes 1179656 | tf_op jit(solution)/shard_map/ppermute | solution.py:509
  35.4 8.0 %collective-permute-start.10 = (f32[32,128]{1,0:T(8,128)S(1)}, f32[32,128]{1,0:T(8,128)S(1)}, u32[]{:S(2)}, u32[]{:S(2)}) collective-permute-start(f32[32,128]{1,0:T(8,128)S(1)} %pad_maximum_fusion.7.refs_5_), channel_id=1, source_target_pairs={{0,2},{1,3},{2,0},{3,1},{4,6},{5,7},{6,4},{7,5},{8,10},{9,11},{10,... | collective-permute-start | bytes 49160 | tf_op jit(solution)/shard_map/ppermute | solution.py:528
  37.6 16.4 %collective-permute-start.2 = (bf16[512,384]{1,0:T(8,128)(2,1)S(1)}, bf16[512,384]{1,0:T(8,128)(2,1)S(1)}, u32[]{:S(2)}, u32[]{:S(2)}) collective-permute-start(bf16[512,384]{1,0:T(8,128)(2,1)S(1)} %collective-permute-done.1.refs_2_), channel_id=1, source_target_pairs={{0,4},{1,5},{2,6},{3,7},{4,0},{5,1},{6,2},{7,3},{8,12},{9,13},{10,... | collective-permute-start | bytes 1179656 | tf_op jit(solution)/shard_map/ppermute | solution.py:509
  40.9 13.2 %collective-permute-start.4 = (bf16[512,384]{1,0:T(8,128)(2,1)S(1)}, bf16[512,384]{1,0:T(8,128)(2,1)S(1)}, u32[]{:S(2)}, u32[]{:S(2)}) collective-permute-start(bf16[512,384]{1,0:T(8,128)(2,1)S(1)} %collective-permute-done.3.refs_5_), channel_id=1, source_target_pairs={{0,2},{1,3},{2,0},{3,1},{4,6},{5,7},{6,4},{7,5},{8,10},{9,11},{10,... | collective-permute-start | bytes 1179656 | tf_op jit(solution)/shard_map/ppermute | solution.py:509
  49.2 14.3 %collective-permute-start.23 = (bf16[256,512]{1,0:T(8,128)(2,1)S(1)}, bf16[256,512]{1,0:T(8,128)(2,1)S(1)}, u32[]{:S(2)}, u32[]{:S(2)}) collective-permute-start(bf16[256,512]{1,0:T(8,128)(2,1)S(1)} %get-tuple-element.109.refs_1_.refs_11_), channel_id=1, source_target_pairs={{0,4},{1,5},{2,6},{3,7},{4,0},{5,1},{6,2},{7,3},{8,12},{9,13},{10,... | collective-permute-start | bytes 786440 | tf_op jit(solution)/shard_map/ppermute | solution.py:509
  51.3 12.7 %collective-permute-start.19 = (bf16[256,512]{1,0:T(8,128)(2,1)S(1)}, bf16[256,512]{1,0:T(8,128)(2,1)S(1)}, u32[]{:S(2)}, u32[]{:S(2)}) collective-permute-start(bf16[256,512]{1,0:T(8,128)(2,1)S(1)} %get-tuple-element.109.refs_1_.refs_11_), channel_id=1, source_target_pairs={{0,2},{1,3},{2,0},{3,1},{4,6},{5,7},{6,4},{7,5},{8,10},{9,11},{10,... | collective-permute-start | bytes 786440 | tf_op jit(solution)/shard_map/ppermute | solution.py:509
  54.0 9.6 %collective-permute-start.18 = (bf16[256,512]{1,0:T(8,128)(2,1)S(1)}, bf16[256,512]{1,0:T(8,128)(2,1)S(1)}, u32[]{:S(2)}, u32[]{:S(2)}) collective-permute-start(bf16[256,512]{1,0:T(8,128)(2,1)S(1)} %get-tuple-element.110.refs_0_.refs_10_), channel_id=1, source_target_pairs={{0,2},{1,3},{2,0},{3,1},{4,6},{5,7},{6,4},{7,5},{8,10},{9,11},{10,... | collective-permute-start | bytes 786440 | tf_op jit(solution)/shard_map/ppermute | solution.py:509
  54.1 10.4 %collective-permute-start.22 = (bf16[256,512]{1,0:T(8,128)(2,1)S(1)}, bf16[256,512]{1,0:T(8,128)(2,1)S(1)}, u32[]{:S(2)}, u32[]{:S(2)}) collective-permute-start(bf16[256,512]{1,0:T(8,128)(2,1)S(1)} %get-tuple-element.110.refs_0_.refs_10_), channel_id=1, source_target_pairs={{0,4},{1,5},{2,6},{3,7},{4,0},{5,1},{6,2},{7,3},{8,12},{9,13},{10,... | collective-permute-start | bytes 786440 | tf_op jit(solution)/shard_map/ppermute | solution.py:509
  63.6 49.0 %collective-permute-start.16 = (bf16[256,512]{1,0:T(8,128)(2,1)S(1)}, bf16[256,512]{1,0:T(8,128)(2,1)S(1)}, u32[]{:S(2)}, u32[]{:S(2)}) collective-permute-start(bf16[256,512]{1,0:T(8,128)(2,1)S(1)} %get-tuple-element.110.refs_0_.refs_10_), channel_id=1, source_target_pairs={{0,1},{1,0},{2,3},{3,2},{4,5},{5,4},{6,7},{7,6},{8,9},{9,8},{10,11... | collective-permute-start | bytes 786440 | tf_op jit(solution)/shard_map/ppermute | solution.py:509
  63.6 49.2 %collective-permute-start.17 = (bf16[256,512]{1,0:T(8,128)(2,1)S(1)}, bf16[256,512]{1,0:T(8,128)(2,1)S(1)}, u32[]{:S(2)}, u32[]{:S(2)}) collective-permute-start(bf16[256,512]{1,0:T(8,128)(2,1)S(1)} %get-tuple-element.109.refs_1_.refs_11_), channel_id=1, source_target_pairs={{0,1},{1,0},{2,3},{3,2},{4,5},{5,4},{6,7},{7,6},{8,9},{9,8},{10,11... | collective-permute-start | bytes 786440 | tf_op jit(solution)/shard_map/ppermute | solution.py:509
  64.1 51.9 %collective-permute-start.26 = (bf16[256,512]{1,0:T(8,128)(2,1)S(1)}, bf16[256,512]{1,0:T(8,128)(2,1)}, u32[]{:S(2)}, u32[]{:S(2)}) collective-permute-start(bf16[256,512]{1,0:T(8,128)(2,1)S(1)} %collective-permute-done.18.refs_4_.refs_14_), channel_id=1, source_target_pairs={{0,4},{1,5},{2,6},{3,7},{4,0},{5,1},{6,2},{7,3},{8,12},{9,13},{10,... | collective-permute-start | bytes 786440 | tf_op jit(solution)/shard_map/ppermute | solution.py:509
  64.5 52.1 %collective-permute-start.20 = (bf16[256,512]{1,0:T(8,128)(2,1)S(1)}, bf16[256,512]{1,0:T(8,128)(2,1)}, u32[]{:S(2)}, u32[]{:S(2)}) collective-permute-start(bf16[256,512]{1,0:T(8,128)(2,1)S(1)} %collective-permute-done.18.refs_4_.refs_14_), channel_id=1, source_target_pairs={{0,1},{1,0},{2,3},{3,2},{4,5},{5,4},{6,7},{7,6},{8,9},{9,8},{10,11... | collective-permute-start | bytes 786440 | tf_op jit(solution)/shard_map/ppermute | solution.py:509
  64.5 51.8 %collective-permute-start.27 = (bf16[256,512]{1,0:T(8,128)(2,1)S(1)}, bf16[256,512]{1,0:T(8,128)(2,1)}, u32[]{:S(2)}, u32[]{:S(2)}) collective-permute-start(bf16[256,512]{1,0:T(8,128)(2,1)S(1)} %collective-permute-done.23.refs_9_.refs_19_), channel_id=1, source_target_pairs={{0,2},{1,3},{2,0},{3,1},{4,6},{5,7},{6,4},{7,5},{8,10},{9,11},{10,... | collective-permute-start | bytes 786440 | tf_op jit(solution)/shard_map/ppermute | solution.py:509
  135.5 18.6 %collective-permute-start.34 = (bf16[32,1920]{1,0:T(8,128)(2,1)}, bf16[32,1920]{1,0:T(8,128)(2,1)}, u32[]{:S(2)}, u32[]{:S(2)}) collective-permute-start(bf16[32,1920]{1,0:T(8,128)(2,1)} %pad_maximum_fusion.4), channel_id=1, source_target_pairs={{0,2},{1,3},{2,0},{3,1},{4,6},{5,7},{6,4},{7,5},{8,10},{9,11},{10,... | collective-permute-start | bytes 368648 | tf_op jit(solution)/shard_map/ppermute | solution.py:509
  148.9 25.9 %collective-permute-start.41 = (bf16[512,384]{1,0:T(8,128)(2,1)}, bf16[512,384]{1,0:T(8,128)(2,1)}, u32[]{:S(2)}, u32[]{:S(2)}) collective-permute-start(bf16[512,384]{1,0:T(8,128)(2,1)} %get-tuple-element.88), channel_id=1, source_target_pairs={{0,2},{1,3},{2,0},{3,1},{4,6},{5,7},{6,4},{7,5},{8,10},{9,11},{10,... | collective-permute-start | bytes 1179656 | tf_op jit(solution)/shard_map/ppermute | solution.py:509
  149.0 23.1 %collective-permute-start.35 = (bf16[32,1920]{1,0:T(8,128)(2,1)}, bf16[32,1920]{1,0:T(8,128)(2,1)}, u32[]{:S(2)}, u32[]{:S(2)}) collective-permute-start(bf16[32,1920]{1,0:T(8,128)(2,1)} %pad_maximum_fusion.4), channel_id=1, source_target_pairs={{0,4},{1,5},{2,6},{3,7},{4,0},{5,1},{6,2},{7,3},{8,12},{9,13},{10,... | collective-permute-start | bytes 368648 | tf_op jit(solution)/shard_map/ppermute | solution.py:509
  154.1 18.1 %collective-permute-start.36 = (bf16[32,1920]{1,0:T(8,128)(2,1)}, bf16[32,1920]{1,0:T(8,128)(2,1)}, u32[]{:S(2)}, u32[]{:S(2)}) collective-permute-start(bf16[32,1920]{1,0:T(8,128)(2,1)} %collective-permute-done.34), channel_id=1, source_target_pairs={{0,4},{1,5},{2,6},{3,7},{4,0},{5,1},{6,2},{7,3},{8,12},{9,13},{10,... | collective-permute-start | bytes 368648 | tf_op jit(solution)/shard_map/ppermute | solution.py:509
  168.4 34.8 %collective-permute-start.40 = (bf16[512,384]{1,0:T(8,128)(2,1)}, bf16[512,384]{1,0:T(8,128)(2,1)S(1)}, u32[]{:S(2)}, u32[]{:S(2)}) collective-permute-start(bf16[512,384]{1,0:T(8,128)(2,1)} %get-tuple-element.86), channel_id=1, source_target_pairs={{0,2},{1,3},{2,0},{3,1},{4,6},{5,7},{6,4},{7,5},{8,10},{9,11},{10,... | collective-permute-start | bytes 1179656 | tf_op jit(solution)/shard_map/ppermute | solution.py:509
  170.1 37.0 %collective-permute-start.43 = (bf16[512,384]{1,0:T(8,128)(2,1)}, bf16[512,384]{1,0:T(8,128)(2,1)S(1)}, u32[]{:S(2)}, u32[]{:S(2)}) collective-permute-start(bf16[512,384]{1,0:T(8,128)(2,1)} %get-tuple-element.90), channel_id=1, source_target_pairs={{0,4},{1,5},{2,6},{3,7},{4,0},{5,1},{6,2},{7,3},{8,12},{9,13},{10,... | collective-permute-start | bytes 1179656 | tf_op jit(solution)/shard_map/ppermute | solution.py:509
  172.1 18.8 %collective-permute-start.44 = (bf16[512,384]{1,0:T(8,128)(2,1)}, bf16[512,384]{1,0:T(8,128)(2,1)}, u32[]{:S(2)}, u32[]{:S(2)}) collective-permute-start(bf16[512,384]{1,0:T(8,128)(2,1)} %get-tuple-element.92), channel_id=1, source_target_pairs={{0,4},{1,5},{2,6},{3,7},{4,0},{5,1},{6,2},{7,3},{8,12},{9,13},{10,... | collective-permute-start | bytes 1179656 | tf_op jit(solution)/shard_map/ppermute | solution.py:509
  173.3 19.8 %collective-permute-start.37 = (bf16[128,1920]{1,0:T(8,128)(2,1)S(1)}, bf16[128,1920]{1,0:T(8,128)(2,1)S(1)}, u32[]{:S(2)}, u32[]{:S(2)}) collective-permute-start(bf16[128,1920]{1,0:T(8,128)(2,1)S(1)} %pad_maximum_fusion.1), channel_id=1, source_target_pairs={{0,1},{1,0},{2,3},{3,2},{4,5},{5,4},{6,7},{7,6},{8,9},{9,8},{10,11... | collective-permute-start | bytes 1474568 | tf_op jit(solution)/shard_map/ppermute | solution.py:509
  176.6 28.5 %collective-permute-start.42 = (bf16[512,384]{1,0:T(8,128)(2,1)}, bf16[512,384]{1,0:T(8,128)(2,1)}, u32[]{:S(2)}, u32[]{:S(2)}) collective-permute-start(bf16[512,384]{1,0:T(8,128)(2,1)} %add_convert_fusion.4), channel_id=1, source_target_pairs={{0,4},{1,5},{2,6},{3,7},{4,0},{5,1},{6,2},{7,3},{8,12},{9,13},{10,... | collective-permute-start | bytes 1179656 | tf_op jit(solution)/shard_map/ppermute | solution.py:509
  192.7 16.2 %collective-permute-start.45 = (bf16[512,384]{1,0:T(8,128)(2,1)}, bf16[512,384]{1,0:T(8,128)(2,1)}, u32[]{:S(2)}, u32[]{:S(2)}) collective-permute-start(bf16[512,384]{1,0:T(8,128)(2,1)} %add_convert_fusion.1), channel_id=1, source_target_pairs={{0,2},{1,3},{2,0},{3,1},{4,6},{5,7},{6,4},{7,5},{8,10},{9,11},{10,... | collective-permute-start | bytes 1179656 | tf_op jit(solution)/shard_map/ppermute | solution.py:509
  201.6 15.9 %collective-permute-start.50 = (bf16[128,512]{1,0:T(8,128)(2,1)S(1)}, bf16[128,512]{1,0:T(8,128)(2,1)S(1)}, u32[]{:S(2)}, u32[]{:S(2)}) collective-permute-start(bf16[128,512]{1,0:T(8,128)(2,1)S(1)} %get-tuple-element.99), channel_id=1, source_target_pairs={{0,8},{8,0},{16,24},{24,16},{1,9},{9,1},{17,25},{25,17},{2,10},{10... | collective-permute-start | bytes 393224 | tf_op jit(solution)/shard_map/ppermute | solution.py:512
  203.2 15.6 %collective-permute-start.51 = (bf16[128,512]{1,0:T(8,128)(2,1)S(1)}, bf16[128,512]{1,0:T(8,128)(2,1)S(1)}, u32[]{:S(2)}, u32[]{:S(2)}) collective-permute-start(bf16[128,512]{1,0:T(8,128)(2,1)S(1)} %get-tuple-element.101), channel_id=1, source_target_pairs={{0,16},{8,24},{16,0},{24,8},{1,17},{9,25},{17,1},{25,9},{2,18},{10... | collective-permute-start | bytes 393224 | tf_op jit(solution)/shard_map/ppermute | solution.py:512
  205.1 13.7 %collective-permute-start.52 = (bf16[128,512]{1,0:T(8,128)(2,1)S(1)}, bf16[128,512]{1,0:T(8,128)(2,1)S(1)}, u32[]{:S(2)}, u32[]{:S(2)}) collective-permute-start(bf16[128,512]{1,0:T(8,128)(2,1)S(1)} %get-tuple-element.100), channel_id=1, source_target_pairs={{0,24},{8,16},{16,8},{24,0},{1,25},{9,17},{17,9},{25,1},{2,26},{10... | collective-permute-start | bytes 393224 | tf_op jit(solution)/shard_map/ppermute | solution.py:512
  214.4 16.4 %collective-permute-start.48 = (bf16[256,384]{1,0:T(8,128)(2,1)S(1)}, bf16[256,384]{1,0:T(8,128)(2,1)S(1)}, u32[]{:S(2)}, u32[]{:S(2)}) collective-permute-start(bf16[256,384]{1,0:T(8,128)(2,1)S(1)} %get-tuple-element.104), channel_id=1, source_target_pairs={{0,16},{8,24},{16,0},{24,8},{1,17},{9,25},{17,1},{25,9},{2,18},{10... | collective-permute-start | bytes 589832 | tf_op jit(solution)/shard_map/ppermute | solution.py:512
  217.5 13.4 %collective-permute-start.49 = (bf16[256,384]{1,0:T(8,128)(2,1)S(1)}, bf16[256,384]{1,0:T(8,128)(2,1)S(1)}, u32[]{:S(2)}, u32[]{:S(2)}) collective-permute-start(bf16[256,384]{1,0:T(8,128)(2,1)S(1)} %get-tuple-element.103), channel_id=1, source_target_pairs={{0,24},{8,16},{16,8},{24,0},{1,25},{9,17},{17,9},{25,1},{2,26},{10... | collective-permute-start | bytes 589832 | tf_op jit(solution)/shard_map/ppermute | solution.py:512
  (64 other events, 530.7 us)

commit v4 on v3

--- a/solution.py
+++ b/solution.py
@@ -18,8 +18,13 @@
 epsilon = 1e-05
 loss_scale = 64.0
 scale = HEAD_DIM ** (-0.5)
-VMEM = 48 * 1024 * 1024
-COST = pl.CostEstimate(flops=1024, bytes_accessed=1024, transcendentals=0)
+VMEM = 20 * 1024 * 1024
+SMALL = 20 * 1024 * 1024
+
+
+def cost(micros):
+    return pl.CostEstimate(flops=int(micros * 1e8), bytes_accessed=int(micros * 3.5e6), transcendentals=0)
+
 BF16 = jnp.bfloat16
 F32 = jnp.float32
 
@@ -28,6 +33,10 @@
     return pltpu.CompilerParams(
         vmem_limit_bytes=VMEM, dimension_semantics=("arbitrary",) * grid
     )
+
+
+def held(space, *values):
+    return [pltpu.with_memory_space_constraint(x, space) for x in values]
 
 
 def mm(a, b, dims=((1,), (0,))):
@@ -71,15 +80,15 @@
             ],
         ),
         out_shape=[
-            jax.ShapeDtypeStruct((passages * length, width), BF16),
+            pltpu.VMEM((passages * length, width), BF16),
             jax.ShapeDtypeStruct((steps, step, width), F32),
-            jax.ShapeDtypeStruct((passages * length, 2 * part), F32),
+            pltpu.VMEM((passages * length, 2 * part), F32),
         ],
         compiler_params=params(),
-        cost_estimate=COST,
+        cost_estimate=cost(7),
         name="norm_project",
-    )(where, hidden, gain[None], *weights)
-    return normal, sums.reshape(passages, width), product
+    )(where, *held(pltpu.HBM, hidden), gain[None], *weights)
+    return normal, sums, product
 
 
 WIDE = 2 * HEAD_DIM
@@ -204,11 +213,11 @@
             out_specs=out,
             scratch_shapes=[pltpu.VMEM((pieces * depth, 2 * part), BF16)],
         ),
-        out_shape=jax.ShapeDtypeStruct((total, 2 * part), F32),
+        out_shape=pltpu.VMEM((total, 2 * part), F32),
         compiler_params=params(),
-        cost_estimate=COST,
+        cost_estimate=cost(4.5),
         name="project_more",
-    )(where, *([rows] * pieces), *flat, before)
+    )(where, *held(pltpu.VMEM, *([rows] * pieces)), *flat, *held(pltpu.VMEM, before))
 
 
 def forward(where, rows, weights, groups, before):
@@ -241,9 +250,9 @@
             jax.ShapeDtypeStruct((steps, batch, heads), F32),
         ],
         compiler_params=params(),
-        cost_estimate=COST,
+        cost_estimate=cost(6.5),
         name="project_attend",
-    )(where, *([rows] * pieces), *flat, before)
+    )(where, *held(pltpu.VMEM, *([rows] * pieces)), *flat, *held(pltpu.VMEM, before))
 
 
 def backward_kernel(groups, probs_ref, projected_ref, d_ref, out_ref):
@@ -313,19 +322,21 @@
             pl.BlockSpec((1, batch, heads), lambda i: (i, 0, 0)),
         ],
         out_specs=pl.BlockSpec((step, out_width), lambda i: (i, 0)),
-        out_shape=jax.ShapeDtypeStruct((total, out_width), BF16),
+        out_shape=pltpu.VMEM((total, out_width), BF16),
         compiler_params=params(),
-        cost_estimate=COST,
+        cost_estimate=cost(3.4),
         name="attend_back",
     )(probs, projected, d_attended.reshape(steps, batch, heads))
 
 
-def score_kernel(chips, where_ref, mine_ref, other_ref, sum_ref, final_ref, ws_ref, prior_ref,
-                 *refs):
+def score_kernel(chips, where_ref, own_ref, sib_ref, own_far_ref, sib_far_ref, sum_ref, sib_sum_ref,
+                 final_ref, ws_ref, prior_ref, prior_sib_ref, *refs):
     pieces, refs = refs[: 4 * chips], refs[4 * chips :]
     unit_ref, inverse_ref, score_ref, attn_ref, product_ref = refs
     chip, core = where_ref[0], where_ref[1]
-    mine, other = mine_ref[...], other_ref[...]
+    mine = jnp.concatenate([own_ref[...], sib_ref[...]], 0)
+    other = jnp.concatenate([own_far_ref[...], sib_far_ref[...]], 0)
+    sums = [ref[k] for ref in (sum_ref, sib_sum_ref) for k in range(ref.shape[0])]
     attn = jnp.concatenate(
         [jnp.where(core == 0, mine, other), jnp.where(core == 0, other, mine)], 1
     )
@@ -347,23 +358,26 @@
     product = jnp.concatenate(
         [jnp.where(core == 0, own, far), jnp.where(core == 0, far, own)], 1
     )
-    pooled = (sum_ref[...] + product) * (1.0 / PASSAGE_LEN)
+    pooled = (jnp.concatenate(sums, 0) + product) * (1.0 / PASSAGE_LEN)
     inverse = lax.rsqrt(jnp.mean(pooled * pooled, -1, keepdims=True) + epsilon)
     unit = pooled * inverse
     score = jnp.sum(unit * (final_ref[...] * ws_ref[...]), -1, keepdims=True)
     unit_ref[...] = unit
     inverse_ref[...] = jnp.broadcast_to(inverse, inverse_ref.shape)
-    score_ref[...] = score + prior_ref[...]
-
-
-def score_pass(where, mine, other, sums, final_gain, w_score, prior, pieces):
-    count, width = sums.shape
-    lanes = prior.shape[1]
-    inner = 2 * mine.shape[1]
+    lane = lax.broadcasted_iota(jnp.int32, score_ref.shape, 1)
+    half = score_ref.shape[1] // 2
+    prior = jnp.concatenate([prior_ref[...], prior_sib_ref[...]], 0)
+    score_ref[...] = jnp.where(lane < half, score, 0.0) + prior
+
+
+def score_pass(where, attn, sums, final_gain, w_score, priors, pieces):
+    count, width = 2 * attn[0].shape[0], sums[0].shape[2]
+    lanes = priors[0].shape[1]
+    inner = 2 * attn[0].shape[1]
     vmem = pl.BlockSpec(memory_space=pltpu.VMEM)
     return pl.pallas_call(
         functools.partial(score_kernel, len(pieces) // 4),
-        in_specs=[pl.BlockSpec(memory_space=pltpu.SMEM)] + [vmem] * (6 + len(pieces)),
+        in_specs=[pl.BlockSpec(memory_space=pltpu.SMEM)] + [vmem] * (10 + len(pieces)),
         out_specs=[vmem] * 4,
         out_shape=[
             jax.ShapeDtypeStruct((count, width), F32),
@@ -372,32 +386,36 @@
             jax.ShapeDtypeStruct((count, inner), BF16),
         ],
         scratch_shapes=[pltpu.VMEM((2 * count, inner), F32)],
-        compiler_params=pltpu.CompilerParams(vmem_limit_bytes=VMEM),
-        cost_estimate=COST,
+        compiler_params=pltpu.CompilerParams(vmem_limit_bytes=SMALL),
+        cost_estimate=cost(2),
         name="pool_score",
-    )(where, mine, other, sums, final_gain[None], w_score[None], prior, *pieces)
+    )(where, *attn, *sums, final_gain[None], w_score[None], *priors, *pieces)
 
 
 def list_kernel(blocks, chips, passages, where_ref, place_ref, bounds_ref, unit_ref, inverse_ref,
-                final_ref, ws_ref, *refs):
+                attn_ref, final_ref, ws_ref, *refs):
     scores = [ref[...] for ref in refs[:blocks]]
-    weights = [ref[...] for ref in refs[blocks : 2 * blocks]]
-    pieces, refs = refs[2 * blocks : 2 * blocks + 4 * chips], refs[2 * blocks + 4 * chips :]
-    d_rows_ref, d_att_ref, loss_ref, back_ref = refs
+    pieces, refs = refs[blocks : blocks + 4 * chips], refs[blocks + 4 * chips :]
+    d_att_ref, payload_ref, back_ref = refs
     chip, core = where_ref[0], where_ref[1]
-    starts, ends = bounds_ref[0:1], bounds_ref[1:2]
     pair = 2 * passages
-    lanes = starts.shape[1]
+    lanes = bounds_ref.shape[1]
+    lane = lax.broadcasted_iota(jnp.int32, bounds_ref.shape, 1)
+    ends, reach = bounds_ref[...], 1
+    while reach < lanes:
+        ends = ends + jnp.where(lane >= reach, pltpu.roll(ends, reach, 1), 0)
+        reach *= 2
+    starts, ends = (ends - bounds_ref[...])[:1], ends[:1]
     row = lax.broadcasted_iota(jnp.int32, (pair, lanes), 0)
-    offset = jnp.where(
-        row < passages, core * passages + row, (1 - core) * passages + row - passages
-    )
+    near = jnp.where(row < passages, core * passages + row, (1 - core) * passages + row - passages)
+    far = jnp.where(row < passages, (1 - core) * passages + row, core * passages + row - passages)
     members = []
     for j in range(blocks):
-        place = place_ref[j] * pair + offset
+        place = place_ref[j] * pair + (near if j <= blocks // 2 else far)
         members.append((place >= starts) & (place < ends))
+    high = scores[0].shape[1] // 2
     column = [jnp.broadcast_to(score[:, :1], (pair, lanes)) for score in scores]
-    heavy = [jnp.broadcast_to(weight[:, :1], (pair, lanes)) for weight in weights]
+    heavy = [jnp.broadcast_to(score[:, high : high + 1], (pair, lanes)) for score in scores]
     peak = functools.reduce(
         jnp.maximum,
         [jnp.max(jnp.where(m, s, -1e30), 0, keepdims=True) for m, s in zip(members, column)],
@@ -414,16 +432,13 @@
     log_prob = column[0][:, :1] - jnp.sum(jnp.where(own, log_norm, 0.0), 1, keepdims=True)
     target = heavy[0][:, :1] / jnp.sum(jnp.where(own, label_total, 0.0), 1, keepdims=True)
     loss = -loss_scale * jnp.sum((target * log_prob)[:passages], 0, keepdims=True)
-    loss_ref[...] = jnp.broadcast_to(loss, loss_ref.shape)
     d_score = loss_scale * (jnp.exp(log_prob) - target)
     unit = unit_ref[...]
     d_unit = d_score * (ws_ref[...] * final_ref[...])
     mean = jnp.mean(d_unit * unit, -1, keepdims=True)
     d_pooled = inverse_ref[:, :1] * (d_unit - unit * mean)
-    d_rows = (d_pooled * (1.0 / PASSAGE_LEN)).astype(BF16)
-    d_rows_ref[...] = d_rows
     depth, part = pieces[0].shape
-    half = d_rows.shape[1] // 2
+    half = d_pooled.shape[1] // 2
     own = jnp.where(core == 0, d_pooled[:, :half], d_pooled[:, half:])
     far = jnp.where(core == 0, d_pooled[:, half:], d_pooled[:, :half])
     cut = [own[:, :part], own[:, part:], far[:, :part], far[:, part:]]
@@ -435,9 +450,19 @@
     back = back_ref[...]
     half = back.shape[1] // 2
     d_att_ref[...] = jnp.where(core == 0, back[:, :half], back[:, half:])
-
-
-def list_pass(where, places, bounds, unit, inverse, final_gain, w_score, scores, weights, pieces,
+    attn = attn_ref[...].astype(F32)
+    columns = [jnp.where(core == 0, attn[:, :half], attn[:, half:])]
+    columns += [x.astype(F32) for x in cut[:2]]
+    rest = jnp.broadcast_to(loss, (pair, 128))
+    for _ in range(3):
+        columns.append(rest.astype(BF16).astype(F32))
+        rest = rest - columns[-1]
+    columns = jnp.concatenate(columns, 1)
+    turned = jnp.concatenate([columns[passages:], columns[:passages]], 0)
+    payload_ref[...] = jnp.where(core == 0, columns, turned).astype(BF16)
+
+
+def list_pass(where, places, bounds, unit, inverse, attn, final_gain, w_score, scores, pieces,
               passages):
     count, width = unit.shape
     chips = len(pieces) // 4
@@ -446,19 +471,66 @@
     smem = pl.BlockSpec(memory_space=pltpu.SMEM)
     return pl.pallas_call(
         functools.partial(list_kernel, len(scores), chips, passages),
-        in_specs=[smem] * 2 + [vmem] * (5 + 2 * len(scores) + len(pieces)),
-        out_specs=[vmem] * 3,
+        in_specs=[smem] * 2 + [vmem] * (6 + len(scores) + len(pieces)),
+        out_specs=[vmem] * 2,
         out_shape=[
-            jax.ShapeDtypeStruct((count, width), BF16),
             jax.ShapeDtypeStruct((count, inner // 2), F32),
-            jax.ShapeDtypeStruct((8, 128), F32),
+            jax.ShapeDtypeStruct((count, (inner + width) // 2 + 3 * 128), BF16),
         ],
         scratch_shapes=[pltpu.VMEM((count, inner), F32)],
-        compiler_params=pltpu.CompilerParams(vmem_limit_bytes=VMEM),
-        cost_estimate=COST,
+        compiler_params=pltpu.CompilerParams(vmem_limit_bytes=SMALL),
+        cost_estimate=cost(2.5),
         name="list_grad",
-    )(where, places, bounds, unit, inverse, final_gain[None], w_score[None], *scores, *weights,
+    )(where, places, bounds, unit, inverse, attn, final_gain[None], w_score[None], *scores,
       *pieces)
+
+
+EXTRA = 16
+
+
+def out_kernel(chips, where_ref, left_ref, *refs):
+    near, far, out_ref = refs[:chips], refs[chips], refs[chips + 1]
+    core = where_ref[1]
+    cols = out_ref.shape[1] // 2
+    own_rows = out_ref.shape[0] - EXTRA
+    lead = far.shape[1] - 3 * 128 - cols
+    mine = jnp.concatenate([ref[...] for ref in near], 0)
+    other = far[...]
+    down = ((0,), (0,))
+    products = [mm(left_ref[...], x[:, lead : lead + cols], down) for x in (mine, other)]
+    out_ref[:own_rows, :cols] = jnp.where(core == 0, *products).astype(BF16)
+    out_ref[:own_rows, cols:] = jnp.where(core == 0, *products[::-1]).astype(BF16)
+
+    count = mine.shape[0] // chips
+    losses = []
+    for s in range(chips):
+        total = 0.0
+        for x in (mine, other):
+            row = x[s * count : s * count + EXTRA, lead + cols :].astype(F32)
+            total = total + (row[:, :128] + row[:, 128:256] + row[:, 256:])
+        losses.append(total)
+    while len(losses) > 1:
+        losses = [a + b for a, b in zip(losses[0::2], losses[1::2])]
+    rest = losses[0]
+    parts = []
+    for _ in range(3):
+        parts.append(rest.astype(BF16).astype(F32))
+        rest = rest - parts[-1]
+    row = jnp.concatenate(parts + [jnp.zeros_like(rest)], 1).astype(BF16)
+    out_ref[own_rows:] = jnp.concatenate([row] * (2 * cols // row.shape[1]), 1)
+
+
+def out_pass(where, left, near, far, cols):
+    vmem = pl.BlockSpec(memory_space=pltpu.VMEM)
+    return pl.pallas_call(
+        functools.partial(out_kernel, len(near)),
+        in_specs=[pl.BlockSpec(memory_space=pltpu.SMEM)] + [vmem] * (2 + len(near)),
+        out_specs=vmem,
+        out_shape=jax.ShapeDtypeStruct((left.shape[1] + EXTRA, 2 * cols), BF16),
+        compiler_params=pltpu.CompilerParams(vmem_limit_bytes=SMALL),
+        cost_estimate=cost(1),
+        name="out_rows",
+    )(where, left, *near, far)
 
 
 def grad_kernel(where_ref, own_ref, sib_ref, d_own_ref, d_sib_ref, a_ref, b_ref):
@@ -495,9 +567,38 @@
         ),
         out_shape=[jax.ShapeDtypeStruct((depth, part), BF16)] * 2,
         compiler_params=params(),
-        cost_estimate=COST,
+        cost_estimate=cost(3.8),
         name="grad_rows",
-    )(where, own, sib, d_own, d_sib)
+    )(where, *held(pltpu.VMEM, own, sib), *held(pltpu.VMEM, d_own, d_sib))
+
+
+def pick_kernel(starts, sizes, where_ref, mine_ref, come_ref, a_ref, b_ref):
+    core = where_ref[1]
+    mine, come = mine_ref[...].astype(F32), come_ref[...].astype(F32)
+    rows = mine.shape[0]
+    halves = []
+    for h in range(2):
+        spans = [slice(a + h * n, a + (h + 1) * n) for a, n in zip(starts, sizes)]
+        halves.append([jnp.concatenate([x[:, t] for t in spans], 1) for x in (mine, come)])
+    first = jnp.where(core == 0, halves[0][0], halves[1][1]).astype(BF16)
+    second = jnp.where(core == 0, halves[0][1], halves[1][0]).astype(BF16)
+    part = a_ref.shape[1]
+    a_ref[:rows], b_ref[:rows] = first[:, :part], first[:, part:]
+    a_ref[rows:], b_ref[rows:] = second[:, :part], second[:, part:]
+
+
+def pick(where, mine, come, starts, sizes):
+    rows = mine.shape[0]
+    vmem = pl.BlockSpec(memory_space=pltpu.VMEM)
+    return pl.pallas_call(
+        functools.partial(pick_kernel, starts, sizes),
+        in_specs=[pl.BlockSpec(memory_space=pltpu.SMEM), vmem, vmem],
+        out_specs=[vmem] * 2,
+        out_shape=[jax.ShapeDtypeStruct((2 * rows, sum(sizes) // 2), BF16)] * 2,
+        compiler_params=pltpu.CompilerParams(vmem_limit_bytes=SMALL),
+        cost_estimate=cost(1),
+        name="pick_columns",
+    )(where, mine, come)
 
 
 def solution(mesh):
@@ -522,28 +623,36 @@
     def neighbour(value, kind):
         moves = []
         for pair in range(pairs):
-            other = partner(kind, pair)
-            if 0 <= other < pairs:
-                moves += [(2 * pair + core, 2 * other + core) for core in (0, 1)]
+            for core in (0, 1):
+                other = partner(kind + core, pair)
+                if 0 <= other < pairs:
+                    moves.append((2 * pair + core, 2 * other + core))
         return lax.ppermute(value, ("list", "fsdp"), moves)
 
-    def gathered(value, order):
+    def after(value, *others):
+        return lax.optimization_barrier((value, others))[0]
+
+    def gathered(value, order, gates=()):
         have = {0: value}
-        for bit in order:
-            have.update({s ^ (bit >> 1): across(part, bit) for s, part in list(have.items())})
+        for k, bit in enumerate(order):
+            near, far = gates[k - 1] if 0 < k <= len(gates) else (None, None)
+            ready = {
+                s: after(part, far if s else near) if k and gates else part
+                for s, part in have.items()
+            }
+            have.update({s ^ (bit >> 1): across(part, bit) for s, part in ready.items()})
         return have
 
-    def scattered(parts, order):
-        current = dict(parts)
-        for bit in order:
-            flag = bit >> 1
-            come = {s ^ flag: across(current[s], bit) for s in sorted(current)[::-1] if s & flag}
-            current = {
-                s: (current[s].astype(F32) + come[s].astype(F32)).astype(BF16)
-                for s in current
-                if not s & flag
-            }
-        return current[0]
+    def joined(parts, come, bit):
+        return {
+            s: (parts[s].astype(F32) + come[s].astype(F32)).astype(BF16)
+            for s in parts
+            if not s & (bit >> 1)
+        }
+
+    def sent(parts, bit):
+        flag = bit >> 1
+        return {s ^ flag: across(parts[s], bit) for s in sorted(parts)[::-1] if s & flag}
 
     def local(hidden, norm_gain, w_qkv, w_out, final_gain, w_score, prior, labels, lengths):
         passages, _, width = hidden.shape
@@ -565,18 +674,19 @@
 
         starts = (0, 2 * width_q, 2 * (width_q + width_k))
         sizes = (width_q, width_k, width_k)
-
-        def half(value, h):
-            return jnp.concatenate(
-                [value[:, a + h * n : a + (h + 1) * n] for a, n in zip(starts, sizes)], 1
-            )
-
         come = across(w_qkv, 1)
-        both = ordered(w_qkv, come, 0)
-        pair_rows = jnp.where(first_core, half(both, 0), half(both, 1))
-        middle = pair_rows.shape[1] // 2
-        part_a = gathered(pair_rows[:, :middle], bits)
-        part_b = gathered(pair_rows[:, middle:], bits[::-1])
+        pair_a, pair_b = pick(where, w_qkv, come, starts, sizes)
+        w_out = after(w_out, come)
+        out_come = across(w_out, 1)
+        hidden_sib = across(after(hidden, come), 1)
+
+        normal, sums, before_own = norm(where, hidden, norm_gain, (pair_a, pair_b))
+        normal_sib, sums_sib, before_sib = norm(
+            where, after(hidden_sib, before_own), norm_gain, (pair_a, pair_b)
+        )
+        gates = ((before_own, before_sib),) * (len(bits) - 1)
+        part_a = gathered(pair_a, bits, gates)
+        part_b = gathered(pair_b, bits[::-1], gates)
         chips = n_fsdp // 2
         last = max(bin(s).count("1") for s in range(chips))
         weights = [{}, {}, {}]
@@ -584,67 +694,98 @@
             ones = bin(s).count("1")
             weights[2 if ones == last else 1 if ones else 0][s] = (part_a[s], part_b[s])
 
-        hidden, w_out, come = lax.optimization_barrier((hidden, w_out, come))
-        hidden_sib = across(hidden, 1)
         cols = w_out.shape[1] // 2
-        both = ordered(w_out, across(w_out, 1), 0)
+        both = ordered(w_out, out_come, 0)
         out_pair = jnp.where(first_core, both[:, :cols], both[:, cols:])
-        out_pair, weights[1] = lax.optimization_barrier((out_pair, weights[1]))
-        out_a = gathered(out_pair[:, : cols // 2], bits)
-        out_b = gathered(out_pair[:, cols // 2 :], bits[::-1])
-        pieces = []
-        for s in range(chips):
-            pieces += [out_a[s], out_b[s], across(out_a[s], 1), across(out_b[s], 1)]
-
-        normal, sums, before_own = norm(where, hidden, norm_gain, weights[0][0])
-        normal_sib, sums_sib, before_sib = norm(where, hidden_sib, norm_gain, weights[0][0])
-        sums = jnp.concatenate([sums, sums_sib], 0)
-        lanes = -(-lengths.shape[0] // 128) * 128
-        label_weight = jnp.exp(labels.astype(F32))
-        small = jnp.broadcast_to(
-            jnp.concatenate([prior, label_weight])[:, None], (2 * passages, 128)
-        )
-        small_sib = across(small, 1)
-        prior_pair = jnp.concatenate([small[:passages], small_sib[:passages]], 0)
-        heavy = jnp.concatenate([small[passages:], small_sib[passages:]], 0)
-        heavies = [heavy] + [neighbour(heavy, kind) for kind in range(4)]
-        pair = lax.axis_index("list") * (n_fsdp // 2) + chip
-        places = jnp.stack([pair] + [partner(kind, pair) for kind in range(4)]).astype(jnp.int32)
-        ends = jnp.cumsum(lengths)
-        bounds = jnp.pad(jnp.stack([ends - lengths, ends]), ((0, 0), (0, lanes - lengths.shape[0])))
-
+        prior, labels, lengths, out_pair = after((prior, labels, lengths, out_pair), before_sib)
         if weights[1]:
-            before_own = partial_project(where, normal, weights[1], before_own)
-            before_sib = partial_project(where, normal_sib, weights[1], before_sib)
-        weights[2], before_own, before_sib, heavies, prior_pair, bounds = lax.optimization_barrier(
-            (weights[2], before_own, before_sib, heavies, prior_pair, bounds)
-        )
+            normal_first = after(normal, before_sib)
+            before_own = partial_project(where, normal_first, weights[1], before_own)
+            before_sib = partial_project(
+                where, after(normal_sib, before_own), weights[1], before_sib
+            )
+            out_pair = after(out_pair, before_sib)
+        before_own, before_sib, weights[2] = after((before_own, before_sib, weights[2]), before_sib)
         proj_sib, probs_sib, attn_sib = forward(where, normal_sib, weights[2], groups, before_sib)
         attn_sib = attn_sib.reshape(passages, -1)
         attn_sib_other = across(attn_sib, 1)
-        proj_own, probs_own, attn_own = forward(where, normal, weights[2], groups, before_own)
+        gates = ((attn_sib, attn_sib),) * (len(bits) - 1)
+        out_a = gathered(out_pair[:, : cols // 2], bits, gates)
+        out_b = gathered(out_pair[:, cols // 2 :], bits[::-1], gates)
+        lanes = -(-lengths.shape[0] // 128) * 128
+        label_weight = jnp.exp(labels.astype(F32))
+        small = jnp.concatenate(
+            [jnp.broadcast_to(x[:, None], (passages, 64)) for x in (prior, label_weight)], 1
+        )
+        small_sib = across(small, 1)
+        pair = lax.axis_index("list") * (n_fsdp // 2) + chip
+        places = [pair] + [
+            jnp.where(first_core == near, partner(2 * kind, pair), partner(2 * kind + 1, pair))
+            for near in (True, False)
+            for kind in range(2)
+        ]
+        places = jnp.stack(places).astype(jnp.int32)
+        bounds = jnp.broadcast_to(
+            jnp.pad(lengths, (0, lanes - lengths.shape[0]))[None], (8, lanes)
+        )
+
+        normal_last = after(normal, probs_sib, places, bounds, small_sib)
+        proj_own, probs_own, attn_own = forward(where, normal_last, weights[2], groups, before_own)
         attn_own = attn_own.reshape(passages, -1)
         attn_own_other = across(attn_own, 1)
-        mine = jnp.concatenate([attn_own, attn_sib], 0)
-        other = jnp.concatenate([attn_sib_other, attn_own_other], 0)
+        pieces = []
+        for s in range(chips):
+            gate = probs_sib if bin(s).count("1") == last else before_sib
+            pieces += [out_a[s], out_b[s]]
+            pieces += [across(after(x, gate), 1) for x in (out_a[s], out_b[s])]
         unit, inverse, score, attn = score_pass(
-            where, mine, other, sums, final_gain, w_score, prior_pair, pieces
+            where,
+            (attn_own, attn_sib, attn_sib_other, attn_own_other),
+            (sums, sums_sib),
+            final_gain,
+            w_score,
+            (small, small_sib),
+            pieces,
         )
-        scores = [score] + [neighbour(score, kind) for kind in range(4)]
-        d_rows, d_attended, loss_part = list_pass(
-            where, places, bounds, unit, inverse, final_gain, w_score, scores, heavies, pieces,
+        near = [neighbour(score, kind) for kind in (0, 2)]
+        scores = [score] + near + [across(x, 1) for x in near]
+        d_attended, payload = list_pass(
+            where, places, bounds, unit, inverse, attn, final_gain, w_score, scores, pieces,
             passages,
         )
 
         d_own = backward(probs_own, proj_own, d_attended[:passages], groups)
-        d_sib = backward(probs_sib, proj_sib, d_attended[passages:], groups)
-        depth = pair_rows.shape[0]
-        blocks = {
-            s: grad_block(where, s, normal, normal_sib, d_own, d_sib, depth)
-            for s in sorted(range(n_fsdp // 2), key=lambda s: -bin(s).count("1"))
-        }
-        sum_a = scattered({s: blocks[s][0] for s in blocks}, bits)
-        sum_b = scattered({s: blocks[s][1] for s in blocks}, bits[::-1])
+        d_sib = backward(
+            after(probs_sib, d_own), proj_sib, d_attended[passages:], groups
+        )
+        depth = pair_a.shape[0]
+        parts_a, parts_b, come_a, come_b = {}, {}, {}, {}
+        flag_a, flag_b = bits[0] >> 1, bits[-1] >> 1
+        before = d_sib
+        for s in sorted(range(chips), key=lambda s: (-bin(s).count("1"), s)):
+            gate = (before, come_a, come_b) if s == 0 else before
+            parts_a[s], parts_b[s] = grad_block(
+                where, s, normal, normal_sib, d_own, after(d_sib, gate), depth
+            )
+            if s & flag_a and s & flag_b:
+                come_a[s ^ flag_a] = across(parts_a[s], bits[0])
+                come_b[s ^ flag_b] = across(parts_b[s], bits[-1])
+            before = parts_a[s]
+        first_a, first_b = dict(come_a), dict(come_b)
+        for s in range(chips):
+            if s & flag_a and s ^ flag_a not in first_a:
+                first_a[s ^ flag_a] = across(parts_a[s], bits[0])
+            if s & flag_b and s ^ flag_b not in first_b:
+                first_b[s ^ flag_b] = across(parts_b[s], bits[-1])
+        left_a, left_b = joined(parts_a, first_a, bits[0]), joined(parts_b, first_b, bits[-1])
+        gate = (left_a, left_b)
+        for bit_a, bit_b in zip(bits[1:], bits[::-1][1:]):
+            left_a = joined(left_a, sent(left_a, bit_a), bit_a)
+            left_b = joined(left_b, sent(left_b, bit_b), bit_b)
+        sum_a, sum_b = left_a[0], left_b[0]
+        gates = ((parts_a[0], parts_a[0]),) * (len(bits) - 1)
+        plane = gathered(after(payload, d_own), bits, gates)
+        plane = after([plane[s] for s in range(chips)], gate)
         chip_sum = jnp.concatenate([sum_a, sum_b], 1)
         upper, lower = chip_sum[: depth // 2], chip_sum[depth // 2 :]
         keep = jnp.where(first_core, upper, lower)
@@ -667,50 +808,26 @@
 
         grad_qkv = list_scatter(rows_sum)
 
-        inner = attn.shape[1]
-        attn_halves = attn[:, : inner // 2], attn[:, inner // 2 :]
-        row_halves = d_rows[:, :cols], d_rows[:, cols:]
-        loss = loss_part[:1]
-        parts = []
-        for _ in range(3):
-            upper = lax.reduce_precision(loss, 8, 7)
-            parts.append(upper.astype(BF16))
-            loss = loss - upper
-        extra = jnp.broadcast_to(jnp.concatenate(parts, 1), (2 * passages, 3 * 128))
-        payload = jnp.concatenate(
-            [
-                jnp.where(first_core, *attn_halves),
-                jnp.where(first_core, *row_halves),
-                extra,
-            ],
-            1,
+        far = across(jnp.concatenate(plane, 0), 1)
+        inner = 2 * width_q
+        left = ordered(
+            jnp.concatenate([x[:, :width_q] for x in plane], 0), far[:, :width_q], 1
         )
-        plane = gathered(payload, bits)
-        plane = jnp.concatenate([plane[s] for s in range(chips)], 0)
-        far = across(plane, 1)
         own_rows = inner // n_fsdp
-        far = far.reshape(chips, 2, passages, -1)[:, ::-1].reshape(plane.shape)
-        left = ordered(plane[:, : inner // 2], far[:, : inner // 2], 1)
-        span = slice(inner // 2, inner // 2 + cols)
-        right = ordered(plane[:, span], far[:, span], 1)
         left = lax.dynamic_slice_in_dim(left, index * own_rows, own_rows, 1)
-        grad_out = list_scatter(
-            lax.dot_general(left, right, (((0,), (0,)), ((), ())), preferred_element_type=F32)
-        )
-
-        def loss_of(value):
-            rows = value[:, inner // 2 + cols :].reshape(chips, 2 * passages, 3, 128)
-            return sum(rows[:, 0, k, 0].astype(F32) for k in range(3))
-
-        losses = loss_of(plane) + loss_of(far)
-        while losses.shape[0] > 1:
-            losses = losses[0::2] + losses[1::2]
-        loss = jnp.broadcast_to(losses[:, None], (8, 128))
-        distance = 1
-        while distance < n_list:
-            loss = loss + along(loss, distance)
-            distance *= 2
-        return (loss[0, 0], grad_qkv, grad_out)
+        rows = out_pass(where, left, plane, far, cols)
+        blocks = rows.shape[1] // n_list
+        block = lambda which: lax.dynamic_slice_in_dim(rows, which * blocks, blocks, 1)
+        come = [block(place)]
+        come += [along(block(place ^ distance), distance) for distance in range(1, n_list)]
+        grad_out = sum(x[:own_rows].astype(F32) for x in come)
+        losses = []
+        for x in come:
+            x = x[own_rows].astype(F32)
+            losses.append(x[0] + x[128] + x[256])
+        while len(losses) > 1:
+            losses = [a + b for a, b in zip(losses[0::2], losses[1::2])]
+        return (losses[0], grad_qkv, grad_out)
 
     placed = (
         P(("list", "fsdp"), None, None),

time: 234 us -> 178 us (0.76)
  waiting for transfers between devices: 65.4 us -> 41.1 us
  starting transfers between devices: 58.5 us -> 42.2 us
  other arithmetic: 17.1 us -> 6.93 us
  Pallas kernels: 66.1 us -> 58.4 us
  between operations: 2.65 us -> 10.1 us
  local copies, waits for them, and re-layouts: 20.4 us -> 18 us
    ppermute x37 -> x39, waiting for transfers between devices: 45.2 us -> 21.1 us  [across(): lax.ppermute(value, 'fsdp', [(i, i ^ distance) for i in range(n_fsdp)])]
    ppermute x37 -> x39, starting transfers between devices: 34.9 us -> 27.3 us  [across(): lax.ppermute(value, 'fsdp', [(i, i ^ distance) for i in range(n_fsdp)])]
    concatenate x9 -> x2, other arithmetic: 5.73 us -> 0.12 us  [the longest x1 0.08 us: local(): jnp.concatenate([jnp.broadcast_to(x[:, None], (passages, 64)) for x in (p...]
    ppermute x8 -> x6, starting transfers between devices: 14.1 us -> 9.59 us  [along(): lax.ppermute(value, 'list', [(i, i ^ distance) for i in range(n_list)])]
    pallas_call x4, Pallas kernels: 17.3 us -> 13 us  [grad_block(): pl.pallas_call(grad_kernel, grid_spec=pltpu.PrefetchScalarGridSpec(num_sc...]
    pallas_call x2, Pallas kernels: 13.7 us -> 9.51 us  [forward(): pl.pallas_call(functools.partial(forward_kernel, pieces, groups), grid_sp...]
    ppermute x8 -> x2, starting transfers between devices: 9.46 us -> 5.37 us  [neighbour(): return lax.ppermute(value, ('list', 'fsdp'), moves)]
    reshape x5 -> x0, local copies, waits for them, and re-layouts: 2.44 us -> none  [the longest x2 1.64 us: norm(): return (normal, sums.reshape(passages, width), product)]
  transfers between devices with their start and end apart: 53 -> 47, of which waited for: 11 -> 21; matrix products, arithmetic and copies ran while one was open for 10% -> 5% of each run, Pallas kernels for 26% -> 24%
where the time goes in v4:
time: 178 us; the launch traced here: 177 us
  Pallas kernels  58.4 us (33%)
  starting transfers between devices  42.2 us (24%)
  waiting for transfers between devices  41.1 us (23%)
  local copies, waits for them, and re-layouts  18 us (10%)
  between operations  10.1 us (6%)
  other arithmetic  6.93 us (4%)
    ppermute x39, starting transfers between devices, across(): lax.ppermute(value, 'fsdp', [(i, i ^ distance) for i in range(n_fsdp)])  27.3 us
    ppermute x39, waiting for transfers between devices, across(): lax.ppermute(value, 'fsdp', [(i, i ^ distance) for i in range(n_fsdp)])  21.1 us
    ppermute x6, waiting for transfers between devices, along(): lax.ppermute(value, 'list', [(i, i ^ distance) for i in range(n_list)])  16.8 us
    unnamed x68, local copies, waits for them, and re-layouts  13.9 us
    pallas_call x4, Pallas kernels, grad_block(): pl.pallas_call(grad_kernel, grid_spec=pltpu.PrefetchScalarGridSpec(num_sc...  13 us
    pallas_call x2, Pallas kernels, norm(): pl.pallas_call(norm_kernel, grid_spec=pltpu.PrefetchScalarGridSpec(num_sc...  12.9 us
    ppermute x6, starting transfers between devices, along(): lax.ppermute(value, 'list', [(i, i ^ distance) for i in range(n_list)])  9.59 us
    pallas_call x2, Pallas kernels, forward(): pl.pallas_call(functools.partial(forward_kernel, pieces, groups), grid_sp...  9.51 us
  transfers between devices with their start and end apart: 47, of which 21 were waited for; matrix products, arithmetic and copies ran while one was open for 5% of the time, Pallas kernels for 24%

profile of v4, /device:TPU:0, one launch (start us, length us, event | category | flops | bytes accessed | tf_op | source)
XLA Modules:
  0.0 176.7 jit_solution(7264296348248294920)
XLA Ops:
  1.1 2.1 %collective-permute-done.come_ref = bf16[256,1536]{1,0:T(8,128)(2,1)S(1)} collective-permute-done((bf16[256,1536]{1,0:T(8,128)(2,1)}, bf16[256,1536]{1,0:T(8,128)(2,1)S(1)}, u32[]{:S(2)}, u32[]{:S(2)}) %collective-permute-start) | collective-permute-done | bytes 786464 | tf_op jit(solution)/shard_map/ppermute | solution.py:610
  5.8 2.9 %collective-permute-start.3 = (bf16[512,384]{1,0:T(8,128)(2,1)S(1)}, bf16[512,384]{1,0:T(8,128)(2,1)}, u32[]{:S(2)}, u32[]{:S(2)}) collective-permute-start(bf16[512,384]{1,0:T(8,128)(2,1)S(1)} %get-tuple-element.86.a_ref), channel_id=1, source_target_pairs={{0,2},{1,3},{2,0},{3,1},{4,6},{5,7},{6,4},{7,5},{8,10},{9,11},{10,... | collective-permute-start | bytes 1179656 | tf_op jit(solution)/shard_map/ppermute | solution.py:610
  10.9 6.4 %norm_project.2 = (bf16[1024,2048]{1,0:T(8,128)(2,1)S(1)}, f32[4,4,2048]{2,1,0:T(4,128)S(1)}, f32[1024,768]{1,0:T(8,128)S(1)}) custom-call(s32[2]{0:T(128)S(1)} %pad_add_fusion.where_ref, bf16[16,64,2048]{2,1,0:T(8,128)(2,1)} %hidden_ref.1, f32[1,2048]{1,0:T(1,128)S(1)} %bitcast.21, bf16[512,384]{1,0:T(8,128)(2,1)S(1)} %get-tuple-element.86.a_ref, ...), custom_call_target="tpu_custom_call" | custom-call | flops 700000000 | bytes 24500000 | tf_op jit(solution)/shard_map/norm_project/pallas_call | solution.py:65
  18.3 6.4 %norm_project.3 = (bf16[1024,2048]{1,0:T(8,128)(2,1)S(1)}, f32[4,4,2048]{2,1,0:T(4,128)S(1)}, f32[1024,768]{1,0:T(8,128)S(1)}) custom-call(s32[2]{0:T(128)S(1)} %pad_add_fusion.where_ref, bf16[16,64,2048]{2,1,0:T(8,128)(2,1)} %collective-permute-done.2.hidden_ref, f32[1,2048]{1,0:T(1,128)S(1)} %bitcast.22, bf16[512,384]{1,0:T(8,128)(2,1)S(1)} %get-tuple-element.86.a_ref, ...), custom_call_target="tpu_custom_call" | custom-call | flops 700000000 | bytes 24500000 | tf_op jit(solution)/shard_map/norm_project/pallas_call | solution.py:65
  24.8 2.0 %collective-permute-start.7 = (bf16[512,384]{1,0:T(8,128)(2,1)}, bf16[512,384]{1,0:T(8,128)(2,1)S(1)}, u32[]{:S(2)}, u32[]{:S(2)}) collective-permute-start(bf16[512,384]{1,0:T(8,128)(2,1)} %collective-permute-done.3.refs_2_), channel_id=1, source_target_pairs={{0,4},{1,5},{2,6},{3,7},{4,0},{5,1},{6,2},{7,3},{8,12},{9,13},{10,... | collective-permute-start | bytes 1179656 | tf_op jit(solution)/shard_map/ppermute | solution.py:610
  29.3 3.9 %project_more.2.refs_3_ = f32[1024,768]{1,0:T(8,128)S(1)} custom-call(s32[2]{0:T(128)S(1)} %pad_add_fusion.where_ref, bf16[1024,2048]{1,0:T(8,128)(2,1)S(1)} %get-tuple-element.96.refs_0_.refs_1_.own_ref, bf16[1024,2048]{1,0:T(8,128)(2,1)S(1)} %get-tuple-element.96.refs_0_.refs_1_.own_ref, bf16[512,384]{1,0:T(8,128)(2,1)} %collective-permute-done.3.refs_2_, ...), custom_call_target="tpu_custom_call" | custom-call | flops 450000000 | bytes 15750000 | tf_op jit(solution)/shard_map/project_more/pallas_call | solution.py:205
  33.3 3.9 %project_more.3.refs_3_ = f32[1024,768]{1,0:T(8,128)S(1)} custom-call(s32[2]{0:T(128)S(1)} %pad_add_fusion.where_ref, bf16[1024,2048]{1,0:T(8,128)(2,1)S(1)} %get-tuple-element.87.refs_0_.refs_1_.sib_ref, bf16[1024,2048]{1,0:T(8,128)(2,1)S(1)} %get-tuple-element.87.refs_0_.refs_1_.sib_ref, bf16[512,384]{1,0:T(8,128)(2,1)} %collective-permute-done.3.refs_2_, ...), custom_call_target="tpu_custom_call" | custom-call | flops 450000000 | bytes 15750000 | tf_op jit(solution)/shard_map/project_more/pallas_call | solution.py:205
  39.6 4.8 %project_attend.2 = (bf16[1024,768]{1,0:T(8,128)(2,1)S(1)}, bf16[2,2,1024,128]{3,2,1,0:T(8,128)(2,1)S(1)}, f32[2,8,512]{2,1,0:T(8,128)S(1)}) custom-call(s32[2]{0:T(128)S(1)} %pad_add_fusion.where_ref, bf16[1024,2048]{1,0:T(8,128)(2,1)S(1)} %get-tuple-element.87.refs_0_.refs_1_.sib_ref, bf16[512,384]{1,0:T(8,128)(2,1)S(1)} %collective-permute-done.7.refs_1_, ...), custom_call_target="tpu_custom_call" | custom-call | flops 650000000 | bytes 22750000 | tf_op jit(solution)/shard_map/project_attend/pallas_call | solution.py:232
  52.9 2.7 %collective-permute-done.15.refs_5_.refs_10_ = bf16[256,512]{1,0:T(8,128)(2,1)S(1)} collective-permute-done((bf16[256,512]{1,0:T(8,128)(2,1)S(1)}, bf16[256,512]{1,0:T(8,128)(2,1)S(1)}, u32[]{:S(2)}, u32[]{:S(2)}) %collective-permute-start.15) | collective-permute-done | bytes 262176 | tf_op jit(solution)/shard_map/ppermute | solution.py:610
  57.7 2.2 %copy-done.1 = bf16[1024,2048]{1,0:T(8,128)(2,1)S(1)} copy-done((bf16[1024,2048]{1,0:T(8,128)(2,1)S(1)}, bf16[1024,2048]{1,0:T(8,128)(2,1)}, u32[]{:S(2)}) %copy-start.1) | copy-done | bytes 4194328
  61.9 4.7 %project_attend.3 = (bf16[1024,768]{1,0:T(8,128)(2,1)S(1)}, bf16[2,2,1024,128]{3,2,1,0:T(8,128)(2,1)S(1)}, f32[2,8,512]{2,1,0:T(8,128)S(1)}) custom-call(s32[2]{0:T(128)S(1)} %pad_add_fusion.where_ref, bf16[1024,2048]{1,0:T(8,128)(2,1)S(1)} %copy-done.1, bf16[512,384]{1,0:T(8,128)(2,1)S(1)} %copy-done.8, bf16[512,384]{1,0:T(8,128)(2,1)S(1)} %copy-done.10, ...), custom_call_target="tpu_custom_call" | custom-call | flops 650000000 | bytes 22750000 | tf_op jit(solution)/shard_map/project_attend/pallas_call | solution.py:232
  71.4 2.7 %pool_score.1 = (f32[32,2048]{1,0:T(8,128)S(1)}, f32[32,128]{1,0:T(8,128)S(1)}, f32[32,128]{1,0:T(8,128)S(1)}, bf16[32,1024]{1,0:T(8,128)(2,1)S(1)}) custom-call(s32[2]{0:T(128)S(1)} %pad_add_fusion.where_ref, f32[16,512]{1,0:T(8,128)S(1)} %bitcast.20, f32[16,512]{1,0:T(8,128)S(1)} %bitcast.18, f32[16,512]{1,0:T(8,128)S(1)} %collective-permute-done.10.own_far_ref, ...), custom_call_target="tpu_custom_call" | custom-call | flops 200000000 | bytes 7000000 | tf_op jit(solution)/shard_map/pool_score/pallas_call | solution.py:378
  74.1 2.9 %collective-permute-start.26 = (f32[32,128]{1,0:T(8,128)S(1)}, f32[32,128]{1,0:T(8,128)S(1)}, u32[]{:S(2)}, u32[]{:S(2)}) collective-permute-start(f32[32,128]{1,0:T(8,128)S(1)} %get-tuple-element.119.refs_0_), channel_id=1, source_target_pairs={{0,2},{2,0},{3,5},{4,6},{5,3},{6,4},{7,9},{8,10},{9,7},{10,8},{11,... | collective-permute-start | bytes 49160 | tf_op jit(solution)/shard_map/ppermute | solution.py:630
  77.0 2.4 %collective-permute-start.27 = (f32[32,128]{1,0:T(8,128)S(1)}, f32[32,128]{1,0:T(8,128)S(1)}, u32[]{:S(2)}, u32[]{:S(2)}) collective-permute-start(f32[32,128]{1,0:T(8,128)S(1)} %get-tuple-element.119.refs_0_), channel_id=1, source_target_pairs={{0,4},{2,6},{4,0},{5,9},{6,2},{7,11},{8,12},{9,5},{10,14},{11,7},{... | collective-permute-start | bytes 49160 | tf_op jit(solution)/shard_map/ppermute | solution.py:630
  79.7 2.9 %collective-permute-done.27.refs_2_ = f32[32,128]{1,0:T(8,128)S(1)} collective-permute-done((f32[32,128]{1,0:T(8,128)S(1)}, f32[32,128]{1,0:T(8,128)S(1)}, u32[]{:S(2)}, u32[]{:S(2)}) %collective-permute-start.27) | collective-permute-done | bytes 16416 | tf_op jit(solution)/shard_map/ppermute | solution.py:630
  83.8 3.9 %list_grad.1 = (f32[32,512]{1,0:T(8,128)S(1)}, bf16[32,1920]{1,0:T(8,128)(2,1)S(1)}) custom-call(s32[2]{0:T(128)S(1)} %pad_add_fusion.where_ref, s32[5]{0:T(128)S(1)} %stack.35.place_ref, s32[8,128]{1,0:T(8,128)S(1)} %broadcast_in_dim.13.bounds_ref, f32[32,2048]{1,0:T(8,128)S(1)} %get-tuple-element.116.unit_ref, ...), custom_call_target="tpu_custom_call" | custom-call | flops 250000000 | bytes 8750000 | tf_op jit(solution)/shard_map/list_grad/pallas_call | solution.py:472
  87.8 3.4 %attend_back.2.d_own_ref = bf16[1024,768]{1,0:T(8,128)(2,1)S(1)} custom-call(bf16[2,2,1024,128]{3,2,1,0:T(8,128)(2,1)S(1)} %get-tuple-element.121.probs_ref, bf16[1024,768]{1,0:T(8,128)(2,1)S(1)} %get-tuple-element.122.projected_ref, f32[2,8,512]{2,1,0:T(8,128)S(1)} %get-tuple-element.164.d_ref), custom_call_target="tpu_custom_call" | custom-call | flops 340000000 | bytes 11900000 | tf_op jit(solution)/shard_map/attend_back/pallas_call | solution.py:316
  91.3 3.4 %attend_back.3.d_sib_ref = bf16[1024,768]{1,0:T(8,128)(2,1)S(1)} custom-call(bf16[2,2,1024,128]{3,2,1,0:T(8,128)(2,1)S(1)} %copy-done.16, bf16[1024,768]{1,0:T(8,128)(2,1)S(1)} %copy-done.12, f32[2,8,512]{2,1,0:T(8,128)S(1)} %get-tuple-element.163.d_ref), custom_call_target="tpu_custom_call" | custom-call | flops 340000000 | bytes 11900000 | tf_op jit(solution)/shard_map/attend_back/pallas_call | solution.py:316
  94.7 2.9 %grad_rows.4 = (bf16[512,384]{1,0:T(8,128)(2,1)S(1)}, bf16[512,384]{1,0:T(8,128)(2,1)S(1)}) custom-call(s32[2]{0:T(128)S(1)} %pad_add_fusion.where_ref, bf16[1024,2048]{1,0:T(8,128)(2,1)S(1)} %copy-done.2, bf16[1024,2048]{1,0:T(8,128)(2,1)S(1)} %copy-done.5, bf16[1024,768]{1,0:T(8,128)(2,1)S(1)} %attend_back.2.d_own_ref, ...), custom_call_target="tpu_custom_call" | custom-call | flops 380000000 | bytes 13300000 | tf_op jit(solution)/shard_map/grad_rows/pallas_call | solution.py:555
  98.7 1.8 collective-permute-start.32
  100.5 3.6 %grad_rows.5 = (bf16[512,384]{1,0:T(8,128)(2,1)}, bf16[512,384]{1,0:T(8,128)(2,1)S(1)}) custom-call(s32[2]{0:T(128)S(1)} %pad_add_fusion.where_ref, bf16[1024,2048]{1,0:T(8,128)(2,1)S(1)} %copy-done.2, bf16[1024,2048]{1,0:T(8,128)(2,1)S(1)} %copy-done.5, bf16[1024,768]{1,0:T(8,128)(2,1)S(1)} %attend_back.2.d_own_ref, bf16[1024,768]{1,0:T(8,128)(2,1)S(1)} %attend_back.3.d_sib_ref), custom_call_target="tpu_custom_call" | custom-call | flops 380000000 | bytes 13300000 | tf_op jit(solution)/shard_map/grad_rows/pallas_call | solution.py:555
  104.1 3.6 %grad_rows.6 = (bf16[512,384]{1,0:T(8,128)(2,1)S(1)}, bf16[512,384]{1,0:T(8,128)(2,1)}) custom-call(s32[2]{0:T(128)S(1)} %pad_add_fusion.where_ref, bf16[1024,2048]{1,0:T(8,128)(2,1)S(1)} %copy-done.2, bf16[1024,2048]{1,0:T(8,128)(2,1)S(1)} %copy-done.5, bf16[1024,768]{1,0:T(8,128)(2,1)S(1)} %attend_back.2.d_own_ref, bf16[1024,768]{1,0:T(8,128)(2,1)S(1)} %attend_back.3.d_sib_ref), custom_call_target="tpu_custom_call" | custom-call | flops 380000000 | bytes 13300000 | tf_op jit(solution)/shard_map/grad_rows/pallas_call | solution.py:555
  107.7 1.9 %collective-permute-done.31 = bf16[512,384]{1,0:T(8,128)(2,1)S(1)} collective-permute-done((bf16[512,384]{1,0:T(8,128)(2,1)S(1)}, bf16[512,384]{1,0:T(8,128)(2,1)S(1)}, u32[]{:S(2)}, u32[]{:S(2)}) %collective-permute-start.31) | collective-permute-done | bytes 393248 | tf_op jit(solution)/shard_map/ppermute | solution.py:610
  111.2 2.1 %collective-permute-start.30 = (bf16[32,1920]{1,0:T(8,128)(2,1)S(1)}, bf16[32,1920]{1,0:T(8,128)(2,1)S(1)}, u32[]{:S(2)}, u32[]{:S(2)}) collective-permute-start(bf16[32,1920]{1,0:T(8,128)(2,1)S(1)} %get-tuple-element.141.refs_0_), channel_id=1, source_target_pairs={{0,2},{1,3},{2,0},{3,1},{4,6},{5,7},{6,4},{7,5},{8,10},{9,11},{10,... | collective-permute-start | bytes 368648 | tf_op jit(solution)/shard_map/ppermute | solution.py:610
  115.4 2.2 %copy-done.3 = bf16[1024,2048]{1,0:T(8,128)(2,1)S(1)} copy-done((bf16[1024,2048]{1,0:T(8,128)(2,1)S(1)}, bf16[1024,2048]{1,0:T(8,128)(2,1)}, u32[]{:S(2)}) %copy-start.3) | copy-done | bytes 4194328
  117.6 2.2 %copy-done.6 = bf16[1024,2048]{1,0:T(8,128)(2,1)S(1)} copy-done((bf16[1024,2048]{1,0:T(8,128)(2,1)S(1)}, bf16[1024,2048]{1,0:T(8,128)(2,1)}, u32[]{:S(2)}) %copy-start.6) | copy-done | bytes 4194328
  119.8 2.9 %grad_rows.7 = (bf16[512,384]{1,0:T(8,128)(2,1)S(1)}, bf16[512,384]{1,0:T(8,128)(2,1)S(1)}) custom-call(s32[2]{0:T(128)S(1)} %pad_add_fusion.where_ref, bf16[1024,2048]{1,0:T(8,128)(2,1)S(1)} %copy-done.3, bf16[1024,2048]{1,0:T(8,128)(2,1)S(1)} %copy-done.6, bf16[1024,768]{1,0:T(8,128)(2,1)S(1)} %attend_back.2.d_own_ref, ...), custom_call_target="tpu_custom_call" | custom-call | flops 380000000 | bytes 13300000 | tf_op jit(solution)/shard_map/grad_rows/pallas_call | solution.py:555
  126.1 5.2 %collective-permute-done.36 = bf16[512,384]{1,0:T(8,128)(2,1)} collective-permute-done((bf16[512,384]{1,0:T(8,128)(2,1)}, bf16[512,384]{1,0:T(8,128)(2,1)}, u32[]{:S(2)}, u32[]{:S(2)}) %collective-permute-start.36) | collective-permute-done | bytes 393248 | tf_op jit(solution)/shard_map/ppermute | solution.py:610
  136.4 3.5 %collective-permute-start.46 = (bf16[256,384]{1,0:T(8,128)(2,1)S(1)}, bf16[256,384]{1,0:T(8,128)(2,1)S(1)}, u32[]{:S(2)}, u32[]{:S(2)}) collective-permute-start(bf16[256,384]{1,0:T(8,128)(2,1)S(1)} %get-tuple-element.150), channel_id=1, source_target_pairs={{0,24},{8,16},{16,8},{24,0},{1,25},{9,17},{17,9},{25,1},{2,26},{10... | collective-permute-start | bytes 589832 | tf_op jit(solution)/shard_map/ppermute | solution.py:613
  143.1 2.9 %collective-permute-start.39 = (bf16[144,512]{1,0:T(8,128)(2,1)S(1)}, bf16[144,512]{1,0:T(8,128)(2,1)S(1)}, u32[]{:S(2)}, u32[]{:S(2)}) collective-permute-start(bf16[144,512]{1,0:T(8,128)(2,1)S(1)} %get-tuple-element.155), channel_id=1, source_target_pairs={{0,16},{8,24},{16,0},{24,8},{1,17},{9,25},{17,1},{25,9},{2,18},{10... | collective-permute-start | bytes 442376 | tf_op jit(solution)/shard_map/ppermute | solution.py:613
  149.6 14.5 %collective-permute-done.45 = bf16[256,384]{1,0:T(8,128)(2,1)S(1)} collective-permute-done((bf16[256,384]{1,0:T(8,128)(2,1)S(1)}, bf16[256,384]{1,0:T(8,128)(2,1)S(1)}, u32[]{:S(2)}, u32[]{:S(2)}) %collective-permute-start.45) | collective-permute-done | bytes 196640 | tf_op jit(solution)/shard_map/ppermute | solution.py:613
  165.0 2.3 %collective-permute-done.39 = bf16[144,512]{1,0:T(8,128)(2,1)S(1)} collective-permute-done((bf16[144,512]{1,0:T(8,128)(2,1)S(1)}, bf16[144,512]{1,0:T(8,128)(2,1)S(1)}, u32[]{:S(2)}, u32[]{:S(2)}) %collective-permute-start.39) | collective-permute-done | bytes 147488 | tf_op jit(solution)/shard_map/ppermute | solution.py:613
  (191 shorter events, 51.1 us)
Async XLA Ops:
  3.3 15.0 %collective-permute-start.2 = (bf16[16,64,2048]{2,1,0:T(8,128)(2,1)}, bf16[16,64,2048]{2,1,0:T(8,128)(2,1)}, u32[]{:S(2)}, u32[]{:S(2)}) collective-permute-start(bf16[16,64,2048]{2,1,0:T(8,128)(2,1)} %hidden_ref.1), channel_id=1, source_target_pairs={{0,1},{1,0},{2,3},{3,2},{4,5},{5,4},{6,7},{7,6},{8,9},{9,8},{10,11... | collective-permute-start | bytes 12582920 | tf_op jit(solution)/shard_map/ppermute | solution.py:610
  3.6 14.3 %collective-permute-start.1 = (bf16[128,2048]{1,0:T(8,128)(2,1)}, bf16[128,2048]{1,0:T(8,128)(2,1)S(1)}, u32[]{:S(2)}, u32[]{:S(2)}) collective-permute-start(bf16[128,2048]{1,0:T(8,128)(2,1)} %param.12), channel_id=1, source_target_pairs={{0,1},{1,0},{2,3},{3,2},{4,5},{5,4},{6,7},{7,6},{8,9},{9,8},{10,11... | collective-permute-start | bytes 1572872 | tf_op jit(solution)/shard_map/ppermute | solution.py:610
  5.8 19.0 %collective-permute-start.3 = (bf16[512,384]{1,0:T(8,128)(2,1)S(1)}, bf16[512,384]{1,0:T(8,128)(2,1)}, u32[]{:S(2)}, u32[]{:S(2)}) collective-permute-start(bf16[512,384]{1,0:T(8,128)(2,1)S(1)} %get-tuple-element.86.a_ref), channel_id=1, source_target_pairs={{0,2},{1,3},{2,0},{3,1},{4,6},{5,7},{6,4},{7,5},{8,10},{9,11},{10,... | collective-permute-start | bytes 1179656 | tf_op jit(solution)/shard_map/ppermute | solution.py:610
  8.7 18.1 %collective-permute-start.6 = (bf16[512,384]{1,0:T(8,128)(2,1)S(1)}, bf16[512,384]{1,0:T(8,128)(2,1)}, u32[]{:S(2)}, u32[]{:S(2)}) collective-permute-start(bf16[512,384]{1,0:T(8,128)(2,1)S(1)} %get-tuple-element.85.b_ref), channel_id=1, source_target_pairs={{0,4},{1,5},{2,6},{3,7},{4,0},{5,1},{6,2},{7,3},{8,12},{9,13},{10,... | collective-permute-start | bytes 1179656 | tf_op jit(solution)/shard_map/ppermute | solution.py:610
  17.4 11.0 %collective-permute-start.4 = (bf16[512,384]{1,0:T(8,128)(2,1)S(1)}, bf16[512,384]{1,0:T(8,128)(2,1)S(1)}, u32[]{:S(2)}, u32[]{:S(2)}) collective-permute-start(bf16[512,384]{1,0:T(8,128)(2,1)S(1)} %get-tuple-element.85.b_ref), channel_id=1, source_target_pairs={{0,2},{1,3},{2,0},{3,1},{4,6},{5,7},{6,4},{7,5},{8,10},{9,11},{10,... | collective-permute-start | bytes 1179656 | tf_op jit(solution)/shard_map/ppermute | solution.py:610
  18.0 11.4 %collective-permute-start.5 = (bf16[512,384]{1,0:T(8,128)(2,1)S(1)}, bf16[512,384]{1,0:T(8,128)(2,1)S(1)}, u32[]{:S(2)}, u32[]{:S(2)}) collective-permute-start(bf16[512,384]{1,0:T(8,128)(2,1)S(1)} %get-tuple-element.86.a_ref), channel_id=1, source_target_pairs={{0,4},{1,5},{2,6},{3,7},{4,0},{5,1},{6,2},{7,3},{8,12},{9,13},{10,... | collective-permute-start | bytes 1179656 | tf_op jit(solution)/shard_map/ppermute | solution.py:610
  24.8 14.7 %collective-permute-start.7 = (bf16[512,384]{1,0:T(8,128)(2,1)}, bf16[512,384]{1,0:T(8,128)(2,1)S(1)}, u32[]{:S(2)}, u32[]{:S(2)}) collective-permute-start(bf16[512,384]{1,0:T(8,128)(2,1)} %collective-permute-done.3.refs_2_), channel_id=1, source_target_pairs={{0,4},{1,5},{2,6},{3,7},{4,0},{5,1},{6,2},{7,3},{8,12},{9,13},{10,... | collective-permute-start | bytes 1179656 | tf_op jit(solution)/shard_map/ppermute | solution.py:610
  26.8 12.7 %collective-permute-start.8 = (bf16[512,384]{1,0:T(8,128)(2,1)}, bf16[512,384]{1,0:T(8,128)(2,1)S(1)}, u32[]{:S(2)}, u32[]{:S(2)}) collective-permute-start(bf16[512,384]{1,0:T(8,128)(2,1)} %collective-permute-done.6.refs_5_), channel_id=1, source_target_pairs={{0,2},{1,3},{2,0},{3,1},{4,6},{5,7},{6,4},{7,5},{8,10},{9,11},{10,... | collective-permute-start | bytes 1179656 | tf_op jit(solution)/shard_map/ppermute | solution.py:610
  38.0 11.0 %collective-permute-start.14 = (bf16[256,512]{1,0:T(8,128)(2,1)}, bf16[256,512]{1,0:T(8,128)(2,1)}, u32[]{:S(2)}, u32[]{:S(2)}) collective-permute-start(bf16[256,512]{1,0:T(8,128)(2,1)} %get-tuple-element.109.refs_0_.refs_5_), channel_id=1, source_target_pairs={{0,2},{1,3},{2,0},{3,1},{4,6},{5,7},{6,4},{7,5},{8,10},{9,11},{10,... | collective-permute-start | bytes 786440 | tf_op jit(solution)/shard_map/ppermute | solution.py:610
  39.5 10.5 %collective-permute-start.19 = (bf16[256,512]{1,0:T(8,128)(2,1)S(1)}, bf16[256,512]{1,0:T(8,128)(2,1)}, u32[]{:S(2)}, u32[]{:S(2)}) collective-permute-start(bf16[256,512]{1,0:T(8,128)(2,1)S(1)} %get-tuple-element.106.refs_1_.refs_6_), channel_id=1, source_target_pairs={{0,4},{1,5},{2,6},{3,7},{4,0},{5,1},{6,2},{7,3},{8,12},{9,13},{10,... | collective-permute-start | bytes 786440 | tf_op jit(solution)/shard_map/ppermute | solution.py:610
  46.5 9.0 %collective-permute-start.15 = (bf16[256,512]{1,0:T(8,128)(2,1)S(1)}, bf16[256,512]{1,0:T(8,128)(2,1)S(1)}, u32[]{:S(2)}, u32[]{:S(2)}) collective-permute-start(bf16[256,512]{1,0:T(8,128)(2,1)S(1)} %get-tuple-element.106.refs_1_.refs_6_), channel_id=1, source_target_pairs={{0,2},{1,3},{2,0},{3,1},{4,6},{5,7},{6,4},{7,5},{8,10},{9,11},{10,... | collective-permute-start | bytes 786440 | tf_op jit(solution)/shard_map/ppermute | solution.py:610
  48.0 9.0 %collective-permute-start.18 = (bf16[256,512]{1,0:T(8,128)(2,1)}, bf16[256,512]{1,0:T(8,128)(2,1)}, u32[]{:S(2)}, u32[]{:S(2)}) collective-permute-start(bf16[256,512]{1,0:T(8,128)(2,1)} %get-tuple-element.109.refs_0_.refs_5_), channel_id=1, source_target_pairs={{0,4},{1,5},{2,6},{3,7},{4,0},{5,1},{6,2},{7,3},{8,12},{9,13},{10,... | collective-permute-start | bytes 786440 | tf_op jit(solution)/shard_map/ppermute | solution.py:610
  49.0 17.6 %collective-permute-start.22 = (bf16[256,512]{1,0:T(8,128)(2,1)}, bf16[256,512]{1,0:T(8,128)(2,1)}, u32[]{:S(2)}, u32[]{:S(2)}) collective-permute-start(bf16[256,512]{1,0:T(8,128)(2,1)} %collective-permute-done.14.refs_4_.refs_9_), channel_id=1, source_target_pairs={{0,4},{1,5},{2,6},{3,7},{4,0},{5,1},{6,2},{7,3},{8,12},{9,13},{10,... | collective-permute-start | bytes 786440 | tf_op jit(solution)/shard_map/ppermute | solution.py:610
  50.1 17.2 %collective-permute-start.23 = (bf16[256,512]{1,0:T(8,128)(2,1)}, bf16[256,512]{1,0:T(8,128)(2,1)}, u32[]{:S(2)}, u32[]{:S(2)}) collective-permute-start(bf16[256,512]{1,0:T(8,128)(2,1)} %collective-permute-done.19.refs_9_.refs_14_), channel_id=1, source_target_pairs={{0,2},{1,3},{2,0},{3,1},{4,6},{5,7},{6,4},{7,5},{8,10},{9,11},{10,... | collective-permute-start | bytes 786440 | tf_op jit(solution)/shard_map/ppermute | solution.py:610
  52.7 15.9 %collective-permute-start.12 = (bf16[256,512]{1,0:T(8,128)(2,1)}, bf16[256,512]{1,0:T(8,128)(2,1)}, u32[]{:S(2)}, u32[]{:S(2)}) collective-permute-start(bf16[256,512]{1,0:T(8,128)(2,1)} %get-tuple-element.109.refs_0_.refs_5_), channel_id=1, source_target_pairs={{0,1},{1,0},{2,3},{3,2},{4,5},{5,4},{6,7},{7,6},{8,9},{9,8},{10,11... | collective-permute-start | bytes 786440 | tf_op jit(solution)/shard_map/ppermute | solution.py:610
  56.3 12.7 %collective-permute-start.13 = (bf16[256,512]{1,0:T(8,128)(2,1)S(1)}, bf16[256,512]{1,0:T(8,128)(2,1)}, u32[]{:S(2)}, u32[]{:S(2)}) collective-permute-start(bf16[256,512]{1,0:T(8,128)(2,1)S(1)} %get-tuple-element.106.refs_1_.refs_6_), channel_id=1, source_target_pairs={{0,1},{1,0},{2,3},{3,2},{4,5},{5,4},{6,7},{7,6},{8,9},{9,8},{10,11... | collective-permute-start | bytes 786440 | tf_op jit(solution)/shard_map/ppermute | solution.py:610
  56.9 12.2 %collective-permute-start.16 = (bf16[256,512]{1,0:T(8,128)(2,1)}, bf16[256,512]{1,0:T(8,128)(2,1)}, u32[]{:S(2)}, u32[]{:S(2)}) collective-permute-start(bf16[256,512]{1,0:T(8,128)(2,1)} %collective-permute-done.14.refs_4_.refs_9_), channel_id=1, source_target_pairs={{0,1},{1,0},{2,3},{3,2},{4,5},{5,4},{6,7},{7,6},{8,9},{9,8},{10,11... | collective-permute-start | bytes 786440 | tf_op jit(solution)/shard_map/ppermute | solution.py:610
  97.6 12.0 %collective-permute-start.31 = (bf16[512,384]{1,0:T(8,128)(2,1)S(1)}, bf16[512,384]{1,0:T(8,128)(2,1)S(1)}, u32[]{:S(2)}, u32[]{:S(2)}) collective-permute-start(bf16[512,384]{1,0:T(8,128)(2,1)S(1)} %get-tuple-element.128), channel_id=1, source_target_pairs={{0,2},{1,3},{2,0},{3,1},{4,6},{5,7},{6,4},{7,5},{8,10},{9,11},{10,... | collective-permute-start | bytes 1179656 | tf_op jit(solution)/shard_map/ppermute | solution.py:610
  98.7 14.9 %collective-permute-start.32 = (bf16[512,384]{1,0:T(8,128)(2,1)S(1)}, bf16[512,384]{1,0:T(8,128)(2,1)S(1)}, u32[]{:S(2)}, u32[]{:S(2)}) collective-permute-start(bf16[512,384]{1,0:T(8,128)(2,1)S(1)} %get-tuple-element.133), channel_id=1, source_target_pairs={{0,4},{1,5},{2,6},{3,7},{4,0},{5,1},{6,2},{7,3},{8,12},{9,13},{10,... | collective-permute-start | bytes 1179656 | tf_op jit(solution)/shard_map/ppermute | solution.py:610
  104.1 19.5 %collective-permute-start.35 = (bf16[512,384]{1,0:T(8,128)(2,1)}, bf16[512,384]{1,0:T(8,128)(2,1)}, u32[]{:S(2)}, u32[]{:S(2)}) collective-permute-start(bf16[512,384]{1,0:T(8,128)(2,1)} %get-tuple-element.130), channel_id=1, source_target_pairs={{0,2},{1,3},{2,0},{3,1},{4,6},{5,7},{6,4},{7,5},{8,10},{9,11},{10,... | collective-permute-start | bytes 1179656 | tf_op jit(solution)/shard_map/ppermute | solution.py:610
  110.5 14.3 %collective-permute-start.41 = (bf16[512,384]{1,0:T(8,128)(2,1)}, bf16[512,384]{1,0:T(8,128)(2,1)}, u32[]{:S(2)}, u32[]{:S(2)}) collective-permute-start(bf16[512,384]{1,0:T(8,128)(2,1)} %add_convert_fusion.4), channel_id=1, source_target_pairs={{0,4},{1,5},{2,6},{3,7},{4,0},{5,1},{6,2},{7,3},{8,12},{9,13},{10,... | collective-permute-start | bytes 1179656 | tf_op jit(solution)/shard_map/ppermute | solution.py:610
  111.2 11.5 %collective-permute-start.30 = (bf16[32,1920]{1,0:T(8,128)(2,1)S(1)}, bf16[32,1920]{1,0:T(8,128)(2,1)S(1)}, u32[]{:S(2)}, u32[]{:S(2)}) collective-permute-start(bf16[32,1920]{1,0:T(8,128)(2,1)S(1)} %get-tuple-element.141.refs_0_), channel_id=1, source_target_pairs={{0,2},{1,3},{2,0},{3,1},{4,6},{5,7},{6,4},{7,5},{8,10},{9,11},{10,... | collective-permute-start | bytes 368648 | tf_op jit(solution)/shard_map/ppermute | solution.py:610
  113.3 18.1 %collective-permute-start.36 = (bf16[512,384]{1,0:T(8,128)(2,1)}, bf16[512,384]{1,0:T(8,128)(2,1)}, u32[]{:S(2)}, u32[]{:S(2)}) collective-permute-start(bf16[512,384]{1,0:T(8,128)(2,1)} %get-tuple-element.139), channel_id=1, source_target_pairs={{0,4},{1,5},{2,6},{3,7},{4,0},{5,1},{6,2},{7,3},{8,12},{9,13},{10,... | collective-permute-start | bytes 1179656 | tf_op jit(solution)/shard_map/ppermute | solution.py:610
  114.4 16.9 %collective-permute-start.42 = (bf16[512,384]{1,0:T(8,128)(2,1)}, bf16[512,384]{1,0:T(8,128)(2,1)}, u32[]{:S(2)}, u32[]{:S(2)}) collective-permute-start(bf16[512,384]{1,0:T(8,128)(2,1)} %add_convert_fusion.2), channel_id=1, source_target_pairs={{0,2},{1,3},{2,0},{3,1},{4,6},{5,7},{6,4},{7,5},{8,10},{9,11},{10,... | collective-permute-start | bytes 1179656 | tf_op jit(solution)/shard_map/ppermute | solution.py:610
  122.7 10.0 %collective-permute-start.33 = (bf16[32,1920]{1,0:T(8,128)(2,1)S(1)}, bf16[32,1920]{1,0:T(8,128)(2,1)S(1)}, u32[]{:S(2)}, u32[]{:S(2)}) collective-permute-start(bf16[32,1920]{1,0:T(8,128)(2,1)S(1)} %get-tuple-element.141.refs_0_), channel_id=1, source_target_pairs={{0,4},{1,5},{2,6},{3,7},{4,0},{5,1},{6,2},{7,3},{8,12},{9,13},{10,... | collective-permute-start | bytes 368648 | tf_op jit(solution)/shard_map/ppermute | solution.py:610
  123.5 10.5 %collective-permute-start.34 = (bf16[32,1920]{1,0:T(8,128)(2,1)S(1)}, bf16[32,1920]{1,0:T(8,128)(2,1)S(1)}, u32[]{:S(2)}, u32[]{:S(2)}) collective-permute-start(bf16[32,1920]{1,0:T(8,128)(2,1)S(1)} %collective-permute-done.30.refs_1_), channel_id=1, source_target_pairs={{0,4},{1,5},{2,6},{3,7},{4,0},{5,1},{6,2},{7,3},{8,12},{9,13},{10,... | collective-permute-start | bytes 368648 | tf_op jit(solution)/shard_map/ppermute | solution.py:610
  136.4 12.1 %collective-permute-start.46 = (bf16[256,384]{1,0:T(8,128)(2,1)S(1)}, bf16[256,384]{1,0:T(8,128)(2,1)S(1)}, u32[]{:S(2)}, u32[]{:S(2)}) collective-permute-start(bf16[256,384]{1,0:T(8,128)(2,1)S(1)} %get-tuple-element.150), channel_id=1, source_target_pairs={{0,24},{8,16},{16,8},{24,0},{1,25},{9,17},{17,9},{25,1},{2,26},{10... | collective-permute-start | bytes 589832 | tf_op jit(solution)/shard_map/ppermute | solution.py:613
  139.9 24.2 %collective-permute-start.45 = (bf16[256,384]{1,0:T(8,128)(2,1)S(1)}, bf16[256,384]{1,0:T(8,128)(2,1)S(1)}, u32[]{:S(2)}, u32[]{:S(2)}) collective-permute-start(bf16[256,384]{1,0:T(8,128)(2,1)S(1)} %get-tuple-element.151), channel_id=1, source_target_pairs={{0,16},{8,24},{16,0},{24,8},{1,17},{9,25},{17,1},{25,9},{2,18},{10... | collective-permute-start | bytes 589832 | tf_op jit(solution)/shard_map/ppermute | solution.py:613
  139.9 24.2 %collective-permute-start.44 = (bf16[256,384]{1,0:T(8,128)(2,1)S(1)}, bf16[256,384]{1,0:T(8,128)(2,1)S(1)}, u32[]{:S(2)}, u32[]{:S(2)}) collective-permute-start(bf16[256,384]{1,0:T(8,128)(2,1)S(1)} %get-tuple-element.149), channel_id=1, source_target_pairs={{0,8},{8,0},{16,24},{24,16},{1,9},{9,1},{17,25},{25,17},{2,10},{10... | collective-permute-start | bytes 589832 | tf_op jit(solution)/shard_map/ppermute | solution.py:613
  142.0 23.0 %collective-permute-start.38 = (bf16[144,512]{1,0:T(8,128)(2,1)S(1)}, bf16[144,512]{1,0:T(8,128)(2,1)S(1)}, u32[]{:S(2)}, u32[]{:S(2)}) collective-permute-start(bf16[144,512]{1,0:T(8,128)(2,1)S(1)} %get-tuple-element.156), channel_id=1, source_target_pairs={{0,8},{8,0},{16,24},{24,16},{1,9},{9,1},{17,25},{25,17},{2,10},{10... | collective-permute-start | bytes 442376 | tf_op jit(solution)/shard_map/ppermute | solution.py:613
  143.1 24.1 %collective-permute-start.39 = (bf16[144,512]{1,0:T(8,128)(2,1)S(1)}, bf16[144,512]{1,0:T(8,128)(2,1)S(1)}, u32[]{:S(2)}, u32[]{:S(2)}) collective-permute-start(bf16[144,512]{1,0:T(8,128)(2,1)S(1)} %get-tuple-element.155), channel_id=1, source_target_pairs={{0,16},{8,24},{16,0},{24,8},{1,17},{9,25},{17,1},{25,9},{2,18},{10... | collective-permute-start | bytes 442376 | tf_op jit(solution)/shard_map/ppermute | solution.py:613
  148.6 19.9 %collective-permute-start.40 = (bf16[144,512]{1,0:T(8,128)(2,1)S(1)}, bf16[144,512]{1,0:T(8,128)(2,1)S(1)}, u32[]{:S(2)}, u32[]{:S(2)}) collective-permute-start(bf16[144,512]{1,0:T(8,128)(2,1)S(1)} %get-tuple-element.154), channel_id=1, source_target_pairs={{0,24},{8,16},{16,8},{24,0},{1,25},{9,17},{17,9},{25,1},{2,26},{10... | collective-permute-start | bytes 442376 | tf_op jit(solution)/shard_map/ppermute | solution.py:613
  (51 other events, 235.3 us)

commit v5 on v4

--- a/solution.py
+++ b/solution.py
@@ -18,12 +18,12 @@
 epsilon = 1e-05
 loss_scale = 64.0
 scale = HEAD_DIM ** (-0.5)
-VMEM = 20 * 1024 * 1024
-SMALL = 20 * 1024 * 1024
+VMEM = 16 * 1024 * 1024
+SMALL = 10 * 1024 * 1024
 
 
 def cost(micros):
-    return pl.CostEstimate(flops=int(micros * 1e8), bytes_accessed=int(micros * 3.5e6), transcendentals=0)
+    return pl.CostEstimate(flops=int(micros * 5e8), bytes_accessed=int(micros * 3.5e6), transcendentals=0)
 
 BF16 = jnp.bfloat16
 F32 = jnp.float32
@@ -128,62 +128,66 @@
     return jnp.concatenate([ref[rows, at : at + WIDE], ref[rows, at + WIDE : at + GROUP]], 0)
 
 
-def project(refs, pieces, whole):
-    blocks, refs = refs[:pieces], refs[pieces:]
-    weights, refs = refs[: 2 * pieces], refs[2 * pieces :]
-    join(weights, whole)
-    rows = blocks[0][...]
-    if pieces > 1:
-        rows = jnp.concatenate([rows] + [block[...] for block in blocks[1:]], 1)
-    return mm(rows, whole[...]), refs
-
-
-def partial_kernel(pieces, before, where_ref, *refs):
-    refs, whole = refs[:-1], refs[-1]
-    product, refs = project(refs, pieces, whole)
-    refs[-1][...] = product + refs[0][...] if before else product
-
-
-def forward_kernel(pieces, groups, where_ref, *refs):
-    refs, whole = refs[:-1], refs[-1]
-    projected, refs = project(refs, pieces, whole)
-    before_ref, projected_ref, probs_ref, sum_ref = refs
-    projected = projected + before_ref[...]
-    projected_ref[...] = projected.astype(BF16)
+def product_of(chip, rows_ref, rows, shifts, weights):
+    depth = weights[0].shape[0]
+    out = []
+    for part in range(2):
+        total = None
+        for k, s in enumerate(shifts):
+            start = pl.multiple_of((chip ^ s) * depth, depth)
+            x = mm(rows_ref[rows, pl.ds(start, depth)], weights[2 * k + part][...])
+            total = x if total is None else total + x
+        out.append(total)
+    return out
+
+
+def partial_kernel(shifts, step, where_ref, rows_ref, before_ref, *refs):
+    weights, out_ref = refs[:-1], refs[-1]
+    part = weights[0].shape[1]
+    for i in range(rows_ref.shape[0] // step):
+        rows = slice(i * step, (i + 1) * step)
+        a, b = product_of(where_ref[0], rows_ref, rows, shifts, weights)
+        out_ref[rows, :part] = a + before_ref[rows, :part]
+        out_ref[rows, part:] = b + before_ref[rows, part:]
+
+
+def forward_kernel(shifts, groups, batch, where_ref, rows_ref, before_ref, *refs):
+    weights, refs = refs[: 2 * len(shifts)], refs[2 * len(shifts) :]
+    projected_ref, probs_ref, sum_ref = refs
+    part = weights[0].shape[1]
     ones = ones_block(1)
     width_q = groups * GROUP
     width_k = groups * HEAD_DIM
-    count = projected_ref.shape[0] // PASSAGE_LEN
-    spans = [slice(i * PASSAGE_LEN, (i + 1) * PASSAGE_LEN) for i in range(count)]
-    keys = [diagonals(projected_ref[r, width_q : width_q + width_k], scale) for r in spans]
-    values = [diagonals(projected_ref[r, width_q + width_k :], 1.0) for r in spans]
-    for g in range(groups):
-        scores = jnp.concatenate(
-            [mm(stacked(projected_ref, r, g), keys[i][g], ((1,), (1,))) for i, r in enumerate(spans)],
-            0,
-        )
-        expo = jnp.exp(scores - segment_max(scores))
-        total = mm(expo.astype(BF16), ones)
-        probs = (expo / total).astype(BF16)
-        probs_ref[0, g] = probs
-        for i in range(count):
-            attended = mm(probs[i * WIDE : (i + 1) * WIDE], values[i][g])
-            attended = attended.astype(BF16).astype(F32)
-            for j in range(2):
-                at = g * GROUP + j * WIDE
-                sum_ref[0, i : i + 1, at : at + WIDE] = jnp.sum(
-                    attended[j * HEAD_DIM : (j + 1) * HEAD_DIM], 0, keepdims=True
-                )
-
-
-def join(weights, whole):
-    @pl.when(pl.program_id(0) == 0)
-    def _():
-        depth, part = weights[0].shape
-        for k in range(len(weights) // 2):
-            rows = slice(k * depth, (k + 1) * depth)
-            whole[rows, :part] = weights[2 * k][...]
-            whole[rows, part:] = weights[2 * k + 1][...]
+    step = batch * PASSAGE_LEN
+    for n in range(rows_ref.shape[0] // step):
+        rows = slice(n * step, (n + 1) * step)
+        a, b = product_of(where_ref[0], rows_ref, rows, shifts, weights)
+        projected_ref[rows, :part] = (a + before_ref[rows, :part]).astype(BF16)
+        projected_ref[rows, part:] = (b + before_ref[rows, part:]).astype(BF16)
+        spans = [
+            slice(n * step + i * PASSAGE_LEN, n * step + (i + 1) * PASSAGE_LEN)
+            for i in range(batch)
+        ]
+        keys = [diagonals(projected_ref[r, width_q : width_q + width_k], scale) for r in spans]
+        values = [diagonals(projected_ref[r, width_q + width_k :], 1.0) for r in spans]
+        for g in range(groups):
+            scores = [
+                mm(stacked(projected_ref, r, g), keys[i][g], ((1,), (1,)))
+                for i, r in enumerate(spans)
+            ]
+            scores = jnp.concatenate(scores, 0)
+            expo = jnp.exp(scores - segment_max(scores))
+            total = mm(expo.astype(BF16), ones)
+            probs = (expo / total).astype(BF16)
+            probs_ref[n, g] = probs
+            for i in range(batch):
+                attended = mm(probs[i * WIDE : (i + 1) * WIDE], values[i][g])
+                attended = attended.astype(BF16).astype(F32)
+                for j in range(2):
+                    at = g * GROUP + j * WIDE
+                    sum_ref[n, i : i + 1, at : at + WIDE] = jnp.sum(
+                        attended[j * HEAD_DIM : (j + 1) * HEAD_DIM], 0, keepdims=True
+                    )
 
 
 def row_step(total, batch):
@@ -191,77 +195,63 @@
     return batch, batch * PASSAGE_LEN
 
 
-def block_of(step, depth, s):
-    return pl.BlockSpec((step, depth), lambda i, w: (i, w[0] ^ s))
+def local_call(kernel, name, micros, where, operands, out_shape):
+    vmem = pl.BlockSpec(memory_space=pltpu.VMEM)
+    return pl.pallas_call(
+        kernel,
+        in_specs=[pl.BlockSpec(memory_space=pltpu.SMEM)] + [vmem] * len(operands),
+        out_specs=jax.tree.map(lambda _: vmem, out_shape),
+        out_shape=out_shape,
+        compiler_params=pltpu.CompilerParams(vmem_limit_bytes=VMEM),
+        cost_estimate=cost(micros),
+        name=name,
+    )(where, *operands)
 
 
 def partial_project(where, rows, weights, before):
-    total, width = rows.shape
-    depth, part = next(iter(weights.values()))[0].shape
-    _, step = row_step(total, BATCH)
-    pieces = len(weights)
-    flat = [x for s in weights for x in weights[s]]
-    out = pl.BlockSpec((step, 2 * part), lambda i, w: (i, 0))
-    return pl.pallas_call(
-        functools.partial(partial_kernel, pieces, True),
-        grid_spec=pltpu.PrefetchScalarGridSpec(
-            num_scalar_prefetch=1,
-            grid=(total // step,),
-            in_specs=[block_of(step, depth, s) for s in weights]
-            + [pl.BlockSpec(x.shape, lambda i, w: (0, 0)) for x in flat]
-            + [out],
-            out_specs=out,
-            scratch_shapes=[pltpu.VMEM((pieces * depth, 2 * part), BF16)],
-        ),
-        out_shape=pltpu.VMEM((total, 2 * part), F32),
-        compiler_params=params(),
-        cost_estimate=cost(4.5),
-        name="project_more",
-    )(where, *held(pltpu.VMEM, *([rows] * pieces)), *flat, *held(pltpu.VMEM, before))
+    _, step = row_step(rows.shape[0], BATCH)
+    return local_call(
+        functools.partial(partial_kernel, tuple(weights), step),
+        "project_more",
+        4.5,
+        where,
+        [rows, before] + [x for s in weights for x in weights[s]],
+        jax.ShapeDtypeStruct(before.shape, F32),
+    )
 
 
 def forward(where, rows, weights, groups, before):
-    total, width = rows.shape
-    pieces = len(weights)
-    flat = [x for s in weights for x in weights[s]]
-    depth, part = flat[0].shape
-    out_width = 2 * part
+    total = rows.shape[0]
     batch, step = row_step(total, BATCH)
     steps = total // step
     heads = groups * GROUP
-    return pl.pallas_call(
-        functools.partial(forward_kernel, pieces, groups),
-        grid_spec=pltpu.PrefetchScalarGridSpec(
-            num_scalar_prefetch=1,
-            grid=(steps,),
-            in_specs=[block_of(step, depth, s) for s in weights]
-            + [pl.BlockSpec(x.shape, lambda i, w: (0, 0)) for x in flat]
-            + [pl.BlockSpec((step, out_width), lambda i, w: (i, 0))],
-            out_specs=[
-                pl.BlockSpec((step, out_width), lambda i, w: (i, 0)),
-                pl.BlockSpec((1, groups, batch * WIDE, WIDE), lambda i, w: (i, 0, 0, 0)),
-                pl.BlockSpec((1, batch, heads), lambda i, w: (i, 0, 0)),
-            ],
-            scratch_shapes=[pltpu.VMEM((pieces * depth, out_width), BF16)],
-        ),
-        out_shape=[
-            jax.ShapeDtypeStruct((total, out_width), BF16),
+    return local_call(
+        functools.partial(forward_kernel, tuple(weights), groups, batch),
+        "project_attend",
+        6.5,
+        where,
+        [rows, before] + [x for s in weights for x in weights[s]],
+        [
+            jax.ShapeDtypeStruct(before.shape, BF16),
             jax.ShapeDtypeStruct((steps, groups, batch * WIDE, WIDE), BF16),
             jax.ShapeDtypeStruct((steps, batch, heads), F32),
         ],
-        compiler_params=params(),
-        cost_estimate=cost(6.5),
-        name="project_attend",
-    )(where, *held(pltpu.VMEM, *([rows] * pieces)), *flat, *held(pltpu.VMEM, before))
-
-
-def backward_kernel(groups, probs_ref, projected_ref, d_ref, out_ref):
+    )
+
+
+def backward_kernel(groups, where_ref, probs_ref, projected_ref, d_ref, out_ref):
+    for n in range(probs_ref.shape[0]):
+        backward_step(groups, n, probs_ref, projected_ref, d_ref, out_ref)
+
+
+def backward_step(groups, n, probs_ref, projected_ref, d_ref, out_ref):
     low = low_lanes(HEAD_DIM)
     ones = ones_block(2)
     width_q = groups * GROUP
     width_k = groups * HEAD_DIM
-    count = projected_ref.shape[0] // PASSAGE_LEN
-    spans = [slice(i * PASSAGE_LEN, (i + 1) * PASSAGE_LEN) for i in range(count)]
+    count = d_ref.shape[1]
+    at = n * count
+    spans = [slice((at + i) * PASSAGE_LEN, (at + i + 1) * PASSAGE_LEN) for i in range(count)]
     keys = [diagonals(projected_ref[r, width_q : width_q + width_k], scale) for r in spans]
     values = [diagonals(projected_ref[r, width_q + width_k :], 1.0) for r in spans]
     down = ((0,), (0,))
@@ -273,11 +263,11 @@
         return kept + pltpu.roll(kept, HEAD_DIM, 1)
 
     for g in range(groups):
-        probs = probs_ref[0, g]
+        probs = probs_ref[n, g]
         d_rows = []
         for i in range(count):
             row = [
-                d_ref[0, i : i + 1, g * GROUP + j * WIDE : g * GROUP + (j + 1) * WIDE]
+                d_ref[n, i : i + 1, g * GROUP + j * WIDE : g * GROUP + (j + 1) * WIDE]
                 for j in range(2)
             ]
             d_rows.append(
@@ -307,26 +297,17 @@
         out_ref[r, width_q + width_k :] = jnp.where(low, *d_values[i]).astype(BF16)
 
 
-def backward(probs, projected, d_attended, groups):
-    total, out_width = projected.shape
+def backward(where, probs, projected, d_attended, groups):
     steps = probs.shape[0]
-    step = total // steps
-    batch = step // PASSAGE_LEN
-    heads = groups * GROUP
-    return pl.pallas_call(
+    batch = probs.shape[2] // WIDE
+    return local_call(
         functools.partial(backward_kernel, groups),
-        grid=(steps,),
-        in_specs=[
-            pl.BlockSpec((1,) + probs.shape[1:], lambda i: (i, 0, 0, 0)),
-            pl.BlockSpec((step, out_width), lambda i: (i, 0)),
-            pl.BlockSpec((1, batch, heads), lambda i: (i, 0, 0)),
-        ],
-        out_specs=pl.BlockSpec((step, out_width), lambda i: (i, 0)),
-        out_shape=pltpu.VMEM((total, out_width), BF16),
-        compiler_params=params(),
-        cost_estimate=cost(3.4),
-        name="attend_back",
-    )(probs, projected, d_attended.reshape(steps, batch, heads))
+        "attend_back",
+        3.4,
+        where,
+        [probs, projected, d_attended.reshape(steps, batch, groups * GROUP)],
+        jax.ShapeDtypeStruct(projected.shape, BF16),
+    )
 
 
 def score_kernel(chips, where_ref, own_ref, sib_ref, own_far_ref, sib_far_ref, sum_ref, sib_sum_ref,
@@ -393,10 +374,10 @@
 
 
 def list_kernel(blocks, chips, passages, where_ref, place_ref, bounds_ref, unit_ref, inverse_ref,
-                attn_ref, final_ref, ws_ref, *refs):
+                final_ref, ws_ref, *refs):
     scores = [ref[...] for ref in refs[:blocks]]
     pieces, refs = refs[blocks : blocks + 4 * chips], refs[blocks + 4 * chips :]
-    d_att_ref, payload_ref, back_ref = refs
+    d_att_ref, d_rows_ref, loss_ref, back_ref = refs
     chip, core = where_ref[0], where_ref[1]
     pair = 2 * passages
     lanes = bounds_ref.shape[1]
@@ -450,19 +431,12 @@
     back = back_ref[...]
     half = back.shape[1] // 2
     d_att_ref[...] = jnp.where(core == 0, back[:, :half], back[:, half:])
-    attn = attn_ref[...].astype(F32)
-    columns = [jnp.where(core == 0, attn[:, :half], attn[:, half:])]
-    columns += [x.astype(F32) for x in cut[:2]]
-    rest = jnp.broadcast_to(loss, (pair, 128))
-    for _ in range(3):
-        columns.append(rest.astype(BF16).astype(F32))
-        rest = rest - columns[-1]
-    columns = jnp.concatenate(columns, 1)
-    turned = jnp.concatenate([columns[passages:], columns[:passages]], 0)
-    payload_ref[...] = jnp.where(core == 0, columns, turned).astype(BF16)
-
-
-def list_pass(where, places, bounds, unit, inverse, attn, final_gain, w_score, scores, pieces,
+    loss_ref[...] = jnp.broadcast_to(loss, loss_ref.shape)
+    d_rows_ref[:, :part] = cut[0]
+    d_rows_ref[:, part:] = cut[1]
+
+
+def list_pass(where, places, bounds, unit, inverse, final_gain, w_score, scores, pieces,
               passages):
     count, width = unit.shape
     chips = len(pieces) // 4
@@ -471,18 +445,49 @@
     smem = pl.BlockSpec(memory_space=pltpu.SMEM)
     return pl.pallas_call(
         functools.partial(list_kernel, len(scores), chips, passages),
-        in_specs=[smem] * 2 + [vmem] * (6 + len(scores) + len(pieces)),
-        out_specs=[vmem] * 2,
+        in_specs=[smem] * 2 + [vmem] * (5 + len(scores) + len(pieces)),
+        out_specs=[vmem] * 3,
         out_shape=[
             jax.ShapeDtypeStruct((count, inner // 2), F32),
-            jax.ShapeDtypeStruct((count, (inner + width) // 2 + 3 * 128), BF16),
+            jax.ShapeDtypeStruct((count, width // 2), BF16),
+            jax.ShapeDtypeStruct((8, 128), F32),
         ],
         scratch_shapes=[pltpu.VMEM((count, inner), F32)],
         compiler_params=pltpu.CompilerParams(vmem_limit_bytes=SMALL),
         cost_estimate=cost(2.5),
         name="list_grad",
-    )(where, places, bounds, unit, inverse, attn, final_gain[None], w_score[None], *scores,
+    )(where, places, bounds, unit, inverse, final_gain[None], w_score[None], *scores,
       *pieces)
+
+
+def payload_kernel(passages, where_ref, attn_ref, d_rows_ref, loss_ref, out_ref):
+    core = where_ref[1]
+    attn = attn_ref[...].astype(F32)
+    half = attn.shape[1] // 2
+    columns = [jnp.where(core == 0, attn[:, :half], attn[:, half:]), d_rows_ref[...].astype(F32)]
+    rest = jnp.broadcast_to(loss_ref[:1], (attn.shape[0], 128))
+    for _ in range(3):
+        columns.append(rest.astype(BF16).astype(F32))
+        rest = rest - columns[-1]
+    columns = jnp.concatenate(columns, 1)
+    turned = jnp.concatenate([columns[passages:], columns[:passages]], 0)
+    out_ref[...] = jnp.where(core == 0, columns, turned).astype(BF16)
+
+
+def payload_pass(where, attn, d_rows, loss):
+    count = attn.shape[0]
+    vmem = pl.BlockSpec(memory_space=pltpu.VMEM)
+    return pl.pallas_call(
+        functools.partial(payload_kernel, count // 2),
+        in_specs=[pl.BlockSpec(memory_space=pltpu.SMEM)] + [vmem] * 3,
+        out_specs=vmem,
+        out_shape=jax.ShapeDtypeStruct(
+            (count, attn.shape[1] // 2 + d_rows.shape[1] + 3 * 128), BF16
+        ),
+        compiler_params=pltpu.CompilerParams(vmem_limit_bytes=SMALL),
+        cost_estimate=cost(1),
+        name="out_payload",
+    )(where, attn, d_rows, loss)
 
 
 EXTRA = 16
@@ -533,43 +538,30 @@
     )(where, left, *near, far)
 
 
-def grad_kernel(where_ref, own_ref, sib_ref, d_own_ref, d_sib_ref, a_ref, b_ref):
+def grad_kernel(blocks, where_ref, own_ref, sib_ref, d_own_ref, d_sib_ref, *out):
+    depth, part = out[0].shape
+    tile = min(depth, 256)
     down = ((0,), (0,))
-    out = mm(own_ref[...], d_own_ref[...], down) + mm(sib_ref[...], d_sib_ref[...], down)
-    out = out.astype(BF16)
-    a_ref[...] = out[:, : a_ref.shape[1]]
-    b_ref[...] = out[:, a_ref.shape[1] :]
-
-
-def grad_block(where, s, own, sib, d_own, d_sib, depth):
-    rows = own.shape[0]
-    width = d_own.shape[1]
-    tile = min(depth, 256)
-    tiles = depth // tile
-    part = width // 2
-
-    def lhs(i, w):
-        return (0, (w[0] ^ s) * tiles + i)
-
-    whole = lambda i, w: (0, 0)
-    return pl.pallas_call(
-        grad_kernel,
-        grid_spec=pltpu.PrefetchScalarGridSpec(
-            num_scalar_prefetch=1,
-            grid=(tiles,),
-            in_specs=[
-                pl.BlockSpec((rows, tile), lhs),
-                pl.BlockSpec((rows, tile), lhs),
-                pl.BlockSpec((rows, width), whole),
-                pl.BlockSpec((rows, width), whole),
-            ],
-            out_specs=[pl.BlockSpec((tile, part), lambda i, w: (i, 0))] * 2,
-        ),
-        out_shape=[jax.ShapeDtypeStruct((depth, part), BF16)] * 2,
-        compiler_params=params(),
-        cost_estimate=cost(3.8),
-        name="grad_rows",
-    )(where, *held(pltpu.VMEM, own, sib), *held(pltpu.VMEM, d_own, d_sib))
+    for n, s in enumerate(blocks):
+        for i in range(depth // tile):
+            start = pl.multiple_of((where_ref[0] ^ s) * depth + i * tile, tile)
+            cols = pl.ds(start, tile)
+            total = mm(own_ref[:, cols], d_own_ref[...], down)
+            total = (total + mm(sib_ref[:, cols], d_sib_ref[...], down)).astype(BF16)
+            out[2 * n][i * tile : (i + 1) * tile] = total[:, :part]
+            out[2 * n + 1][i * tile : (i + 1) * tile] = total[:, part:]
+
+
+def grad_blocks(where, blocks, own, sib, d_own, d_sib, depth):
+    part = d_own.shape[1] // 2
+    return local_call(
+        functools.partial(grad_kernel, tuple(blocks)),
+        "grad_rows",
+        2.5 * len(blocks),
+        where,
+        [own, sib, d_own, d_sib],
+        [jax.ShapeDtypeStruct((depth, part), BF16)] * (2 * len(blocks)),
+    )
 
 
 def pick_kernel(starts, sizes, where_ref, mine_ref, come_ref, a_ref, b_ref):
@@ -632,14 +624,13 @@
     def after(value, *others):
         return lax.optimization_barrier((value, others))[0]
 
-    def gathered(value, order, gates=()):
+    def gathered(value, order, near=(), far=()):
         have = {0: value}
-        for k, bit in enumerate(order):
-            near, far = gates[k - 1] if 0 < k <= len(gates) else (None, None)
-            ready = {
-                s: after(part, far if s else near) if k and gates else part
-                for s, part in have.items()
-            }
+        for bit in order:
+            first = [part for s, part in have.items() if s]
+            ready = dict(have)
+            if first:
+                ready = {s: after(part, far if s else near, first) for s, part in have.items()}
             have.update({s ^ (bit >> 1): across(part, bit) for s, part in ready.items()})
         return have
 
@@ -681,37 +672,7 @@
         hidden_sib = across(after(hidden, come), 1)
 
         normal, sums, before_own = norm(where, hidden, norm_gain, (pair_a, pair_b))
-        normal_sib, sums_sib, before_sib = norm(
-            where, after(hidden_sib, before_own), norm_gain, (pair_a, pair_b)
-        )
-        gates = ((before_own, before_sib),) * (len(bits) - 1)
-        part_a = gathered(pair_a, bits, gates)
-        part_b = gathered(pair_b, bits[::-1], gates)
-        chips = n_fsdp // 2
-        last = max(bin(s).count("1") for s in range(chips))
-        weights = [{}, {}, {}]
-        for s in range(chips):
-            ones = bin(s).count("1")
-            weights[2 if ones == last else 1 if ones else 0][s] = (part_a[s], part_b[s])
-
-        cols = w_out.shape[1] // 2
-        both = ordered(w_out, out_come, 0)
-        out_pair = jnp.where(first_core, both[:, :cols], both[:, cols:])
-        prior, labels, lengths, out_pair = after((prior, labels, lengths, out_pair), before_sib)
-        if weights[1]:
-            normal_first = after(normal, before_sib)
-            before_own = partial_project(where, normal_first, weights[1], before_own)
-            before_sib = partial_project(
-                where, after(normal_sib, before_own), weights[1], before_sib
-            )
-            out_pair = after(out_pair, before_sib)
-        before_own, before_sib, weights[2] = after((before_own, before_sib, weights[2]), before_sib)
-        proj_sib, probs_sib, attn_sib = forward(where, normal_sib, weights[2], groups, before_sib)
-        attn_sib = attn_sib.reshape(passages, -1)
-        attn_sib_other = across(attn_sib, 1)
-        gates = ((attn_sib, attn_sib),) * (len(bits) - 1)
-        out_a = gathered(out_pair[:, : cols // 2], bits, gates)
-        out_b = gathered(out_pair[:, cols // 2 :], bits[::-1], gates)
+        prior, labels, lengths, out_come = after((prior, labels, lengths, out_come), before_own)
         lanes = -(-lengths.shape[0] // 128) * 128
         label_weight = jnp.exp(labels.astype(F32))
         small = jnp.concatenate(
@@ -729,14 +690,47 @@
             jnp.pad(lengths, (0, lanes - lengths.shape[0]))[None], (8, lanes)
         )
 
-        normal_last = after(normal, probs_sib, places, bounds, small_sib)
+        cols = w_out.shape[1] // 2
+        both = ordered(w_out, out_come, 0)
+        out_pair = jnp.where(first_core, both[:, :cols], both[:, cols:])
+        normal_sib, sums_sib, before_sib = norm(
+            where,
+            after(hidden_sib, before_own, places, bounds, small_sib, out_pair),
+            norm_gain,
+            (pair_a, pair_b),
+        )
+        part_a = gathered(pair_a, bits, far=before_own)
+        part_b = gathered(pair_b, bits[::-1], far=before_own)
+        chips = n_fsdp // 2
+        last = max(bin(s).count("1") for s in range(chips))
+        weights = [{}, {}, {}]
+        for s in range(chips):
+            ones = bin(s).count("1")
+            weights[2 if ones == last else 1 if ones else 0][s] = (part_a[s], part_b[s])
+
+        out_pair = after(out_pair, weights[1], before_sib)
+        if weights[1]:
+            normal_first = after(normal, before_sib)
+            before_own = partial_project(where, normal_first, weights[1], before_own)
+            before_sib = partial_project(
+                where, after(normal_sib, before_own), weights[1], before_sib
+            )
+        before_own, before_sib, weights[2] = after(
+            (before_own, before_sib, weights[2]), before_sib
+        )
+        proj_sib, probs_sib, attn_sib = forward(where, normal_sib, weights[2], groups, before_sib)
+        attn_sib = attn_sib.reshape(passages, -1)
+        attn_sib_other = across(attn_sib, 1)
+        normal_last = after(normal, probs_sib)
         proj_own, probs_own, attn_own = forward(where, normal_last, weights[2], groups, before_own)
         attn_own = attn_own.reshape(passages, -1)
         attn_own_other = across(attn_own, 1)
+        out_a = gathered(out_pair[:, : cols // 2], bits, before_sib, before_sib)
+        out_b = gathered(out_pair[:, cols // 2 :], bits[::-1], before_sib, before_sib)
         pieces = []
         for s in range(chips):
-            gate = probs_sib if bin(s).count("1") == last else before_sib
             pieces += [out_a[s], out_b[s]]
+            gate = probs_own if bin(s).count("1") == last else ()
             pieces += [across(after(x, gate), 1) for x in (out_a[s], out_b[s])]
         unit, inverse, score, attn = score_pass(
             where,
@@ -749,44 +743,59 @@
         )
         near = [neighbour(score, kind) for kind in (0, 2)]
         scores = [score] + near + [across(x, 1) for x in near]
-        d_attended, payload = list_pass(
-            where, places, bounds, unit, inverse, attn, final_gain, w_score, scores, pieces,
-            passages,
+        d_attended, d_rows, loss_part = list_pass(
+            where, places, bounds, unit, inverse, final_gain, w_score, scores, pieces, passages
         )
 
-        d_own = backward(probs_own, proj_own, d_attended[:passages], groups)
+        d_own = backward(where, probs_own, proj_own, d_attended[:passages], groups)
+        payload = payload_pass(where, attn, d_rows, loss_part)
         d_sib = backward(
-            after(probs_sib, d_own), proj_sib, d_attended[passages:], groups
+            where, after(probs_sib, d_own), proj_sib, d_attended[passages:], groups
         )
         depth = pair_a.shape[0]
-        parts_a, parts_b, come_a, come_b = {}, {}, {}, {}
         flag_a, flag_b = bits[0] >> 1, bits[-1] >> 1
-        before = d_sib
-        for s in sorted(range(chips), key=lambda s: (-bin(s).count("1"), s)):
-            gate = (before, come_a, come_b) if s == 0 else before
-            parts_a[s], parts_b[s] = grad_block(
-                where, s, normal, normal_sib, d_own, after(d_sib, gate), depth
-            )
-            if s & flag_a and s & flag_b:
-                come_a[s ^ flag_a] = across(parts_a[s], bits[0])
-                come_b[s ^ flag_b] = across(parts_b[s], bits[-1])
-            before = parts_a[s]
-        first_a, first_b = dict(come_a), dict(come_b)
-        for s in range(chips):
-            if s & flag_a and s ^ flag_a not in first_a:
+        lead = [s for s in range(chips) if s & flag_a and s & flag_b]
+        rest = [s for s in range(1, chips) if s not in lead]
+
+        def grads(blocks, *gate):
+            out = grad_blocks(where, blocks, normal, normal_sib, d_own, after(d_sib, gate), depth)
+            return dict(zip(blocks, out[0::2])), dict(zip(blocks, out[1::2]))
+
+        parts_a, parts_b = grads(lead)
+        first_a = {s ^ flag_a: across(parts_a[s], bits[0]) for s in lead}
+        first_b = {s ^ flag_b: across(parts_b[s], bits[-1]) for s in lead}
+        plane = gathered(payload, bits)
+        plane = [plane[s] for s in range(chips)]
+        more_a, more_b = grads(rest, parts_a, plane)
+        far = across(jnp.concatenate(plane, 0), 1)
+        own_a, own_b = grads([0], more_a, first_a, first_b, far)
+        parts_a.update(more_a)
+        parts_b.update(more_b)
+        parts_a.update(own_a)
+        parts_b.update(own_b)
+        for s in rest:
+            if s & flag_a:
                 first_a[s ^ flag_a] = across(parts_a[s], bits[0])
-            if s & flag_b and s ^ flag_b not in first_b:
+            if s & flag_b:
                 first_b[s ^ flag_b] = across(parts_b[s], bits[-1])
         left_a, left_b = joined(parts_a, first_a, bits[0]), joined(parts_b, first_b, bits[-1])
-        gate = (left_a, left_b)
         for bit_a, bit_b in zip(bits[1:], bits[::-1][1:]):
             left_a = joined(left_a, sent(left_a, bit_a), bit_a)
             left_b = joined(left_b, sent(left_b, bit_b), bit_b)
         sum_a, sum_b = left_a[0], left_b[0]
-        gates = ((parts_a[0], parts_a[0]),) * (len(bits) - 1)
-        plane = gathered(after(payload, d_own), bits, gates)
-        plane = after([plane[s] for s in range(chips)], gate)
-        chip_sum = jnp.concatenate([sum_a, sum_b], 1)
+        place = lax.axis_index("list")
+        inner = 2 * width_q
+        left = ordered(
+            jnp.concatenate([x[:, :width_q] for x in plane], 0), far[:, :width_q], 1
+        )
+        own_rows = inner // n_fsdp
+        left = lax.dynamic_slice_in_dim(left, index * own_rows, own_rows, 1)
+        rows = out_pass(where, left, plane, far, cols)
+        blocks = rows.shape[1] // n_list
+        block = lambda which: lax.dynamic_slice_in_dim(rows, which * blocks, blocks, 1)
+        come_out = [block(place)]
+        come_out += [along(block(place ^ distance), distance) for distance in range(1, n_list)]
+        chip_sum = after(jnp.concatenate([sum_a, sum_b], 1), come_out)
         upper, lower = chip_sum[: depth // 2], chip_sum[depth // 2 :]
         keep = jnp.where(first_core, upper, lower)
         come = across(jnp.where(first_core, lower, upper), 1)
@@ -808,21 +817,9 @@
 
         grad_qkv = list_scatter(rows_sum)
 
-        far = across(jnp.concatenate(plane, 0), 1)
-        inner = 2 * width_q
-        left = ordered(
-            jnp.concatenate([x[:, :width_q] for x in plane], 0), far[:, :width_q], 1
-        )
-        own_rows = inner // n_fsdp
-        left = lax.dynamic_slice_in_dim(left, index * own_rows, own_rows, 1)
-        rows = out_pass(where, left, plane, far, cols)
-        blocks = rows.shape[1] // n_list
-        block = lambda which: lax.dynamic_slice_in_dim(rows, which * blocks, blocks, 1)
-        come = [block(place)]
-        come += [along(block(place ^ distance), distance) for distance in range(1, n_list)]
-        grad_out = sum(x[:own_rows].astype(F32) for x in come)
+        grad_out = sum(x[:own_rows].astype(F32) for x in come_out)
         losses = []
-        for x in come:
+        for x in come_out:
             x = x[own_rows].astype(F32)
             losses.append(x[0] + x[128] + x[256])
         while len(losses) > 1:

time: 178 us -> 168 us (0.944)
  local copies, waits for them, and re-layouts: 18 us -> 10.5 us
  Pallas kernels: 58.4 us -> 51.4 us
  waiting for transfers between devices: 41.1 us -> 46.2 us
  starting transfers between devices: 42.2 us -> 45 us
  other arithmetic: 6.93 us -> 4.47 us
    unnamed x68 -> x66, local copies, waits for them, and re-layouts: 13.9 us -> 7.94 us
    pallas_call x10, Pallas kernels: 37.3 us -> 32 us  [the longest x9 31.4 us: local_call(): pl.pallas_call(kernel, in_specs=[pl.BlockSpec(memory_space=pltpu.SMEM)] +...]
    convert_element_type x4, other arithmetic: 4.27 us -> 0.51 us  [joined(): (parts[s].astype(F32) + come[s].astype(F32)).astype(BF16)]
    ppermute x39, waiting for transfers between devices: 21.1 us -> 24.5 us  [across(): lax.ppermute(value, 'fsdp', [(i, i ^ distance) for i in range(n_fsdp)])]
    ppermute x6, waiting for transfers between devices: 16.8 us -> 19.3 us  [along(): lax.ppermute(value, 'list', [(i, i ^ distance) for i in range(n_list)])]
    ppermute x39, starting transfers between devices: 27.3 us -> 29.7 us  [across(): lax.ppermute(value, 'fsdp', [(i, i ^ distance) for i in range(n_fsdp)])]
  transfers between devices with their start and end apart: 47 -> 47, of which waited for: 21 -> 20; matrix products, arithmetic and copies ran while one was open for 5% -> 3% of each run, Pallas kernels for 24% -> 27%
where the time goes in v5:
time: 168 us
  Pallas kernels  51.4 us (31%)
  waiting for transfers between devices  46.2 us (28%)
  starting transfers between devices  45 us (27%)
  local copies, waits for them, and re-layouts  10.5 us (6%)
  between operations  10.2 us (6%)
  other arithmetic  4.47 us (3%)
    pallas_call x9, Pallas kernels, local_call(): pl.pallas_call(kernel, in_specs=[pl.BlockSpec(memory_space=pltpu.SMEM)] +...  31.4 us
    ppermute x39, starting transfers between devices, across(): lax.ppermute(value, 'fsdp', [(i, i ^ distance) for i in range(n_fsdp)])  29.7 us
    ppermute x39, waiting for transfers between devices, across(): lax.ppermute(value, 'fsdp', [(i, i ^ distance) for i in range(n_fsdp)])  24.5 us
    ppermute x6, waiting for transfers between devices, along(): lax.ppermute(value, 'list', [(i, i ^ distance) for i in range(n_list)])  19.3 us
    pallas_call x2, Pallas kernels, norm(): pl.pallas_call(norm_kernel, grid_spec=pltpu.PrefetchScalarGridSpec(num_sc...  13.1 us
    ppermute x6, starting transfers between devices, along(): lax.ppermute(value, 'list', [(i, i ^ distance) for i in range(n_list)])  8.53 us
    unnamed x66, local copies, waits for them, and re-layouts  7.94 us
    ppermute x2, starting transfers between devices, neighbour(): return lax.ppermute(value, ('list', 'fsdp'), moves)  6.74 us
  transfers between devices with their start and end apart: 47, of which 20 were waited for; matrix products, arithmetic and copies ran while one was open for 3% of the time, Pallas kernels for 27%

profile of v5, /device:TPU:0, one launch (start us, length us, event | category | flops | bytes accessed | tf_op | source)
XLA Modules:
  0.0 167.7 jit_solution(10336648882524915169)
XLA Ops:
  1.1 2.1 %collective-permute-done.come_ref = bf16[256,1536]{1,0:T(8,128)(2,1)S(1)} collective-permute-done((bf16[256,1536]{1,0:T(8,128)(2,1)}, bf16[256,1536]{1,0:T(8,128)(2,1)S(1)}, u32[]{:S(2)}, u32[]{:S(2)}) %collective-permute-start) | collective-permute-done | bytes 786464 | tf_op jit(solution)/shard_map/ppermute | solution.py:602
  5.7 2.9 %collective-permute-start.4 = (bf16[512,384]{1,0:T(8,128)(2,1)S(1)}, bf16[512,384]{1,0:T(8,128)(2,1)S(1)}, u32[]{:S(2)}, u32[]{:S(2)}) collective-permute-start(bf16[512,384]{1,0:T(8,128)(2,1)S(1)} %get-tuple-element.78.a_ref), channel_id=1, source_target_pairs={{0,2},{1,3},{2,0},{3,1},{4,6},{5,7},{6,4},{7,5},{8,10},{9,11},{10,... | collective-permute-start | bytes 1179656 | tf_op jit(solution)/shard_map/ppermute | solution.py:602
  11.0 6.5 %norm_project.2 = (bf16[1024,2048]{1,0:T(8,128)(2,1)S(1)}, f32[4,4,2048]{2,1,0:T(4,128)S(1)}, f32[1024,768]{1,0:T(8,128)S(1)}) custom-call(s32[2]{0:T(128)S(1)} %pad_add_fusion.where_ref, bf16[16,64,2048]{2,1,0:T(8,128)(2,1)} %hidden_ref.1, f32[1,2048]{1,0:T(1,128)S(1)} %bitcast.25, bf16[512,384]{1,0:T(8,128)(2,1)S(1)} %get-tuple-element.78.a_ref, ...), custom_call_target="tpu_custom_call" | custom-call | flops 3500000000 | bytes 24500000 | tf_op jit(solution)/shard_map/norm_project/pallas_call | solution.py:65
  18.1 1.8 %collective-permute-start.7 = (bf16[512,384]{1,0:T(8,128)(2,1)S(1)}, bf16[512,384]{1,0:T(8,128)(2,1)S(1)}, u32[]{:S(2)}, u32[]{:S(2)}) collective-permute-start(bf16[512,384]{1,0:T(8,128)(2,1)S(1)} %get-tuple-element.78.a_ref), channel_id=1, source_target_pairs={{0,4},{1,5},{2,6},{3,7},{4,0},{5,1},{6,2},{7,3},{8,12},{9,13},{10,... | collective-permute-start | bytes 1179656 | tf_op jit(solution)/shard_map/ppermute | solution.py:602
  25.6 6.6 %norm_project.3 = (bf16[1024,2048]{1,0:T(8,128)(2,1)S(1)}, f32[4,4,2048]{2,1,0:T(4,128)S(1)}, f32[1024,768]{1,0:T(8,128)S(1)}) custom-call(s32[2]{0:T(128)S(1)} %pad_add_fusion.where_ref, bf16[16,64,2048]{2,1,0:T(8,128)(2,1)} %collective-permute-done.1.hidden_ref, f32[1,2048]{1,0:T(1,128)S(1)} %bitcast.26, bf16[512,384]{1,0:T(8,128)(2,1)S(1)} %get-tuple-element.78.a_ref, ...), custom_call_target="tpu_custom_call" | custom-call | flops 3500000000 | bytes 24500000 | tf_op jit(solution)/shard_map/norm_project/pallas_call | solution.py:65
  34.7 2.9 %project_more.2.before_ref = f32[1024,768]{1,0:T(8,128)S(1)} custom-call(s32[2]{0:T(128)S(1)} %pad_add_fusion.where_ref, bf16[1024,2048]{1,0:T(8,128)(2,1)S(1)} %get-tuple-element.86.rows_ref.own_ref, f32[1024,768]{1,0:T(8,128)S(1)} %get-tuple-element.67.before_ref, bf16[512,384]{1,0:T(8,128)(2,1)S(1)} %collective-permute-done.4.refs_0_, ...), custom_call_target="tpu_custom_call" | custom-call | flops 2249999872 | bytes 15750000 | tf_op jit(solution)/shard_map/project_more/pallas_call | solution.py:200
  37.6 2.9 %project_more.3.before_ref = f32[1024,768]{1,0:T(8,128)S(1)} custom-call(s32[2]{0:T(128)S(1)} %pad_add_fusion.where_ref, bf16[1024,2048]{1,0:T(8,128)(2,1)S(1)} %get-tuple-element.79.rows_ref.sib_ref, f32[1024,768]{1,0:T(8,128)S(1)} %get-tuple-element.75.before_ref, bf16[512,384]{1,0:T(8,128)(2,1)S(1)} %collective-permute-done.4.refs_0_, ...), custom_call_target="tpu_custom_call" | custom-call | flops 2249999872 | bytes 15750000 | tf_op jit(solution)/shard_map/project_more/pallas_call | solution.py:200
  44.8 4.4 %project_attend.2 = (bf16[1024,768]{1,0:T(8,128)(2,1)S(1)}, bf16[2,2,1024,128]{3,2,1,0:T(8,128)(2,1)S(1)}, f32[2,8,512]{2,1,0:T(8,128)S(1)}) custom-call(s32[2]{0:T(128)S(1)} %pad_add_fusion.where_ref, bf16[1024,2048]{1,0:T(8,128)(2,1)S(1)} %get-tuple-element.79.rows_ref.sib_ref, f32[1024,768]{1,0:T(8,128)S(1)} %project_more.3.before_ref, ...), custom_call_target="tpu_custom_call" | custom-call | flops 3249999872 | bytes 22750000 | tf_op jit(solution)/shard_map/project_attend/pallas_call | solution.py:200
  50.2 1.8 %collective-permute-done.16.refs_5_.refs_10_ = bf16[256,512]{1,0:T(8,128)(2,1)S(1)} collective-permute-done((bf16[256,512]{1,0:T(8,128)(2,1)S(1)}, bf16[256,512]{1,0:T(8,128)(2,1)S(1)}, u32[]{:S(2)}, u32[]{:S(2)}) %collective-permute-start.16) | collective-permute-done | bytes 262176 | tf_op jit(solution)/shard_map/ppermute | solution.py:602
  53.5 1.9 %collective-permute-done.23.refs_13_.refs_18_ = bf16[256,512]{1,0:T(8,128)(2,1)S(1)} collective-permute-done((bf16[256,512]{1,0:T(8,128)(2,1)S(1)}, bf16[256,512]{1,0:T(8,128)(2,1)S(1)}, u32[]{:S(2)}, u32[]{:S(2)}) %collective-permute-start.23) | collective-permute-done | bytes 262176 | tf_op jit(solution)/shard_map/ppermute | solution.py:602
  56.4 4.4 %project_attend.3 = (bf16[1024,768]{1,0:T(8,128)(2,1)S(1)}, bf16[2,2,1024,128]{3,2,1,0:T(8,128)(2,1)S(1)}, f32[2,8,512]{2,1,0:T(8,128)S(1)}) custom-call(s32[2]{0:T(128)S(1)} %pad_add_fusion.where_ref, bf16[1024,2048]{1,0:T(8,128)(2,1)S(1)} %get-tuple-element.86.rows_ref.own_ref, f32[1024,768]{1,0:T(8,128)S(1)} %project_more.2.before_ref, ...), custom_call_target="tpu_custom_call" | custom-call | flops 3249999872 | bytes 22750000 | tf_op jit(solution)/shard_map/project_attend/pallas_call | solution.py:200
  61.3 3.3 %collective-permute-done.22.refs_12_.refs_17_ = bf16[256,512]{1,0:T(8,128)(2,1)S(1)} collective-permute-done((bf16[256,512]{1,0:T(8,128)(2,1)S(1)}, bf16[256,512]{1,0:T(8,128)(2,1)S(1)}, u32[]{:S(2)}, u32[]{:S(2)}) %collective-permute-start.22) | collective-permute-done | bytes 262176 | tf_op jit(solution)/shard_map/ppermute | solution.py:602
  70.8 3.3 %collective-permute-start.27 = (f32[32,128]{1,0:T(8,128)S(1)}, f32[32,128]{1,0:T(8,128)S(1)}, u32[]{:S(2)}, u32[]{:S(2)}) collective-permute-start(f32[32,128]{1,0:T(8,128)S(1)} %get-tuple-element.103.refs_0_), channel_id=1, source_target_pairs={{0,4},{2,6},{4,0},{5,9},{6,2},{7,11},{8,12},{9,5},{10,14},{11,7},{... | collective-permute-start | bytes 49160 | tf_op jit(solution)/shard_map/ppermute | solution.py:622
  74.2 3.4 %collective-permute-start.26 = (f32[32,128]{1,0:T(8,128)S(1)}, f32[32,128]{1,0:T(8,128)}, u32[]{:S(2)}, u32[]{:S(2)}) collective-permute-start(f32[32,128]{1,0:T(8,128)S(1)} %get-tuple-element.103.refs_0_), channel_id=1, source_target_pairs={{0,2},{2,0},{3,5},{4,6},{5,3},{6,4},{7,9},{8,10},{9,7},{10,8},{11,... | collective-permute-start | bytes 49160 | tf_op jit(solution)/shard_map/ppermute | solution.py:622
  77.7 2.3 %collective-permute-done.26.refs_1_ = f32[32,128]{1,0:T(8,128)} collective-permute-done((f32[32,128]{1,0:T(8,128)S(1)}, f32[32,128]{1,0:T(8,128)}, u32[]{:S(2)}, u32[]{:S(2)}) %collective-permute-start.26) | collective-permute-done | bytes 16416 | tf_op jit(solution)/shard_map/ppermute | solution.py:622
  85.3 3.1 %list_grad.1 = (f32[32,512]{1,0:T(8,128)S(1)}, bf16[32,1024]{1,0:T(8,128)(2,1)S(1)}, f32[8,128]{1,0:T(8,128)S(1)}) custom-call(s32[2]{0:T(128)S(1)} %pad_add_fusion.where_ref, s32[5]{0:T(128)S(1)} %stack.35.place_ref, s32[8,128]{1,0:T(8,128)S(1)} %broadcast_in_dim.13.bounds_ref, f32[32,2048]{1,0:T(8,128)S(1)} %copy-done.18, ...), custom_call_target="tpu_custom_call" | custom-call | flops 1250000000 | bytes 8750000 | tf_op jit(solution)/shard_map/list_grad/pallas_call | solution.py:446
  90.5 3.9 %attend_back.2.d_own_ref = bf16[1024,768]{1,0:T(8,128)(2,1)S(1)} custom-call(s32[2]{0:T(128)S(1)} %pad_add_fusion.where_ref, bf16[2,2,1024,128]{3,2,1,0:T(8,128)(2,1)S(1)} %copy-done.27, bf16[1024,768]{1,0:T(8,128)(2,1)S(1)} %copy-done.23, f32[2,8,512]{2,1,0:T(8,128)S(1)} %get-tuple-element.138.d_ref), custom_call_target="tpu_custom_call" | custom-call | flops 1700000000 | bytes 11900000 | tf_op jit(solution)/shard_map/attend_back/pallas_call | solution.py:200
  94.4 1.8 %collective-permute-start.31 = (bf16[32,1920]{1,0:T(8,128)(2,1)S(1)}, bf16[32,1920]{1,0:T(8,128)(2,1)S(1)}, u32[]{:S(2)}, u32[]{:S(2)}) collective-permute-start(bf16[32,1920]{1,0:T(8,128)(2,1)S(1)} %out_payload.1.refs_0_), channel_id=1, source_target_pairs={{0,4},{1,5},{2,6},{3,7},{4,0},{5,1},{6,2},{7,3},{8,12},{9,13},{10,... | collective-permute-start | bytes 368648 | tf_op jit(solution)/shard_map/ppermute | solution.py:602
  96.5 3.9 %attend_back.3.d_sib_ref = bf16[1024,768]{1,0:T(8,128)(2,1)S(1)} custom-call(s32[2]{0:T(128)S(1)} %pad_add_fusion.where_ref, bf16[2,2,1024,128]{3,2,1,0:T(8,128)(2,1)S(1)} %copy-done.25, bf16[1024,768]{1,0:T(8,128)(2,1)S(1)} %copy-done.21, f32[2,8,512]{2,1,0:T(8,128)S(1)} %get-tuple-element.137.d_ref), custom_call_target="tpu_custom_call" | custom-call | flops 1700000000 | bytes 11900000 | tf_op jit(solution)/shard_map/attend_back/pallas_call | solution.py:200
  100.5 2.4 %grad_rows.3 = (bf16[512,384]{1,0:T(8,128)(2,1)S(1)}, bf16[512,384]{1,0:T(8,128)(2,1)S(1)}) custom-call(s32[2]{0:T(128)S(1)} %pad_add_fusion.where_ref, bf16[1024,2048]{1,0:T(8,128)(2,1)S(1)} %copy-done.1, bf16[1024,2048]{1,0:T(8,128)(2,1)S(1)} %copy-done.3, bf16[1024,768]{1,0:T(8,128)(2,1)S(1)} %attend_back.2.d_own_ref, ...), custom_call_target="tpu_custom_call" | custom-call | flops 1250000000 | bytes 8750000 | tf_op jit(solution)/shard_map/grad_rows/pallas_call | solution.py:200
  102.9 1.8 %collective-permute-start.38 = (bf16[512,384]{1,0:T(8,128)(2,1)S(1)}, bf16[512,384]{1,0:T(8,128)(2,1)S(1)}, u32[]{:S(2)}, u32[]{:S(2)}) collective-permute-start(bf16[512,384]{1,0:T(8,128)(2,1)S(1)} %get-tuple-element.116), channel_id=1, source_target_pairs={{0,4},{1,5},{2,6},{3,7},{4,0},{5,1},{6,2},{7,3},{8,12},{9,13},{10,... | collective-permute-start | bytes 1179656 | tf_op jit(solution)/shard_map/ppermute | solution.py:602
  106.4 4.1 %grad_rows.4 = (bf16[512,384]{1,0:T(8,128)(2,1)S(1)}, bf16[512,384]{1,0:T(8,128)(2,1)S(1)}, bf16[512,384]{1,0:T(8,128)(2,1)S(1)}, bf16[512,384]{1,0:T(8,128)(2,1)S(1)}) custom-call(s32[2]{0:T(128)S(1)} %pad_add_fusion.where_ref, bf16[1024,2048]{1,0:T(8,128)(2,1)S(1)} %copy-done.1, bf16[1024,2048]{1,0:T(8,128)(2,1)S(1)} %copy-done.3, ...), custom_call_target="tpu_custom_call" | custom-call | flops 2500000000 | bytes 17500000 | tf_op jit(solution)/shard_map/grad_rows/pallas_call | solution.py:200
  111.7 4.1 %collective-permute-done.37 = bf16[512,384]{1,0:T(8,128)(2,1)S(1)} collective-permute-done((bf16[512,384]{1,0:T(8,128)(2,1)S(1)}, bf16[512,384]{1,0:T(8,128)(2,1)S(1)}, u32[]{:S(2)}, u32[]{:S(2)}) %collective-permute-start.37) | collective-permute-done | bytes 393248 | tf_op jit(solution)/shard_map/ppermute | solution.py:602
  116.0 1.8 %collective-permute-start.42 = (bf16[512,384]{1,0:T(8,128)(2,1)S(1)}, bf16[512,384]{1,0:T(8,128)(2,1)S(1)}, u32[]{:S(2)}, u32[]{:S(2)}) collective-permute-start(bf16[512,384]{1,0:T(8,128)(2,1)S(1)} %add_convert_fusion.1), channel_id=1, source_target_pairs={{0,2},{1,3},{2,0},{3,1},{4,6},{5,7},{6,4},{7,5},{8,10},{9,11},{10,... | collective-permute-start | bytes 1179656 | tf_op jit(solution)/shard_map/ppermute | solution.py:602
  119.4 3.0 %collective-permute-start.36 = (bf16[144,512]{1,0:T(8,128)(2,1)S(1)}, bf16[144,512]{1,0:T(8,128)(2,1)S(1)}, u32[]{:S(2)}, u32[]{:S(2)}) collective-permute-start(bf16[144,512]{1,0:T(8,128)(2,1)S(1)} %get-tuple-element.128), channel_id=1, source_target_pairs={{0,24},{8,16},{16,8},{24,0},{1,25},{9,17},{17,9},{25,1},{2,26},{10... | collective-permute-start | bytes 442376 | tf_op jit(solution)/shard_map/ppermute | solution.py:605
  124.4 2.4 %grad_rows.5 = (bf16[512,384]{1,0:T(8,128)(2,1)S(1)}, bf16[512,384]{1,0:T(8,128)(2,1)S(1)}) custom-call(s32[2]{0:T(128)S(1)} %pad_add_fusion.where_ref, bf16[1024,2048]{1,0:T(8,128)(2,1)S(1)} %copy-done.1, bf16[1024,2048]{1,0:T(8,128)(2,1)S(1)} %copy-done.3, bf16[1024,768]{1,0:T(8,128)(2,1)S(1)} %attend_back.2.d_own_ref, ...), custom_call_target="tpu_custom_call" | custom-call | flops 1250000000 | bytes 8750000 | tf_op jit(solution)/shard_map/grad_rows/pallas_call | solution.py:200
  126.9 4.9 %collective-permute-done.42 = bf16[512,384]{1,0:T(8,128)(2,1)S(1)} collective-permute-done((bf16[512,384]{1,0:T(8,128)(2,1)S(1)}, bf16[512,384]{1,0:T(8,128)(2,1)S(1)}, u32[]{:S(2)}, u32[]{:S(2)}) %collective-permute-start.42) | collective-permute-done | bytes 393248 | tf_op jit(solution)/shard_map/ppermute | solution.py:602
  134.4 2.8 %collective-permute-done.34 = bf16[144,512]{1,0:T(8,128)(2,1)S(1)} collective-permute-done((bf16[144,512]{1,0:T(8,128)(2,1)S(1)}, bf16[144,512]{1,0:T(8,128)(2,1)S(1)}, u32[]{:S(2)}, u32[]{:S(2)}) %collective-permute-start.34) | collective-permute-done | bytes 147488 | tf_op jit(solution)/shard_map/ppermute | solution.py:605
  146.0 2.5 %collective-permute-start.46 = (bf16[256,384]{1,0:T(8,128)(2,1)S(1)}, bf16[256,384]{1,0:T(8,128)(2,1)S(1)}, u32[]{:S(2)}, u32[]{:S(2)}) collective-permute-start(bf16[256,384]{1,0:T(8,128)(2,1)S(1)} %get-tuple-element.124), channel_id=1, source_target_pairs={{0,24},{8,16},{16,8},{24,0},{1,25},{9,17},{17,9},{25,1},{2,26},{10... | collective-permute-start | bytes 589832 | tf_op jit(solution)/shard_map/ppermute | solution.py:605
  149.2 2.7 %collective-permute-done.44 = bf16[256,384]{1,0:T(8,128)(2,1)S(1)} collective-permute-done((bf16[256,384]{1,0:T(8,128)(2,1)S(1)}, bf16[256,384]{1,0:T(8,128)(2,1)S(1)}, u32[]{:S(2)}, u32[]{:S(2)}) %collective-permute-start.44) | collective-permute-done | bytes 196640 | tf_op jit(solution)/shard_map/ppermute | solution.py:605
  151.9 6.5 %collective-permute-done.46 = bf16[256,384]{1,0:T(8,128)(2,1)S(1)} collective-permute-done((bf16[256,384]{1,0:T(8,128)(2,1)S(1)}, bf16[256,384]{1,0:T(8,128)(2,1)S(1)}, u32[]{:S(2)}, u32[]{:S(2)}) %collective-permute-start.46) | collective-permute-done | bytes 196640 | tf_op jit(solution)/shard_map/ppermute | solution.py:605
  158.5 7.3 %collective-permute-done.45 = bf16[256,384]{1,0:T(8,128)(2,1)S(1)} collective-permute-done((bf16[256,384]{1,0:T(8,128)(2,1)S(1)}, bf16[256,384]{1,0:T(8,128)(2,1)S(1)}, u32[]{:S(2)}, u32[]{:S(2)}) %collective-permute-start.45) | collective-permute-done | bytes 196640 | tf_op jit(solution)/shard_map/ppermute | solution.py:605
  (190 shorter events, 48.2 us)
Async XLA Ops:
  3.3 22.3 %collective-permute-start.1 = (bf16[16,64,2048]{2,1,0:T(8,128)(2,1)}, bf16[16,64,2048]{2,1,0:T(8,128)(2,1)}, u32[]{:S(2)}, u32[]{:S(2)}) collective-permute-start(bf16[16,64,2048]{2,1,0:T(8,128)(2,1)} %hidden_ref.1), channel_id=1, source_target_pairs={{0,1},{1,0},{2,3},{3,2},{4,5},{5,4},{6,7},{7,6},{8,9},{9,8},{10,11... | collective-permute-start | bytes 12582920 | tf_op jit(solution)/shard_map/ppermute | solution.py:602
  3.6 18.2 %collective-permute-start.2 = (bf16[128,2048]{1,0:T(8,128)(2,1)}, bf16[128,2048]{1,0:T(8,128)(2,1)S(1)}, u32[]{:S(2)}, u32[]{:S(2)}) collective-permute-start(bf16[128,2048]{1,0:T(8,128)(2,1)} %param.12), channel_id=1, source_target_pairs={{0,1},{1,0},{2,3},{3,2},{4,5},{5,4},{6,7},{7,6},{8,9},{9,8},{10,11... | collective-permute-start | bytes 1572872 | tf_op jit(solution)/shard_map/ppermute | solution.py:602
  5.7 12.3 %collective-permute-start.4 = (bf16[512,384]{1,0:T(8,128)(2,1)S(1)}, bf16[512,384]{1,0:T(8,128)(2,1)S(1)}, u32[]{:S(2)}, u32[]{:S(2)}) collective-permute-start(bf16[512,384]{1,0:T(8,128)(2,1)S(1)} %get-tuple-element.78.a_ref), channel_id=1, source_target_pairs={{0,2},{1,3},{2,0},{3,1},{4,6},{5,7},{6,4},{7,5},{8,10},{9,11},{10,... | collective-permute-start | bytes 1179656 | tf_op jit(solution)/shard_map/ppermute | solution.py:602
  8.7 11.2 %collective-permute-start.5 = (bf16[512,384]{1,0:T(8,128)(2,1)S(1)}, bf16[512,384]{1,0:T(8,128)(2,1)S(1)}, u32[]{:S(2)}, u32[]{:S(2)}) collective-permute-start(bf16[512,384]{1,0:T(8,128)(2,1)S(1)} %get-tuple-element.77.b_ref), channel_id=1, source_target_pairs={{0,4},{1,5},{2,6},{3,7},{4,0},{5,1},{6,2},{7,3},{8,12},{9,13},{10,... | collective-permute-start | bytes 1179656 | tf_op jit(solution)/shard_map/ppermute | solution.py:602
  18.1 14.2 %collective-permute-start.7 = (bf16[512,384]{1,0:T(8,128)(2,1)S(1)}, bf16[512,384]{1,0:T(8,128)(2,1)S(1)}, u32[]{:S(2)}, u32[]{:S(2)}) collective-permute-start(bf16[512,384]{1,0:T(8,128)(2,1)S(1)} %get-tuple-element.78.a_ref), channel_id=1, source_target_pairs={{0,4},{1,5},{2,6},{3,7},{4,0},{5,1},{6,2},{7,3},{8,12},{9,13},{10,... | collective-permute-start | bytes 1179656 | tf_op jit(solution)/shard_map/ppermute | solution.py:602
  19.8 12.4 %collective-permute-start.6 = (bf16[512,384]{1,0:T(8,128)(2,1)S(1)}, bf16[512,384]{1,0:T(8,128)(2,1)S(1)}, u32[]{:S(2)}, u32[]{:S(2)}) collective-permute-start(bf16[512,384]{1,0:T(8,128)(2,1)S(1)} %get-tuple-element.77.b_ref), channel_id=1, source_target_pairs={{0,2},{1,3},{2,0},{3,1},{4,6},{5,7},{6,4},{7,5},{8,10},{9,11},{10,... | collective-permute-start | bytes 1179656 | tf_op jit(solution)/shard_map/ppermute | solution.py:602
  21.3 19.2 %collective-permute-start.8 = (bf16[512,384]{1,0:T(8,128)(2,1)S(1)}, bf16[512,384]{1,0:T(8,128)(2,1)S(1)}, u32[]{:S(2)}, u32[]{:S(2)}) collective-permute-start(bf16[512,384]{1,0:T(8,128)(2,1)S(1)} %collective-permute-done.4.refs_0_), channel_id=1, source_target_pairs={{0,4},{1,5},{2,6},{3,7},{4,0},{5,1},{6,2},{7,3},{8,12},{9,13},{10,... | collective-permute-start | bytes 1179656 | tf_op jit(solution)/shard_map/ppermute | solution.py:602
  24.3 16.3 %collective-permute-start.9 = (bf16[512,384]{1,0:T(8,128)(2,1)S(1)}, bf16[512,384]{1,0:T(8,128)(2,1)S(1)}, u32[]{:S(2)}, u32[]{:S(2)}) collective-permute-start(bf16[512,384]{1,0:T(8,128)(2,1)S(1)} %collective-permute-done.5.refs_3_), channel_id=1, source_target_pairs={{0,2},{1,3},{2,0},{3,1},{4,6},{5,7},{6,4},{7,5},{8,10},{9,11},{10,... | collective-permute-start | bytes 1179656 | tf_op jit(solution)/shard_map/ppermute | solution.py:602
  32.3 10.4 %collective-permute-start.15 = (bf16[256,512]{1,0:T(8,128)(2,1)S(1)}, bf16[256,512]{1,0:T(8,128)(2,1)S(1)}, u32[]{:S(2)}, u32[]{:S(2)}) collective-permute-start(bf16[256,512]{1,0:T(8,128)(2,1)S(1)} %get-tuple-element.93.refs_1_.refs_6_), channel_id=1, source_target_pairs={{0,4},{1,5},{2,6},{3,7},{4,0},{5,1},{6,2},{7,3},{8,12},{9,13},{10,... | collective-permute-start | bytes 786440 | tf_op jit(solution)/shard_map/ppermute | solution.py:602
  33.2 16.9 %collective-permute-start.14 = (bf16[256,512]{1,0:T(8,128)(2,1)S(1)}, bf16[256,512]{1,0:T(8,128)(2,1)S(1)}, u32[]{:S(2)}, u32[]{:S(2)}) collective-permute-start(bf16[256,512]{1,0:T(8,128)(2,1)S(1)} %get-tuple-element.94.refs_0_.refs_5_), channel_id=1, source_target_pairs={{0,2},{1,3},{2,0},{3,1},{4,6},{5,7},{6,4},{7,5},{8,10},{9,11},{10,... | collective-permute-start | bytes 786440 | tf_op jit(solution)/shard_map/ppermute | solution.py:602
  40.6 25.4 %collective-permute-start.12 = (bf16[256,512]{1,0:T(8,128)(2,1)S(1)}, bf16[256,512]{1,0:T(8,128)(2,1)S(1)}, u32[]{:S(2)}, u32[]{:S(2)}) collective-permute-start(bf16[256,512]{1,0:T(8,128)(2,1)S(1)} %get-tuple-element.94.refs_0_.refs_5_), channel_id=1, source_target_pairs={{0,1},{1,0},{2,3},{3,2},{4,5},{5,4},{6,7},{7,6},{8,9},{9,8},{10,11... | collective-permute-start | bytes 786440 | tf_op jit(solution)/shard_map/ppermute | solution.py:602
  40.6 25.6 %collective-permute-start.13 = (bf16[256,512]{1,0:T(8,128)(2,1)S(1)}, bf16[256,512]{1,0:T(8,128)(2,1)S(1)}, u32[]{:S(2)}, u32[]{:S(2)}) collective-permute-start(bf16[256,512]{1,0:T(8,128)(2,1)S(1)} %get-tuple-element.93.refs_1_.refs_6_), channel_id=1, source_target_pairs={{0,1},{1,0},{2,3},{3,2},{4,5},{5,4},{6,7},{7,6},{8,9},{9,8},{10,11... | collective-permute-start | bytes 786440 | tf_op jit(solution)/shard_map/ppermute | solution.py:602
  42.8 9.2 %collective-permute-start.16 = (bf16[256,512]{1,0:T(8,128)(2,1)S(1)}, bf16[256,512]{1,0:T(8,128)(2,1)S(1)}, u32[]{:S(2)}, u32[]{:S(2)}) collective-permute-start(bf16[256,512]{1,0:T(8,128)(2,1)S(1)} %get-tuple-element.93.refs_1_.refs_6_), channel_id=1, source_target_pairs={{0,2},{1,3},{2,0},{3,1},{4,6},{5,7},{6,4},{7,5},{8,10},{9,11},{10,... | collective-permute-start | bytes 786440 | tf_op jit(solution)/shard_map/ppermute | solution.py:602
  44.2 11.1 %collective-permute-start.23 = (bf16[256,512]{1,0:T(8,128)(2,1)S(1)}, bf16[256,512]{1,0:T(8,128)(2,1)S(1)}, u32[]{:S(2)}, u32[]{:S(2)}) collective-permute-start(bf16[256,512]{1,0:T(8,128)(2,1)S(1)} %collective-permute-done.15.refs_9_.refs_14_), channel_id=1, source_target_pairs={{0,2},{1,3},{2,0},{3,1},{4,6},{5,7},{6,4},{7,5},{8,10},{9,11},{10,... | collective-permute-start | bytes 786440 | tf_op jit(solution)/shard_map/ppermute | solution.py:602
  50.1 16.3 %collective-permute-start.21 = (bf16[256,512]{1,0:T(8,128)(2,1)S(1)}, bf16[256,512]{1,0:T(8,128)(2,1)S(1)}, u32[]{:S(2)}, u32[]{:S(2)}) collective-permute-start(bf16[256,512]{1,0:T(8,128)(2,1)S(1)} %collective-permute-done.15.refs_9_.refs_14_), channel_id=1, source_target_pairs={{0,1},{1,0},{2,3},{3,2},{4,5},{5,4},{6,7},{7,6},{8,9},{9,8},{10,11... | collective-permute-start | bytes 786440 | tf_op jit(solution)/shard_map/ppermute | solution.py:602
  52.0 9.2 %collective-permute-start.19 = (bf16[256,512]{1,0:T(8,128)(2,1)S(1)}, bf16[256,512]{1,0:T(8,128)(2,1)S(1)}, u32[]{:S(2)}, u32[]{:S(2)}) collective-permute-start(bf16[256,512]{1,0:T(8,128)(2,1)S(1)} %get-tuple-element.94.refs_0_.refs_5_), channel_id=1, source_target_pairs={{0,4},{1,5},{2,6},{3,7},{4,0},{5,1},{6,2},{7,3},{8,12},{9,13},{10,... | collective-permute-start | bytes 786440 | tf_op jit(solution)/shard_map/ppermute | solution.py:602
  55.3 9.2 %collective-permute-start.22 = (bf16[256,512]{1,0:T(8,128)(2,1)S(1)}, bf16[256,512]{1,0:T(8,128)(2,1)S(1)}, u32[]{:S(2)}, u32[]{:S(2)}) collective-permute-start(bf16[256,512]{1,0:T(8,128)(2,1)S(1)} %collective-permute-done.14.refs_4_.refs_9_), channel_id=1, source_target_pairs={{0,4},{1,5},{2,6},{3,7},{4,0},{5,1},{6,2},{7,3},{8,12},{9,13},{10,... | collective-permute-start | bytes 786440 | tf_op jit(solution)/shard_map/ppermute | solution.py:602
  94.4 11.8 %collective-permute-start.31 = (bf16[32,1920]{1,0:T(8,128)(2,1)S(1)}, bf16[32,1920]{1,0:T(8,128)(2,1)S(1)}, u32[]{:S(2)}, u32[]{:S(2)}) collective-permute-start(bf16[32,1920]{1,0:T(8,128)(2,1)S(1)} %out_payload.1.refs_0_), channel_id=1, source_target_pairs={{0,4},{1,5},{2,6},{3,7},{4,0},{5,1},{6,2},{7,3},{8,12},{9,13},{10,... | collective-permute-start | bytes 368648 | tf_op jit(solution)/shard_map/ppermute | solution.py:602
  96.2 10.1 %collective-permute-start.32 = (bf16[32,1920]{1,0:T(8,128)(2,1)S(1)}, bf16[32,1920]{1,0:T(8,128)(2,1)S(1)}, u32[]{:S(2)}, u32[]{:S(2)}) collective-permute-start(bf16[32,1920]{1,0:T(8,128)(2,1)S(1)} %collective-permute-done.30.refs_1_), channel_id=1, source_target_pairs={{0,4},{1,5},{2,6},{3,7},{4,0},{5,1},{6,2},{7,3},{8,12},{9,13},{10,... | collective-permute-start | bytes 368648 | tf_op jit(solution)/shard_map/ppermute | solution.py:602
  102.9 13.0 %collective-permute-start.38 = (bf16[512,384]{1,0:T(8,128)(2,1)S(1)}, bf16[512,384]{1,0:T(8,128)(2,1)S(1)}, u32[]{:S(2)}, u32[]{:S(2)}) collective-permute-start(bf16[512,384]{1,0:T(8,128)(2,1)S(1)} %get-tuple-element.116), channel_id=1, source_target_pairs={{0,4},{1,5},{2,6},{3,7},{4,0},{5,1},{6,2},{7,3},{8,12},{9,13},{10,... | collective-permute-start | bytes 1179656 | tf_op jit(solution)/shard_map/ppermute | solution.py:602
  104.7 11.0 %collective-permute-start.37 = (bf16[512,384]{1,0:T(8,128)(2,1)S(1)}, bf16[512,384]{1,0:T(8,128)(2,1)S(1)}, u32[]{:S(2)}, u32[]{:S(2)}) collective-permute-start(bf16[512,384]{1,0:T(8,128)(2,1)S(1)} %get-tuple-element.112), channel_id=1, source_target_pairs={{0,2},{1,3},{2,0},{3,1},{4,6},{5,7},{6,4},{7,5},{8,10},{9,11},{10,... | collective-permute-start | bytes 1179656 | tf_op jit(solution)/shard_map/ppermute | solution.py:602
  106.3 11.4 %collective-permute-start.33 = (bf16[128,1920]{1,0:T(8,128)(2,1)S(1)}, bf16[128,1920]{1,0:T(8,128)(2,1)S(1)}, u32[]{:S(2)}, u32[]{:S(2)}) collective-permute-start(bf16[128,1920]{1,0:T(8,128)(2,1)S(1)} %pad_maximum_fusion.2), channel_id=1, source_target_pairs={{0,1},{1,0},{2,3},{3,2},{4,5},{5,4},{6,7},{7,6},{8,9},{9,8},{10,11... | collective-permute-start | bytes 1474568 | tf_op jit(solution)/shard_map/ppermute | solution.py:602
  110.5 16.3 %collective-permute-start.41 = (bf16[512,384]{1,0:T(8,128)(2,1)S(1)}, bf16[512,384]{1,0:T(8,128)(2,1)S(1)}, u32[]{:S(2)}, u32[]{:S(2)}) collective-permute-start(bf16[512,384]{1,0:T(8,128)(2,1)S(1)} %get-tuple-element.120), channel_id=1, source_target_pairs={{0,4},{1,5},{2,6},{3,7},{4,0},{5,1},{6,2},{7,3},{8,12},{9,13},{10,... | collective-permute-start | bytes 1179656 | tf_op jit(solution)/shard_map/ppermute | solution.py:602
  111.0 22.5 %collective-permute-start.39 = (bf16[512,384]{1,0:T(8,128)(2,1)S(1)}, bf16[512,384]{1,0:T(8,128)(2,1)S(1)}, u32[]{:S(2)}, u32[]{:S(2)}) collective-permute-start(bf16[512,384]{1,0:T(8,128)(2,1)S(1)} %get-tuple-element.114), channel_id=1, source_target_pairs={{0,2},{1,3},{2,0},{3,1},{4,6},{5,7},{6,4},{7,5},{8,10},{9,11},{10,... | collective-permute-start | bytes 1179656 | tf_op jit(solution)/shard_map/ppermute | solution.py:602
  115.8 17.7 %collective-permute-start.40 = (bf16[512,384]{1,0:T(8,128)(2,1)S(1)}, bf16[512,384]{1,0:T(8,128)(2,1)S(1)}, u32[]{:S(2)}, u32[]{:S(2)}) collective-permute-start(bf16[512,384]{1,0:T(8,128)(2,1)S(1)} %add_convert_fusion.4), channel_id=1, source_target_pairs={{0,4},{1,5},{2,6},{3,7},{4,0},{5,1},{6,2},{7,3},{8,12},{9,13},{10,... | collective-permute-start | bytes 1179656 | tf_op jit(solution)/shard_map/ppermute | solution.py:602
  116.0 15.7 %collective-permute-start.42 = (bf16[512,384]{1,0:T(8,128)(2,1)S(1)}, bf16[512,384]{1,0:T(8,128)(2,1)S(1)}, u32[]{:S(2)}, u32[]{:S(2)}) collective-permute-start(bf16[512,384]{1,0:T(8,128)(2,1)S(1)} %add_convert_fusion.1), channel_id=1, source_target_pairs={{0,2},{1,3},{2,0},{3,1},{4,6},{5,7},{6,4},{7,5},{8,10},{9,11},{10,... | collective-permute-start | bytes 1179656 | tf_op jit(solution)/shard_map/ppermute | solution.py:602
  119.4 14.3 %collective-permute-start.36 = (bf16[144,512]{1,0:T(8,128)(2,1)S(1)}, bf16[144,512]{1,0:T(8,128)(2,1)S(1)}, u32[]{:S(2)}, u32[]{:S(2)}) collective-permute-start(bf16[144,512]{1,0:T(8,128)(2,1)S(1)} %get-tuple-element.128), channel_id=1, source_target_pairs={{0,24},{8,16},{16,8},{24,0},{1,25},{9,17},{17,9},{25,1},{2,26},{10... | collective-permute-start | bytes 442376 | tf_op jit(solution)/shard_map/ppermute | solution.py:605
  126.8 7.5 %collective-permute-start.35 = (bf16[144,512]{1,0:T(8,128)(2,1)S(1)}, bf16[144,512]{1,0:T(8,128)(2,1)S(1)}, u32[]{:S(2)}, u32[]{:S(2)}) collective-permute-start(bf16[144,512]{1,0:T(8,128)(2,1)S(1)} %get-tuple-element.129), channel_id=1, source_target_pairs={{0,16},{8,24},{16,0},{24,8},{1,17},{9,25},{17,1},{25,9},{2,18},{10... | collective-permute-start | bytes 442376 | tf_op jit(solution)/shard_map/ppermute | solution.py:605
  137.2 6.9 %collective-permute-start.43 = (bf16[256,768]{1,0:T(8,128)(2,1)S(1)}, bf16[256,768]{1,0:T(8,128)(2,1)S(1)}, u32[]{:S(2)}, u32[]{:S(2)}) collective-permute-start(bf16[256,768]{1,0:T(8,128)(2,1)S(1)} %get-tuple-element.127), channel_id=1, source_target_pairs={{0,1},{1,0},{2,3},{3,2},{4,5},{5,4},{6,7},{7,6},{8,9},{9,8},{10,11... | collective-permute-start | bytes 1179656 | tf_op jit(solution)/shard_map/ppermute | solution.py:602
  144.6 7.4 %collective-permute-start.44 = (bf16[256,384]{1,0:T(8,128)(2,1)S(1)}, bf16[256,384]{1,0:T(8,128)(2,1)S(1)}, u32[]{:S(2)}, u32[]{:S(2)}) collective-permute-start(bf16[256,384]{1,0:T(8,128)(2,1)S(1)} %get-tuple-element.123), channel_id=1, source_target_pairs={{0,8},{8,0},{16,24},{24,16},{1,9},{9,1},{17,25},{25,17},{2,10},{10... | collective-permute-start | bytes 589832 | tf_op jit(solution)/shard_map/ppermute | solution.py:605
  146.0 12.5 %collective-permute-start.46 = (bf16[256,384]{1,0:T(8,128)(2,1)S(1)}, bf16[256,384]{1,0:T(8,128)(2,1)S(1)}, u32[]{:S(2)}, u32[]{:S(2)}) collective-permute-start(bf16[256,384]{1,0:T(8,128)(2,1)S(1)} %get-tuple-element.124), channel_id=1, source_target_pairs={{0,24},{8,16},{16,8},{24,0},{1,25},{9,17},{17,9},{25,1},{2,26},{10... | collective-permute-start | bytes 589832 | tf_op jit(solution)/shard_map/ppermute | solution.py:605
  148.5 17.3 %collective-permute-start.45 = (bf16[256,384]{1,0:T(8,128)(2,1)S(1)}, bf16[256,384]{1,0:T(8,128)(2,1)S(1)}, u32[]{:S(2)}, u32[]{:S(2)}) collective-permute-start(bf16[256,384]{1,0:T(8,128)(2,1)S(1)} %get-tuple-element.125), channel_id=1, source_target_pairs={{0,16},{8,24},{16,0},{24,8},{1,17},{9,25},{17,1},{25,9},{2,18},{10... | collective-permute-start | bytes 589832 | tf_op jit(solution)/shard_map/ppermute | solution.py:605
  (50 other events, 291.4 us)

commit v6 on v5

--- a/solution.py
+++ b/solution.py
@@ -18,8 +18,8 @@
 epsilon = 1e-05
 loss_scale = 64.0
 scale = HEAD_DIM ** (-0.5)
-VMEM = 16 * 1024 * 1024
-SMALL = 10 * 1024 * 1024
+VMEM = 10 * 1024 * 1024
+SMALL = 6 * 1024 * 1024
 
 
 def cost(micros):
@@ -521,8 +521,39 @@
     for _ in range(3):
         parts.append(rest.astype(BF16).astype(F32))
         rest = rest - parts[-1]
-    row = jnp.concatenate(parts + [jnp.zeros_like(rest)], 1).astype(BF16)
+    index = lax.broadcasted_iota(jnp.int32, rest.shape, 0)
+    row = jnp.where(index == 0, parts[0], jnp.where(index == 1, parts[1], parts[2])).astype(BF16)
     out_ref[own_rows:] = jnp.concatenate([row] * (2 * cols // row.shape[1]), 1)
+
+
+def total_kernel(*refs):
+    blocks, (out_ref, loss_ref) = refs[:-2], refs[-2:]
+    own_rows = out_ref.shape[0]
+    out_ref[...] = sum(ref[:own_rows].astype(F32) for ref in blocks)
+    losses = []
+    for ref in blocks:
+        rows = ref[own_rows:].astype(F32)
+        losses.append(rows[0:1] + rows[1:2] + rows[2:3])
+    while len(losses) > 1:
+        losses = [a + b for a, b in zip(losses[0::2], losses[1::2])]
+    loss_ref[...] = jnp.broadcast_to(losses[0][:, :128], loss_ref.shape)
+
+
+def total_pass(blocks):
+    vmem = pl.BlockSpec(memory_space=pltpu.VMEM)
+    rows, width = blocks[0].shape
+    return pl.pallas_call(
+        total_kernel,
+        in_specs=[vmem] * len(blocks),
+        out_specs=[vmem] * 2,
+        out_shape=[
+            jax.ShapeDtypeStruct((rows - EXTRA, width), F32),
+            jax.ShapeDtypeStruct((8, 128), F32),
+        ],
+        compiler_params=pltpu.CompilerParams(vmem_limit_bytes=SMALL),
+        cost_estimate=cost(1),
+        name="out_total",
+    )(*blocks)
 
 
 def out_pass(where, left, near, far, cols):
@@ -624,13 +655,16 @@
     def after(value, *others):
         return lax.optimization_barrier((value, others))[0]
 
-    def gathered(value, order, near=(), far=()):
+    def gathered(value, order, far=(), wait=True):
         have = {0: value}
         for bit in order:
             first = [part for s, part in have.items() if s]
             ready = dict(have)
             if first:
-                ready = {s: after(part, far if s else near, first) for s, part in have.items()}
+                ready = {
+                    s: after(part, far, first) if s else after(part, first) if wait else part
+                    for s, part in have.items()
+                }
             have.update({s ^ (bit >> 1): across(part, bit) for s, part in ready.items()})
         return have
 
@@ -725,12 +759,12 @@
         proj_own, probs_own, attn_own = forward(where, normal_last, weights[2], groups, before_own)
         attn_own = attn_own.reshape(passages, -1)
         attn_own_other = across(attn_own, 1)
-        out_a = gathered(out_pair[:, : cols // 2], bits, before_sib, before_sib)
-        out_b = gathered(out_pair[:, cols // 2 :], bits[::-1], before_sib, before_sib)
+        out_a = gathered(out_pair[:, : cols // 2], bits, before_sib, False)
+        out_b = gathered(out_pair[:, cols // 2 :], bits[::-1], before_sib, False)
         pieces = []
         for s in range(chips):
             pieces += [out_a[s], out_b[s]]
-            gate = probs_own if bin(s).count("1") == last else ()
+            gate = probs_own
             pieces += [across(after(x, gate), 1) for x in (out_a[s], out_b[s])]
         unit, inverse, score, attn = score_pass(
             where,
@@ -768,21 +802,17 @@
         plane = [plane[s] for s in range(chips)]
         more_a, more_b = grads(rest, parts_a, plane)
         far = across(jnp.concatenate(plane, 0), 1)
-        own_a, own_b = grads([0], more_a, first_a, first_b, far)
+        for s in rest:
+            if s & flag_a:
+                first_a[s ^ flag_a] = across(more_a[s], bits[0])
+            if s & flag_b:
+                first_b[s ^ flag_b] = across(more_b[s], bits[-1])
+        own_a, own_b = grads([0], more_a, first_a, first_b)
         parts_a.update(more_a)
         parts_b.update(more_b)
         parts_a.update(own_a)
         parts_b.update(own_b)
-        for s in rest:
-            if s & flag_a:
-                first_a[s ^ flag_a] = across(parts_a[s], bits[0])
-            if s & flag_b:
-                first_b[s ^ flag_b] = across(parts_b[s], bits[-1])
         left_a, left_b = joined(parts_a, first_a, bits[0]), joined(parts_b, first_b, bits[-1])
-        for bit_a, bit_b in zip(bits[1:], bits[::-1][1:]):
-            left_a = joined(left_a, sent(left_a, bit_a), bit_a)
-            left_b = joined(left_b, sent(left_b, bit_b), bit_b)
-        sum_a, sum_b = left_a[0], left_b[0]
         place = lax.axis_index("list")
         inner = 2 * width_q
         left = ordered(
@@ -795,7 +825,11 @@
         block = lambda which: lax.dynamic_slice_in_dim(rows, which * blocks, blocks, 1)
         come_out = [block(place)]
         come_out += [along(block(place ^ distance), distance) for distance in range(1, n_list)]
-        chip_sum = after(jnp.concatenate([sum_a, sum_b], 1), come_out)
+        for bit_a, bit_b in zip(bits[1:], bits[::-1][1:]):
+            far_a, far_b = after((sent(left_a, bit_a), sent(left_b, bit_b)), come_out)
+            left_a, left_b = joined(left_a, far_a, bit_a), joined(left_b, far_b, bit_b)
+        sum_a, sum_b = left_a[0], left_b[0]
+        chip_sum = jnp.concatenate([sum_a, sum_b], 1)
         upper, lower = chip_sum[: depth // 2], chip_sum[depth // 2 :]
         keep = jnp.where(first_core, upper, lower)
         come = across(jnp.where(first_core, lower, upper), 1)
@@ -817,14 +851,8 @@
 
         grad_qkv = list_scatter(rows_sum)
 
-        grad_out = sum(x[:own_rows].astype(F32) for x in come_out)
-        losses = []
-        for x in come_out:
-            x = x[own_rows].astype(F32)
-            losses.append(x[0] + x[128] + x[256])
-        while len(losses) > 1:
-            losses = [a + b for a, b in zip(losses[0::2], losses[1::2])]
-        return (losses[0], grad_qkv, grad_out)
+        grad_out, losses = total_pass(come_out)
+        return (losses[0, 0], grad_qkv, grad_out)
 
     placed = (
         P(("list", "fsdp"), None, None),

time: 168 us -> 151 us (0.90)
  waiting for transfers between devices: 46.2 us -> 33.6 us
  between operations: 10.2 us -> 1.29 us
  starting transfers between devices: 45 us -> 49 us
    ppermute x39, waiting for transfers between devices: 24.5 us -> 14.6 us  [across(): lax.ppermute(value, 'fsdp', [(i, i ^ distance) for i in range(n_fsdp)])]
    ppermute x6, starting transfers between devices: 8.53 us -> 12.5 us  [along(): lax.ppermute(value, 'list', [(i, i ^ distance) for i in range(n_list)])]
    ppermute x6, waiting for transfers between devices: 19.3 us -> 17.4 us  [along(): lax.ppermute(value, 'list', [(i, i ^ distance) for i in range(n_list)])]
    unnamed x66 -> x72, local copies, waits for them, and re-layouts: 7.94 us -> 9.88 us
  transfers between devices with their start and end apart: 47 -> 47, of which waited for: 20 -> 20; matrix products, arithmetic and copies ran while one was open for 3% -> 2% of each run, Pallas kernels for 27% -> 31%
where the time goes in v6:
time: 151 us; the launch traced here: 150 us
  Pallas kernels  51.8 us (34%)
  starting transfers between devices  49 us (32%)
  waiting for transfers between devices  33.6 us (22%)
  local copies, waits for them, and re-layouts  10.9 us (7%)
  other arithmetic  3.71 us (2%)
    pallas_call x9, Pallas kernels, local_call(): pl.pallas_call(kernel, in_specs=[pl.BlockSpec(memory_space=pltpu.SMEM)] +...  31.4 us
    ppermute x39, starting transfers between devices, across(): lax.ppermute(value, 'fsdp', [(i, i ^ distance) for i in range(n_fsdp)])  29.9 us
    ppermute x6, waiting for transfers between devices, along(): lax.ppermute(value, 'list', [(i, i ^ distance) for i in range(n_list)])  17.4 us
    ppermute x39, waiting for transfers between devices, across(): lax.ppermute(value, 'fsdp', [(i, i ^ distance) for i in range(n_fsdp)])  14.6 us
    pallas_call x2, Pallas kernels, norm(): pl.pallas_call(norm_kernel, grid_spec=pltpu.PrefetchScalarGridSpec(num_sc...  13.1 us
    ppermute x6, starting transfers between devices, along(): lax.ppermute(value, 'list', [(i, i ^ distance) for i in range(n_list)])  12.5 us
    unnamed x72, local copies, waits for them, and re-layouts  9.88 us
    ppermute x2, starting transfers between devices, neighbour(): return lax.ppermute(value, ('list', 'fsdp'), moves)  6.54 us
  transfers between devices with their start and end apart: 47, of which 20 were waited for; matrix products, arithmetic and copies ran while one was open for 2% of the time, Pallas kernels for 31%

profile of v6, /device:TPU:0, one launch (start us, length us, event | category | flops | bytes accessed | tf_op | source)
XLA Modules:
  0.0 150.2 jit_solution(7598517914206434629)
XLA Ops:
  1.1 2.1 %collective-permute-done.come_ref = bf16[256,1536]{1,0:T(8,128)(2,1)S(1)} collective-permute-done((bf16[256,1536]{1,0:T(8,128)(2,1)}, bf16[256,1536]{1,0:T(8,128)(2,1)S(1)}, u32[]{:S(2)}, u32[]{:S(2)}) %collective-permute-start) | collective-permute-done | bytes 786464 | tf_op jit(solution)/shard_map/ppermute | solution.py:633
  5.7 2.9 %collective-permute-start.4 = (bf16[512,384]{1,0:T(8,128)(2,1)S(1)}, bf16[512,384]{1,0:T(8,128)(2,1)S(1)}, u32[]{:S(2)}, u32[]{:S(2)}) collective-permute-start(bf16[512,384]{1,0:T(8,128)(2,1)S(1)} %get-tuple-element.85.a_ref), channel_id=1, source_target_pairs={{0,2},{1,3},{2,0},{3,1},{4,6},{5,7},{6,4},{7,5},{8,10},{9,11},{10,... | collective-permute-start | bytes 1179656 | tf_op jit(solution)/shard_map/ppermute | solution.py:633
  8.7 1.5 %collective-permute-start.5 = (bf16[512,384]{1,0:T(8,128)(2,1)S(1)}, bf16[512,384]{1,0:T(8,128)(2,1)S(1)}, u32[]{:S(2)}, u32[]{:S(2)}) collective-permute-start(bf16[512,384]{1,0:T(8,128)(2,1)S(1)} %get-tuple-element.84.b_ref), channel_id=1, source_target_pairs={{0,4},{1,5},{2,6},{3,7},{4,0},{5,1},{6,2},{7,3},{8,12},{9,13},{10,... | collective-permute-start | bytes 1179656 | tf_op jit(solution)/shard_map/ppermute | solution.py:633
  11.0 6.5 %norm_project.2 = (bf16[1024,2048]{1,0:T(8,128)(2,1)S(1)}, f32[4,4,2048]{2,1,0:T(4,128)S(1)}, f32[1024,768]{1,0:T(8,128)S(1)}) custom-call(s32[2]{0:T(128)S(1)} %pad_add_fusion.where_ref, bf16[16,64,2048]{2,1,0:T(8,128)(2,1)} %hidden_ref.1, f32[1,2048]{1,0:T(1,128)S(1)} %bitcast.25, bf16[512,384]{1,0:T(8,128)(2,1)S(1)} %get-tuple-element.85.a_ref, ...), custom_call_target="tpu_custom_call" | custom-call | flops 3500000000 | bytes 24500000 | tf_op jit(solution)/shard_map/norm_project/pallas_call | solution.py:65
  18.1 1.8 %collective-permute-start.7 = (bf16[512,384]{1,0:T(8,128)(2,1)S(1)}, bf16[512,384]{1,0:T(8,128)(2,1)S(1)}, u32[]{:S(2)}, u32[]{:S(2)}) collective-permute-start(bf16[512,384]{1,0:T(8,128)(2,1)S(1)} %get-tuple-element.85.a_ref), channel_id=1, source_target_pairs={{0,4},{1,5},{2,6},{3,7},{4,0},{5,1},{6,2},{7,3},{8,12},{9,13},{10,... | collective-permute-start | bytes 1179656 | tf_op jit(solution)/shard_map/ppermute | solution.py:633
  22.6 1.6 %maximum_select_fusion = bf16[256,2048]{1,0:T(8,128)(2,1)S(1)} fusion(bf16[128,2048]{1,0:T(8,128)(2,1)} %copy-done.32, bf16[128,2048]{1,0:T(8,128)(2,1)S(1)} %copy-done.31, pred[]{:T(512)S(6)} %eq.9), kind=kLoop, calls=%fused_computation | loop fusion | flops 4718592 | bytes 2097153 | tf_op jit(solution)/shard_map/jit(_where)/select_n | solution.py:694
  25.6 6.6 %norm_project.3 = (bf16[1024,2048]{1,0:T(8,128)(2,1)S(1)}, f32[4,4,2048]{2,1,0:T(4,128)S(1)}, f32[1024,768]{1,0:T(8,128)S(1)}) custom-call(s32[2]{0:T(128)S(1)} %pad_add_fusion.where_ref, bf16[16,64,2048]{2,1,0:T(8,128)(2,1)} %collective-permute-done.1.hidden_ref, f32[1,2048]{1,0:T(1,128)S(1)} %bitcast.26, bf16[512,384]{1,0:T(8,128)(2,1)S(1)} %get-tuple-element.85.a_ref, ...), custom_call_target="tpu_custom_call" | custom-call | flops 3500000000 | bytes 24500000 | tf_op jit(solution)/shard_map/norm_project/pallas_call | solution.py:65
  34.7 2.9 %project_more.2.before_ref = f32[1024,768]{1,0:T(8,128)S(1)} custom-call(s32[2]{0:T(128)S(1)} %pad_add_fusion.where_ref, bf16[1024,2048]{1,0:T(8,128)(2,1)S(1)} %get-tuple-element.93.rows_ref.own_ref, f32[1024,768]{1,0:T(8,128)S(1)} %get-tuple-element.74.before_ref, bf16[512,384]{1,0:T(8,128)(2,1)S(1)} %collective-permute-done.4.refs_0_, ...), custom_call_target="tpu_custom_call" | custom-call | flops 2249999872 | bytes 15750000 | tf_op jit(solution)/shard_map/project_more/pallas_call | solution.py:200
  38.5 2.9 %project_more.3.before_ref = f32[1024,768]{1,0:T(8,128)S(1)} custom-call(s32[2]{0:T(128)S(1)} %pad_add_fusion.where_ref, bf16[1024,2048]{1,0:T(8,128)(2,1)S(1)} %get-tuple-element.86.rows_ref.sib_ref, f32[1024,768]{1,0:T(8,128)S(1)} %get-tuple-element.82.before_ref, bf16[512,384]{1,0:T(8,128)(2,1)S(1)} %collective-permute-done.4.refs_0_, ...), custom_call_target="tpu_custom_call" | custom-call | flops 2249999872 | bytes 15750000 | tf_op jit(solution)/shard_map/project_more/pallas_call | solution.py:200
  42.5 4.4 %project_attend.2 = (bf16[1024,768]{1,0:T(8,128)(2,1)S(1)}, bf16[2,2,1024,128]{3,2,1,0:T(8,128)(2,1)S(1)}, f32[2,8,512]{2,1,0:T(8,128)S(1)}) custom-call(s32[2]{0:T(128)S(1)} %pad_add_fusion.where_ref, bf16[1024,2048]{1,0:T(8,128)(2,1)S(1)} %get-tuple-element.86.rows_ref.sib_ref, f32[1024,768]{1,0:T(8,128)S(1)} %project_more.3.before_ref, ...), custom_call_target="tpu_custom_call" | custom-call | flops 3249999872 | bytes 22750000 | tf_op jit(solution)/shard_map/project_attend/pallas_call | solution.py:200
  50.9 4.4 %project_attend.3 = (bf16[1024,768]{1,0:T(8,128)(2,1)S(1)}, bf16[2,2,1024,128]{3,2,1,0:T(8,128)(2,1)S(1)}, f32[2,8,512]{2,1,0:T(8,128)S(1)}) custom-call(s32[2]{0:T(128)S(1)} %pad_add_fusion.where_ref, bf16[1024,2048]{1,0:T(8,128)(2,1)S(1)} %get-tuple-element.93.rows_ref.own_ref, f32[1024,768]{1,0:T(8,128)S(1)} %project_more.2.before_ref, ...), custom_call_target="tpu_custom_call" | custom-call | flops 3249999872 | bytes 22750000 | tf_op jit(solution)/shard_map/project_attend/pallas_call | solution.py:200
  61.7 1.7 %pool_score.1 = (f32[32,2048]{1,0:T(8,128)S(1)}, f32[32,128]{1,0:T(8,128)S(1)}, f32[32,128]{1,0:T(8,128)S(1)}, bf16[32,1024]{1,0:T(8,128)(2,1)S(1)}) custom-call(s32[2]{0:T(128)S(1)} %pad_add_fusion.where_ref, f32[16,512]{1,0:T(8,128)S(1)} %bitcast.20, f32[16,512]{1,0:T(8,128)S(1)} %bitcast.18, f32[16,512]{1,0:T(8,128)S(1)} %collective-permute-done.10.own_far_ref, ...), custom_call_target="tpu_custom_call" | custom-call | flops 1000000000 | bytes 7000000 | tf_op jit(solution)/shard_map/pool_score/pallas_call | solution.py:359
  64.1 2.5 %collective-permute-start.27 = (f32[32,128]{1,0:T(8,128)S(1)}, f32[32,128]{1,0:T(8,128)S(1)}, u32[]{:S(2)}, u32[]{:S(2)}) collective-permute-start(f32[32,128]{1,0:T(8,128)S(1)} %get-tuple-element.114.refs_0_), channel_id=1, source_target_pairs={{0,4},{2,6},{4,0},{5,9},{6,2},{7,11},{8,12},{9,5},{10,14},{11,7},{... | collective-permute-start | bytes 49160 | tf_op jit(solution)/shard_map/ppermute | solution.py:653
  66.6 4.0 %collective-permute-start.26 = (f32[32,128]{1,0:T(8,128)S(1)}, f32[32,128]{1,0:T(8,128)S(1)}, u32[]{:S(2)}, u32[]{:S(2)}) collective-permute-start(f32[32,128]{1,0:T(8,128)S(1)} %get-tuple-element.114.refs_0_), channel_id=1, source_target_pairs={{0,2},{2,0},{3,5},{4,6},{5,3},{6,4},{7,9},{8,10},{9,7},{10,8},{11,... | collective-permute-start | bytes 49160 | tf_op jit(solution)/shard_map/ppermute | solution.py:653
  70.7 1.6 %collective-permute-done.26.refs_1_ = f32[32,128]{1,0:T(8,128)S(1)} collective-permute-done((f32[32,128]{1,0:T(8,128)S(1)}, f32[32,128]{1,0:T(8,128)S(1)}, u32[]{:S(2)}, u32[]{:S(2)}) %collective-permute-start.26) | collective-permute-done | bytes 16416 | tf_op jit(solution)/shard_map/ppermute | solution.py:653
  78.3 2.7 %list_grad.1 = (f32[32,512]{1,0:T(8,128)S(1)}, bf16[32,1024]{1,0:T(8,128)(2,1)S(1)}, f32[8,128]{1,0:T(8,128)S(1)}) custom-call(s32[2]{0:T(128)S(1)} %pad_add_fusion.where_ref, s32[5]{0:T(128)S(1)} %stack.35.place_ref, s32[8,128]{1,0:T(8,128)S(1)} %broadcast_in_dim.13.bounds_ref, f32[32,2048]{1,0:T(8,128)S(1)} %copy-done.20, ...), custom_call_target="tpu_custom_call" | custom-call | flops 1250000000 | bytes 8750000 | tf_op jit(solution)/shard_map/list_grad/pallas_call | solution.py:446
  81.6 2.1 %collective-permute-start.30 = (bf16[32,1920]{1,0:T(8,128)(2,1)S(1)}, bf16[32,1920]{1,0:T(8,128)(2,1)S(1)}, u32[]{:S(2)}, u32[]{:S(2)}) collective-permute-start(bf16[32,1920]{1,0:T(8,128)(2,1)S(1)} %out_payload.1.refs_0_), channel_id=1, source_target_pairs={{0,2},{1,3},{2,0},{3,1},{4,6},{5,7},{6,4},{7,5},{8,10},{9,11},{10,... | collective-permute-start | bytes 368648 | tf_op jit(solution)/shard_map/ppermute | solution.py:633
  83.7 3.9 %attend_back.2.d_own_ref = bf16[1024,768]{1,0:T(8,128)(2,1)S(1)} custom-call(s32[2]{0:T(128)S(1)} %pad_add_fusion.where_ref, bf16[2,2,1024,128]{3,2,1,0:T(8,128)(2,1)S(1)} %copy-done.30, bf16[1024,768]{1,0:T(8,128)(2,1)S(1)} %copy-done.26, f32[2,8,512]{2,1,0:T(8,128)S(1)} %get-tuple-element.153.d_ref), custom_call_target="tpu_custom_call" | custom-call | flops 1700000000 | bytes 11900000 | tf_op jit(solution)/shard_map/attend_back/pallas_call | solution.py:200
  89.7 3.9 %attend_back.3.d_sib_ref = bf16[1024,768]{1,0:T(8,128)(2,1)S(1)} custom-call(s32[2]{0:T(128)S(1)} %pad_add_fusion.where_ref, bf16[2,2,1024,128]{3,2,1,0:T(8,128)(2,1)S(1)} %copy-done.28, bf16[1024,768]{1,0:T(8,128)(2,1)S(1)} %copy-done.24, f32[2,8,512]{2,1,0:T(8,128)S(1)} %get-tuple-element.152.d_ref), custom_call_target="tpu_custom_call" | custom-call | flops 1700000000 | bytes 11900000 | tf_op jit(solution)/shard_map/attend_back/pallas_call | solution.py:200
  93.7 2.4 %grad_rows.3 = (bf16[512,384]{1,0:T(8,128)(2,1)S(1)}, bf16[512,384]{1,0:T(8,128)(2,1)S(1)}) custom-call(s32[2]{0:T(128)S(1)} %pad_add_fusion.where_ref, bf16[1024,2048]{1,0:T(8,128)(2,1)S(1)} %copy-done.1, bf16[1024,2048]{1,0:T(8,128)(2,1)S(1)} %copy-done.3, bf16[1024,768]{1,0:T(8,128)(2,1)S(1)} %attend_back.2.d_own_ref, ...), custom_call_target="tpu_custom_call" | custom-call | flops 1250000000 | bytes 8750000 | tf_op jit(solution)/shard_map/grad_rows/pallas_call | solution.py:200
  97.4 1.6 %collective-permute-start.38 = (bf16[512,384]{1,0:T(8,128)(2,1)S(1)}, bf16[512,384]{1,0:T(8,128)(2,1)S(1)}, u32[]{:S(2)}, u32[]{:S(2)}) collective-permute-start(bf16[512,384]{1,0:T(8,128)(2,1)S(1)} %get-tuple-element.124), channel_id=1, source_target_pairs={{0,2},{1,3},{2,0},{3,1},{4,6},{5,7},{6,4},{7,5},{8,10},{9,11},{10,... | collective-permute-start | bytes 1179656 | tf_op jit(solution)/shard_map/ppermute | solution.py:633
  99.1 4.1 %grad_rows.4 = (bf16[512,384]{1,0:T(8,128)(2,1)S(1)}, bf16[512,384]{1,0:T(8,128)(2,1)S(1)}, bf16[512,384]{1,0:T(8,128)(2,1)S(1)}, bf16[512,384]{1,0:T(8,128)(2,1)S(1)}) custom-call(s32[2]{0:T(128)S(1)} %pad_add_fusion.where_ref, bf16[1024,2048]{1,0:T(8,128)(2,1)S(1)} %copy-done.1, bf16[1024,2048]{1,0:T(8,128)(2,1)S(1)} %copy-done.3, ...), custom_call_target="tpu_custom_call" | custom-call | flops 2500000000 | bytes 17500000 | tf_op jit(solution)/shard_map/grad_rows/pallas_call | solution.py:200
  104.6 3.8 %collective-permute-done.38 = bf16[512,384]{1,0:T(8,128)(2,1)S(1)} collective-permute-done((bf16[512,384]{1,0:T(8,128)(2,1)S(1)}, bf16[512,384]{1,0:T(8,128)(2,1)S(1)}, u32[]{:S(2)}, u32[]{:S(2)}) %collective-permute-start.38) | collective-permute-done | bytes 393248 | tf_op jit(solution)/shard_map/ppermute | solution.py:633
  111.4 3.9 %collective-permute-start.36 = (bf16[144,512]{1,0:T(8,128)(2,1)S(1)}, bf16[144,512]{1,0:T(8,128)(2,1)S(1)}, u32[]{:S(2)}, u32[]{:S(2)}) collective-permute-start(bf16[144,512]{1,0:T(8,128)(2,1)S(1)} %get-tuple-element.142), channel_id=1, source_target_pairs={{0,24},{8,16},{16,8},{24,0},{1,25},{9,17},{17,9},{25,1},{2,26},{10... | collective-permute-start | bytes 442376 | tf_op jit(solution)/shard_map/ppermute | solution.py:636
  115.3 2.6 %collective-permute-start.35 = (bf16[144,512]{1,0:T(8,128)(2,1)S(1)}, bf16[144,512]{1,0:T(8,128)(2,1)S(1)}, u32[]{:S(2)}, u32[]{:S(2)}) collective-permute-start(bf16[144,512]{1,0:T(8,128)(2,1)S(1)} %get-tuple-element.143), channel_id=1, source_target_pairs={{0,16},{8,24},{16,0},{24,8},{1,17},{9,25},{17,1},{25,9},{2,18},{10... | collective-permute-start | bytes 442376 | tf_op jit(solution)/shard_map/ppermute | solution.py:636
  117.9 2.5 %collective-permute-start.34 = (bf16[144,512]{1,0:T(8,128)(2,1)S(1)}, bf16[144,512]{1,0:T(8,128)(2,1)S(1)}, u32[]{:S(2)}, u32[]{:S(2)}) collective-permute-start(bf16[144,512]{1,0:T(8,128)(2,1)S(1)} %get-tuple-element.144), channel_id=1, source_target_pairs={{0,8},{8,0},{16,24},{24,16},{1,9},{9,1},{17,25},{25,17},{2,10},{10... | collective-permute-start | bytes 442376 | tf_op jit(solution)/shard_map/ppermute | solution.py:636
  120.4 2.4 %grad_rows.5 = (bf16[512,384]{1,0:T(8,128)(2,1)S(1)}, bf16[512,384]{1,0:T(8,128)(2,1)S(1)}) custom-call(s32[2]{0:T(128)S(1)} %pad_add_fusion.where_ref, bf16[1024,2048]{1,0:T(8,128)(2,1)S(1)} %copy-done.1, bf16[1024,2048]{1,0:T(8,128)(2,1)S(1)} %copy-done.3, bf16[1024,768]{1,0:T(8,128)(2,1)S(1)} %attend_back.2.d_own_ref, ...), custom_call_target="tpu_custom_call" | custom-call | flops 1250000000 | bytes 8750000 | tf_op jit(solution)/shard_map/grad_rows/pallas_call | solution.py:200
  126.3 1.6 %collective-permute-done.43 = bf16[256,768]{1,0:T(8,128)(2,1)S(1)} collective-permute-done((bf16[256,768]{1,0:T(8,128)(2,1)S(1)}, bf16[256,768]{1,0:T(8,128)(2,1)S(1)}, u32[]{:S(2)}, u32[]{:S(2)}) %collective-permute-start.43) | collective-permute-done | bytes 393248 | tf_op jit(solution)/shard_map/ppermute | solution.py:633
  129.5 1.8 %collective-permute-start.46 = (bf16[256,384]{1,0:T(8,128)(2,1)S(1)}, bf16[256,384]{1,0:T(8,128)(2,1)S(1)}, u32[]{:S(2)}, u32[]{:S(2)}) collective-permute-start(bf16[256,384]{1,0:T(8,128)(2,1)S(1)} %get-tuple-element.138), channel_id=1, source_target_pairs={{0,24},{8,16},{16,8},{24,0},{1,25},{9,17},{17,9},{25,1},{2,26},{10... | collective-permute-start | bytes 589832 | tf_op jit(solution)/shard_map/ppermute | solution.py:636
  133.2 2.2 %collective-permute-done.44 = bf16[256,384]{1,0:T(8,128)(2,1)S(1)} collective-permute-done((bf16[256,384]{1,0:T(8,128)(2,1)S(1)}, bf16[256,384]{1,0:T(8,128)(2,1)S(1)}, u32[]{:S(2)}, u32[]{:S(2)}) %collective-permute-start.44) | collective-permute-done | bytes 196640 | tf_op jit(solution)/shard_map/ppermute | solution.py:636
  135.4 5.9 %collective-permute-done.46 = bf16[256,384]{1,0:T(8,128)(2,1)S(1)} collective-permute-done((bf16[256,384]{1,0:T(8,128)(2,1)S(1)}, bf16[256,384]{1,0:T(8,128)(2,1)S(1)}, u32[]{:S(2)}, u32[]{:S(2)}) %collective-permute-start.46) | collective-permute-done | bytes 196640 | tf_op jit(solution)/shard_map/ppermute | solution.py:636
  141.3 8.0 %collective-permute-done.45 = bf16[256,384]{1,0:T(8,128)(2,1)S(1)} collective-permute-done((bf16[256,384]{1,0:T(8,128)(2,1)S(1)}, bf16[256,384]{1,0:T(8,128)(2,1)S(1)}, u32[]{:S(2)}, u32[]{:S(2)}) %collective-permute-start.45) | collective-permute-done | bytes 196640 | tf_op jit(solution)/shard_map/ppermute | solution.py:636
  (188 shorter events, 45.9 us)
Async XLA Ops:
  3.3 22.3 %collective-permute-start.1 = (bf16[16,64,2048]{2,1,0:T(8,128)(2,1)}, bf16[16,64,2048]{2,1,0:T(8,128)(2,1)}, u32[]{:S(2)}, u32[]{:S(2)}) collective-permute-start(bf16[16,64,2048]{2,1,0:T(8,128)(2,1)} %hidden_ref.1), channel_id=1, source_target_pairs={{0,1},{1,0},{2,3},{3,2},{4,5},{5,4},{6,7},{7,6},{8,9},{9,8},{10,11... | collective-permute-start | bytes 12582920 | tf_op jit(solution)/shard_map/ppermute | solution.py:633
  3.6 18.2 %collective-permute-start.2 = (bf16[128,2048]{1,0:T(8,128)(2,1)}, bf16[128,2048]{1,0:T(8,128)(2,1)S(1)}, u32[]{:S(2)}, u32[]{:S(2)}) collective-permute-start(bf16[128,2048]{1,0:T(8,128)(2,1)} %param.12), channel_id=1, source_target_pairs={{0,1},{1,0},{2,3},{3,2},{4,5},{5,4},{6,7},{7,6},{8,9},{9,8},{10,11... | collective-permute-start | bytes 1572872 | tf_op jit(solution)/shard_map/ppermute | solution.py:633
  5.7 12.3 %collective-permute-start.4 = (bf16[512,384]{1,0:T(8,128)(2,1)S(1)}, bf16[512,384]{1,0:T(8,128)(2,1)S(1)}, u32[]{:S(2)}, u32[]{:S(2)}) collective-permute-start(bf16[512,384]{1,0:T(8,128)(2,1)S(1)} %get-tuple-element.85.a_ref), channel_id=1, source_target_pairs={{0,2},{1,3},{2,0},{3,1},{4,6},{5,7},{6,4},{7,5},{8,10},{9,11},{10,... | collective-permute-start | bytes 1179656 | tf_op jit(solution)/shard_map/ppermute | solution.py:633
  8.7 11.2 %collective-permute-start.5 = (bf16[512,384]{1,0:T(8,128)(2,1)S(1)}, bf16[512,384]{1,0:T(8,128)(2,1)S(1)}, u32[]{:S(2)}, u32[]{:S(2)}) collective-permute-start(bf16[512,384]{1,0:T(8,128)(2,1)S(1)} %get-tuple-element.84.b_ref), channel_id=1, source_target_pairs={{0,4},{1,5},{2,6},{3,7},{4,0},{5,1},{6,2},{7,3},{8,12},{9,13},{10,... | collective-permute-start | bytes 1179656 | tf_op jit(solution)/shard_map/ppermute | solution.py:633
  18.1 14.2 %collective-permute-start.7 = (bf16[512,384]{1,0:T(8,128)(2,1)S(1)}, bf16[512,384]{1,0:T(8,128)(2,1)S(1)}, u32[]{:S(2)}, u32[]{:S(2)}) collective-permute-start(bf16[512,384]{1,0:T(8,128)(2,1)S(1)} %get-tuple-element.85.a_ref), channel_id=1, source_target_pairs={{0,4},{1,5},{2,6},{3,7},{4,0},{5,1},{6,2},{7,3},{8,12},{9,13},{10,... | collective-permute-start | bytes 1179656 | tf_op jit(solution)/shard_map/ppermute | solution.py:633
  19.8 12.4 %collective-permute-start.6 = (bf16[512,384]{1,0:T(8,128)(2,1)S(1)}, bf16[512,384]{1,0:T(8,128)(2,1)S(1)}, u32[]{:S(2)}, u32[]{:S(2)}) collective-permute-start(bf16[512,384]{1,0:T(8,128)(2,1)S(1)} %get-tuple-element.84.b_ref), channel_id=1, source_target_pairs={{0,2},{1,3},{2,0},{3,1},{4,6},{5,7},{6,4},{7,5},{8,10},{9,11},{10,... | collective-permute-start | bytes 1179656 | tf_op jit(solution)/shard_map/ppermute | solution.py:633
  21.3 20.1 %collective-permute-start.8 = (bf16[512,384]{1,0:T(8,128)(2,1)S(1)}, bf16[512,384]{1,0:T(8,128)(2,1)S(1)}, u32[]{:S(2)}, u32[]{:S(2)}) collective-permute-start(bf16[512,384]{1,0:T(8,128)(2,1)S(1)} %collective-permute-done.4.refs_0_), channel_id=1, source_target_pairs={{0,4},{1,5},{2,6},{3,7},{4,0},{5,1},{6,2},{7,3},{8,12},{9,13},{10,... | collective-permute-start | bytes 1179656 | tf_op jit(solution)/shard_map/ppermute | solution.py:633
  24.3 18.2 %collective-permute-start.9 = (bf16[512,384]{1,0:T(8,128)(2,1)S(1)}, bf16[512,384]{1,0:T(8,128)(2,1)S(1)}, u32[]{:S(2)}, u32[]{:S(2)}) collective-permute-start(bf16[512,384]{1,0:T(8,128)(2,1)S(1)} %collective-permute-done.5.refs_3_), channel_id=1, source_target_pairs={{0,2},{1,3},{2,0},{3,1},{4,6},{5,7},{6,4},{7,5},{8,10},{9,11},{10,... | collective-permute-start | bytes 1179656 | tf_op jit(solution)/shard_map/ppermute | solution.py:633
  32.3 15.5 %collective-permute-start.19 = (bf16[256,512]{1,0:T(8,128)(2,1)S(1)}, bf16[256,512]{1,0:T(8,128)(2,1)S(1)}, u32[]{:S(2)}, u32[]{:S(2)}) collective-permute-start(bf16[256,512]{1,0:T(8,128)(2,1)S(1)} %get-tuple-element.102.refs_1_.refs_6_), channel_id=1, source_target_pairs={{0,4},{1,5},{2,6},{3,7},{4,0},{5,1},{6,2},{7,3},{8,12},{9,13},{10,... | collective-permute-start | bytes 786440 | tf_op jit(solution)/shard_map/ppermute | solution.py:633
  33.2 23.1 %collective-permute-start.15 = (bf16[256,512]{1,0:T(8,128)(2,1)S(1)}, bf16[256,512]{1,0:T(8,128)(2,1)S(1)}, u32[]{:S(2)}, u32[]{:S(2)}) collective-permute-start(bf16[256,512]{1,0:T(8,128)(2,1)S(1)} %get-tuple-element.102.refs_1_.refs_6_), channel_id=1, source_target_pairs={{0,2},{1,3},{2,0},{3,1},{4,6},{5,7},{6,4},{7,5},{8,10},{9,11},{10,... | collective-permute-start | bytes 786440 | tf_op jit(solution)/shard_map/ppermute | solution.py:633
  37.6 19.2 %collective-permute-start.18 = (bf16[256,512]{1,0:T(8,128)(2,1)S(1)}, bf16[256,512]{1,0:T(8,128)(2,1)S(1)}, u32[]{:S(2)}, u32[]{:S(2)}) collective-permute-start(bf16[256,512]{1,0:T(8,128)(2,1)S(1)} %get-tuple-element.101.refs_0_.refs_5_), channel_id=1, source_target_pairs={{0,4},{1,5},{2,6},{3,7},{4,0},{5,1},{6,2},{7,3},{8,12},{9,13},{10,... | collective-permute-start | bytes 786440 | tf_op jit(solution)/shard_map/ppermute | solution.py:633
  41.5 8.1 %collective-permute-start.14 = (bf16[256,512]{1,0:T(8,128)(2,1)S(1)}, bf16[256,512]{1,0:T(8,128)(2,1)S(1)}, u32[]{:S(2)}, u32[]{:S(2)}) collective-permute-start(bf16[256,512]{1,0:T(8,128)(2,1)S(1)} %get-tuple-element.101.refs_0_.refs_5_), channel_id=1, source_target_pairs={{0,2},{1,3},{2,0},{3,1},{4,6},{5,7},{6,4},{7,5},{8,10},{9,11},{10,... | collective-permute-start | bytes 786440 | tf_op jit(solution)/shard_map/ppermute | solution.py:633
  47.8 9.1 %collective-permute-start.23 = (bf16[256,512]{1,0:T(8,128)(2,1)S(1)}, bf16[256,512]{1,0:T(8,128)(2,1)S(1)}, u32[]{:S(2)}, u32[]{:S(2)}) collective-permute-start(bf16[256,512]{1,0:T(8,128)(2,1)S(1)} %collective-permute-done.19.refs_9_.refs_14_), channel_id=1, source_target_pairs={{0,2},{1,3},{2,0},{3,1},{4,6},{5,7},{6,4},{7,5},{8,10},{9,11},{10,... | collective-permute-start | bytes 786440 | tf_op jit(solution)/shard_map/ppermute | solution.py:633
  49.6 7.8 %collective-permute-start.22 = (bf16[256,512]{1,0:T(8,128)(2,1)S(1)}, bf16[256,512]{1,0:T(8,128)(2,1)S(1)}, u32[]{:S(2)}, u32[]{:S(2)}) collective-permute-start(bf16[256,512]{1,0:T(8,128)(2,1)S(1)} %collective-permute-done.14.refs_4_.refs_9_), channel_id=1, source_target_pairs={{0,4},{1,5},{2,6},{3,7},{4,0},{5,1},{6,2},{7,3},{8,12},{9,13},{10,... | collective-permute-start | bytes 786440 | tf_op jit(solution)/shard_map/ppermute | solution.py:633
  64.1 6.6 %collective-permute-start.27 = (f32[32,128]{1,0:T(8,128)S(1)}, f32[32,128]{1,0:T(8,128)S(1)}, u32[]{:S(2)}, u32[]{:S(2)}) collective-permute-start(f32[32,128]{1,0:T(8,128)S(1)} %get-tuple-element.114.refs_0_), channel_id=1, source_target_pairs={{0,4},{2,6},{4,0},{5,9},{6,2},{7,11},{8,12},{9,5},{10,14},{11,7},{... | collective-permute-start | bytes 49160 | tf_op jit(solution)/shard_map/ppermute | solution.py:653
  66.6 5.7 %collective-permute-start.26 = (f32[32,128]{1,0:T(8,128)S(1)}, f32[32,128]{1,0:T(8,128)S(1)}, u32[]{:S(2)}, u32[]{:S(2)}) collective-permute-start(f32[32,128]{1,0:T(8,128)S(1)} %get-tuple-element.114.refs_0_), channel_id=1, source_target_pairs={{0,2},{2,0},{3,5},{4,6},{5,3},{6,4},{7,9},{8,10},{9,7},{10,8},{11,... | collective-permute-start | bytes 49160 | tf_op jit(solution)/shard_map/ppermute | solution.py:653
  81.6 6.0 %collective-permute-start.30 = (bf16[32,1920]{1,0:T(8,128)(2,1)S(1)}, bf16[32,1920]{1,0:T(8,128)(2,1)S(1)}, u32[]{:S(2)}, u32[]{:S(2)}) collective-permute-start(bf16[32,1920]{1,0:T(8,128)(2,1)S(1)} %out_payload.1.refs_0_), channel_id=1, source_target_pairs={{0,2},{1,3},{2,0},{3,1},{4,6},{5,7},{6,4},{7,5},{8,10},{9,11},{10,... | collective-permute-start | bytes 368648 | tf_op jit(solution)/shard_map/ppermute | solution.py:633
  87.6 11.3 %collective-permute-start.31 = (bf16[32,1920]{1,0:T(8,128)(2,1)S(1)}, bf16[32,1920]{1,0:T(8,128)(2,1)S(1)}, u32[]{:S(2)}, u32[]{:S(2)}) collective-permute-start(bf16[32,1920]{1,0:T(8,128)(2,1)S(1)} %out_payload.1.refs_0_), channel_id=1, source_target_pairs={{0,4},{1,5},{2,6},{3,7},{4,0},{5,1},{6,2},{7,3},{8,12},{9,13},{10,... | collective-permute-start | bytes 368648 | tf_op jit(solution)/shard_map/ppermute | solution.py:633
  88.9 10.1 %collective-permute-start.32 = (bf16[32,1920]{1,0:T(8,128)(2,1)S(1)}, bf16[32,1920]{1,0:T(8,128)(2,1)S(1)}, u32[]{:S(2)}, u32[]{:S(2)}) collective-permute-start(bf16[32,1920]{1,0:T(8,128)(2,1)S(1)} %collective-permute-done.30.refs_1_), channel_id=1, source_target_pairs={{0,4},{1,5},{2,6},{3,7},{4,0},{5,1},{6,2},{7,3},{8,12},{9,13},{10,... | collective-permute-start | bytes 368648 | tf_op jit(solution)/shard_map/ppermute | solution.py:633
  96.1 12.5 %collective-permute-start.40 = (bf16[512,384]{1,0:T(8,128)(2,1)S(1)}, bf16[512,384]{1,0:T(8,128)(2,1)S(1)}, u32[]{:S(2)}, u32[]{:S(2)}) collective-permute-start(bf16[512,384]{1,0:T(8,128)(2,1)S(1)} %get-tuple-element.129), channel_id=1, source_target_pairs={{0,4},{1,5},{2,6},{3,7},{4,0},{5,1},{6,2},{7,3},{8,12},{9,13},{10,... | collective-permute-start | bytes 1179656 | tf_op jit(solution)/shard_map/ppermute | solution.py:633
  97.4 11.1 %collective-permute-start.38 = (bf16[512,384]{1,0:T(8,128)(2,1)S(1)}, bf16[512,384]{1,0:T(8,128)(2,1)S(1)}, u32[]{:S(2)}, u32[]{:S(2)}) collective-permute-start(bf16[512,384]{1,0:T(8,128)(2,1)S(1)} %get-tuple-element.124), channel_id=1, source_target_pairs={{0,2},{1,3},{2,0},{3,1},{4,6},{5,7},{6,4},{7,5},{8,10},{9,11},{10,... | collective-permute-start | bytes 1179656 | tf_op jit(solution)/shard_map/ppermute | solution.py:633
  99.0 11.2 %collective-permute-start.33 = (bf16[128,1920]{1,0:T(8,128)(2,1)S(1)}, bf16[128,1920]{1,0:T(8,128)(2,1)S(1)}, u32[]{:S(2)}, u32[]{:S(2)}) collective-permute-start(bf16[128,1920]{1,0:T(8,128)(2,1)S(1)} %pad_maximum_fusion.1), channel_id=1, source_target_pairs={{0,1},{1,0},{2,3},{3,2},{4,5},{5,4},{6,7},{7,6},{8,9},{9,8},{10,11... | collective-permute-start | bytes 1474568 | tf_op jit(solution)/shard_map/ppermute | solution.py:633
  103.2 12.1 %collective-permute-start.39 = (bf16[512,384]{1,0:T(8,128)(2,1)S(1)}, bf16[512,384]{1,0:T(8,128)(2,1)S(1)}, u32[]{:S(2)}, u32[]{:S(2)}) collective-permute-start(bf16[512,384]{1,0:T(8,128)(2,1)S(1)} %get-tuple-element.128), channel_id=1, source_target_pairs={{0,4},{1,5},{2,6},{3,7},{4,0},{5,1},{6,2},{7,3},{8,12},{9,13},{10,... | collective-permute-start | bytes 1179656 | tf_op jit(solution)/shard_map/ppermute | solution.py:633
  104.0 13.9 %collective-permute-start.37 = (bf16[512,384]{1,0:T(8,128)(2,1)S(1)}, bf16[512,384]{1,0:T(8,128)(2,1)S(1)}, u32[]{:S(2)}, u32[]{:S(2)}) collective-permute-start(bf16[512,384]{1,0:T(8,128)(2,1)S(1)} %get-tuple-element.126), channel_id=1, source_target_pairs={{0,2},{1,3},{2,0},{3,1},{4,6},{5,7},{6,4},{7,5},{8,10},{9,11},{10,... | collective-permute-start | bytes 1179656 | tf_op jit(solution)/shard_map/ppermute | solution.py:633
  108.6 14.8 %collective-permute-start.41 = (bf16[512,384]{1,0:T(8,128)(2,1)S(1)}, bf16[512,384]{1,0:T(8,128)(2,1)S(1)}, u32[]{:S(2)}, u32[]{:S(2)}) collective-permute-start(bf16[512,384]{1,0:T(8,128)(2,1)S(1)} %add_convert_fusion.4), channel_id=1, source_target_pairs={{0,4},{1,5},{2,6},{3,7},{4,0},{5,1},{6,2},{7,3},{8,12},{9,13},{10,... | collective-permute-start | bytes 1179656 | tf_op jit(solution)/shard_map/ppermute | solution.py:633
  108.8 15.7 %collective-permute-start.42 = (bf16[512,384]{1,0:T(8,128)(2,1)S(1)}, bf16[512,384]{1,0:T(8,128)(2,1)S(1)}, u32[]{:S(2)}, u32[]{:S(2)}) collective-permute-start(bf16[512,384]{1,0:T(8,128)(2,1)S(1)} %add_convert_fusion.3), channel_id=1, source_target_pairs={{0,2},{1,3},{2,0},{3,1},{4,6},{5,7},{6,4},{7,5},{8,10},{9,11},{10,... | collective-permute-start | bytes 1179656 | tf_op jit(solution)/shard_map/ppermute | solution.py:633
  111.4 13.2 %collective-permute-start.36 = (bf16[144,512]{1,0:T(8,128)(2,1)S(1)}, bf16[144,512]{1,0:T(8,128)(2,1)S(1)}, u32[]{:S(2)}, u32[]{:S(2)}) collective-permute-start(bf16[144,512]{1,0:T(8,128)(2,1)S(1)} %get-tuple-element.142), channel_id=1, source_target_pairs={{0,24},{8,16},{16,8},{24,0},{1,25},{9,17},{17,9},{25,1},{2,26},{10... | collective-permute-start | bytes 442376 | tf_op jit(solution)/shard_map/ppermute | solution.py:636
  115.3 10.3 %collective-permute-start.35 = (bf16[144,512]{1,0:T(8,128)(2,1)S(1)}, bf16[144,512]{1,0:T(8,128)(2,1)S(1)}, u32[]{:S(2)}, u32[]{:S(2)}) collective-permute-start(bf16[144,512]{1,0:T(8,128)(2,1)S(1)} %get-tuple-element.143), channel_id=1, source_target_pairs={{0,16},{8,24},{16,0},{24,8},{1,17},{9,25},{17,1},{25,9},{2,18},{10... | collective-permute-start | bytes 442376 | tf_op jit(solution)/shard_map/ppermute | solution.py:636
  117.9 7.8 %collective-permute-start.34 = (bf16[144,512]{1,0:T(8,128)(2,1)S(1)}, bf16[144,512]{1,0:T(8,128)(2,1)S(1)}, u32[]{:S(2)}, u32[]{:S(2)}) collective-permute-start(bf16[144,512]{1,0:T(8,128)(2,1)S(1)} %get-tuple-element.144), channel_id=1, source_target_pairs={{0,8},{8,0},{16,24},{24,16},{1,9},{9,1},{17,25},{25,17},{2,10},{10... | collective-permute-start | bytes 442376 | tf_op jit(solution)/shard_map/ppermute | solution.py:636
  128.4 7.0 %collective-permute-start.44 = (bf16[256,384]{1,0:T(8,128)(2,1)S(1)}, bf16[256,384]{1,0:T(8,128)(2,1)S(1)}, u32[]{:S(2)}, u32[]{:S(2)}) collective-permute-start(bf16[256,384]{1,0:T(8,128)(2,1)S(1)} %get-tuple-element.137), channel_id=1, source_target_pairs={{0,8},{8,0},{16,24},{24,16},{1,9},{9,1},{17,25},{25,17},{2,10},{10... | collective-permute-start | bytes 589832 | tf_op jit(solution)/shard_map/ppermute | solution.py:636
  129.5 11.8 %collective-permute-start.46 = (bf16[256,384]{1,0:T(8,128)(2,1)S(1)}, bf16[256,384]{1,0:T(8,128)(2,1)S(1)}, u32[]{:S(2)}, u32[]{:S(2)}) collective-permute-start(bf16[256,384]{1,0:T(8,128)(2,1)S(1)} %get-tuple-element.138), channel_id=1, source_target_pairs={{0,24},{8,16},{16,8},{24,0},{1,25},{9,17},{17,9},{25,1},{2,26},{10... | collective-permute-start | bytes 589832 | tf_op jit(solution)/shard_map/ppermute | solution.py:636
  131.3 18.0 %collective-permute-start.45 = (bf16[256,384]{1,0:T(8,128)(2,1)S(1)}, bf16[256,384]{1,0:T(8,128)(2,1)S(1)}, u32[]{:S(2)}, u32[]{:S(2)}) collective-permute-start(bf16[256,384]{1,0:T(8,128)(2,1)S(1)} %get-tuple-element.139), channel_id=1, source_target_pairs={{0,16},{8,24},{16,0},{24,8},{1,17},{9,25},{17,1},{25,9},{2,18},{10... | collective-permute-start | bytes 589832 | tf_op jit(solution)/shard_map/ppermute | solution.py:636
  (53 other events, 257.0 us)

commit v7 on v6

--- a/solution.py
+++ b/solution.py
@@ -313,7 +313,7 @@
 def score_kernel(chips, where_ref, own_ref, sib_ref, own_far_ref, sib_far_ref, sum_ref, sib_sum_ref,
                  final_ref, ws_ref, prior_ref, prior_sib_ref, *refs):
     pieces, refs = refs[: 4 * chips], refs[4 * chips :]
-    unit_ref, inverse_ref, score_ref, attn_ref, product_ref = refs
+    score_ref, attn_ref, d_att_ref, d_rows_ref, product_ref = refs
     chip, core = where_ref[0], where_ref[1]
     mine = jnp.concatenate([own_ref[...], sib_ref[...]], 0)
     other = jnp.concatenate([own_far_ref[...], sib_far_ref[...]], 0)
@@ -342,13 +342,27 @@
     pooled = (jnp.concatenate(sums, 0) + product) * (1.0 / PASSAGE_LEN)
     inverse = lax.rsqrt(jnp.mean(pooled * pooled, -1, keepdims=True) + epsilon)
     unit = pooled * inverse
-    score = jnp.sum(unit * (final_ref[...] * ws_ref[...]), -1, keepdims=True)
-    unit_ref[...] = unit
-    inverse_ref[...] = jnp.broadcast_to(inverse, inverse_ref.shape)
+    direction = final_ref[...] * ws_ref[...]
+    score = jnp.sum(unit * direction, -1, keepdims=True)
     lane = lax.broadcasted_iota(jnp.int32, score_ref.shape, 1)
     half = score_ref.shape[1] // 2
     prior = jnp.concatenate([prior_ref[...], prior_sib_ref[...]], 0)
     score_ref[...] = jnp.where(lane < half, score, 0.0) + prior
+
+    mean = jnp.mean(unit * direction, -1, keepdims=True)
+    d_rows = inverse * (direction - unit * mean) * (1.0 / PASSAGE_LEN)
+    half = d_rows.shape[1] // 2
+    own = jnp.where(core == 0, d_rows[:, :half], d_rows[:, half:])
+    far = jnp.where(core == 0, d_rows[:, half:], d_rows[:, :half])
+    d_rows_ref[...] = own
+    cut = [x.astype(BF16) for x in (own[:, :part], own[:, part:], far[:, :part], far[:, part:])]
+    for s in range(chips):
+        back = sum(mm(cut[k], pieces[4 * s + k][...], ((1,), (1,))) for k in range(4))
+        start = pl.multiple_of((chip ^ s) * depth, depth)
+        product_ref[:count, pl.ds(start, depth)] = back.astype(BF16).astype(F32)
+    back = product_ref[:count]
+    half = back.shape[1] // 2
+    d_att_ref[...] = jnp.where(core == 0, back[:, :half], back[:, half:])
 
 
 def score_pass(where, attn, sums, final_gain, w_score, priors, pieces):
@@ -361,10 +375,10 @@
         in_specs=[pl.BlockSpec(memory_space=pltpu.SMEM)] + [vmem] * (10 + len(pieces)),
         out_specs=[vmem] * 4,
         out_shape=[
-            jax.ShapeDtypeStruct((count, width), F32),
-            jax.ShapeDtypeStruct((count, lanes), F32),
             jax.ShapeDtypeStruct((count, lanes), F32),
             jax.ShapeDtypeStruct((count, inner), BF16),
+            jax.ShapeDtypeStruct((count, inner // 2), F32),
+            jax.ShapeDtypeStruct((count, width // 2), F32),
         ],
         scratch_shapes=[pltpu.VMEM((2 * count, inner), F32)],
         compiler_params=pltpu.CompilerParams(vmem_limit_bytes=SMALL),
@@ -373,12 +387,11 @@
     )(where, *attn, *sums, final_gain[None], w_score[None], *priors, *pieces)
 
 
-def list_kernel(blocks, chips, passages, where_ref, place_ref, bounds_ref, unit_ref, inverse_ref,
-                final_ref, ws_ref, *refs):
+def list_kernel(blocks, passages, where_ref, place_ref, bounds_ref, rows_ref, own_ref, sib_ref,
+                *refs):
     scores = [ref[...] for ref in refs[:blocks]]
-    pieces, refs = refs[blocks : blocks + 4 * chips], refs[blocks + 4 * chips :]
-    d_att_ref, d_rows_ref, loss_ref, back_ref = refs
-    chip, core = where_ref[0], where_ref[1]
+    d_rows_ref, loss_ref, d_own_ref, d_sib_ref = refs[blocks:]
+    core = where_ref[1]
     pair = 2 * passages
     lanes = bounds_ref.shape[1]
     lane = lax.broadcasted_iota(jnp.int32, bounds_ref.shape, 1)
@@ -414,50 +427,32 @@
     target = heavy[0][:, :1] / jnp.sum(jnp.where(own, label_total, 0.0), 1, keepdims=True)
     loss = -loss_scale * jnp.sum((target * log_prob)[:passages], 0, keepdims=True)
     d_score = loss_scale * (jnp.exp(log_prob) - target)
-    unit = unit_ref[...]
-    d_unit = d_score * (ws_ref[...] * final_ref[...])
-    mean = jnp.mean(d_unit * unit, -1, keepdims=True)
-    d_pooled = inverse_ref[:, :1] * (d_unit - unit * mean)
-    depth, part = pieces[0].shape
-    half = d_pooled.shape[1] // 2
-    own = jnp.where(core == 0, d_pooled[:, :half], d_pooled[:, half:])
-    far = jnp.where(core == 0, d_pooled[:, half:], d_pooled[:, :half])
-    cut = [own[:, :part], own[:, part:], far[:, :part], far[:, part:]]
-    cut = [(x * (1.0 / PASSAGE_LEN)).astype(BF16) for x in cut]
-    for s in range(chips):
-        back = sum(mm(cut[k], pieces[4 * s + k][...], ((1,), (1,))) for k in range(4))
-        start = pl.multiple_of((chip ^ s) * depth, depth)
-        back_ref[:, pl.ds(start, depth)] = back.astype(BF16).astype(F32)
-    back = back_ref[...]
-    half = back.shape[1] // 2
-    d_att_ref[...] = jnp.where(core == 0, back[:, :half], back[:, half:])
     loss_ref[...] = jnp.broadcast_to(loss, loss_ref.shape)
-    d_rows_ref[:, :part] = cut[0]
-    d_rows_ref[:, part:] = cut[1]
-
-
-def list_pass(where, places, bounds, unit, inverse, final_gain, w_score, scores, pieces,
-              passages):
-    count, width = unit.shape
-    chips = len(pieces) // 4
-    inner = chips * pieces[0].shape[0]
+    d_rows_ref[...] = (rows_ref[...] * d_score).astype(BF16)
+    for k, (ref, out_ref) in enumerate(((own_ref, d_own_ref), (sib_ref, d_sib_ref))):
+        for i in range(passages):
+            rows = slice(i * PASSAGE_LEN, (i + 1) * PASSAGE_LEN)
+            at = k * passages + i
+            out_ref[rows] = (ref[rows].astype(F32) * d_score[at : at + 1]).astype(BF16)
+
+
+def list_pass(where, places, bounds, rows, d_own, d_sib, scores):
     vmem = pl.BlockSpec(memory_space=pltpu.VMEM)
     smem = pl.BlockSpec(memory_space=pltpu.SMEM)
     return pl.pallas_call(
-        functools.partial(list_kernel, len(scores), chips, passages),
-        in_specs=[smem] * 2 + [vmem] * (5 + len(scores) + len(pieces)),
-        out_specs=[vmem] * 3,
+        functools.partial(list_kernel, len(scores), rows.shape[0] // 2),
+        in_specs=[smem] * 2 + [vmem] * (4 + len(scores)),
+        out_specs=[vmem] * 4,
         out_shape=[
-            jax.ShapeDtypeStruct((count, inner // 2), F32),
-            jax.ShapeDtypeStruct((count, width // 2), BF16),
+            jax.ShapeDtypeStruct(rows.shape, BF16),
             jax.ShapeDtypeStruct((8, 128), F32),
+            jax.ShapeDtypeStruct(d_own.shape, BF16),
+            jax.ShapeDtypeStruct(d_sib.shape, BF16),
         ],
-        scratch_shapes=[pltpu.VMEM((count, inner), F32)],
         compiler_params=pltpu.CompilerParams(vmem_limit_bytes=SMALL),
         cost_estimate=cost(2.5),
         name="list_grad",
-    )(where, places, bounds, unit, inverse, final_gain[None], w_score[None], *scores,
-      *pieces)
+    )(where, places, bounds, rows, d_own, d_sib, *scores)
 
 
 def payload_kernel(passages, where_ref, attn_ref, d_rows_ref, loss_ref, out_ref):
@@ -766,7 +761,7 @@
             pieces += [out_a[s], out_b[s]]
             gate = probs_own
             pieces += [across(after(x, gate), 1) for x in (out_a[s], out_b[s])]
-        unit, inverse, score, attn = score_pass(
+        score, attn, d_attended, direction = score_pass(
             where,
             (attn_own, attn_sib, attn_sib_other, attn_own_other),
             (sums, sums_sib),
@@ -777,15 +772,15 @@
         )
         near = [neighbour(score, kind) for kind in (0, 2)]
         scores = [score] + near + [across(x, 1) for x in near]
-        d_attended, d_rows, loss_part = list_pass(
-            where, places, bounds, unit, inverse, final_gain, w_score, scores, pieces, passages
-        )
-
         d_own = backward(where, probs_own, proj_own, d_attended[:passages], groups)
-        payload = payload_pass(where, attn, d_rows, loss_part)
         d_sib = backward(
             where, after(probs_sib, d_own), proj_sib, d_attended[passages:], groups
         )
+        d_rows, loss_part, d_own, d_sib = list_pass(
+            where, places, bounds, direction, d_own, d_sib, scores
+        )
+        inner = attn.shape[1]
+        payload = payload_pass(where, attn, d_rows, loss_part)
         depth = pair_a.shape[0]
         flag_a, flag_b = bits[0] >> 1, bits[-1] >> 1
         lead = [s for s in range(chips) if s & flag_a and s & flag_b]
@@ -798,8 +793,7 @@
         parts_a, parts_b = grads(lead)
         first_a = {s ^ flag_a: across(parts_a[s], bits[0]) for s in lead}
         first_b = {s ^ flag_b: across(parts_b[s], bits[-1]) for s in lead}
-        plane = gathered(payload, bits)
-        plane = [plane[s] for s in range(chips)]
+        plane = [payload] + [across(payload, 2 * s) for s in range(1, chips)]
         more_a, more_b = grads(rest, parts_a, plane)
         far = across(jnp.concatenate(plane, 0), 1)
         for s in rest:
@@ -807,7 +801,7 @@
                 first_a[s ^ flag_a] = across(more_a[s], bits[0])
             if s & flag_b:
                 first_b[s ^ flag_b] = across(more_b[s], bits[-1])
-        own_a, own_b = grads([0], more_a, first_a, first_b)
+        own_a, own_b = grads([0], more_a, first_a, first_b, far)
         parts_a.update(more_a)
         parts_b.update(more_b)
         parts_a.update(own_a)

time: 151 us -> 149 us (0.987)
    ppermute x6, waiting for transfers between devices: 17.4 us -> 19.8 us  [along(): lax.ppermute(value, 'list', [(i, i ^ distance) for i in range(n_list)])]
    unnamed x72 -> x44, local copies, waits for them, and re-layouts: 9.88 us -> 7.6 us
    ppermute x6, starting transfers between devices: 12.5 us -> 10.6 us  [along(): lax.ppermute(value, 'list', [(i, i ^ distance) for i in range(n_list)])]
    ppermute x39, starting transfers between devices: 29.9 us -> 31.5 us  [across(): lax.ppermute(value, 'fsdp', [(i, i ^ distance) for i in range(n_fsdp)])]
    ppermute x2, waiting for transfers between devices: 1.62 us -> 0.01 us  [neighbour(): return lax.ppermute(value, ('list', 'fsdp'), moves)]
  transfers between devices with their start and end apart: 47 -> 47, of which waited for: 20 -> 18; matrix products, arithmetic and copies ran while one was open for 2% -> 2% of each run, Pallas kernels for 31% -> 32%
where the time goes in v7:
time: 149 us
  Pallas kernels  52.5 us (35%)
  starting transfers between devices  48.6 us (33%)
  waiting for transfers between devices  33.6 us (23%)
  local copies, waits for them, and re-layouts  9.4 us (6%)
  other arithmetic  3.36 us (2%)
    ppermute x39, starting transfers between devices, across(): lax.ppermute(value, 'fsdp', [(i, i ^ distance) for i in range(n_fsdp)])  31.5 us
    pallas_call x9, Pallas kernels, local_call(): pl.pallas_call(kernel, in_specs=[pl.BlockSpec(memory_space=pltpu.SMEM)] +...  31.3 us
    ppermute x6, waiting for transfers between devices, along(): lax.ppermute(value, 'list', [(i, i ^ distance) for i in range(n_list)])  19.8 us
    ppermute x39, waiting for transfers between devices, across(): lax.ppermute(value, 'fsdp', [(i, i ^ distance) for i in range(n_fsdp)])  13.8 us
    pallas_call x2, Pallas kernels, norm(): pl.pallas_call(norm_kernel, grid_spec=pltpu.PrefetchScalarGridSpec(num_sc...  13.1 us
    ppermute x6, starting transfers between devices, along(): lax.ppermute(value, 'list', [(i, i ^ distance) for i in range(n_list)])  10.6 us
    unnamed x44, local copies, waits for them, and re-layouts  7.6 us
    ppermute x2, starting transfers between devices, neighbour(): return lax.ppermute(value, ('list', 'fsdp'), moves)  6.45 us
  transfers between devices with their start and end apart: 47, of which 18 were waited for; matrix products, arithmetic and copies ran while one was open for 2% of the time, Pallas kernels for 32%

profile of v7, /device:TPU:0, one launch (start us, length us, event | category | flops | bytes accessed | tf_op | source)
XLA Modules:
  0.0 148.7 jit_solution(5435751831670527279)
XLA Ops:
  1.1 2.1 %collective-permute-done.come_ref = bf16[256,1536]{1,0:T(8,128)(2,1)S(1)} collective-permute-done((bf16[256,1536]{1,0:T(8,128)(2,1)}, bf16[256,1536]{1,0:T(8,128)(2,1)S(1)}, u32[]{:S(2)}, u32[]{:S(2)}) %collective-permute-start) | collective-permute-done | bytes 786464 | tf_op jit(solution)/shard_map/ppermute | solution.py:628
  5.7 2.9 %collective-permute-start.4 = (bf16[512,384]{1,0:T(8,128)(2,1)S(1)}, bf16[512,384]{1,0:T(8,128)(2,1)S(1)}, u32[]{:S(2)}, u32[]{:S(2)}) collective-permute-start(bf16[512,384]{1,0:T(8,128)(2,1)S(1)} %get-tuple-element.84.a_ref), channel_id=1, source_target_pairs={{0,2},{1,3},{2,0},{3,1},{4,6},{5,7},{6,4},{7,5},{8,10},{9,11},{10,... | collective-permute-start | bytes 1179656 | tf_op jit(solution)/shard_map/ppermute | solution.py:628
  11.0 6.5 %norm_project.2 = (bf16[1024,2048]{1,0:T(8,128)(2,1)S(1)}, f32[4,4,2048]{2,1,0:T(4,128)S(1)}, f32[1024,768]{1,0:T(8,128)S(1)}) custom-call(s32[2]{0:T(128)S(1)} %pad_add_fusion.where_ref, bf16[16,64,2048]{2,1,0:T(8,128)(2,1)} %hidden_ref.1, f32[1,2048]{1,0:T(1,128)S(1)} %bitcast.23, bf16[512,384]{1,0:T(8,128)(2,1)S(1)} %get-tuple-element.84.a_ref, ...), custom_call_target="tpu_custom_call" | custom-call | flops 3500000000 | bytes 24500000 | tf_op jit(solution)/shard_map/norm_project/pallas_call | solution.py:65
  18.1 1.8 %collective-permute-start.7 = (bf16[512,384]{1,0:T(8,128)(2,1)S(1)}, bf16[512,384]{1,0:T(8,128)(2,1)S(1)}, u32[]{:S(2)}, u32[]{:S(2)}) collective-permute-start(bf16[512,384]{1,0:T(8,128)(2,1)S(1)} %get-tuple-element.84.a_ref), channel_id=1, source_target_pairs={{0,4},{1,5},{2,6},{3,7},{4,0},{5,1},{6,2},{7,3},{8,12},{9,13},{10,... | collective-permute-start | bytes 1179656 | tf_op jit(solution)/shard_map/ppermute | solution.py:628
  24.5 6.6 %norm_project.3 = (bf16[1024,2048]{1,0:T(8,128)(2,1)S(1)}, f32[4,4,2048]{2,1,0:T(4,128)S(1)}, f32[1024,768]{1,0:T(8,128)S(1)}) custom-call(s32[2]{0:T(128)S(1)} %pad_add_fusion.where_ref, bf16[16,64,2048]{2,1,0:T(8,128)(2,1)} %collective-permute-done.1.hidden_ref, f32[1,2048]{1,0:T(1,128)S(1)} %bitcast.24, bf16[512,384]{1,0:T(8,128)(2,1)S(1)} %get-tuple-element.84.a_ref, ...), custom_call_target="tpu_custom_call" | custom-call | flops 3500000000 | bytes 24500000 | tf_op jit(solution)/shard_map/norm_project/pallas_call | solution.py:65
  34.0 2.9 %project_more.2.before_ref = f32[1024,768]{1,0:T(8,128)S(1)} custom-call(s32[2]{0:T(128)S(1)} %pad_add_fusion.where_ref, bf16[1024,2048]{1,0:T(8,128)(2,1)S(1)} %get-tuple-element.92.rows_ref.own_ref, f32[1024,768]{1,0:T(8,128)S(1)} %get-tuple-element.73.before_ref, bf16[512,384]{1,0:T(8,128)(2,1)S(1)} %collective-permute-done.4.refs_0_, ...), custom_call_target="tpu_custom_call" | custom-call | flops 2249999872 | bytes 15750000 | tf_op jit(solution)/shard_map/project_more/pallas_call | solution.py:200
  36.9 1.6 %collective-permute-start.18 = (bf16[256,512]{1,0:T(8,128)(2,1)S(1)}, bf16[256,512]{1,0:T(8,128)(2,1)S(1)}, u32[]{:S(2)}, u32[]{:S(2)}) collective-permute-start(bf16[256,512]{1,0:T(8,128)(2,1)S(1)} %get-tuple-element.100.refs_0_), channel_id=1, source_target_pairs={{0,4},{1,5},{2,6},{3,7},{4,0},{5,1},{6,2},{7,3},{8,12},{9,13},{10,... | collective-permute-start | bytes 786440 | tf_op jit(solution)/shard_map/ppermute | solution.py:628
  38.5 2.9 %project_more.3.before_ref = f32[1024,768]{1,0:T(8,128)S(1)} custom-call(s32[2]{0:T(128)S(1)} %pad_add_fusion.where_ref, bf16[1024,2048]{1,0:T(8,128)(2,1)S(1)} %get-tuple-element.85.rows_ref.sib_ref, f32[1024,768]{1,0:T(8,128)S(1)} %get-tuple-element.81.before_ref, bf16[512,384]{1,0:T(8,128)(2,1)S(1)} %collective-permute-done.4.refs_0_, ...), custom_call_target="tpu_custom_call" | custom-call | flops 2249999872 | bytes 15750000 | tf_op jit(solution)/shard_map/project_more/pallas_call | solution.py:200
  42.1 4.4 %project_attend.2 = (bf16[1024,768]{1,0:T(8,128)(2,1)S(1)}, bf16[2,2,1024,128]{3,2,1,0:T(8,128)(2,1)S(1)}, f32[2,8,512]{2,1,0:T(8,128)S(1)}) custom-call(s32[2]{0:T(128)S(1)} %pad_add_fusion.where_ref, bf16[1024,2048]{1,0:T(8,128)(2,1)S(1)} %get-tuple-element.85.rows_ref.sib_ref, f32[1024,768]{1,0:T(8,128)S(1)} %project_more.3.before_ref, ...), custom_call_target="tpu_custom_call" | custom-call | flops 3249999872 | bytes 22750000 | tf_op jit(solution)/shard_map/project_attend/pallas_call | solution.py:200
  48.0 3.5 %collective-permute-done.14.refs_4_ = bf16[256,512]{1,0:T(8,128)(2,1)S(1)} collective-permute-done((bf16[256,512]{1,0:T(8,128)(2,1)S(1)}, bf16[256,512]{1,0:T(8,128)(2,1)S(1)}, u32[]{:S(2)}, u32[]{:S(2)}) %collective-permute-start.14) | collective-permute-done | bytes 262176 | tf_op jit(solution)/shard_map/ppermute | solution.py:628
  52.4 4.4 %project_attend.3 = (bf16[1024,768]{1,0:T(8,128)(2,1)S(1)}, bf16[2,2,1024,128]{3,2,1,0:T(8,128)(2,1)S(1)}, f32[2,8,512]{2,1,0:T(8,128)S(1)}) custom-call(s32[2]{0:T(128)S(1)} %pad_add_fusion.where_ref, bf16[1024,2048]{1,0:T(8,128)(2,1)S(1)} %get-tuple-element.92.rows_ref.own_ref, f32[1024,768]{1,0:T(8,128)S(1)} %project_more.2.before_ref, ...), custom_call_target="tpu_custom_call" | custom-call | flops 3249999872 | bytes 22750000 | tf_op jit(solution)/shard_map/project_attend/pallas_call | solution.py:200
  62.3 2.9 %pool_score.1 = (f32[32,128]{1,0:T(8,128)S(1)}, bf16[32,1024]{1,0:T(8,128)(2,1)S(1)}, f32[32,512]{1,0:T(8,128)S(1)}, f32[32,1024]{1,0:T(8,128)S(1)}) custom-call(s32[2]{0:T(128)S(1)} %pad_add_fusion.where_ref, f32[16,512]{1,0:T(8,128)S(1)} %bitcast.20, f32[16,512]{1,0:T(8,128)S(1)} %bitcast.18, f32[16,512]{1,0:T(8,128)S(1)} %collective-permute-done.10.own_far_ref, ...), custom_call_target="tpu_custom_call" | custom-call | flops 1000000000 | bytes 7000000 | tf_op jit(solution)/shard_map/pool_score/pallas_call | solution.py:373
  65.2 3.0 %collective-permute-start.27 = (f32[32,128]{1,0:T(8,128)S(1)}, f32[32,128]{1,0:T(8,128)S(1)}, u32[]{:S(2)}, u32[]{:S(2)}) collective-permute-start(f32[32,128]{1,0:T(8,128)S(1)} %get-tuple-element.116.refs_0_), channel_id=1, source_target_pairs={{0,4},{2,6},{4,0},{5,9},{6,2},{7,11},{8,12},{9,5},{10,14},{11,7},{... | collective-permute-start | bytes 49160 | tf_op jit(solution)/shard_map/ppermute | solution.py:648
  68.2 3.4 %collective-permute-start.26 = (f32[32,128]{1,0:T(8,128)S(1)}, f32[32,128]{1,0:T(8,128)S(1)}, u32[]{:S(2)}, u32[]{:S(2)}) collective-permute-start(f32[32,128]{1,0:T(8,128)S(1)} %get-tuple-element.116.refs_0_), channel_id=1, source_target_pairs={{0,2},{2,0},{3,5},{4,6},{5,3},{6,4},{7,9},{8,10},{9,7},{10,8},{11,... | collective-permute-start | bytes 49160 | tf_op jit(solution)/shard_map/ppermute | solution.py:648
  71.6 3.9 %attend_back.2.own_ref = bf16[1024,768]{1,0:T(8,128)(2,1)S(1)} custom-call(s32[2]{0:T(128)S(1)} %pad_add_fusion.where_ref, bf16[2,2,1024,128]{3,2,1,0:T(8,128)(2,1)S(1)} %get-tuple-element.99.probs_ref, bf16[1024,768]{1,0:T(8,128)(2,1)S(1)} %get-tuple-element.112.projected_ref, f32[2,8,512]{2,1,0:T(8,128)S(1)} %get-tuple-element.151.d_ref), custom_call_target="tpu_custom_call" | custom-call | flops 1700000000 | bytes 11900000 | tf_op jit(solution)/shard_map/attend_back/pallas_call | solution.py:200
  76.2 3.9 %attend_back.3.sib_ref = bf16[1024,768]{1,0:T(8,128)(2,1)S(1)} custom-call(s32[2]{0:T(128)S(1)} %pad_add_fusion.where_ref, bf16[2,2,1024,128]{3,2,1,0:T(8,128)(2,1)S(1)} %get-tuple-element.114.probs_ref, bf16[1024,768]{1,0:T(8,128)(2,1)S(1)} %get-tuple-element.115.projected_ref, f32[2,8,512]{2,1,0:T(8,128)S(1)} %get-tuple-element.150.d_ref), custom_call_target="tpu_custom_call" | custom-call | flops 1700000000 | bytes 11900000 | tf_op jit(solution)/shard_map/attend_back/pallas_call | solution.py:200
  80.1 1.8 %list_grad.1 = (bf16[32,1024]{1,0:T(8,128)(2,1)S(1)}, f32[8,128]{1,0:T(8,128)S(1)}, bf16[1024,768]{1,0:T(8,128)(2,1)S(1)}, bf16[1024,768]{1,0:T(8,128)(2,1)S(1)}) custom-call(s32[2]{0:T(128)S(1)} %pad_add_fusion.where_ref, s32[5]{0:T(128)S(1)} %stack.35.place_ref, s32[8,128]{1,0:T(8,128)S(1)} %broadcast_in_dim.13.bounds_ref, ...), custom_call_target="tpu_custom_call" | custom-call | flops 1250000000 | bytes 8750000 | tf_op jit(solution)/shard_map/list_grad/pallas_call | solution.py:442
  86.1 2.2 %copy-done.1 = bf16[1024,2048]{1,0:T(8,128)(2,1)S(1)} copy-done((bf16[1024,2048]{1,0:T(8,128)(2,1)S(1)}, bf16[1024,2048]{1,0:T(8,128)(2,1)}, u32[]{:S(2)}) %copy-start.1) | copy-done | bytes 4194328
  88.3 2.2 %copy-done.4 = bf16[1024,2048]{1,0:T(8,128)(2,1)S(1)} copy-done((bf16[1024,2048]{1,0:T(8,128)(2,1)S(1)}, bf16[1024,2048]{1,0:T(8,128)(2,1)}, u32[]{:S(2)}) %copy-start.4) | copy-done | bytes 4194328
  90.5 2.4 %grad_rows.3 = (bf16[512,384]{1,0:T(8,128)(2,1)S(1)}, bf16[512,384]{1,0:T(8,128)(2,1)S(1)}) custom-call(s32[2]{0:T(128)S(1)} %pad_add_fusion.where_ref, bf16[1024,2048]{1,0:T(8,128)(2,1)S(1)} %copy-done.1, bf16[1024,2048]{1,0:T(8,128)(2,1)S(1)} %copy-done.4, bf16[1024,768]{1,0:T(8,128)(2,1)S(1)} %get-tuple-element.120.d_own_ref, ...), custom_call_target="tpu_custom_call" | custom-call | flops 1250000000 | bytes 8750000 | tf_op jit(solution)/shard_map/grad_rows/pallas_call | solution.py:200
  96.2 4.1 %grad_rows.4 = (bf16[512,384]{1,0:T(8,128)(2,1)S(1)}, bf16[512,384]{1,0:T(8,128)(2,1)S(1)}, bf16[512,384]{1,0:T(8,128)(2,1)S(1)}, bf16[512,384]{1,0:T(8,128)(2,1)S(1)}) custom-call(s32[2]{0:T(128)S(1)} %pad_add_fusion.where_ref, bf16[1024,2048]{1,0:T(8,128)(2,1)S(1)} %copy-done.2, bf16[1024,2048]{1,0:T(8,128)(2,1)S(1)} %copy-done.4, ...), custom_call_target="tpu_custom_call" | custom-call | flops 2500000000 | bytes 17500000 | tf_op jit(solution)/shard_map/grad_rows/pallas_call | solution.py:200
  105.2 2.2 %collective-permute-start.42 = (bf16[512,384]{1,0:T(8,128)(2,1)S(1)}, bf16[512,384]{1,0:T(8,128)(2,1)S(1)}, u32[]{:S(2)}, u32[]{:S(2)}) collective-permute-start(bf16[512,384]{1,0:T(8,128)(2,1)S(1)} %add_convert_fusion.3), channel_id=1, source_target_pairs={{0,2},{1,3},{2,0},{3,1},{4,6},{5,7},{6,4},{7,5},{8,10},{9,11},{10,... | collective-permute-start | bytes 1179656 | tf_op jit(solution)/shard_map/ppermute | solution.py:628
  108.9 2.5 %collective-permute-start.36 = (bf16[144,512]{1,0:T(8,128)(2,1)S(1)}, bf16[144,512]{1,0:T(8,128)(2,1)S(1)}, u32[]{:S(2)}, u32[]{:S(2)}) collective-permute-start(bf16[144,512]{1,0:T(8,128)(2,1)S(1)} %get-tuple-element.140), channel_id=1, source_target_pairs={{0,24},{8,16},{16,8},{24,0},{1,25},{9,17},{17,9},{25,1},{2,26},{10... | collective-permute-start | bytes 442376 | tf_op jit(solution)/shard_map/ppermute | solution.py:631
  112.2 2.6 %collective-permute-start.35 = (bf16[144,512]{1,0:T(8,128)(2,1)S(1)}, bf16[144,512]{1,0:T(8,128)(2,1)S(1)}, u32[]{:S(2)}, u32[]{:S(2)}) collective-permute-start(bf16[144,512]{1,0:T(8,128)(2,1)S(1)} %get-tuple-element.141), channel_id=1, source_target_pairs={{0,16},{8,24},{16,0},{24,8},{1,17},{9,25},{17,1},{25,9},{2,18},{10... | collective-permute-start | bytes 442376 | tf_op jit(solution)/shard_map/ppermute | solution.py:631
  114.8 2.0 %collective-permute-start.34 = (bf16[144,512]{1,0:T(8,128)(2,1)S(1)}, bf16[144,512]{1,0:T(8,128)(2,1)S(1)}, u32[]{:S(2)}, u32[]{:S(2)}) collective-permute-start(bf16[144,512]{1,0:T(8,128)(2,1)S(1)} %get-tuple-element.142), channel_id=1, source_target_pairs={{0,8},{8,0},{16,24},{24,16},{1,9},{9,1},{17,25},{25,17},{2,10},{10... | collective-permute-start | bytes 442376 | tf_op jit(solution)/shard_map/ppermute | solution.py:631
  116.8 2.4 %grad_rows.5 = (bf16[512,384]{1,0:T(8,128)(2,1)S(1)}, bf16[512,384]{1,0:T(8,128)(2,1)S(1)}) custom-call(s32[2]{0:T(128)S(1)} %pad_add_fusion.where_ref, bf16[1024,2048]{1,0:T(8,128)(2,1)S(1)} %copy-done.2, bf16[1024,2048]{1,0:T(8,128)(2,1)S(1)} %copy-done.4, bf16[1024,768]{1,0:T(8,128)(2,1)S(1)} %get-tuple-element.120.d_own_ref, ...), custom_call_target="tpu_custom_call" | custom-call | flops 1250000000 | bytes 8750000 | tf_op jit(solution)/shard_map/grad_rows/pallas_call | solution.py:200
  119.2 3.8 %collective-permute-done.35.refs_2_ = bf16[144,512]{1,0:T(8,128)(2,1)S(1)} collective-permute-done((bf16[144,512]{1,0:T(8,128)(2,1)S(1)}, bf16[144,512]{1,0:T(8,128)(2,1)S(1)}, u32[]{:S(2)}, u32[]{:S(2)}) %collective-permute-start.35) | collective-permute-done | bytes 147488 | tf_op jit(solution)/shard_map/ppermute | solution.py:631
  125.0 1.6 %collective-permute-done.43 = bf16[256,768]{1,0:T(8,128)(2,1)S(1)} collective-permute-done((bf16[256,768]{1,0:T(8,128)(2,1)S(1)}, bf16[256,768]{1,0:T(8,128)(2,1)S(1)}, u32[]{:S(2)}, u32[]{:S(2)}) %collective-permute-start.43) | collective-permute-done | bytes 393248 | tf_op jit(solution)/shard_map/ppermute | solution.py:628
  127.1 2.5 %collective-permute-start.46 = (bf16[256,384]{1,0:T(8,128)(2,1)S(1)}, bf16[256,384]{1,0:T(8,128)(2,1)S(1)}, u32[]{:S(2)}, u32[]{:S(2)}) collective-permute-start(bf16[256,384]{1,0:T(8,128)(2,1)S(1)} %get-tuple-element.136), channel_id=1, source_target_pairs={{0,24},{8,16},{16,8},{24,0},{1,25},{9,17},{17,9},{25,1},{2,26},{10... | collective-permute-start | bytes 589832 | tf_op jit(solution)/shard_map/ppermute | solution.py:631
  131.9 2.2 %collective-permute-done.44 = bf16[256,384]{1,0:T(8,128)(2,1)S(1)} collective-permute-done((bf16[256,384]{1,0:T(8,128)(2,1)S(1)}, bf16[256,384]{1,0:T(8,128)(2,1)S(1)}, u32[]{:S(2)}, u32[]{:S(2)}) %collective-permute-start.44) | collective-permute-done | bytes 196640 | tf_op jit(solution)/shard_map/ppermute | solution.py:631
  134.1 5.5 %collective-permute-done.46 = bf16[256,384]{1,0:T(8,128)(2,1)S(1)} collective-permute-done((bf16[256,384]{1,0:T(8,128)(2,1)S(1)}, bf16[256,384]{1,0:T(8,128)(2,1)S(1)}, u32[]{:S(2)}, u32[]{:S(2)}) %collective-permute-start.46) | collective-permute-done | bytes 196640 | tf_op jit(solution)/shard_map/ppermute | solution.py:631
  139.6 8.3 %collective-permute-done.45 = bf16[256,384]{1,0:T(8,128)(2,1)S(1)} collective-permute-done((bf16[256,384]{1,0:T(8,128)(2,1)S(1)}, bf16[256,384]{1,0:T(8,128)(2,1)S(1)}, u32[]{:S(2)}, u32[]{:S(2)}) %collective-permute-start.45) | collective-permute-done | bytes 196640 | tf_op jit(solution)/shard_map/ppermute | solution.py:631
  (160 shorter events, 42.3 us)
Async XLA Ops:
  3.3 21.2 %collective-permute-start.1 = (bf16[16,64,2048]{2,1,0:T(8,128)(2,1)}, bf16[16,64,2048]{2,1,0:T(8,128)(2,1)}, u32[]{:S(2)}, u32[]{:S(2)}) collective-permute-start(bf16[16,64,2048]{2,1,0:T(8,128)(2,1)} %hidden_ref.1), channel_id=1, source_target_pairs={{0,1},{1,0},{2,3},{3,2},{4,5},{5,4},{6,7},{7,6},{8,9},{9,8},{10,11... | collective-permute-start | bytes 12582920 | tf_op jit(solution)/shard_map/ppermute | solution.py:628
  3.6 18.2 %collective-permute-start.2 = (bf16[128,2048]{1,0:T(8,128)(2,1)}, bf16[128,2048]{1,0:T(8,128)(2,1)S(1)}, u32[]{:S(2)}, u32[]{:S(2)}) collective-permute-start(bf16[128,2048]{1,0:T(8,128)(2,1)} %param.12), channel_id=1, source_target_pairs={{0,1},{1,0},{2,3},{3,2},{4,5},{5,4},{6,7},{7,6},{8,9},{9,8},{10,11... | collective-permute-start | bytes 1572872 | tf_op jit(solution)/shard_map/ppermute | solution.py:628
  5.7 12.3 %collective-permute-start.4 = (bf16[512,384]{1,0:T(8,128)(2,1)S(1)}, bf16[512,384]{1,0:T(8,128)(2,1)S(1)}, u32[]{:S(2)}, u32[]{:S(2)}) collective-permute-start(bf16[512,384]{1,0:T(8,128)(2,1)S(1)} %get-tuple-element.84.a_ref), channel_id=1, source_target_pairs={{0,2},{1,3},{2,0},{3,1},{4,6},{5,7},{6,4},{7,5},{8,10},{9,11},{10,... | collective-permute-start | bytes 1179656 | tf_op jit(solution)/shard_map/ppermute | solution.py:628
  8.7 11.2 %collective-permute-start.5 = (bf16[512,384]{1,0:T(8,128)(2,1)S(1)}, bf16[512,384]{1,0:T(8,128)(2,1)S(1)}, u32[]{:S(2)}, u32[]{:S(2)}) collective-permute-start(bf16[512,384]{1,0:T(8,128)(2,1)S(1)} %get-tuple-element.83.b_ref), channel_id=1, source_target_pairs={{0,4},{1,5},{2,6},{3,7},{4,0},{5,1},{6,2},{7,3},{8,12},{9,13},{10,... | collective-permute-start | bytes 1179656 | tf_op jit(solution)/shard_map/ppermute | solution.py:628
  18.1 13.1 %collective-permute-start.7 = (bf16[512,384]{1,0:T(8,128)(2,1)S(1)}, bf16[512,384]{1,0:T(8,128)(2,1)S(1)}, u32[]{:S(2)}, u32[]{:S(2)}) collective-permute-start(bf16[512,384]{1,0:T(8,128)(2,1)S(1)} %get-tuple-element.84.a_ref), channel_id=1, source_target_pairs={{0,4},{1,5},{2,6},{3,7},{4,0},{5,1},{6,2},{7,3},{8,12},{9,13},{10,... | collective-permute-start | bytes 1179656 | tf_op jit(solution)/shard_map/ppermute | solution.py:628
  19.8 12.1 %collective-permute-start.6 = (bf16[512,384]{1,0:T(8,128)(2,1)S(1)}, bf16[512,384]{1,0:T(8,128)(2,1)S(1)}, u32[]{:S(2)}, u32[]{:S(2)}) collective-permute-start(bf16[512,384]{1,0:T(8,128)(2,1)S(1)} %get-tuple-element.83.b_ref), channel_id=1, source_target_pairs={{0,2},{1,3},{2,0},{3,1},{4,6},{5,7},{6,4},{7,5},{8,10},{9,11},{10,... | collective-permute-start | bytes 1179656 | tf_op jit(solution)/shard_map/ppermute | solution.py:628
  21.3 20.1 %collective-permute-start.8 = (bf16[512,384]{1,0:T(8,128)(2,1)S(1)}, bf16[512,384]{1,0:T(8,128)(2,1)S(1)}, u32[]{:S(2)}, u32[]{:S(2)}) collective-permute-start(bf16[512,384]{1,0:T(8,128)(2,1)S(1)} %collective-permute-done.4.refs_0_), channel_id=1, source_target_pairs={{0,4},{1,5},{2,6},{3,7},{4,0},{5,1},{6,2},{7,3},{8,12},{9,13},{10,... | collective-permute-start | bytes 1179656 | tf_op jit(solution)/shard_map/ppermute | solution.py:628
  23.3 18.8 %collective-permute-start.9 = (bf16[512,384]{1,0:T(8,128)(2,1)S(1)}, bf16[512,384]{1,0:T(8,128)(2,1)S(1)}, u32[]{:S(2)}, u32[]{:S(2)}) collective-permute-start(bf16[512,384]{1,0:T(8,128)(2,1)S(1)} %collective-permute-done.5.refs_3_), channel_id=1, source_target_pairs={{0,2},{1,3},{2,0},{3,1},{4,6},{5,7},{6,4},{7,5},{8,10},{9,11},{10,... | collective-permute-start | bytes 1179656 | tf_op jit(solution)/shard_map/ppermute | solution.py:628
  31.9 14.6 %collective-permute-start.19 = (bf16[256,512]{1,0:T(8,128)(2,1)S(1)}, bf16[256,512]{1,0:T(8,128)(2,1)S(1)}, u32[]{:S(2)}, u32[]{:S(2)}) collective-permute-start(bf16[256,512]{1,0:T(8,128)(2,1)S(1)} %get-tuple-element.101.refs_1_), channel_id=1, source_target_pairs={{0,4},{1,5},{2,6},{3,7},{4,0},{5,1},{6,2},{7,3},{8,12},{9,13},{10,... | collective-permute-start | bytes 786440 | tf_op jit(solution)/shard_map/ppermute | solution.py:628
  33.2 23.7 %collective-permute-start.15 = (bf16[256,512]{1,0:T(8,128)(2,1)S(1)}, bf16[256,512]{1,0:T(8,128)(2,1)S(1)}, u32[]{:S(2)}, u32[]{:S(2)}) collective-permute-start(bf16[256,512]{1,0:T(8,128)(2,1)S(1)} %get-tuple-element.101.refs_1_), channel_id=1, source_target_pairs={{0,2},{1,3},{2,0},{3,1},{4,6},{5,7},{6,4},{7,5},{8,10},{9,11},{10,... | collective-permute-start | bytes 786440 | tf_op jit(solution)/shard_map/ppermute | solution.py:628
  36.9 20.5 %collective-permute-start.18 = (bf16[256,512]{1,0:T(8,128)(2,1)S(1)}, bf16[256,512]{1,0:T(8,128)(2,1)S(1)}, u32[]{:S(2)}, u32[]{:S(2)}) collective-permute-start(bf16[256,512]{1,0:T(8,128)(2,1)S(1)} %get-tuple-element.100.refs_0_), channel_id=1, source_target_pairs={{0,4},{1,5},{2,6},{3,7},{4,0},{5,1},{6,2},{7,3},{8,12},{9,13},{10,... | collective-permute-start | bytes 786440 | tf_op jit(solution)/shard_map/ppermute | solution.py:628
  41.5 10.1 %collective-permute-start.14 = (bf16[256,512]{1,0:T(8,128)(2,1)S(1)}, bf16[256,512]{1,0:T(8,128)(2,1)S(1)}, u32[]{:S(2)}, u32[]{:S(2)}) collective-permute-start(bf16[256,512]{1,0:T(8,128)(2,1)S(1)} %get-tuple-element.100.refs_0_), channel_id=1, source_target_pairs={{0,2},{1,3},{2,0},{3,1},{4,6},{5,7},{6,4},{7,5},{8,10},{9,11},{10,... | collective-permute-start | bytes 786440 | tf_op jit(solution)/shard_map/ppermute | solution.py:628
  46.5 11.0 %collective-permute-start.23 = (bf16[256,512]{1,0:T(8,128)(2,1)S(1)}, bf16[256,512]{1,0:T(8,128)(2,1)S(1)}, u32[]{:S(2)}, u32[]{:S(2)}) collective-permute-start(bf16[256,512]{1,0:T(8,128)(2,1)S(1)} %collective-permute-done.19.refs_9_), channel_id=1, source_target_pairs={{0,2},{1,3},{2,0},{3,1},{4,6},{5,7},{6,4},{7,5},{8,10},{9,11},{10,... | collective-permute-start | bytes 786440 | tf_op jit(solution)/shard_map/ppermute | solution.py:628
  51.6 6.4 %collective-permute-start.22 = (bf16[256,512]{1,0:T(8,128)(2,1)S(1)}, bf16[256,512]{1,0:T(8,128)(2,1)S(1)}, u32[]{:S(2)}, u32[]{:S(2)}) collective-permute-start(bf16[256,512]{1,0:T(8,128)(2,1)S(1)} %collective-permute-done.14.refs_4_), channel_id=1, source_target_pairs={{0,4},{1,5},{2,6},{3,7},{4,0},{5,1},{6,2},{7,3},{8,12},{9,13},{10,... | collective-permute-start | bytes 786440 | tf_op jit(solution)/shard_map/ppermute | solution.py:628
  65.2 10.4 %collective-permute-start.27 = (f32[32,128]{1,0:T(8,128)S(1)}, f32[32,128]{1,0:T(8,128)S(1)}, u32[]{:S(2)}, u32[]{:S(2)}) collective-permute-start(f32[32,128]{1,0:T(8,128)S(1)} %get-tuple-element.116.refs_0_), channel_id=1, source_target_pairs={{0,4},{2,6},{4,0},{5,9},{6,2},{7,11},{8,12},{9,5},{10,14},{11,7},{... | collective-permute-start | bytes 49160 | tf_op jit(solution)/shard_map/ppermute | solution.py:648
  68.2 7.5 %collective-permute-start.26 = (f32[32,128]{1,0:T(8,128)S(1)}, f32[32,128]{1,0:T(8,128)S(1)}, u32[]{:S(2)}, u32[]{:S(2)}) collective-permute-start(f32[32,128]{1,0:T(8,128)S(1)} %get-tuple-element.116.refs_0_), channel_id=1, source_target_pairs={{0,2},{2,0},{3,5},{4,6},{5,3},{6,4},{7,9},{8,10},{9,7},{10,8},{11,... | collective-permute-start | bytes 49160 | tf_op jit(solution)/shard_map/ppermute | solution.py:648
  82.5 12.5 %collective-permute-start.32 = (bf16[32,1920]{1,0:T(8,128)(2,1)S(1)}, bf16[32,1920]{1,0:T(8,128)(2,1)S(1)}, u32[]{:S(2)}, u32[]{:S(2)}) collective-permute-start(bf16[32,1920]{1,0:T(8,128)(2,1)S(1)} %out_payload.1.refs_0_), channel_id=1, source_target_pairs={{0,6},{1,7},{2,4},{3,5},{4,2},{5,3},{6,0},{7,1},{8,14},{9,15},{10,... | collective-permute-start | bytes 368648 | tf_op jit(solution)/shard_map/ppermute | solution.py:628
  84.1 10.9 %collective-permute-start.31 = (bf16[32,1920]{1,0:T(8,128)(2,1)S(1)}, bf16[32,1920]{1,0:T(8,128)(2,1)S(1)}, u32[]{:S(2)}, u32[]{:S(2)}) collective-permute-start(bf16[32,1920]{1,0:T(8,128)(2,1)S(1)} %out_payload.1.refs_0_), channel_id=1, source_target_pairs={{0,4},{1,5},{2,6},{3,7},{4,0},{5,1},{6,2},{7,3},{8,12},{9,13},{10,... | collective-permute-start | bytes 368648 | tf_op jit(solution)/shard_map/ppermute | solution.py:628
  85.1 9.9 %collective-permute-start.30 = (bf16[32,1920]{1,0:T(8,128)(2,1)S(1)}, bf16[32,1920]{1,0:T(8,128)(2,1)}, u32[]{:S(2)}, u32[]{:S(2)}) collective-permute-start(bf16[32,1920]{1,0:T(8,128)(2,1)S(1)} %out_payload.1.refs_0_), channel_id=1, source_target_pairs={{0,2},{1,3},{2,0},{3,1},{4,6},{5,7},{6,4},{7,5},{8,10},{9,11},{10,... | collective-permute-start | bytes 368648 | tf_op jit(solution)/shard_map/ppermute | solution.py:628
  92.9 12.2 %collective-permute-start.40 = (bf16[512,384]{1,0:T(8,128)(2,1)S(1)}, bf16[512,384]{1,0:T(8,128)(2,1)S(1)}, u32[]{:S(2)}, u32[]{:S(2)}) collective-permute-start(bf16[512,384]{1,0:T(8,128)(2,1)S(1)} %get-tuple-element.127), channel_id=1, source_target_pairs={{0,4},{1,5},{2,6},{3,7},{4,0},{5,1},{6,2},{7,3},{8,12},{9,13},{10,... | collective-permute-start | bytes 1179656 | tf_op jit(solution)/shard_map/ppermute | solution.py:628
  93.4 10.2 %collective-permute-start.38 = (bf16[512,384]{1,0:T(8,128)(2,1)S(1)}, bf16[512,384]{1,0:T(8,128)(2,1)S(1)}, u32[]{:S(2)}, u32[]{:S(2)}) collective-permute-start(bf16[512,384]{1,0:T(8,128)(2,1)S(1)} %get-tuple-element.122), channel_id=1, source_target_pairs={{0,2},{1,3},{2,0},{3,1},{4,6},{5,7},{6,4},{7,5},{8,10},{9,11},{10,... | collective-permute-start | bytes 1179656 | tf_op jit(solution)/shard_map/ppermute | solution.py:628
  96.1 11.4 %collective-permute-start.33 = (bf16[128,1920]{1,0:T(8,128)(2,1)S(1)}, bf16[128,1920]{1,0:T(8,128)(2,1)S(1)}, u32[]{:S(2)}, u32[]{:S(2)}) collective-permute-start(bf16[128,1920]{1,0:T(8,128)(2,1)S(1)} %pad_maximum_fusion.1), channel_id=1, source_target_pairs={{0,1},{1,0},{2,3},{3,2},{4,5},{5,4},{6,7},{7,6},{8,9},{9,8},{10,11... | collective-permute-start | bytes 1474568 | tf_op jit(solution)/shard_map/ppermute | solution.py:628
  100.2 12.0 %collective-permute-start.39 = (bf16[512,384]{1,0:T(8,128)(2,1)S(1)}, bf16[512,384]{1,0:T(8,128)(2,1)S(1)}, u32[]{:S(2)}, u32[]{:S(2)}) collective-permute-start(bf16[512,384]{1,0:T(8,128)(2,1)S(1)} %get-tuple-element.126), channel_id=1, source_target_pairs={{0,4},{1,5},{2,6},{3,7},{4,0},{5,1},{6,2},{7,3},{8,12},{9,13},{10,... | collective-permute-start | bytes 1179656 | tf_op jit(solution)/shard_map/ppermute | solution.py:628
  101.3 13.5 %collective-permute-start.37 = (bf16[512,384]{1,0:T(8,128)(2,1)S(1)}, bf16[512,384]{1,0:T(8,128)(2,1)S(1)}, u32[]{:S(2)}, u32[]{:S(2)}) collective-permute-start(bf16[512,384]{1,0:T(8,128)(2,1)S(1)} %get-tuple-element.124), channel_id=1, source_target_pairs={{0,2},{1,3},{2,0},{3,1},{4,6},{5,7},{6,4},{7,5},{8,10},{9,11},{10,... | collective-permute-start | bytes 1179656 | tf_op jit(solution)/shard_map/ppermute | solution.py:628
  103.7 20.7 %collective-permute-start.41 = (bf16[512,384]{1,0:T(8,128)(2,1)S(1)}, bf16[512,384]{1,0:T(8,128)(2,1)S(1)}, u32[]{:S(2)}, u32[]{:S(2)}) collective-permute-start(bf16[512,384]{1,0:T(8,128)(2,1)S(1)} %add_convert_fusion.4), channel_id=1, source_target_pairs={{0,4},{1,5},{2,6},{3,7},{4,0},{5,1},{6,2},{7,3},{8,12},{9,13},{10,... | collective-permute-start | bytes 1179656 | tf_op jit(solution)/shard_map/ppermute | solution.py:628
  105.2 19.1 %collective-permute-start.42 = (bf16[512,384]{1,0:T(8,128)(2,1)S(1)}, bf16[512,384]{1,0:T(8,128)(2,1)S(1)}, u32[]{:S(2)}, u32[]{:S(2)}) collective-permute-start(bf16[512,384]{1,0:T(8,128)(2,1)S(1)} %add_convert_fusion.3), channel_id=1, source_target_pairs={{0,2},{1,3},{2,0},{3,1},{4,6},{5,7},{6,4},{7,5},{8,10},{9,11},{10,... | collective-permute-start | bytes 1179656 | tf_op jit(solution)/shard_map/ppermute | solution.py:628
  108.9 10.3 %collective-permute-start.36 = (bf16[144,512]{1,0:T(8,128)(2,1)S(1)}, bf16[144,512]{1,0:T(8,128)(2,1)S(1)}, u32[]{:S(2)}, u32[]{:S(2)}) collective-permute-start(bf16[144,512]{1,0:T(8,128)(2,1)S(1)} %get-tuple-element.140), channel_id=1, source_target_pairs={{0,24},{8,16},{16,8},{24,0},{1,25},{9,17},{17,9},{25,1},{2,26},{10... | collective-permute-start | bytes 442376 | tf_op jit(solution)/shard_map/ppermute | solution.py:631
  112.2 10.8 %collective-permute-start.35 = (bf16[144,512]{1,0:T(8,128)(2,1)S(1)}, bf16[144,512]{1,0:T(8,128)(2,1)S(1)}, u32[]{:S(2)}, u32[]{:S(2)}) collective-permute-start(bf16[144,512]{1,0:T(8,128)(2,1)S(1)} %get-tuple-element.141), channel_id=1, source_target_pairs={{0,16},{8,24},{16,0},{24,8},{1,17},{9,25},{17,1},{25,9},{2,18},{10... | collective-permute-start | bytes 442376 | tf_op jit(solution)/shard_map/ppermute | solution.py:631
  114.8 8.9 %collective-permute-start.34 = (bf16[144,512]{1,0:T(8,128)(2,1)S(1)}, bf16[144,512]{1,0:T(8,128)(2,1)S(1)}, u32[]{:S(2)}, u32[]{:S(2)}) collective-permute-start(bf16[144,512]{1,0:T(8,128)(2,1)S(1)} %get-tuple-element.142), channel_id=1, source_target_pairs={{0,8},{8,0},{16,24},{24,16},{1,9},{9,1},{17,25},{25,17},{2,10},{10... | collective-permute-start | bytes 442376 | tf_op jit(solution)/shard_map/ppermute | solution.py:631
  127.1 7.0 %collective-permute-start.44 = (bf16[256,384]{1,0:T(8,128)(2,1)S(1)}, bf16[256,384]{1,0:T(8,128)(2,1)S(1)}, u32[]{:S(2)}, u32[]{:S(2)}) collective-permute-start(bf16[256,384]{1,0:T(8,128)(2,1)S(1)} %get-tuple-element.135), channel_id=1, source_target_pairs={{0,8},{8,0},{16,24},{24,16},{1,9},{9,1},{17,25},{25,17},{2,10},{10... | collective-permute-start | bytes 589832 | tf_op jit(solution)/shard_map/ppermute | solution.py:631
  127.1 12.4 %collective-permute-start.46 = (bf16[256,384]{1,0:T(8,128)(2,1)S(1)}, bf16[256,384]{1,0:T(8,128)(2,1)S(1)}, u32[]{:S(2)}, u32[]{:S(2)}) collective-permute-start(bf16[256,384]{1,0:T(8,128)(2,1)S(1)} %get-tuple-element.136), channel_id=1, source_target_pairs={{0,24},{8,16},{16,8},{24,0},{1,25},{9,17},{17,9},{25,1},{2,26},{10... | collective-permute-start | bytes 589832 | tf_op jit(solution)/shard_map/ppermute | solution.py:631
  129.7 18.2 %collective-permute-start.45 = (bf16[256,384]{1,0:T(8,128)(2,1)S(1)}, bf16[256,384]{1,0:T(8,128)(2,1)S(1)}, u32[]{:S(2)}, u32[]{:S(2)}) collective-permute-start(bf16[256,384]{1,0:T(8,128)(2,1)S(1)} %get-tuple-element.137), channel_id=1, source_target_pairs={{0,16},{8,24},{16,0},{24,8},{1,17},{9,25},{17,1},{25,9},{2,18},{10... | collective-permute-start | bytes 589832 | tf_op jit(solution)/shard_map/ppermute | solution.py:631
  (39 other events, 214.7 us)

commit v8 on v7

--- a/solution.py
+++ b/solution.py
@@ -18,7 +18,7 @@
 epsilon = 1e-05
 loss_scale = 64.0
 scale = HEAD_DIM ** (-0.5)
-VMEM = 10 * 1024 * 1024
+VMEM = 14 * 1024 * 1024
 SMALL = 6 * 1024 * 1024
 
 
@@ -564,30 +564,49 @@
     )(where, left, *near, far)
 
 
-def grad_kernel(blocks, where_ref, own_ref, sib_ref, d_own_ref, d_sib_ref, *out):
+def grad_kernel(blocks, where_ref, own_ref, sib_ref, d_own_ref, d_sib_ref, *refs):
+    out, (rows_ref, done) = refs[:-2], refs[-2:]
     depth, part = out[0].shape
     tile = min(depth, 256)
     down = ((0,), (0,))
+    copies = []
     for n, s in enumerate(blocks):
+        start = pl.multiple_of((where_ref[0] ^ s) * depth, depth)
+        for k, ref in enumerate((own_ref, sib_ref)):
+            copy = pltpu.make_async_copy(
+                ref.at[:, pl.ds(start, depth)], rows_ref.at[n, k], done.at[n, k]
+            )
+            copy.start()
+            copies.append(copy)
+    for n in range(len(blocks)):
+        copies[2 * n].wait()
+        copies[2 * n + 1].wait()
         for i in range(depth // tile):
-            start = pl.multiple_of((where_ref[0] ^ s) * depth + i * tile, tile)
-            cols = pl.ds(start, tile)
-            total = mm(own_ref[:, cols], d_own_ref[...], down)
-            total = (total + mm(sib_ref[:, cols], d_sib_ref[...], down)).astype(BF16)
-            out[2 * n][i * tile : (i + 1) * tile] = total[:, :part]
-            out[2 * n + 1][i * tile : (i + 1) * tile] = total[:, part:]
+            cols = slice(i * tile, (i + 1) * tile)
+            total = mm(rows_ref[n, 0, :, cols], d_own_ref[...], down)
+            total = (total + mm(rows_ref[n, 1, :, cols], d_sib_ref[...], down)).astype(BF16)
+            out[2 * n][cols] = total[:, :part]
+            out[2 * n + 1][cols] = total[:, part:]
 
 
 def grad_blocks(where, blocks, own, sib, d_own, d_sib, depth):
     part = d_own.shape[1] // 2
-    return local_call(
+    count = len(blocks)
+    vmem = pl.BlockSpec(memory_space=pltpu.VMEM)
+    hbm = pl.BlockSpec(memory_space=pltpu.HBM)
+    return pl.pallas_call(
         functools.partial(grad_kernel, tuple(blocks)),
-        "grad_rows",
-        2.5 * len(blocks),
-        where,
-        [own, sib, d_own, d_sib],
-        [jax.ShapeDtypeStruct((depth, part), BF16)] * (2 * len(blocks)),
-    )
+        in_specs=[pl.BlockSpec(memory_space=pltpu.SMEM), hbm, hbm, vmem, vmem],
+        out_specs=[vmem] * (2 * count),
+        out_shape=[jax.ShapeDtypeStruct((depth, part), BF16)] * (2 * count),
+        scratch_shapes=[
+            pltpu.VMEM((count, 2, own.shape[0], depth), BF16),
+            pltpu.SemaphoreType.DMA((count, 2)),
+        ],
+        compiler_params=pltpu.CompilerParams(vmem_limit_bytes=VMEM),
+        cost_estimate=cost(2.5 * count),
+        name="grad_rows",
+    )(where, *held(pltpu.HBM, own, sib), d_own, d_sib)
 
 
 def pick_kernel(starts, sizes, where_ref, mine_ref, come_ref, a_ref, b_ref):

time: 149 us -> 146 us (0.980)
  Pallas kernels: 52.5 us -> 57.2 us
  local copies, waits for them, and re-layouts: 9.4 us -> 4.79 us
  waiting for transfers between devices: 33.6 us -> 29.7 us
    pallas_call x0 -> x3, Pallas kernels: none -> 13.6 us  [grad_blocks(): pl.pallas_call(functools.partial(grad_kernel, tuple(blocks)), in_specs=[p...]
    pallas_call x9 -> x6, Pallas kernels: 31.3 us -> 22.5 us  [local_call(): pl.pallas_call(kernel, in_specs=[pl.BlockSpec(memory_space=pltpu.SMEM)] +...]
    unnamed x44 -> x38, local copies, waits for them, and re-layouts: 7.6 us -> 3 us
    ppermute x39, waiting for transfers between devices: 13.8 us -> 11.1 us  [across(): lax.ppermute(value, 'fsdp', [(i, i ^ distance) for i in range(n_fsdp)])]
  transfers between devices with their start and end apart: 47 -> 47, of which waited for: 18 -> 15; matrix products, arithmetic and copies ran while one was open for 2% -> 3% of each run, Pallas kernels for 32% -> 36%
where the time goes in v8:
time: 146 us
  Pallas kernels  57.2 us (39%)
  starting transfers between devices  47.9 us (33%)
  waiting for transfers between devices  29.7 us (20%)
  local copies, waits for them, and re-layouts  4.79 us (3%)
  other arithmetic  4.67 us (3%)
    ppermute x39, starting transfers between devices, across(): lax.ppermute(value, 'fsdp', [(i, i ^ distance) for i in range(n_fsdp)])  30.7 us
    pallas_call x6, Pallas kernels, local_call(): pl.pallas_call(kernel, in_specs=[pl.BlockSpec(memory_space=pltpu.SMEM)] +...  22.5 us
    ppermute x6, waiting for transfers between devices, along(): lax.ppermute(value, 'list', [(i, i ^ distance) for i in range(n_list)])  18.7 us
    pallas_call x3, Pallas kernels, grad_blocks(): pl.pallas_call(functools.partial(grad_kernel, tuple(blocks)), in_specs=[p...  13.6 us
    pallas_call x2, Pallas kernels, norm(): pl.pallas_call(norm_kernel, grid_spec=pltpu.PrefetchScalarGridSpec(num_sc...  13.1 us
    ppermute x6, starting transfers between devices, along(): lax.ppermute(value, 'list', [(i, i ^ distance) for i in range(n_list)])  11.3 us
    ppermute x39, waiting for transfers between devices, across(): lax.ppermute(value, 'fsdp', [(i, i ^ distance) for i in range(n_fsdp)])  11.1 us
    ppermute x2, starting transfers between devices, neighbour(): return lax.ppermute(value, ('list', 'fsdp'), moves)  5.89 us
  transfers between devices with their start and end apart: 47, of which 15 were waited for; matrix products, arithmetic and copies ran while one was open for 3% of the time, Pallas kernels for 36%

profile of v8, /device:TPU:0, one launch (start us, length us, event | category | flops | bytes accessed | tf_op | source)
XLA Modules:
  0.0 145.5 jit_solution(11160354968877748819)
XLA Ops:
  1.1 2.1 %collective-permute-done.come_ref = bf16[256,1536]{1,0:T(8,128)(2,1)S(1)} collective-permute-done((bf16[256,1536]{1,0:T(8,128)(2,1)}, bf16[256,1536]{1,0:T(8,128)(2,1)S(1)}, u32[]{:S(2)}, u32[]{:S(2)}) %collective-permute-start) | collective-permute-done | bytes 786464 | tf_op jit(solution)/shard_map/ppermute | solution.py:647
  5.7 2.9 %collective-permute-start.4 = (bf16[512,384]{1,0:T(8,128)(2,1)S(1)}, bf16[512,384]{1,0:T(8,128)(2,1)S(1)}, u32[]{:S(2)}, u32[]{:S(2)}) collective-permute-start(bf16[512,384]{1,0:T(8,128)(2,1)S(1)} %get-tuple-element.84.a_ref), channel_id=1, source_target_pairs={{0,2},{1,3},{2,0},{3,1},{4,6},{5,7},{6,4},{7,5},{8,10},{9,11},{10,... | collective-permute-start | bytes 1179656 | tf_op jit(solution)/shard_map/ppermute | solution.py:647
  11.0 6.5 %norm_project.2 = (bf16[1024,2048]{1,0:T(8,128)(2,1)S(1)}, f32[4,4,2048]{2,1,0:T(4,128)S(1)}, f32[1024,768]{1,0:T(8,128)S(1)}) custom-call(s32[2]{0:T(128)S(1)} %pad_add_fusion.where_ref, bf16[16,64,2048]{2,1,0:T(8,128)(2,1)} %hidden_ref.1, f32[1,2048]{1,0:T(1,128)S(1)} %bitcast.23, bf16[512,384]{1,0:T(8,128)(2,1)S(1)} %get-tuple-element.84.a_ref, ...), custom_call_target="tpu_custom_call" | custom-call | flops 3500000000 | bytes 24500000 | tf_op jit(solution)/shard_map/norm_project/pallas_call | solution.py:65
  18.1 1.8 %collective-permute-start.7 = (bf16[512,384]{1,0:T(8,128)(2,1)S(1)}, bf16[512,384]{1,0:T(8,128)(2,1)S(1)}, u32[]{:S(2)}, u32[]{:S(2)}) collective-permute-start(bf16[512,384]{1,0:T(8,128)(2,1)S(1)} %get-tuple-element.84.a_ref), channel_id=1, source_target_pairs={{0,4},{1,5},{2,6},{3,7},{4,0},{5,1},{6,2},{7,3},{8,12},{9,13},{10,... | collective-permute-start | bytes 1179656 | tf_op jit(solution)/shard_map/ppermute | solution.py:647
  22.6 1.6 %maximum_select_fusion = bf16[256,2048]{1,0:T(8,128)(2,1)S(1)} fusion(bf16[128,2048]{1,0:T(8,128)(2,1)} %copy-done.15, bf16[128,2048]{1,0:T(8,128)(2,1)S(1)} %copy-done.14, pred[]{:T(512)S(6)} %eq.9), kind=kLoop, calls=%fused_computation | loop fusion | flops 4718592 | bytes 2097153 | tf_op jit(solution)/shard_map/jit(_where)/select_n | solution.py:708
  25.6 6.6 %norm_project.3 = (bf16[1024,2048]{1,0:T(8,128)(2,1)S(1)}, f32[4,4,2048]{2,1,0:T(4,128)S(1)}, f32[1024,768]{1,0:T(8,128)S(1)}) custom-call(s32[2]{0:T(128)S(1)} %pad_add_fusion.where_ref, bf16[16,64,2048]{2,1,0:T(8,128)(2,1)} %collective-permute-done.1.hidden_ref, f32[1,2048]{1,0:T(1,128)S(1)} %bitcast.24, bf16[512,384]{1,0:T(8,128)(2,1)S(1)} %get-tuple-element.84.a_ref, ...), custom_call_target="tpu_custom_call" | custom-call | flops 3500000000 | bytes 24500000 | tf_op jit(solution)/shard_map/norm_project/pallas_call | solution.py:65
  34.7 2.9 %project_more.2.before_ref = f32[1024,768]{1,0:T(8,128)S(1)} custom-call(s32[2]{0:T(128)S(1)} %pad_add_fusion.where_ref, bf16[1024,2048]{1,0:T(8,128)(2,1)S(1)} %get-tuple-element.92.rows_ref.own_ref, f32[1024,768]{1,0:T(8,128)S(1)} %get-tuple-element.73.before_ref, bf16[512,384]{1,0:T(8,128)(2,1)S(1)} %collective-permute-done.4.refs_0_, ...), custom_call_target="tpu_custom_call" | custom-call | flops 2249999872 | bytes 15750000 | tf_op jit(solution)/shard_map/project_more/pallas_call | solution.py:200
  38.5 2.9 %project_more.3.before_ref = f32[1024,768]{1,0:T(8,128)S(1)} custom-call(s32[2]{0:T(128)S(1)} %pad_add_fusion.where_ref, bf16[1024,2048]{1,0:T(8,128)(2,1)S(1)} %get-tuple-element.85.rows_ref.sib_ref, f32[1024,768]{1,0:T(8,128)S(1)} %get-tuple-element.81.before_ref, bf16[512,384]{1,0:T(8,128)(2,1)S(1)} %collective-permute-done.4.refs_0_, ...), custom_call_target="tpu_custom_call" | custom-call | flops 2249999872 | bytes 15750000 | tf_op jit(solution)/shard_map/project_more/pallas_call | solution.py:200
  42.5 4.4 %project_attend.2 = (bf16[1024,768]{1,0:T(8,128)(2,1)S(1)}, bf16[2,2,1024,128]{3,2,1,0:T(8,128)(2,1)S(1)}, f32[2,8,512]{2,1,0:T(8,128)S(1)}) custom-call(s32[2]{0:T(128)S(1)} %pad_add_fusion.where_ref, bf16[1024,2048]{1,0:T(8,128)(2,1)S(1)} %get-tuple-element.85.rows_ref.sib_ref, f32[1024,768]{1,0:T(8,128)S(1)} %project_more.3.before_ref, ...), custom_call_target="tpu_custom_call" | custom-call | flops 3249999872 | bytes 22750000 | tf_op jit(solution)/shard_map/project_attend/pallas_call | solution.py:200
  48.0 2.3 %collective-permute-done.14.refs_4_ = bf16[256,512]{1,0:T(8,128)(2,1)S(1)} collective-permute-done((bf16[256,512]{1,0:T(8,128)(2,1)S(1)}, bf16[256,512]{1,0:T(8,128)(2,1)S(1)}, u32[]{:S(2)}, u32[]{:S(2)}) %collective-permute-start.14) | collective-permute-done | bytes 262176 | tf_op jit(solution)/shard_map/ppermute | solution.py:647
  51.9 4.4 %project_attend.3 = (bf16[1024,768]{1,0:T(8,128)(2,1)S(1)}, bf16[2,2,1024,128]{3,2,1,0:T(8,128)(2,1)S(1)}, f32[2,8,512]{2,1,0:T(8,128)S(1)}) custom-call(s32[2]{0:T(128)S(1)} %pad_add_fusion.where_ref, bf16[1024,2048]{1,0:T(8,128)(2,1)S(1)} %get-tuple-element.92.rows_ref.own_ref, f32[1024,768]{1,0:T(8,128)S(1)} %project_more.2.before_ref, ...), custom_call_target="tpu_custom_call" | custom-call | flops 3249999872 | bytes 22750000 | tf_op jit(solution)/shard_map/project_attend/pallas_call | solution.py:200
  61.7 2.9 %pool_score.1 = (f32[32,128]{1,0:T(8,128)S(1)}, bf16[32,1024]{1,0:T(8,128)(2,1)S(1)}, f32[32,512]{1,0:T(8,128)S(1)}, f32[32,1024]{1,0:T(8,128)S(1)}) custom-call(s32[2]{0:T(128)S(1)} %pad_add_fusion.where_ref, f32[16,512]{1,0:T(8,128)S(1)} %bitcast.20, f32[16,512]{1,0:T(8,128)S(1)} %bitcast.18, f32[16,512]{1,0:T(8,128)S(1)} %collective-permute-done.10.own_far_ref, ...), custom_call_target="tpu_custom_call" | custom-call | flops 1000000000 | bytes 7000000 | tf_op jit(solution)/shard_map/pool_score/pallas_call | solution.py:373
  64.6 2.4 %collective-permute-start.27 = (f32[32,128]{1,0:T(8,128)S(1)}, f32[32,128]{1,0:T(8,128)S(1)}, u32[]{:S(2)}, u32[]{:S(2)}) collective-permute-start(f32[32,128]{1,0:T(8,128)S(1)} %get-tuple-element.116.refs_0_), channel_id=1, source_target_pairs={{0,4},{2,6},{4,0},{5,9},{6,2},{7,11},{8,12},{9,5},{10,14},{11,7},{... | collective-permute-start | bytes 49160 | tf_op jit(solution)/shard_map/ppermute | solution.py:667
  67.0 3.5 %collective-permute-start.26 = (f32[32,128]{1,0:T(8,128)S(1)}, f32[32,128]{1,0:T(8,128)S(1)}, u32[]{:S(2)}, u32[]{:S(2)}) collective-permute-start(f32[32,128]{1,0:T(8,128)S(1)} %get-tuple-element.116.refs_0_), channel_id=1, source_target_pairs={{0,2},{2,0},{3,5},{4,6},{5,3},{6,4},{7,9},{8,10},{9,7},{10,8},{11,... | collective-permute-start | bytes 49160 | tf_op jit(solution)/shard_map/ppermute | solution.py:667
  70.5 3.9 %attend_back.2.own_ref = bf16[1024,768]{1,0:T(8,128)(2,1)S(1)} custom-call(s32[2]{0:T(128)S(1)} %pad_add_fusion.where_ref, bf16[2,2,1024,128]{3,2,1,0:T(8,128)(2,1)S(1)} %get-tuple-element.99.probs_ref, bf16[1024,768]{1,0:T(8,128)(2,1)S(1)} %get-tuple-element.112.projected_ref, f32[2,8,512]{2,1,0:T(8,128)S(1)} %get-tuple-element.151.d_ref), custom_call_target="tpu_custom_call" | custom-call | flops 1700000000 | bytes 11900000 | tf_op jit(solution)/shard_map/attend_back/pallas_call | solution.py:200
  75.0 3.9 %attend_back.3.sib_ref = bf16[1024,768]{1,0:T(8,128)(2,1)S(1)} custom-call(s32[2]{0:T(128)S(1)} %pad_add_fusion.where_ref, bf16[2,2,1024,128]{3,2,1,0:T(8,128)(2,1)S(1)} %get-tuple-element.114.probs_ref, bf16[1024,768]{1,0:T(8,128)(2,1)S(1)} %get-tuple-element.115.projected_ref, f32[2,8,512]{2,1,0:T(8,128)S(1)} %get-tuple-element.150.d_ref), custom_call_target="tpu_custom_call" | custom-call | flops 1700000000 | bytes 11900000 | tf_op jit(solution)/shard_map/attend_back/pallas_call | solution.py:200
  79.0 1.8 %list_grad.1 = (bf16[32,1024]{1,0:T(8,128)(2,1)S(1)}, f32[8,128]{1,0:T(8,128)S(1)}, bf16[1024,768]{1,0:T(8,128)(2,1)S(1)}, bf16[1024,768]{1,0:T(8,128)(2,1)S(1)}) custom-call(s32[2]{0:T(128)S(1)} %pad_add_fusion.where_ref, s32[5]{0:T(128)S(1)} %stack.35.place_ref, s32[8,128]{1,0:T(8,128)S(1)} %broadcast_in_dim.13.bounds_ref, ...), custom_call_target="tpu_custom_call" | custom-call | flops 1250000000 | bytes 8750000 | tf_op jit(solution)/shard_map/list_grad/pallas_call | solution.py:442
  82.9 1.6 %collective-permute-start.31 = (bf16[32,1920]{1,0:T(8,128)(2,1)S(1)}, bf16[32,1920]{1,0:T(8,128)(2,1)S(1)}, u32[]{:S(2)}, u32[]{:S(2)}) collective-permute-start(bf16[32,1920]{1,0:T(8,128)(2,1)S(1)} %out_payload.1.refs_0_), channel_id=1, source_target_pairs={{0,4},{1,5},{2,6},{3,7},{4,0},{5,1},{6,2},{7,3},{8,12},{9,13},{10,... | collective-permute-start | bytes 368648 | tf_op jit(solution)/shard_map/ppermute | solution.py:647
  85.0 3.9 %grad_rows.3 = (bf16[512,384]{1,0:T(8,128)(2,1)S(1)}, bf16[512,384]{1,0:T(8,128)(2,1)S(1)}) custom-call(s32[2]{0:T(128)S(1)} %pad_add_fusion.where_ref, bf16[1024,2048]{1,0:T(8,128)(2,1)} %copy-done, bf16[1024,2048]{1,0:T(8,128)(2,1)} %copy-done.1, bf16[1024,768]{1,0:T(8,128)(2,1)S(1)} %get-tuple-element.120.d_own_ref, ...), custom_call_target="tpu_custom_call" | custom-call | flops 1250000000 | bytes 8750000 | tf_op jit(solution)/shard_map/grad_rows/pallas_call | solution.py:597
  92.1 5.8 %grad_rows.4 = (bf16[512,384]{1,0:T(8,128)(2,1)S(1)}, bf16[512,384]{1,0:T(8,128)(2,1)S(1)}, bf16[512,384]{1,0:T(8,128)(2,1)S(1)}, bf16[512,384]{1,0:T(8,128)(2,1)S(1)}) custom-call(s32[2]{0:T(128)S(1)} %pad_add_fusion.where_ref, bf16[1024,2048]{1,0:T(8,128)(2,1)} %copy-done, bf16[1024,2048]{1,0:T(8,128)(2,1)} %copy-done.1, ...), custom_call_target="tpu_custom_call" | custom-call | flops 2500000000 | bytes 17500000 | tf_op jit(solution)/shard_map/grad_rows/pallas_call | solution.py:597
  97.9 1.7 %collective-permute-start.39 = (bf16[512,384]{1,0:T(8,128)(2,1)S(1)}, bf16[512,384]{1,0:T(8,128)(2,1)S(1)}, u32[]{:S(2)}, u32[]{:S(2)}) collective-permute-start(bf16[512,384]{1,0:T(8,128)(2,1)S(1)} %get-tuple-element.126), channel_id=1, source_target_pairs={{0,4},{1,5},{2,6},{3,7},{4,0},{5,1},{6,2},{7,3},{8,12},{9,13},{10,... | collective-permute-start | bytes 1179656 | tf_op jit(solution)/shard_map/ppermute | solution.py:647
  101.7 1.8 %collective-permute-start.42 = (bf16[512,384]{1,0:T(8,128)(2,1)S(1)}, bf16[512,384]{1,0:T(8,128)(2,1)S(1)}, u32[]{:S(2)}, u32[]{:S(2)}) collective-permute-start(bf16[512,384]{1,0:T(8,128)(2,1)S(1)} %add_convert_fusion.3), channel_id=1, source_target_pairs={{0,2},{1,3},{2,0},{3,1},{4,6},{5,7},{6,4},{7,5},{8,10},{9,11},{10,... | collective-permute-start | bytes 1179656 | tf_op jit(solution)/shard_map/ppermute | solution.py:647
  105.0 3.6 %collective-permute-start.36 = (bf16[144,512]{1,0:T(8,128)(2,1)S(1)}, bf16[144,512]{1,0:T(8,128)(2,1)S(1)}, u32[]{:S(2)}, u32[]{:S(2)}) collective-permute-start(bf16[144,512]{1,0:T(8,128)(2,1)S(1)} %get-tuple-element.140), channel_id=1, source_target_pairs={{0,24},{8,16},{16,8},{24,0},{1,25},{9,17},{17,9},{25,1},{2,26},{10... | collective-permute-start | bytes 442376 | tf_op jit(solution)/shard_map/ppermute | solution.py:650
  109.9 2.6 %collective-permute-start.35 = (bf16[144,512]{1,0:T(8,128)(2,1)S(1)}, bf16[144,512]{1,0:T(8,128)(2,1)S(1)}, u32[]{:S(2)}, u32[]{:S(2)}) collective-permute-start(bf16[144,512]{1,0:T(8,128)(2,1)S(1)} %get-tuple-element.141), channel_id=1, source_target_pairs={{0,16},{8,24},{16,0},{24,8},{1,17},{9,25},{17,1},{25,9},{2,18},{10... | collective-permute-start | bytes 442376 | tf_op jit(solution)/shard_map/ppermute | solution.py:650
  112.5 1.6 %collective-permute-start.34 = (bf16[144,512]{1,0:T(8,128)(2,1)S(1)}, bf16[144,512]{1,0:T(8,128)(2,1)S(1)}, u32[]{:S(2)}, u32[]{:S(2)}) collective-permute-start(bf16[144,512]{1,0:T(8,128)(2,1)S(1)} %get-tuple-element.142), channel_id=1, source_target_pairs={{0,8},{8,0},{16,24},{24,16},{1,9},{9,1},{17,25},{25,17},{2,10},{10... | collective-permute-start | bytes 442376 | tf_op jit(solution)/shard_map/ppermute | solution.py:650
  114.0 3.9 %grad_rows.5 = (bf16[512,384]{1,0:T(8,128)(2,1)S(1)}, bf16[512,384]{1,0:T(8,128)(2,1)S(1)}) custom-call(s32[2]{0:T(128)S(1)} %pad_add_fusion.where_ref, bf16[1024,2048]{1,0:T(8,128)(2,1)} %copy-done, bf16[1024,2048]{1,0:T(8,128)(2,1)} %copy-done.1, bf16[1024,768]{1,0:T(8,128)(2,1)S(1)} %get-tuple-element.120.d_own_ref, ...), custom_call_target="tpu_custom_call" | custom-call | flops 1250000000 | bytes 8750000 | tf_op jit(solution)/shard_map/grad_rows/pallas_call | solution.py:597
  118.0 2.7 %collective-permute-done.35.refs_2_ = bf16[144,512]{1,0:T(8,128)(2,1)S(1)} collective-permute-done((bf16[144,512]{1,0:T(8,128)(2,1)S(1)}, bf16[144,512]{1,0:T(8,128)(2,1)S(1)}, u32[]{:S(2)}, u32[]{:S(2)}) %collective-permute-start.35) | collective-permute-done | bytes 147488 | tf_op jit(solution)/shard_map/ppermute | solution.py:650
  121.8 1.6 %collective-permute-done.43 = bf16[256,768]{1,0:T(8,128)(2,1)S(1)} collective-permute-done((bf16[256,768]{1,0:T(8,128)(2,1)S(1)}, bf16[256,768]{1,0:T(8,128)(2,1)S(1)}, u32[]{:S(2)}, u32[]{:S(2)}) %collective-permute-start.43) | collective-permute-done | bytes 393248 | tf_op jit(solution)/shard_map/ppermute | solution.py:647
  124.0 2.6 %collective-permute-start.46 = (bf16[256,384]{1,0:T(8,128)(2,1)S(1)}, bf16[256,384]{1,0:T(8,128)(2,1)S(1)}, u32[]{:S(2)}, u32[]{:S(2)}) collective-permute-start(bf16[256,384]{1,0:T(8,128)(2,1)S(1)} %get-tuple-element.136), channel_id=1, source_target_pairs={{0,24},{8,16},{16,8},{24,0},{1,25},{9,17},{17,9},{25,1},{2,26},{10... | collective-permute-start | bytes 589832 | tf_op jit(solution)/shard_map/ppermute | solution.py:650
  128.7 2.2 %collective-permute-done.44 = bf16[256,384]{1,0:T(8,128)(2,1)S(1)} collective-permute-done((bf16[256,384]{1,0:T(8,128)(2,1)S(1)}, bf16[256,384]{1,0:T(8,128)(2,1)S(1)}, u32[]{:S(2)}, u32[]{:S(2)}) %collective-permute-start.44) | collective-permute-done | bytes 196640 | tf_op jit(solution)/shard_map/ppermute | solution.py:650
  130.9 5.7 %collective-permute-done.46 = bf16[256,384]{1,0:T(8,128)(2,1)S(1)} collective-permute-done((bf16[256,384]{1,0:T(8,128)(2,1)S(1)}, bf16[256,384]{1,0:T(8,128)(2,1)S(1)}, u32[]{:S(2)}, u32[]{:S(2)}) %collective-permute-start.46) | collective-permute-done | bytes 196640 | tf_op jit(solution)/shard_map/ppermute | solution.py:650
  136.5 8.2 %collective-permute-done.45 = bf16[256,384]{1,0:T(8,128)(2,1)S(1)} collective-permute-done((bf16[256,384]{1,0:T(8,128)(2,1)S(1)}, bf16[256,384]{1,0:T(8,128)(2,1)S(1)}, u32[]{:S(2)}, u32[]{:S(2)}) %collective-permute-start.45) | collective-permute-done | bytes 196640 | tf_op jit(solution)/shard_map/ppermute | solution.py:650
  (154 shorter events, 38.0 us)
Async XLA Ops:
  3.3 22.3 %collective-permute-start.1 = (bf16[16,64,2048]{2,1,0:T(8,128)(2,1)}, bf16[16,64,2048]{2,1,0:T(8,128)(2,1)}, u32[]{:S(2)}, u32[]{:S(2)}) collective-permute-start(bf16[16,64,2048]{2,1,0:T(8,128)(2,1)} %hidden_ref.1), channel_id=1, source_target_pairs={{0,1},{1,0},{2,3},{3,2},{4,5},{5,4},{6,7},{7,6},{8,9},{9,8},{10,11... | collective-permute-start | bytes 12582920 | tf_op jit(solution)/shard_map/ppermute | solution.py:647
  3.6 18.2 %collective-permute-start.2 = (bf16[128,2048]{1,0:T(8,128)(2,1)}, bf16[128,2048]{1,0:T(8,128)(2,1)S(1)}, u32[]{:S(2)}, u32[]{:S(2)}) collective-permute-start(bf16[128,2048]{1,0:T(8,128)(2,1)} %param.12), channel_id=1, source_target_pairs={{0,1},{1,0},{2,3},{3,2},{4,5},{5,4},{6,7},{7,6},{8,9},{9,8},{10,11... | collective-permute-start | bytes 1572872 | tf_op jit(solution)/shard_map/ppermute | solution.py:647
  5.7 12.3 %collective-permute-start.4 = (bf16[512,384]{1,0:T(8,128)(2,1)S(1)}, bf16[512,384]{1,0:T(8,128)(2,1)S(1)}, u32[]{:S(2)}, u32[]{:S(2)}) collective-permute-start(bf16[512,384]{1,0:T(8,128)(2,1)S(1)} %get-tuple-element.84.a_ref), channel_id=1, source_target_pairs={{0,2},{1,3},{2,0},{3,1},{4,6},{5,7},{6,4},{7,5},{8,10},{9,11},{10,... | collective-permute-start | bytes 1179656 | tf_op jit(solution)/shard_map/ppermute | solution.py:647
  8.7 11.2 %collective-permute-start.5 = (bf16[512,384]{1,0:T(8,128)(2,1)S(1)}, bf16[512,384]{1,0:T(8,128)(2,1)S(1)}, u32[]{:S(2)}, u32[]{:S(2)}) collective-permute-start(bf16[512,384]{1,0:T(8,128)(2,1)S(1)} %get-tuple-element.83.b_ref), channel_id=1, source_target_pairs={{0,4},{1,5},{2,6},{3,7},{4,0},{5,1},{6,2},{7,3},{8,12},{9,13},{10,... | collective-permute-start | bytes 1179656 | tf_op jit(solution)/shard_map/ppermute | solution.py:647
  18.1 14.2 %collective-permute-start.7 = (bf16[512,384]{1,0:T(8,128)(2,1)S(1)}, bf16[512,384]{1,0:T(8,128)(2,1)S(1)}, u32[]{:S(2)}, u32[]{:S(2)}) collective-permute-start(bf16[512,384]{1,0:T(8,128)(2,1)S(1)} %get-tuple-element.84.a_ref), channel_id=1, source_target_pairs={{0,4},{1,5},{2,6},{3,7},{4,0},{5,1},{6,2},{7,3},{8,12},{9,13},{10,... | collective-permute-start | bytes 1179656 | tf_op jit(solution)/shard_map/ppermute | solution.py:647
  19.8 12.4 %collective-permute-start.6 = (bf16[512,384]{1,0:T(8,128)(2,1)S(1)}, bf16[512,384]{1,0:T(8,128)(2,1)S(1)}, u32[]{:S(2)}, u32[]{:S(2)}) collective-permute-start(bf16[512,384]{1,0:T(8,128)(2,1)S(1)} %get-tuple-element.83.b_ref), channel_id=1, source_target_pairs={{0,2},{1,3},{2,0},{3,1},{4,6},{5,7},{6,4},{7,5},{8,10},{9,11},{10,... | collective-permute-start | bytes 1179656 | tf_op jit(solution)/shard_map/ppermute | solution.py:647
  21.3 20.1 %collective-permute-start.8 = (bf16[512,384]{1,0:T(8,128)(2,1)S(1)}, bf16[512,384]{1,0:T(8,128)(2,1)S(1)}, u32[]{:S(2)}, u32[]{:S(2)}) collective-permute-start(bf16[512,384]{1,0:T(8,128)(2,1)S(1)} %collective-permute-done.4.refs_0_), channel_id=1, source_target_pairs={{0,4},{1,5},{2,6},{3,7},{4,0},{5,1},{6,2},{7,3},{8,12},{9,13},{10,... | collective-permute-start | bytes 1179656 | tf_op jit(solution)/shard_map/ppermute | solution.py:647
  24.3 18.2 %collective-permute-start.9 = (bf16[512,384]{1,0:T(8,128)(2,1)S(1)}, bf16[512,384]{1,0:T(8,128)(2,1)S(1)}, u32[]{:S(2)}, u32[]{:S(2)}) collective-permute-start(bf16[512,384]{1,0:T(8,128)(2,1)S(1)} %collective-permute-done.5.refs_3_), channel_id=1, source_target_pairs={{0,2},{1,3},{2,0},{3,1},{4,6},{5,7},{6,4},{7,5},{8,10},{9,11},{10,... | collective-permute-start | bytes 1179656 | tf_op jit(solution)/shard_map/ppermute | solution.py:647
  32.3 14.6 %collective-permute-start.19 = (bf16[256,512]{1,0:T(8,128)(2,1)S(1)}, bf16[256,512]{1,0:T(8,128)(2,1)S(1)}, u32[]{:S(2)}, u32[]{:S(2)}) collective-permute-start(bf16[256,512]{1,0:T(8,128)(2,1)S(1)} %get-tuple-element.101.refs_1_), channel_id=1, source_target_pairs={{0,4},{1,5},{2,6},{3,7},{4,0},{5,1},{6,2},{7,3},{8,12},{9,13},{10,... | collective-permute-start | bytes 786440 | tf_op jit(solution)/shard_map/ppermute | solution.py:647
  33.2 23.1 %collective-permute-start.15 = (bf16[256,512]{1,0:T(8,128)(2,1)S(1)}, bf16[256,512]{1,0:T(8,128)(2,1)S(1)}, u32[]{:S(2)}, u32[]{:S(2)}) collective-permute-start(bf16[256,512]{1,0:T(8,128)(2,1)S(1)} %get-tuple-element.101.refs_1_), channel_id=1, source_target_pairs={{0,2},{1,3},{2,0},{3,1},{4,6},{5,7},{6,4},{7,5},{8,10},{9,11},{10,... | collective-permute-start | bytes 786440 | tf_op jit(solution)/shard_map/ppermute | solution.py:647
  37.6 19.2 %collective-permute-start.18 = (bf16[256,512]{1,0:T(8,128)(2,1)S(1)}, bf16[256,512]{1,0:T(8,128)(2,1)S(1)}, u32[]{:S(2)}, u32[]{:S(2)}) collective-permute-start(bf16[256,512]{1,0:T(8,128)(2,1)S(1)} %get-tuple-element.100.refs_0_), channel_id=1, source_target_pairs={{0,4},{1,5},{2,6},{3,7},{4,0},{5,1},{6,2},{7,3},{8,12},{9,13},{10,... | collective-permute-start | bytes 786440 | tf_op jit(solution)/shard_map/ppermute | solution.py:647
  41.5 8.9 %collective-permute-start.14 = (bf16[256,512]{1,0:T(8,128)(2,1)S(1)}, bf16[256,512]{1,0:T(8,128)(2,1)S(1)}, u32[]{:S(2)}, u32[]{:S(2)}) collective-permute-start(bf16[256,512]{1,0:T(8,128)(2,1)S(1)} %get-tuple-element.100.refs_0_), channel_id=1, source_target_pairs={{0,2},{1,3},{2,0},{3,1},{4,6},{5,7},{6,4},{7,5},{8,10},{9,11},{10,... | collective-permute-start | bytes 786440 | tf_op jit(solution)/shard_map/ppermute | solution.py:647
  46.9 10.0 %collective-permute-start.23 = (bf16[256,512]{1,0:T(8,128)(2,1)S(1)}, bf16[256,512]{1,0:T(8,128)(2,1)S(1)}, u32[]{:S(2)}, u32[]{:S(2)}) collective-permute-start(bf16[256,512]{1,0:T(8,128)(2,1)S(1)} %collective-permute-done.19.refs_9_), channel_id=1, source_target_pairs={{0,2},{1,3},{2,0},{3,1},{4,6},{5,7},{6,4},{7,5},{8,10},{9,11},{10,... | collective-permute-start | bytes 786440 | tf_op jit(solution)/shard_map/ppermute | solution.py:647
  50.4 7.0 %collective-permute-start.22 = (bf16[256,512]{1,0:T(8,128)(2,1)S(1)}, bf16[256,512]{1,0:T(8,128)(2,1)S(1)}, u32[]{:S(2)}, u32[]{:S(2)}) collective-permute-start(bf16[256,512]{1,0:T(8,128)(2,1)S(1)} %collective-permute-done.14.refs_4_), channel_id=1, source_target_pairs={{0,4},{1,5},{2,6},{3,7},{4,0},{5,1},{6,2},{7,3},{8,12},{9,13},{10,... | collective-permute-start | bytes 786440 | tf_op jit(solution)/shard_map/ppermute | solution.py:647
  64.6 9.9 %collective-permute-start.27 = (f32[32,128]{1,0:T(8,128)S(1)}, f32[32,128]{1,0:T(8,128)S(1)}, u32[]{:S(2)}, u32[]{:S(2)}) collective-permute-start(f32[32,128]{1,0:T(8,128)S(1)} %get-tuple-element.116.refs_0_), channel_id=1, source_target_pairs={{0,4},{2,6},{4,0},{5,9},{6,2},{7,11},{8,12},{9,5},{10,14},{11,7},{... | collective-permute-start | bytes 49160 | tf_op jit(solution)/shard_map/ppermute | solution.py:667
  67.0 7.5 %collective-permute-start.26 = (f32[32,128]{1,0:T(8,128)S(1)}, f32[32,128]{1,0:T(8,128)S(1)}, u32[]{:S(2)}, u32[]{:S(2)}) collective-permute-start(f32[32,128]{1,0:T(8,128)S(1)} %get-tuple-element.116.refs_0_), channel_id=1, source_target_pairs={{0,2},{2,0},{3,5},{4,6},{5,3},{6,4},{7,9},{8,10},{9,7},{10,8},{11,... | collective-permute-start | bytes 49160 | tf_op jit(solution)/shard_map/ppermute | solution.py:667
  81.4 9.6 %collective-permute-start.32 = (bf16[32,1920]{1,0:T(8,128)(2,1)S(1)}, bf16[32,1920]{1,0:T(8,128)(2,1)S(1)}, u32[]{:S(2)}, u32[]{:S(2)}) collective-permute-start(bf16[32,1920]{1,0:T(8,128)(2,1)S(1)} %out_payload.1.refs_0_), channel_id=1, source_target_pairs={{0,6},{1,7},{2,4},{3,5},{4,2},{5,3},{6,0},{7,1},{8,14},{9,15},{10,... | collective-permute-start | bytes 368648 | tf_op jit(solution)/shard_map/ppermute | solution.py:647
  82.9 8.1 %collective-permute-start.31 = (bf16[32,1920]{1,0:T(8,128)(2,1)S(1)}, bf16[32,1920]{1,0:T(8,128)(2,1)S(1)}, u32[]{:S(2)}, u32[]{:S(2)}) collective-permute-start(bf16[32,1920]{1,0:T(8,128)(2,1)S(1)} %out_payload.1.refs_0_), channel_id=1, source_target_pairs={{0,4},{1,5},{2,6},{3,7},{4,0},{5,1},{6,2},{7,3},{8,12},{9,13},{10,... | collective-permute-start | bytes 368648 | tf_op jit(solution)/shard_map/ppermute | solution.py:647
  84.5 6.5 %collective-permute-start.30 = (bf16[32,1920]{1,0:T(8,128)(2,1)S(1)}, bf16[32,1920]{1,0:T(8,128)(2,1)}, u32[]{:S(2)}, u32[]{:S(2)}) collective-permute-start(bf16[32,1920]{1,0:T(8,128)(2,1)S(1)} %out_payload.1.refs_0_), channel_id=1, source_target_pairs={{0,2},{1,3},{2,0},{3,1},{4,6},{5,7},{6,4},{7,5},{8,10},{9,11},{10,... | collective-permute-start | bytes 368648 | tf_op jit(solution)/shard_map/ppermute | solution.py:647
  88.9 12.7 %collective-permute-start.40 = (bf16[512,384]{1,0:T(8,128)(2,1)S(1)}, bf16[512,384]{1,0:T(8,128)(2,1)S(1)}, u32[]{:S(2)}, u32[]{:S(2)}) collective-permute-start(bf16[512,384]{1,0:T(8,128)(2,1)S(1)} %get-tuple-element.127), channel_id=1, source_target_pairs={{0,4},{1,5},{2,6},{3,7},{4,0},{5,1},{6,2},{7,3},{8,12},{9,13},{10,... | collective-permute-start | bytes 1179656 | tf_op jit(solution)/shard_map/ppermute | solution.py:647
  89.6 11.2 %collective-permute-start.38 = (bf16[512,384]{1,0:T(8,128)(2,1)S(1)}, bf16[512,384]{1,0:T(8,128)(2,1)S(1)}, u32[]{:S(2)}, u32[]{:S(2)}) collective-permute-start(bf16[512,384]{1,0:T(8,128)(2,1)S(1)} %get-tuple-element.122), channel_id=1, source_target_pairs={{0,2},{1,3},{2,0},{3,1},{4,6},{5,7},{6,4},{7,5},{8,10},{9,11},{10,... | collective-permute-start | bytes 1179656 | tf_op jit(solution)/shard_map/ppermute | solution.py:647
  92.0 11.5 %collective-permute-start.33 = (bf16[128,1920]{1,0:T(8,128)(2,1)S(1)}, bf16[128,1920]{1,0:T(8,128)(2,1)S(1)}, u32[]{:S(2)}, u32[]{:S(2)}) collective-permute-start(bf16[128,1920]{1,0:T(8,128)(2,1)S(1)} %pad_maximum_fusion.1), channel_id=1, source_target_pairs={{0,1},{1,0},{2,3},{3,2},{4,5},{5,4},{6,7},{7,6},{8,9},{9,8},{10,11... | collective-permute-start | bytes 1474568 | tf_op jit(solution)/shard_map/ppermute | solution.py:647
  97.9 12.0 %collective-permute-start.39 = (bf16[512,384]{1,0:T(8,128)(2,1)S(1)}, bf16[512,384]{1,0:T(8,128)(2,1)S(1)}, u32[]{:S(2)}, u32[]{:S(2)}) collective-permute-start(bf16[512,384]{1,0:T(8,128)(2,1)S(1)} %get-tuple-element.126), channel_id=1, source_target_pairs={{0,4},{1,5},{2,6},{3,7},{4,0},{5,1},{6,2},{7,3},{8,12},{9,13},{10,... | collective-permute-start | bytes 1179656 | tf_op jit(solution)/shard_map/ppermute | solution.py:647
  99.6 12.9 %collective-permute-start.37 = (bf16[512,384]{1,0:T(8,128)(2,1)S(1)}, bf16[512,384]{1,0:T(8,128)(2,1)S(1)}, u32[]{:S(2)}, u32[]{:S(2)}) collective-permute-start(bf16[512,384]{1,0:T(8,128)(2,1)S(1)} %get-tuple-element.124), channel_id=1, source_target_pairs={{0,2},{1,3},{2,0},{3,1},{4,6},{5,7},{6,4},{7,5},{8,10},{9,11},{10,... | collective-permute-start | bytes 1179656 | tf_op jit(solution)/shard_map/ppermute | solution.py:647
  101.0 19.7 %collective-permute-start.41 = (bf16[512,384]{1,0:T(8,128)(2,1)S(1)}, bf16[512,384]{1,0:T(8,128)(2,1)S(1)}, u32[]{:S(2)}, u32[]{:S(2)}) collective-permute-start(bf16[512,384]{1,0:T(8,128)(2,1)S(1)} %add_convert_fusion.4), channel_id=1, source_target_pairs={{0,4},{1,5},{2,6},{3,7},{4,0},{5,1},{6,2},{7,3},{8,12},{9,13},{10,... | collective-permute-start | bytes 1179656 | tf_op jit(solution)/shard_map/ppermute | solution.py:647
  101.7 18.9 %collective-permute-start.42 = (bf16[512,384]{1,0:T(8,128)(2,1)S(1)}, bf16[512,384]{1,0:T(8,128)(2,1)S(1)}, u32[]{:S(2)}, u32[]{:S(2)}) collective-permute-start(bf16[512,384]{1,0:T(8,128)(2,1)S(1)} %add_convert_fusion.3), channel_id=1, source_target_pairs={{0,2},{1,3},{2,0},{3,1},{4,6},{5,7},{6,4},{7,5},{8,10},{9,11},{10,... | collective-permute-start | bytes 1179656 | tf_op jit(solution)/shard_map/ppermute | solution.py:647
  105.0 12.9 %collective-permute-start.36 = (bf16[144,512]{1,0:T(8,128)(2,1)S(1)}, bf16[144,512]{1,0:T(8,128)(2,1)S(1)}, u32[]{:S(2)}, u32[]{:S(2)}) collective-permute-start(bf16[144,512]{1,0:T(8,128)(2,1)S(1)} %get-tuple-element.140), channel_id=1, source_target_pairs={{0,24},{8,16},{16,8},{24,0},{1,25},{9,17},{17,9},{25,1},{2,26},{10... | collective-permute-start | bytes 442376 | tf_op jit(solution)/shard_map/ppermute | solution.py:650
  109.9 10.8 %collective-permute-start.35 = (bf16[144,512]{1,0:T(8,128)(2,1)S(1)}, bf16[144,512]{1,0:T(8,128)(2,1)S(1)}, u32[]{:S(2)}, u32[]{:S(2)}) collective-permute-start(bf16[144,512]{1,0:T(8,128)(2,1)S(1)} %get-tuple-element.141), channel_id=1, source_target_pairs={{0,16},{8,24},{16,0},{24,8},{1,17},{9,25},{17,1},{25,9},{2,18},{10... | collective-permute-start | bytes 442376 | tf_op jit(solution)/shard_map/ppermute | solution.py:650
  112.5 8.2 %collective-permute-start.34 = (bf16[144,512]{1,0:T(8,128)(2,1)S(1)}, bf16[144,512]{1,0:T(8,128)(2,1)S(1)}, u32[]{:S(2)}, u32[]{:S(2)}) collective-permute-start(bf16[144,512]{1,0:T(8,128)(2,1)S(1)} %get-tuple-element.142), channel_id=1, source_target_pairs={{0,8},{8,0},{16,24},{24,16},{1,9},{9,1},{17,25},{25,17},{2,10},{10... | collective-permute-start | bytes 442376 | tf_op jit(solution)/shard_map/ppermute | solution.py:650
  123.9 7.0 %collective-permute-start.44 = (bf16[256,384]{1,0:T(8,128)(2,1)S(1)}, bf16[256,384]{1,0:T(8,128)(2,1)S(1)}, u32[]{:S(2)}, u32[]{:S(2)}) collective-permute-start(bf16[256,384]{1,0:T(8,128)(2,1)S(1)} %get-tuple-element.135), channel_id=1, source_target_pairs={{0,8},{8,0},{16,24},{24,16},{1,9},{9,1},{17,25},{25,17},{2,10},{10... | collective-permute-start | bytes 589832 | tf_op jit(solution)/shard_map/ppermute | solution.py:650
  124.0 12.5 %collective-permute-start.46 = (bf16[256,384]{1,0:T(8,128)(2,1)S(1)}, bf16[256,384]{1,0:T(8,128)(2,1)S(1)}, u32[]{:S(2)}, u32[]{:S(2)}) collective-permute-start(bf16[256,384]{1,0:T(8,128)(2,1)S(1)} %get-tuple-element.136), channel_id=1, source_target_pairs={{0,24},{8,16},{16,8},{24,0},{1,25},{9,17},{17,9},{25,1},{2,26},{10... | collective-permute-start | bytes 589832 | tf_op jit(solution)/shard_map/ppermute | solution.py:650
  126.6 18.1 %collective-permute-start.45 = (bf16[256,384]{1,0:T(8,128)(2,1)S(1)}, bf16[256,384]{1,0:T(8,128)(2,1)S(1)}, u32[]{:S(2)}, u32[]{:S(2)}) collective-permute-start(bf16[256,384]{1,0:T(8,128)(2,1)S(1)} %get-tuple-element.137), channel_id=1, source_target_pairs={{0,16},{8,24},{16,0},{24,8},{1,17},{9,25},{17,1},{25,9},{2,18},{10... | collective-permute-start | bytes 589832 | tf_op jit(solution)/shard_map/ppermute | solution.py:650
  (36 other events, 195.2 us)

commit v9 on v8

--- a/solution.py
+++ b/solution.py
@@ -813,7 +813,11 @@
         first_a = {s ^ flag_a: across(parts_a[s], bits[0]) for s in lead}
         first_b = {s ^ flag_b: across(parts_b[s], bits[-1]) for s in lead}
         plane = [payload] + [across(payload, 2 * s) for s in range(1, chips)]
-        more_a, more_b = grads(rest, parts_a, plane)
+        more_a, more_b = {}, {}
+        for s in rest:
+            block_a, block_b = grads([s], parts_a, plane, more_a)
+            more_a.update(block_a)
+            more_b.update(block_b)
         far = across(jnp.concatenate(plane, 0), 1)
         for s in rest:
             if s & flag_a:

time: 146 us -> 148 us (1.014)
  Pallas kernels: 57.2 us -> 59.3 us
  waiting for transfers between devices: 29.7 us -> 31.7 us
  starting transfers between devices: 47.9 us -> 46 us
    pallas_call x3 -> x4, Pallas kernels: 13.6 us -> 15.7 us  [grad_blocks(): pl.pallas_call(functools.partial(grad_kernel, tuple(blocks)), in_specs=[p...]
    ppermute x6, starting transfers between devices: 11.3 us -> 9.45 us  [along(): lax.ppermute(value, 'list', [(i, i ^ distance) for i in range(n_list)])]
    ppermute x6, waiting for transfers between devices: 18.7 us -> 20.5 us  [along(): lax.ppermute(value, 'list', [(i, i ^ distance) for i in range(n_list)])]
  transfers between devices with their start and end apart: 47 -> 47, of which waited for: 15 -> 15; matrix products, arithmetic and copies ran while one was open for 3% -> 3% of each run, Pallas kernels for 36% -> 37%
where the time goes in v9:
time: 148 us
  Pallas kernels  59.3 us (40%)
  starting transfers between devices  46 us (31%)
  waiting for transfers between devices  31.7 us (21%)
  local copies, waits for them, and re-layouts  4.79 us (3%)
  other arithmetic  4.7 us (3%)
    ppermute x39, starting transfers between devices, across(): lax.ppermute(value, 'fsdp', [(i, i ^ distance) for i in range(n_fsdp)])  30.6 us
    pallas_call x6, Pallas kernels, local_call(): pl.pallas_call(kernel, in_specs=[pl.BlockSpec(memory_space=pltpu.SMEM)] +...  22.5 us
    ppermute x6, waiting for transfers between devices, along(): lax.ppermute(value, 'list', [(i, i ^ distance) for i in range(n_list)])  20.5 us
    pallas_call x4, Pallas kernels, grad_blocks(): pl.pallas_call(functools.partial(grad_kernel, tuple(blocks)), in_specs=[p...  15.7 us
    pallas_call x2, Pallas kernels, norm(): pl.pallas_call(norm_kernel, grid_spec=pltpu.PrefetchScalarGridSpec(num_sc...  13.1 us
    ppermute x39, waiting for transfers between devices, across(): lax.ppermute(value, 'fsdp', [(i, i ^ distance) for i in range(n_fsdp)])  11.1 us
    ppermute x6, starting transfers between devices, along(): lax.ppermute(value, 'list', [(i, i ^ distance) for i in range(n_list)])  9.45 us
    ppermute x2, starting transfers between devices, neighbour(): return lax.ppermute(value, ('list', 'fsdp'), moves)  5.89 us
  transfers between devices with their start and end apart: 47, of which 15 were waited for; matrix products, arithmetic and copies ran while one was open for 3% of the time, Pallas kernels for 37%

profile of v9, /device:TPU:0, one launch (start us, length us, event | category | flops | bytes accessed | tf_op | source)
XLA Modules:
  0.0 147.7 jit_solution(10065864834038015717)
XLA Ops:
  1.1 2.1 %collective-permute-done.come_ref = bf16[256,1536]{1,0:T(8,128)(2,1)S(1)} collective-permute-done((bf16[256,1536]{1,0:T(8,128)(2,1)}, bf16[256,1536]{1,0:T(8,128)(2,1)S(1)}, u32[]{:S(2)}, u32[]{:S(2)}) %collective-permute-start) | collective-permute-done | bytes 786464 | tf_op jit(solution)/shard_map/ppermute | solution.py:647
  5.7 2.9 %collective-permute-start.4 = (bf16[512,384]{1,0:T(8,128)(2,1)S(1)}, bf16[512,384]{1,0:T(8,128)(2,1)S(1)}, u32[]{:S(2)}, u32[]{:S(2)}) collective-permute-start(bf16[512,384]{1,0:T(8,128)(2,1)S(1)} %get-tuple-element.85.a_ref), channel_id=1, source_target_pairs={{0,2},{1,3},{2,0},{3,1},{4,6},{5,7},{6,4},{7,5},{8,10},{9,11},{10,... | collective-permute-start | bytes 1179656 | tf_op jit(solution)/shard_map/ppermute | solution.py:647
  8.7 1.5 %collective-permute-start.5 = (bf16[512,384]{1,0:T(8,128)(2,1)S(1)}, bf16[512,384]{1,0:T(8,128)(2,1)S(1)}, u32[]{:S(2)}, u32[]{:S(2)}) collective-permute-start(bf16[512,384]{1,0:T(8,128)(2,1)S(1)} %get-tuple-element.84.b_ref), channel_id=1, source_target_pairs={{0,4},{1,5},{2,6},{3,7},{4,0},{5,1},{6,2},{7,3},{8,12},{9,13},{10,... | collective-permute-start | bytes 1179656 | tf_op jit(solution)/shard_map/ppermute | solution.py:647
  11.0 6.5 %norm_project.2 = (bf16[1024,2048]{1,0:T(8,128)(2,1)S(1)}, f32[4,4,2048]{2,1,0:T(4,128)S(1)}, f32[1024,768]{1,0:T(8,128)S(1)}) custom-call(s32[2]{0:T(128)S(1)} %pad_add_fusion.where_ref, bf16[16,64,2048]{2,1,0:T(8,128)(2,1)} %hidden_ref.1, f32[1,2048]{1,0:T(1,128)S(1)} %bitcast.23, bf16[512,384]{1,0:T(8,128)(2,1)S(1)} %get-tuple-element.85.a_ref, ...), custom_call_target="tpu_custom_call" | custom-call | flops 3500000000 | bytes 24500000 | tf_op jit(solution)/shard_map/norm_project/pallas_call | solution.py:65
  18.1 1.8 %collective-permute-start.7 = (bf16[512,384]{1,0:T(8,128)(2,1)S(1)}, bf16[512,384]{1,0:T(8,128)(2,1)S(1)}, u32[]{:S(2)}, u32[]{:S(2)}) collective-permute-start(bf16[512,384]{1,0:T(8,128)(2,1)S(1)} %get-tuple-element.85.a_ref), channel_id=1, source_target_pairs={{0,4},{1,5},{2,6},{3,7},{4,0},{5,1},{6,2},{7,3},{8,12},{9,13},{10,... | collective-permute-start | bytes 1179656 | tf_op jit(solution)/shard_map/ppermute | solution.py:647
  22.6 1.6 %maximum_select_fusion = bf16[256,2048]{1,0:T(8,128)(2,1)S(1)} fusion(bf16[128,2048]{1,0:T(8,128)(2,1)} %copy-done.15, bf16[128,2048]{1,0:T(8,128)(2,1)S(1)} %copy-done.14, pred[]{:T(512)S(6)} %eq.9), kind=kLoop, calls=%fused_computation | loop fusion | flops 4718592 | bytes 2097153 | tf_op jit(solution)/shard_map/jit(_where)/select_n | solution.py:708
  25.6 6.6 %norm_project.3 = (bf16[1024,2048]{1,0:T(8,128)(2,1)S(1)}, f32[4,4,2048]{2,1,0:T(4,128)S(1)}, f32[1024,768]{1,0:T(8,128)S(1)}) custom-call(s32[2]{0:T(128)S(1)} %pad_add_fusion.where_ref, bf16[16,64,2048]{2,1,0:T(8,128)(2,1)} %collective-permute-done.1.hidden_ref, f32[1,2048]{1,0:T(1,128)S(1)} %bitcast.24, bf16[512,384]{1,0:T(8,128)(2,1)S(1)} %get-tuple-element.85.a_ref, ...), custom_call_target="tpu_custom_call" | custom-call | flops 3500000000 | bytes 24500000 | tf_op jit(solution)/shard_map/norm_project/pallas_call | solution.py:65
  34.7 2.9 %project_more.2.before_ref = f32[1024,768]{1,0:T(8,128)S(1)} custom-call(s32[2]{0:T(128)S(1)} %pad_add_fusion.where_ref, bf16[1024,2048]{1,0:T(8,128)(2,1)S(1)} %get-tuple-element.93.rows_ref.own_ref, f32[1024,768]{1,0:T(8,128)S(1)} %get-tuple-element.74.before_ref, bf16[512,384]{1,0:T(8,128)(2,1)S(1)} %collective-permute-done.4.refs_0_, ...), custom_call_target="tpu_custom_call" | custom-call | flops 2249999872 | bytes 15750000 | tf_op jit(solution)/shard_map/project_more/pallas_call | solution.py:200
  38.5 2.9 %project_more.3.before_ref = f32[1024,768]{1,0:T(8,128)S(1)} custom-call(s32[2]{0:T(128)S(1)} %pad_add_fusion.where_ref, bf16[1024,2048]{1,0:T(8,128)(2,1)S(1)} %get-tuple-element.86.rows_ref.sib_ref, f32[1024,768]{1,0:T(8,128)S(1)} %get-tuple-element.82.before_ref, bf16[512,384]{1,0:T(8,128)(2,1)S(1)} %collective-permute-done.4.refs_0_, ...), custom_call_target="tpu_custom_call" | custom-call | flops 2249999872 | bytes 15750000 | tf_op jit(solution)/shard_map/project_more/pallas_call | solution.py:200
  42.5 4.4 %project_attend.2 = (bf16[1024,768]{1,0:T(8,128)(2,1)S(1)}, bf16[2,2,1024,128]{3,2,1,0:T(8,128)(2,1)S(1)}, f32[2,8,512]{2,1,0:T(8,128)S(1)}) custom-call(s32[2]{0:T(128)S(1)} %pad_add_fusion.where_ref, bf16[1024,2048]{1,0:T(8,128)(2,1)S(1)} %get-tuple-element.86.rows_ref.sib_ref, f32[1024,768]{1,0:T(8,128)S(1)} %project_more.3.before_ref, ...), custom_call_target="tpu_custom_call" | custom-call | flops 3249999872 | bytes 22750000 | tf_op jit(solution)/shard_map/project_attend/pallas_call | solution.py:200
  48.0 2.3 %collective-permute-done.14.refs_4_ = bf16[256,512]{1,0:T(8,128)(2,1)S(1)} collective-permute-done((bf16[256,512]{1,0:T(8,128)(2,1)S(1)}, bf16[256,512]{1,0:T(8,128)(2,1)S(1)}, u32[]{:S(2)}, u32[]{:S(2)}) %collective-permute-start.14) | collective-permute-done | bytes 262176 | tf_op jit(solution)/shard_map/ppermute | solution.py:647
  51.9 4.4 %project_attend.3 = (bf16[1024,768]{1,0:T(8,128)(2,1)S(1)}, bf16[2,2,1024,128]{3,2,1,0:T(8,128)(2,1)S(1)}, f32[2,8,512]{2,1,0:T(8,128)S(1)}) custom-call(s32[2]{0:T(128)S(1)} %pad_add_fusion.where_ref, bf16[1024,2048]{1,0:T(8,128)(2,1)S(1)} %get-tuple-element.93.rows_ref.own_ref, f32[1024,768]{1,0:T(8,128)S(1)} %project_more.2.before_ref, ...), custom_call_target="tpu_custom_call" | custom-call | flops 3249999872 | bytes 22750000 | tf_op jit(solution)/shard_map/project_attend/pallas_call | solution.py:200
  61.7 2.9 %pool_score.1 = (f32[32,128]{1,0:T(8,128)S(1)}, bf16[32,1024]{1,0:T(8,128)(2,1)S(1)}, f32[32,512]{1,0:T(8,128)S(1)}, f32[32,1024]{1,0:T(8,128)S(1)}) custom-call(s32[2]{0:T(128)S(1)} %pad_add_fusion.where_ref, f32[16,512]{1,0:T(8,128)S(1)} %bitcast.20, f32[16,512]{1,0:T(8,128)S(1)} %bitcast.18, f32[16,512]{1,0:T(8,128)S(1)} %collective-permute-done.10.own_far_ref, ...), custom_call_target="tpu_custom_call" | custom-call | flops 1000000000 | bytes 7000000 | tf_op jit(solution)/shard_map/pool_score/pallas_call | solution.py:373
  64.6 2.4 %collective-permute-start.27 = (f32[32,128]{1,0:T(8,128)S(1)}, f32[32,128]{1,0:T(8,128)S(1)}, u32[]{:S(2)}, u32[]{:S(2)}) collective-permute-start(f32[32,128]{1,0:T(8,128)S(1)} %get-tuple-element.117.refs_0_), channel_id=1, source_target_pairs={{0,4},{2,6},{4,0},{5,9},{6,2},{7,11},{8,12},{9,5},{10,14},{11,7},{... | collective-permute-start | bytes 49160 | tf_op jit(solution)/shard_map/ppermute | solution.py:667
  67.0 3.5 %collective-permute-start.26 = (f32[32,128]{1,0:T(8,128)S(1)}, f32[32,128]{1,0:T(8,128)S(1)}, u32[]{:S(2)}, u32[]{:S(2)}) collective-permute-start(f32[32,128]{1,0:T(8,128)S(1)} %get-tuple-element.117.refs_0_), channel_id=1, source_target_pairs={{0,2},{2,0},{3,5},{4,6},{5,3},{6,4},{7,9},{8,10},{9,7},{10,8},{11,... | collective-permute-start | bytes 49160 | tf_op jit(solution)/shard_map/ppermute | solution.py:667
  70.5 3.9 %attend_back.2.own_ref = bf16[1024,768]{1,0:T(8,128)(2,1)S(1)} custom-call(s32[2]{0:T(128)S(1)} %pad_add_fusion.where_ref, bf16[2,2,1024,128]{3,2,1,0:T(8,128)(2,1)S(1)} %get-tuple-element.100.probs_ref, bf16[1024,768]{1,0:T(8,128)(2,1)S(1)} %get-tuple-element.113.projected_ref, f32[2,8,512]{2,1,0:T(8,128)S(1)} %get-tuple-element.153.d_ref), custom_call_target="tpu_custom_call" | custom-call | flops 1700000000 | bytes 11900000 | tf_op jit(solution)/shard_map/attend_back/pallas_call | solution.py:200
  75.0 3.9 %attend_back.3.sib_ref = bf16[1024,768]{1,0:T(8,128)(2,1)S(1)} custom-call(s32[2]{0:T(128)S(1)} %pad_add_fusion.where_ref, bf16[2,2,1024,128]{3,2,1,0:T(8,128)(2,1)S(1)} %get-tuple-element.115.probs_ref, bf16[1024,768]{1,0:T(8,128)(2,1)S(1)} %get-tuple-element.116.projected_ref, f32[2,8,512]{2,1,0:T(8,128)S(1)} %get-tuple-element.152.d_ref), custom_call_target="tpu_custom_call" | custom-call | flops 1700000000 | bytes 11900000 | tf_op jit(solution)/shard_map/attend_back/pallas_call | solution.py:200
  79.0 1.8 %list_grad.1 = (bf16[32,1024]{1,0:T(8,128)(2,1)S(1)}, f32[8,128]{1,0:T(8,128)S(1)}, bf16[1024,768]{1,0:T(8,128)(2,1)S(1)}, bf16[1024,768]{1,0:T(8,128)(2,1)S(1)}) custom-call(s32[2]{0:T(128)S(1)} %pad_add_fusion.where_ref, s32[5]{0:T(128)S(1)} %stack.35.place_ref, s32[8,128]{1,0:T(8,128)S(1)} %broadcast_in_dim.13.bounds_ref, ...), custom_call_target="tpu_custom_call" | custom-call | flops 1250000000 | bytes 8750000 | tf_op jit(solution)/shard_map/list_grad/pallas_call | solution.py:442
  82.9 1.6 %collective-permute-start.31 = (bf16[32,1920]{1,0:T(8,128)(2,1)S(1)}, bf16[32,1920]{1,0:T(8,128)(2,1)S(1)}, u32[]{:S(2)}, u32[]{:S(2)}) collective-permute-start(bf16[32,1920]{1,0:T(8,128)(2,1)S(1)} %out_payload.1.refs_0_), channel_id=1, source_target_pairs={{0,4},{1,5},{2,6},{3,7},{4,0},{5,1},{6,2},{7,3},{8,12},{9,13},{10,... | collective-permute-start | bytes 368648 | tf_op jit(solution)/shard_map/ppermute | solution.py:647
  85.0 3.9 %grad_rows.4 = (bf16[512,384]{1,0:T(8,128)(2,1)S(1)}, bf16[512,384]{1,0:T(8,128)(2,1)S(1)}) custom-call(s32[2]{0:T(128)S(1)} %pad_add_fusion.where_ref, bf16[1024,2048]{1,0:T(8,128)(2,1)} %copy-done, bf16[1024,2048]{1,0:T(8,128)(2,1)} %copy-done.1, bf16[1024,768]{1,0:T(8,128)(2,1)S(1)} %get-tuple-element.121.d_own_ref, ...), custom_call_target="tpu_custom_call" | custom-call | flops 1250000000 | bytes 8750000 | tf_op jit(solution)/shard_map/grad_rows/pallas_call | solution.py:597
  92.1 3.9 %grad_rows.5 = (bf16[512,384]{1,0:T(8,128)(2,1)S(1)}, bf16[512,384]{1,0:T(8,128)(2,1)S(1)}) custom-call(s32[2]{0:T(128)S(1)} %pad_add_fusion.where_ref, bf16[1024,2048]{1,0:T(8,128)(2,1)} %copy-done, bf16[1024,2048]{1,0:T(8,128)(2,1)} %copy-done.1, bf16[1024,768]{1,0:T(8,128)(2,1)S(1)} %get-tuple-element.121.d_own_ref, ...), custom_call_target="tpu_custom_call" | custom-call | flops 1250000000 | bytes 8750000 | tf_op jit(solution)/shard_map/grad_rows/pallas_call | solution.py:597
  96.8 3.9 %grad_rows.6 = (bf16[512,384]{1,0:T(8,128)(2,1)S(1)}, bf16[512,384]{1,0:T(8,128)(2,1)S(1)}) custom-call(s32[2]{0:T(128)S(1)} %pad_add_fusion.where_ref, bf16[1024,2048]{1,0:T(8,128)(2,1)} %copy-done, bf16[1024,2048]{1,0:T(8,128)(2,1)} %copy-done.1, bf16[1024,768]{1,0:T(8,128)(2,1)S(1)} %get-tuple-element.121.d_own_ref, ...), custom_call_target="tpu_custom_call" | custom-call | flops 1250000000 | bytes 8750000 | tf_op jit(solution)/shard_map/grad_rows/pallas_call | solution.py:597
  103.1 1.7 %collective-permute-start.42 = (bf16[512,384]{1,0:T(8,128)(2,1)S(1)}, bf16[512,384]{1,0:T(8,128)(2,1)S(1)}, u32[]{:S(2)}, u32[]{:S(2)}) collective-permute-start(bf16[512,384]{1,0:T(8,128)(2,1)S(1)} %add_convert_fusion.3), channel_id=1, source_target_pairs={{0,2},{1,3},{2,0},{3,1},{4,6},{5,7},{6,4},{7,5},{8,10},{9,11},{10,... | collective-permute-start | bytes 1179656 | tf_op jit(solution)/shard_map/ppermute | solution.py:647
  107.1 3.7 %collective-permute-start.36 = (bf16[144,512]{1,0:T(8,128)(2,1)S(1)}, bf16[144,512]{1,0:T(8,128)(2,1)S(1)}, u32[]{:S(2)}, u32[]{:S(2)}) collective-permute-start(bf16[144,512]{1,0:T(8,128)(2,1)S(1)} %get-tuple-element.142), channel_id=1, source_target_pairs={{0,24},{8,16},{16,8},{24,0},{1,25},{9,17},{17,9},{25,1},{2,26},{10... | collective-permute-start | bytes 442376 | tf_op jit(solution)/shard_map/ppermute | solution.py:650
  112.8 1.5 %collective-permute-start.34 = (bf16[144,512]{1,0:T(8,128)(2,1)S(1)}, bf16[144,512]{1,0:T(8,128)(2,1)S(1)}, u32[]{:S(2)}, u32[]{:S(2)}) collective-permute-start(bf16[144,512]{1,0:T(8,128)(2,1)S(1)} %get-tuple-element.144), channel_id=1, source_target_pairs={{0,8},{8,0},{16,24},{24,16},{1,9},{9,1},{17,25},{25,17},{2,10},{10... | collective-permute-start | bytes 442376 | tf_op jit(solution)/shard_map/ppermute | solution.py:650
  114.3 3.9 %grad_rows.7 = (bf16[512,384]{1,0:T(8,128)(2,1)S(1)}, bf16[512,384]{1,0:T(8,128)(2,1)S(1)}) custom-call(s32[2]{0:T(128)S(1)} %pad_add_fusion.where_ref, bf16[1024,2048]{1,0:T(8,128)(2,1)} %copy-done, bf16[1024,2048]{1,0:T(8,128)(2,1)} %copy-done.1, bf16[1024,768]{1,0:T(8,128)(2,1)S(1)} %get-tuple-element.121.d_own_ref, ...), custom_call_target="tpu_custom_call" | custom-call | flops 1250000000 | bytes 8750000 | tf_op jit(solution)/shard_map/grad_rows/pallas_call | solution.py:597
  118.3 4.5 %collective-permute-done.35.refs_2_ = bf16[144,512]{1,0:T(8,128)(2,1)S(1)} collective-permute-done((bf16[144,512]{1,0:T(8,128)(2,1)S(1)}, bf16[144,512]{1,0:T(8,128)(2,1)S(1)}, u32[]{:S(2)}, u32[]{:S(2)}) %collective-permute-start.35) | collective-permute-done | bytes 147488 | tf_op jit(solution)/shard_map/ppermute | solution.py:650
  123.9 1.6 %collective-permute-done.43 = bf16[256,768]{1,0:T(8,128)(2,1)S(1)} collective-permute-done((bf16[256,768]{1,0:T(8,128)(2,1)S(1)}, bf16[256,768]{1,0:T(8,128)(2,1)S(1)}, u32[]{:S(2)}, u32[]{:S(2)}) %collective-permute-start.43) | collective-permute-done | bytes 393248 | tf_op jit(solution)/shard_map/ppermute | solution.py:647
  126.1 2.5 %collective-permute-start.46 = (bf16[256,384]{1,0:T(8,128)(2,1)S(1)}, bf16[256,384]{1,0:T(8,128)(2,1)S(1)}, u32[]{:S(2)}, u32[]{:S(2)}) collective-permute-start(bf16[256,384]{1,0:T(8,128)(2,1)S(1)} %get-tuple-element.138), channel_id=1, source_target_pairs={{0,24},{8,16},{16,8},{24,0},{1,25},{9,17},{17,9},{25,1},{2,26},{10... | collective-permute-start | bytes 589832 | tf_op jit(solution)/shard_map/ppermute | solution.py:650
  130.9 2.2 %collective-permute-done.44 = bf16[256,384]{1,0:T(8,128)(2,1)S(1)} collective-permute-done((bf16[256,384]{1,0:T(8,128)(2,1)S(1)}, bf16[256,384]{1,0:T(8,128)(2,1)S(1)}, u32[]{:S(2)}, u32[]{:S(2)}) %collective-permute-start.44) | collective-permute-done | bytes 196640 | tf_op jit(solution)/shard_map/ppermute | solution.py:650
  133.0 5.5 %collective-permute-done.46 = bf16[256,384]{1,0:T(8,128)(2,1)S(1)} collective-permute-done((bf16[256,384]{1,0:T(8,128)(2,1)S(1)}, bf16[256,384]{1,0:T(8,128)(2,1)S(1)}, u32[]{:S(2)}, u32[]{:S(2)}) %collective-permute-start.46) | collective-permute-done | bytes 196640 | tf_op jit(solution)/shard_map/ppermute | solution.py:650
  138.6 8.3 %collective-permute-done.45 = bf16[256,384]{1,0:T(8,128)(2,1)S(1)} collective-permute-done((bf16[256,384]{1,0:T(8,128)(2,1)S(1)}, bf16[256,384]{1,0:T(8,128)(2,1)S(1)}, u32[]{:S(2)}, u32[]{:S(2)}) %collective-permute-start.45) | collective-permute-done | bytes 196640 | tf_op jit(solution)/shard_map/ppermute | solution.py:650
  (155 shorter events, 39.1 us)
Async XLA Ops:
  3.3 22.4 %collective-permute-start.1 = (bf16[16,64,2048]{2,1,0:T(8,128)(2,1)}, bf16[16,64,2048]{2,1,0:T(8,128)(2,1)}, u32[]{:S(2)}, u32[]{:S(2)}) collective-permute-start(bf16[16,64,2048]{2,1,0:T(8,128)(2,1)} %hidden_ref.1), channel_id=1, source_target_pairs={{0,1},{1,0},{2,3},{3,2},{4,5},{5,4},{6,7},{7,6},{8,9},{9,8},{10,11... | collective-permute-start | bytes 12582920 | tf_op jit(solution)/shard_map/ppermute | solution.py:647
  3.6 18.2 %collective-permute-start.2 = (bf16[128,2048]{1,0:T(8,128)(2,1)}, bf16[128,2048]{1,0:T(8,128)(2,1)S(1)}, u32[]{:S(2)}, u32[]{:S(2)}) collective-permute-start(bf16[128,2048]{1,0:T(8,128)(2,1)} %param.12), channel_id=1, source_target_pairs={{0,1},{1,0},{2,3},{3,2},{4,5},{5,4},{6,7},{7,6},{8,9},{9,8},{10,11... | collective-permute-start | bytes 1572872 | tf_op jit(solution)/shard_map/ppermute | solution.py:647
  5.7 12.3 %collective-permute-start.4 = (bf16[512,384]{1,0:T(8,128)(2,1)S(1)}, bf16[512,384]{1,0:T(8,128)(2,1)S(1)}, u32[]{:S(2)}, u32[]{:S(2)}) collective-permute-start(bf16[512,384]{1,0:T(8,128)(2,1)S(1)} %get-tuple-element.85.a_ref), channel_id=1, source_target_pairs={{0,2},{1,3},{2,0},{3,1},{4,6},{5,7},{6,4},{7,5},{8,10},{9,11},{10,... | collective-permute-start | bytes 1179656 | tf_op jit(solution)/shard_map/ppermute | solution.py:647
  8.7 11.2 %collective-permute-start.5 = (bf16[512,384]{1,0:T(8,128)(2,1)S(1)}, bf16[512,384]{1,0:T(8,128)(2,1)S(1)}, u32[]{:S(2)}, u32[]{:S(2)}) collective-permute-start(bf16[512,384]{1,0:T(8,128)(2,1)S(1)} %get-tuple-element.84.b_ref), channel_id=1, source_target_pairs={{0,4},{1,5},{2,6},{3,7},{4,0},{5,1},{6,2},{7,3},{8,12},{9,13},{10,... | collective-permute-start | bytes 1179656 | tf_op jit(solution)/shard_map/ppermute | solution.py:647
  18.1 14.2 %collective-permute-start.7 = (bf16[512,384]{1,0:T(8,128)(2,1)S(1)}, bf16[512,384]{1,0:T(8,128)(2,1)S(1)}, u32[]{:S(2)}, u32[]{:S(2)}) collective-permute-start(bf16[512,384]{1,0:T(8,128)(2,1)S(1)} %get-tuple-element.85.a_ref), channel_id=1, source_target_pairs={{0,4},{1,5},{2,6},{3,7},{4,0},{5,1},{6,2},{7,3},{8,12},{9,13},{10,... | collective-permute-start | bytes 1179656 | tf_op jit(solution)/shard_map/ppermute | solution.py:647
  19.8 12.5 %collective-permute-start.6 = (bf16[512,384]{1,0:T(8,128)(2,1)S(1)}, bf16[512,384]{1,0:T(8,128)(2,1)S(1)}, u32[]{:S(2)}, u32[]{:S(2)}) collective-permute-start(bf16[512,384]{1,0:T(8,128)(2,1)S(1)} %get-tuple-element.84.b_ref), channel_id=1, source_target_pairs={{0,2},{1,3},{2,0},{3,1},{4,6},{5,7},{6,4},{7,5},{8,10},{9,11},{10,... | collective-permute-start | bytes 1179656 | tf_op jit(solution)/shard_map/ppermute | solution.py:647
  21.3 20.1 %collective-permute-start.8 = (bf16[512,384]{1,0:T(8,128)(2,1)S(1)}, bf16[512,384]{1,0:T(8,128)(2,1)S(1)}, u32[]{:S(2)}, u32[]{:S(2)}) collective-permute-start(bf16[512,384]{1,0:T(8,128)(2,1)S(1)} %collective-permute-done.4.refs_0_), channel_id=1, source_target_pairs={{0,4},{1,5},{2,6},{3,7},{4,0},{5,1},{6,2},{7,3},{8,12},{9,13},{10,... | collective-permute-start | bytes 1179656 | tf_op jit(solution)/shard_map/ppermute | solution.py:647
  24.3 18.2 %collective-permute-start.9 = (bf16[512,384]{1,0:T(8,128)(2,1)S(1)}, bf16[512,384]{1,0:T(8,128)(2,1)S(1)}, u32[]{:S(2)}, u32[]{:S(2)}) collective-permute-start(bf16[512,384]{1,0:T(8,128)(2,1)S(1)} %collective-permute-done.5.refs_3_), channel_id=1, source_target_pairs={{0,2},{1,3},{2,0},{3,1},{4,6},{5,7},{6,4},{7,5},{8,10},{9,11},{10,... | collective-permute-start | bytes 1179656 | tf_op jit(solution)/shard_map/ppermute | solution.py:647
  32.4 14.6 %collective-permute-start.19 = (bf16[256,512]{1,0:T(8,128)(2,1)S(1)}, bf16[256,512]{1,0:T(8,128)(2,1)S(1)}, u32[]{:S(2)}, u32[]{:S(2)}) collective-permute-start(bf16[256,512]{1,0:T(8,128)(2,1)S(1)} %get-tuple-element.102.refs_1_), channel_id=1, source_target_pairs={{0,4},{1,5},{2,6},{3,7},{4,0},{5,1},{6,2},{7,3},{8,12},{9,13},{10,... | collective-permute-start | bytes 786440 | tf_op jit(solution)/shard_map/ppermute | solution.py:647
  33.3 23.1 %collective-permute-start.15 = (bf16[256,512]{1,0:T(8,128)(2,1)S(1)}, bf16[256,512]{1,0:T(8,128)(2,1)S(1)}, u32[]{:S(2)}, u32[]{:S(2)}) collective-permute-start(bf16[256,512]{1,0:T(8,128)(2,1)S(1)} %get-tuple-element.102.refs_1_), channel_id=1, source_target_pairs={{0,2},{1,3},{2,0},{3,1},{4,6},{5,7},{6,4},{7,5},{8,10},{9,11},{10,... | collective-permute-start | bytes 786440 | tf_op jit(solution)/shard_map/ppermute | solution.py:647
  37.7 19.1 %collective-permute-start.18 = (bf16[256,512]{1,0:T(8,128)(2,1)S(1)}, bf16[256,512]{1,0:T(8,128)(2,1)S(1)}, u32[]{:S(2)}, u32[]{:S(2)}) collective-permute-start(bf16[256,512]{1,0:T(8,128)(2,1)S(1)} %get-tuple-element.101.refs_0_), channel_id=1, source_target_pairs={{0,4},{1,5},{2,6},{3,7},{4,0},{5,1},{6,2},{7,3},{8,12},{9,13},{10,... | collective-permute-start | bytes 786440 | tf_op jit(solution)/shard_map/ppermute | solution.py:647
  41.5 8.9 %collective-permute-start.14 = (bf16[256,512]{1,0:T(8,128)(2,1)S(1)}, bf16[256,512]{1,0:T(8,128)(2,1)S(1)}, u32[]{:S(2)}, u32[]{:S(2)}) collective-permute-start(bf16[256,512]{1,0:T(8,128)(2,1)S(1)} %get-tuple-element.101.refs_0_), channel_id=1, source_target_pairs={{0,2},{1,3},{2,0},{3,1},{4,6},{5,7},{6,4},{7,5},{8,10},{9,11},{10,... | collective-permute-start | bytes 786440 | tf_op jit(solution)/shard_map/ppermute | solution.py:647
  46.9 10.0 %collective-permute-start.23 = (bf16[256,512]{1,0:T(8,128)(2,1)S(1)}, bf16[256,512]{1,0:T(8,128)(2,1)S(1)}, u32[]{:S(2)}, u32[]{:S(2)}) collective-permute-start(bf16[256,512]{1,0:T(8,128)(2,1)S(1)} %collective-permute-done.19.refs_9_), channel_id=1, source_target_pairs={{0,2},{1,3},{2,0},{3,1},{4,6},{5,7},{6,4},{7,5},{8,10},{9,11},{10,... | collective-permute-start | bytes 786440 | tf_op jit(solution)/shard_map/ppermute | solution.py:647
  50.3 7.0 %collective-permute-start.22 = (bf16[256,512]{1,0:T(8,128)(2,1)S(1)}, bf16[256,512]{1,0:T(8,128)(2,1)S(1)}, u32[]{:S(2)}, u32[]{:S(2)}) collective-permute-start(bf16[256,512]{1,0:T(8,128)(2,1)S(1)} %collective-permute-done.14.refs_4_), channel_id=1, source_target_pairs={{0,4},{1,5},{2,6},{3,7},{4,0},{5,1},{6,2},{7,3},{8,12},{9,13},{10,... | collective-permute-start | bytes 786440 | tf_op jit(solution)/shard_map/ppermute | solution.py:647
  64.6 9.9 %collective-permute-start.27 = (f32[32,128]{1,0:T(8,128)S(1)}, f32[32,128]{1,0:T(8,128)S(1)}, u32[]{:S(2)}, u32[]{:S(2)}) collective-permute-start(f32[32,128]{1,0:T(8,128)S(1)} %get-tuple-element.117.refs_0_), channel_id=1, source_target_pairs={{0,4},{2,6},{4,0},{5,9},{6,2},{7,11},{8,12},{9,5},{10,14},{11,7},{... | collective-permute-start | bytes 49160 | tf_op jit(solution)/shard_map/ppermute | solution.py:667
  67.0 7.5 %collective-permute-start.26 = (f32[32,128]{1,0:T(8,128)S(1)}, f32[32,128]{1,0:T(8,128)S(1)}, u32[]{:S(2)}, u32[]{:S(2)}) collective-permute-start(f32[32,128]{1,0:T(8,128)S(1)} %get-tuple-element.117.refs_0_), channel_id=1, source_target_pairs={{0,2},{2,0},{3,5},{4,6},{5,3},{6,4},{7,9},{8,10},{9,7},{10,8},{11,... | collective-permute-start | bytes 49160 | tf_op jit(solution)/shard_map/ppermute | solution.py:667
  81.4 9.6 %collective-permute-start.32 = (bf16[32,1920]{1,0:T(8,128)(2,1)S(1)}, bf16[32,1920]{1,0:T(8,128)(2,1)S(1)}, u32[]{:S(2)}, u32[]{:S(2)}) collective-permute-start(bf16[32,1920]{1,0:T(8,128)(2,1)S(1)} %out_payload.1.refs_0_), channel_id=1, source_target_pairs={{0,6},{1,7},{2,4},{3,5},{4,2},{5,3},{6,0},{7,1},{8,14},{9,15},{10,... | collective-permute-start | bytes 368648 | tf_op jit(solution)/shard_map/ppermute | solution.py:647
  82.9 8.1 %collective-permute-start.31 = (bf16[32,1920]{1,0:T(8,128)(2,1)S(1)}, bf16[32,1920]{1,0:T(8,128)(2,1)S(1)}, u32[]{:S(2)}, u32[]{:S(2)}) collective-permute-start(bf16[32,1920]{1,0:T(8,128)(2,1)S(1)} %out_payload.1.refs_0_), channel_id=1, source_target_pairs={{0,4},{1,5},{2,6},{3,7},{4,0},{5,1},{6,2},{7,3},{8,12},{9,13},{10,... | collective-permute-start | bytes 368648 | tf_op jit(solution)/shard_map/ppermute | solution.py:647
  84.5 6.5 %collective-permute-start.30 = (bf16[32,1920]{1,0:T(8,128)(2,1)S(1)}, bf16[32,1920]{1,0:T(8,128)(2,1)}, u32[]{:S(2)}, u32[]{:S(2)}) collective-permute-start(bf16[32,1920]{1,0:T(8,128)(2,1)S(1)} %out_payload.1.refs_0_), channel_id=1, source_target_pairs={{0,2},{1,3},{2,0},{3,1},{4,6},{5,7},{6,4},{7,5},{8,10},{9,11},{10,... | collective-permute-start | bytes 368648 | tf_op jit(solution)/shard_map/ppermute | solution.py:647
  88.9 14.1 %collective-permute-start.40 = (bf16[512,384]{1,0:T(8,128)(2,1)S(1)}, bf16[512,384]{1,0:T(8,128)(2,1)S(1)}, u32[]{:S(2)}, u32[]{:S(2)}) collective-permute-start(bf16[512,384]{1,0:T(8,128)(2,1)S(1)} %get-tuple-element.129), channel_id=1, source_target_pairs={{0,4},{1,5},{2,6},{3,7},{4,0},{5,1},{6,2},{7,3},{8,12},{9,13},{10,... | collective-permute-start | bytes 1179656 | tf_op jit(solution)/shard_map/ppermute | solution.py:647
  89.6 15.1 %collective-permute-start.38 = (bf16[512,384]{1,0:T(8,128)(2,1)S(1)}, bf16[512,384]{1,0:T(8,128)(2,1)S(1)}, u32[]{:S(2)}, u32[]{:S(2)}) collective-permute-start(bf16[512,384]{1,0:T(8,128)(2,1)S(1)} %get-tuple-element.123), channel_id=1, source_target_pairs={{0,2},{1,3},{2,0},{3,1},{4,6},{5,7},{6,4},{7,5},{8,10},{9,11},{10,... | collective-permute-start | bytes 1179656 | tf_op jit(solution)/shard_map/ppermute | solution.py:647
  92.0 13.6 %collective-permute-start.33 = (bf16[128,1920]{1,0:T(8,128)(2,1)S(1)}, bf16[128,1920]{1,0:T(8,128)(2,1)S(1)}, u32[]{:S(2)}, u32[]{:S(2)}) collective-permute-start(bf16[128,1920]{1,0:T(8,128)(2,1)S(1)} %pad_maximum_fusion.1), channel_id=1, source_target_pairs={{0,1},{1,0},{2,3},{3,2},{4,5},{5,4},{6,7},{7,6},{8,9},{9,8},{10,11... | collective-permute-start | bytes 1474568 | tf_op jit(solution)/shard_map/ppermute | solution.py:647
  96.0 14.7 %collective-permute-start.37 = (bf16[512,384]{1,0:T(8,128)(2,1)S(1)}, bf16[512,384]{1,0:T(8,128)(2,1)S(1)}, u32[]{:S(2)}, u32[]{:S(2)}) collective-permute-start(bf16[512,384]{1,0:T(8,128)(2,1)S(1)} %get-tuple-element.125), channel_id=1, source_target_pairs={{0,2},{1,3},{2,0},{3,1},{4,6},{5,7},{6,4},{7,5},{8,10},{9,11},{10,... | collective-permute-start | bytes 1179656 | tf_op jit(solution)/shard_map/ppermute | solution.py:647
  100.7 12.0 %collective-permute-start.39 = (bf16[512,384]{1,0:T(8,128)(2,1)S(1)}, bf16[512,384]{1,0:T(8,128)(2,1)S(1)}, u32[]{:S(2)}, u32[]{:S(2)}) collective-permute-start(bf16[512,384]{1,0:T(8,128)(2,1)S(1)} %get-tuple-element.128), channel_id=1, source_target_pairs={{0,4},{1,5},{2,6},{3,7},{4,0},{5,1},{6,2},{7,3},{8,12},{9,13},{10,... | collective-permute-start | bytes 1179656 | tf_op jit(solution)/shard_map/ppermute | solution.py:647
  103.1 19.7 %collective-permute-start.42 = (bf16[512,384]{1,0:T(8,128)(2,1)S(1)}, bf16[512,384]{1,0:T(8,128)(2,1)S(1)}, u32[]{:S(2)}, u32[]{:S(2)}) collective-permute-start(bf16[512,384]{1,0:T(8,128)(2,1)S(1)} %add_convert_fusion.3), channel_id=1, source_target_pairs={{0,2},{1,3},{2,0},{3,1},{4,6},{5,7},{6,4},{7,5},{8,10},{9,11},{10,... | collective-permute-start | bytes 1179656 | tf_op jit(solution)/shard_map/ppermute | solution.py:647
  104.9 17.9 %collective-permute-start.41 = (bf16[512,384]{1,0:T(8,128)(2,1)S(1)}, bf16[512,384]{1,0:T(8,128)(2,1)S(1)}, u32[]{:S(2)}, u32[]{:S(2)}) collective-permute-start(bf16[512,384]{1,0:T(8,128)(2,1)S(1)} %add_convert_fusion.4), channel_id=1, source_target_pairs={{0,4},{1,5},{2,6},{3,7},{4,0},{5,1},{6,2},{7,3},{8,12},{9,13},{10,... | collective-permute-start | bytes 1179656 | tf_op jit(solution)/shard_map/ppermute | solution.py:647
  107.1 11.2 %collective-permute-start.36 = (bf16[144,512]{1,0:T(8,128)(2,1)S(1)}, bf16[144,512]{1,0:T(8,128)(2,1)S(1)}, u32[]{:S(2)}, u32[]{:S(2)}) collective-permute-start(bf16[144,512]{1,0:T(8,128)(2,1)S(1)} %get-tuple-element.142), channel_id=1, source_target_pairs={{0,24},{8,16},{16,8},{24,0},{1,25},{9,17},{17,9},{25,1},{2,26},{10... | collective-permute-start | bytes 442376 | tf_op jit(solution)/shard_map/ppermute | solution.py:650
  110.8 12.0 %collective-permute-start.35 = (bf16[144,512]{1,0:T(8,128)(2,1)S(1)}, bf16[144,512]{1,0:T(8,128)(2,1)S(1)}, u32[]{:S(2)}, u32[]{:S(2)}) collective-permute-start(bf16[144,512]{1,0:T(8,128)(2,1)S(1)} %get-tuple-element.143), channel_id=1, source_target_pairs={{0,16},{8,24},{16,0},{24,8},{1,17},{9,25},{17,1},{25,9},{2,18},{10... | collective-permute-start | bytes 442376 | tf_op jit(solution)/shard_map/ppermute | solution.py:650
  112.8 10.0 %collective-permute-start.34 = (bf16[144,512]{1,0:T(8,128)(2,1)S(1)}, bf16[144,512]{1,0:T(8,128)(2,1)S(1)}, u32[]{:S(2)}, u32[]{:S(2)}) collective-permute-start(bf16[144,512]{1,0:T(8,128)(2,1)S(1)} %get-tuple-element.144), channel_id=1, source_target_pairs={{0,8},{8,0},{16,24},{24,16},{1,9},{9,1},{17,25},{25,17},{2,10},{10... | collective-permute-start | bytes 442376 | tf_op jit(solution)/shard_map/ppermute | solution.py:650
  126.0 7.0 %collective-permute-start.44 = (bf16[256,384]{1,0:T(8,128)(2,1)S(1)}, bf16[256,384]{1,0:T(8,128)(2,1)S(1)}, u32[]{:S(2)}, u32[]{:S(2)}) collective-permute-start(bf16[256,384]{1,0:T(8,128)(2,1)S(1)} %get-tuple-element.137), channel_id=1, source_target_pairs={{0,8},{8,0},{16,24},{24,16},{1,9},{9,1},{17,25},{25,17},{2,10},{10... | collective-permute-start | bytes 589832 | tf_op jit(solution)/shard_map/ppermute | solution.py:650
  126.1 12.5 %collective-permute-start.46 = (bf16[256,384]{1,0:T(8,128)(2,1)S(1)}, bf16[256,384]{1,0:T(8,128)(2,1)S(1)}, u32[]{:S(2)}, u32[]{:S(2)}) collective-permute-start(bf16[256,384]{1,0:T(8,128)(2,1)S(1)} %get-tuple-element.138), channel_id=1, source_target_pairs={{0,24},{8,16},{16,8},{24,0},{1,25},{9,17},{17,9},{25,1},{2,26},{10... | collective-permute-start | bytes 589832 | tf_op jit(solution)/shard_map/ppermute | solution.py:650
  128.7 18.2 %collective-permute-start.45 = (bf16[256,384]{1,0:T(8,128)(2,1)S(1)}, bf16[256,384]{1,0:T(8,128)(2,1)S(1)}, u32[]{:S(2)}, u32[]{:S(2)}) collective-permute-start(bf16[256,384]{1,0:T(8,128)(2,1)S(1)} %get-tuple-element.139), channel_id=1, source_target_pairs={{0,16},{8,24},{16,0},{24,8},{1,17},{9,25},{17,1},{25,9},{2,18},{10... | collective-permute-start | bytes 589832 | tf_op jit(solution)/shard_map/ppermute | solution.py:650
  (36 other events, 199.1 us)
